TPU v7x, 32 devices: a whole 2x2x4 slice. The times are simulated.
32 devices in a mesh: dp: 8 (over y, x, core), chan: 4 (over z).
Axes of the slice: x: 2, y: 2, z: 4, core: 2. Of those that a mesh axis runs over, the one named last changes fastest.
Arguments:
- images: bfloat16 [128, 256, 192], P('dp'), may hold values from -6 to 6
- pixel_mask: int32 [128, 256], P('dp'), may hold values from 0 to 1, as said below
- counts: int32 [128], P('dp'), may hold values from 0 to 256, as said below
- labels: int32 [128], P('dp'), may hold values from 0 to 999
- block_w: float32 [537, 9216], P(None, 'chan')
- chan_side: float32 [101, 1152], P(None, 'chan')
- head_w: float32 [320, 10240], P(None, 'chan'), may hold values from -0.3125 to 0.3125
- head_side: float32 [1280, 1002], P('chan')
- shared: float32 [5784], replicated
- block_mom: float32 [537, 9216], P(None, 'chan')
- side_mom: float32 [101, 1152], P(None, 'chan')
- head_mom: float32 [320, 10240], P(None, 'chan'), may hold values from -0.3125 to 0.3125
- hside_mom: float32 [1280, 1002], P('chan')
- shared_mom: float32 [5784], replicated
- block_ema: float32 [537, 9216], P(None, 'chan')
- side_ema: float32 [101, 1152], P(None, 'chan')
- head_ema: float32 [320, 10240], P(None, 'chan'), may hold values from -0.3125 to 0.3125
- hside_ema: float32 [1280, 1002], P('chan')
- shared_ema: float32 [5784], replicated
- chan_stats: float32 [4, 1152], P(None, 'chan')
- head_stats: float32 [2, 1280], P(None, 'chan')
- proj_stats: float32 [2, 320], P(None, 'chan')
Outputs:
- loss: float32 [], replicated
- new_block: float32 [537, 9216], P(None, 'chan')
- new_side: float32 [101, 1152], P(None, 'chan')
- new_head: float32 [320, 10240], P(None, 'chan')
- new_hside: float32 [1280, 1002], P('chan')
- new_shared: float32 [5784], replicated
- mom_block: float32 [537, 9216], P(None, 'chan')
- mom_side: float32 [101, 1152], P(None, 'chan')
- mom_head: float32 [320, 10240], P(None, 'chan')
- mom_hside: float32 [1280, 1002], P('chan')
- mom_shared: float32 [5784], replicated
- ema_block: float32 [537, 9216], P(None, 'chan')
- ema_side: float32 [101, 1152], P(None, 'chan')
- ema_head: float32 [320, 10240], P(None, 'chan')
- ema_hside: float32 [1280, 1002], P('chan')
- ema_shared: float32 [5784], replicated
- new_chan_stats: float32 [4, 1152], P(None, 'chan')
- new_head_stats: float32 [2, 1280], P(None, 'chan')
- new_proj_stats: float32 [2, 320], P(None, 'chan')
Inputs may be any that keep to these rules, and one draw needn't show every extreme that they name: `pixel_mask`: an image's ones form a rectangle of 4 to 16 rows and columns in the map's top-left corner, or the image has none; image 0 is full and image 1 empty. `counts`: the number of ones in the image's row of pixel_mask.
All inputs are finite; a program needn't handle non-finite values.
Results may differ from a plain program's by a relative error of at most 0.018.
Values may be sent and summed in bfloat16 or wider, within the bound.
A program may use at most 384 MiB of HBM per device.

v0:
```python
import jax
import jax.numpy as jnp
from jax import lax
from jax.sharding import PartitionSpec as P

WIDTH_IN = 192
WIDTH_OUT = 320
SQUEEZE = 48
CLASSES = 1000
EXPERTS = 8
KERNEL = 5
MAP_SIDE = 16


eps_norm = 0.001
highest = lax.Precision.HIGHEST


def pooled(values, pix_mask, pool_div):
    return jnp.einsum("bp,bpc->bc", pix_mask, values, precision=highest) / pool_div[:, None]


def pooled_low(values, mask_low, pool_div):
    return (
        jnp.einsum("bp,bpc->bc", mask_low, values, preferred_element_type=jnp.float32)
        / pool_div[:, None]
    )


def depthwise(values, kernels):
    count, pixels, channels = values.shape
    grid = values.reshape(count, MAP_SIDE, MAP_SIDE, channels)
    reach = KERNEL // 2
    padded = jnp.pad(grid, ((0, 0), (reach, reach), (reach, reach), (0, 0)))
    result = jnp.zeros_like(grid)
    for tap_index in range(KERNEL * KERNEL):
        row_off = tap_index // KERNEL
        col_off = tap_index % KERNEL
        result = (
            result
            + kernels[:, tap_index, None, None, :]
            * padded[:, row_off : row_off + MAP_SIDE, col_off : col_off + MAP_SIDE, :]
        )
    return result.reshape(count, pixels, channels)


def split_shared(shared):
    end_route = WIDTH_IN * EXPERTS
    end_head = end_route + WIDTH_OUT * EXPERTS
    end_norm = end_head + 2 * WIDTH_OUT
    end_squeeze = end_norm + SQUEEZE
    return (
        shared[:end_route].reshape(WIDTH_IN, EXPERTS),
        shared[end_route:end_head].reshape(WIDTH_OUT, EXPERTS),
        shared[end_head : end_head + WIDTH_OUT],
        shared[end_head + WIDTH_OUT : end_norm],
        shared[end_norm:end_squeeze],
        shared[end_squeeze:],
    )


def update(weight, grad, moment, average, grad_sq, weight_sq):
    scaled = grad * jnp.sqrt(weight_sq) * lax.rsqrt(grad_sq + 1e-12)
    moment_new = 0.5 * moment + scaled
    weight_new = weight - 0.2 * (scaled + 0.5 * moment_new)
    average_new = 0.5 * average + 0.5 * weight_new
    return (weight_new, moment_new, average_new)


def route(pooled_in, weight):
    return jax.nn.sigmoid(jnp.dot(pooled_in, weight, precision=highest))


def norm_forward(values, pix_mask, gain, bias, swish):
    mask_cols = pix_mask[:, :, None]
    first_sum = jnp.sum(mask_cols * values, axis=(0, 1))
    second_sum = jnp.sum(mask_cols * values * values, axis=(0, 1))
    first_sum, second_sum, total = lax.psum((first_sum, second_sum, jnp.sum(pix_mask)), "dp")
    mean = first_sum / total
    variance = second_sum / total - mean * mean

    def apply(values, mean, variance, gain, bias):
        normed = (values - mean) * lax.rsqrt(variance + eps_norm) * gain + bias
        if swish:
            normed = jax.nn.silu(normed)
        return normed * mask_cols

    result, backward = jax.vjp(apply, values, mean, variance, gain, bias)
    return (result, (backward, values, mean, total), (mean, variance * (total / (total - 1.0))))


def norm_backward(saved, pix_mask, grad_out):
    backward, values, mean, total = saved
    grad_values, grad_mean, grad_var, grad_gain, grad_bias = backward(grad_out)
    grad_mean, grad_var = lax.psum((grad_mean, grad_var), "dp")
    first_term = (grad_mean - 2.0 * mean * grad_var) / total
    second_term = grad_var / total
    grad_values = grad_values + pix_mask[:, :, None] * (first_term + 2.0 * values * second_term)
    return (grad_values, grad_gain, grad_bias)


def body(
    images,
    pixel_mask,
    counts,
    labels,
    block_w,
    chan_side,
    head_w,
    head_side,
    shared,
    block_mom,
    side_mom,
    head_mom,
    hside_mom,
    shared_mom,
    block_ema,
    side_ema,
    head_ema,
    hside_ema,
    shared_ema,
    chan_stats,
    head_stats,
    proj_stats,
):
    chan_index = lax.axis_index("chan")
    first_chan = (chan_index == 0).astype(jnp.float32)
    pix_mask = pixel_mask.astype(jnp.float32)
    mask_low = pixel_mask.astype(jnp.bfloat16)
    mask_cols = pix_mask[:, :, None]
    pool_div = jnp.maximum(counts, 1).astype(jnp.float32)
    valid = (counts > 0).astype(jnp.float32)
    taps = KERNEL * KERNEL
    route_in, route_head, gain_proj, bias_proj, squeeze_bias, class_bias = split_shared(shared)
    block_three = block_w.reshape(block_w.shape[0], -1, EXPERTS)
    head_three = head_w.reshape(head_w.shape[0], -1, EXPERTS)
    expand_rows = block_three[:WIDTH_IN]
    depth_rows = block_three[WIDTH_IN : WIDTH_IN + taps]
    proj_rows = block_three[WIDTH_IN + taps :]
    share_width = proj_stats.shape[1]
    pooled_in = pooled_low(images, mask_low, pool_div)
    gates_in, route_in_back = jax.vjp(route, pooled_in, route_in)
    mixed_expand = jnp.einsum("be,ice->bic", gates_in, expand_rows, precision=highest).astype(
        jnp.bfloat16
    )
    expand_pre = jnp.einsum(
        "bpi,bic->bpc", images, mixed_expand, preferred_element_type=jnp.float32
    )
    expand_act, saved_one, stats_one = norm_forward(
        expand_pre, pix_mask, chan_side[2 * SQUEEZE], chan_side[2 * SQUEEZE + 1], True
    )

    def depth_piece(values, gates, kernel_rows):
        return depthwise(values, jnp.einsum("be,tce->btc", gates, kernel_rows, precision=highest))

    depth_pre, depth_back = jax.vjp(depth_piece, expand_act, gates_in, depth_rows)
    depth_act, saved_two, stats_two = norm_forward(
        depth_pre, pix_mask, chan_side[2 * SQUEEZE + 2], chan_side[2 * SQUEEZE + 3], True
    )

    def squeeze_piece(values, reduce_rows):
        return jnp.dot(pooled(values, pix_mask, pool_div), reduce_rows.T, precision=highest)

    squeeze_part, squeeze_piece_back = jax.vjp(squeeze_piece, depth_act, chan_side[:SQUEEZE])
    squeeze_total = lax.psum(squeeze_part, "chan")

    def squeeze_gate(totals, bias):
        return jax.nn.silu(totals + bias)

    squeeze_act, squeeze_gate_back = jax.vjp(squeeze_gate, squeeze_total, squeeze_bias)

    def excite_piece(squeezed, values, excite_rows, excite_bias):
        gate = jax.nn.sigmoid(jnp.dot(squeezed, excite_rows, precision=highest) + excite_bias)
        return values * gate[:, None, :]

    excited, excite_back = jax.vjp(
        excite_piece,
        squeeze_act,
        depth_act,
        chan_side[SQUEEZE : 2 * SQUEEZE],
        chan_side[2 * SQUEEZE + 4],
    )
    excited_low = excited.astype(jnp.bfloat16)
    mixed_proj = jnp.einsum("be,oce->boc", gates_in, proj_rows, precision=highest).astype(
        jnp.bfloat16
    )
    proj_part = jnp.einsum(
        "bpc,boc->bpo", excited_low, mixed_proj, preferred_element_type=jnp.float32
    )
    proj_pre = lax.psum(proj_part.astype(jnp.bfloat16), "chan").astype(jnp.float32)
    proj_out, saved_three, stats_three = norm_forward(
        proj_pre, pix_mask, gain_proj, bias_proj, False
    )
    proj_low = proj_out.astype(jnp.bfloat16)
    head_pool = pooled_low(proj_low, mask_low, pool_div)
    gates_head, route_head_back = jax.vjp(route, head_pool, route_head)
    mixed_head = jnp.einsum("be,ice->bic", gates_head, head_three, precision=highest).astype(
        jnp.bfloat16
    )
    head_pre = jnp.einsum("bpi,bic->bpc", proj_low, mixed_head, preferred_element_type=jnp.float32)
    head_act, saved_four, stats_four = norm_forward(
        head_pre, pix_mask, head_side[:, 0], head_side[:, 1], True
    )
    features = pooled(head_act, pix_mask, pool_div)
    classifier = head_side[:, 2:]
    logits = lax.psum(
        jnp.dot(features, classifier, precision=highest).astype(jnp.bfloat16), "chan"
    ).astype(jnp.float32)

    def loss_piece(scores, bias):
        log_probs = jax.nn.log_softmax(scores + bias, axis=1)
        one_hot = (labels[:, None] == jnp.arange(CLASSES)[None, :]).astype(jnp.float32)
        per_image = -(
            0.9 * jnp.sum(log_probs * one_hot, axis=1) + 0.1 * jnp.mean(log_probs, axis=1)
        )
        return jnp.sum(per_image * valid)

    loss_local, loss_back = jax.vjp(loss_piece, logits, class_bias)
    loss_sum, valid_sum = lax.psum((loss_local, jnp.sum(valid)), "dp")
    loss = loss_sum / valid_sum
    grad_logits, grad_class_bias = loss_back(1.0 / valid_sum)
    grad_features = jnp.dot(grad_logits, classifier.T, precision=highest)
    grad_classifier = jnp.dot(features.T, grad_logits, precision=highest)
    grad_head_act = mask_cols * (grad_features / pool_div[:, None])[:, None, :]
    grad_head_pre, grad_gain_four, grad_bias_four = norm_backward(
        saved_four, pix_mask, grad_head_act
    )
    grad_head_low = grad_head_pre.astype(jnp.bfloat16)
    grad_mixed_head = jnp.einsum(
        "bpi,bpc->bic", proj_low, grad_head_low, preferred_element_type=jnp.float32
    )
    grad_proj_low = jnp.einsum(
        "bpc,bic->bpi", grad_head_low, mixed_head, preferred_element_type=jnp.float32
    )
    grad_head_three = jnp.einsum("be,bic->ice", gates_head, grad_mixed_head, precision=highest)
    grad_gates_head = jnp.einsum("bic,ice->be", grad_mixed_head, head_three, precision=highest)
    grad_head_pool, grad_route_head = route_head_back(grad_gates_head)
    grad_proj_low = grad_proj_low + mask_cols * (grad_head_pool / pool_div[:, None])[:, None, :]
    grad_proj_out = lax.psum(grad_proj_low.astype(jnp.bfloat16), "chan").astype(jnp.float32)
    grad_proj_pre, grad_gain_three, grad_bias_three = norm_backward(
        saved_three, pix_mask, grad_proj_out
    )
    grad_proj_bf = grad_proj_pre.astype(jnp.bfloat16)
    grad_mixed_proj = jnp.einsum(
        "bpo,bpc->boc", grad_proj_bf, excited_low, preferred_element_type=jnp.float32
    )
    grad_excited = jnp.einsum(
        "bpo,boc->bpc", grad_proj_bf, mixed_proj, preferred_element_type=jnp.float32
    )
    grad_proj_rows = jnp.einsum("be,boc->oce", gates_in, grad_mixed_proj, precision=highest)
    grad_gates_in = jnp.einsum("boc,oce->be", grad_mixed_proj, proj_rows, precision=highest)
    grad_squeeze_act, grad_depth_act, grad_excite_rows, grad_excite_bias = excite_back(grad_excited)
    grad_squeeze_act = lax.psum(grad_squeeze_act, "chan")
    grad_squeeze_total, grad_squeeze_bias = squeeze_gate_back(grad_squeeze_act)
    grad_depth_more, grad_reduce_rows = squeeze_piece_back(grad_squeeze_total)
    grad_depth_pre, grad_gain_two, grad_bias_two = norm_backward(
        saved_two, pix_mask, grad_depth_act + grad_depth_more
    )
    grad_expand_act, grad_gates_depth, grad_depth_rows = depth_back(grad_depth_pre)
    grad_expand_pre, grad_gain_one, grad_bias_one = norm_backward(
        saved_one, pix_mask, grad_expand_act
    )
    grad_expand_low = grad_expand_pre.astype(jnp.bfloat16)
    grad_mixed_expand = jnp.einsum(
        "bpi,bpc->bic", images, grad_expand_low, preferred_element_type=jnp.float32
    )
    grad_expand_rows = jnp.einsum("be,bic->ice", gates_in, grad_mixed_expand, precision=highest)
    grad_gates_in = (
        grad_gates_in
        + grad_gates_depth
        + jnp.einsum("bic,ice->be", grad_mixed_expand, expand_rows, precision=highest)
    )
    grad_pooled_in, grad_route_in = route_in_back(grad_gates_in)
    grad_block = jnp.concatenate(
        [grad_expand_rows, grad_depth_rows, grad_proj_rows], axis=0
    ).reshape(block_w.shape)
    grad_head_w = grad_head_three.reshape(head_w.shape)
    grad_side = jnp.concatenate(
        [
            grad_reduce_rows,
            grad_excite_rows,
            jnp.stack(
                [grad_gain_one, grad_bias_one, grad_gain_two, grad_bias_two, grad_excite_bias]
            ),
        ],
        axis=0,
    )
    grad_hside = jnp.concatenate(
        [jnp.stack([grad_gain_four, grad_bias_four], axis=1), grad_classifier], axis=1
    )
    grad_shared = jnp.concatenate(
        [
            grad_route_in.reshape(-1),
            grad_route_head.reshape(-1),
            grad_gain_three * first_chan,
            grad_bias_three * first_chan,
            grad_squeeze_bias * first_chan,
            grad_class_bias * first_chan,
        ]
    )
    grads = lax.psum((grad_block, grad_side, grad_head_w, grad_hside), "dp")
    grad_shared = lax.psum(grad_shared, ("dp", "chan"))
    weights = (block_w, chan_side, head_w, head_side)
    moments = (block_mom, side_mom, head_mom, hside_mom)
    averages = (block_ema, side_ema, head_ema, hside_ema)
    squares = lax.psum(
        jnp.stack(
            [jnp.sum(piece * piece) for piece in grads]
            + [jnp.sum(piece * piece) for piece in weights]
        ),
        "chan",
    )
    results = [
        update(
            weights[group],
            grads[group],
            moments[group],
            averages[group],
            squares[group],
            squares[4 + group],
        )
        for group in range(4)
    ]
    results.append(
        update(
            shared,
            grad_shared,
            shared_mom,
            shared_ema,
            jnp.sum(grad_shared * grad_shared),
            jnp.sum(shared * shared),
        )
    )
    new_chan = 0.5 * chan_stats + 0.5 * jnp.stack(
        [stats_one[0], stats_one[1], stats_two[0], stats_two[1]]
    )
    new_head = 0.5 * head_stats + 0.5 * jnp.stack([stats_four[0], stats_four[1]])
    proj_now = lax.dynamic_slice_in_dim(
        jnp.stack([stats_three[0], stats_three[1]]), chan_index * share_width, share_width, 1
    )
    new_proj = 0.5 * proj_stats + 0.5 * proj_now
    return (
        loss,
        results[0][0],
        results[1][0],
        results[2][0],
        results[3][0],
        results[4][0],
        results[0][1],
        results[1][1],
        results[2][1],
        results[3][1],
        results[4][1],
        results[0][2],
        results[1][2],
        results[2][2],
        results[3][2],
        results[4][2],
        new_chan,
        new_head,
        new_proj,
    )


def solution(mesh):
    return jax.shard_map(
        body,
        mesh=mesh,
        in_specs=(
            P("dp", None, None),
            P("dp", None),
            P("dp"),
            P("dp"),
            P(None, "chan"),
            P(None, "chan"),
            P(None, "chan"),
            P("chan", None),
            P(),
            P(None, "chan"),
            P(None, "chan"),
            P(None, "chan"),
            P("chan", None),
            P(),
            P(None, "chan"),
            P(None, "chan"),
            P(None, "chan"),
            P("chan", None),
            P(),
            P(None, "chan"),
            P(None, "chan"),
            P(None, "chan"),
        ),
        out_specs=(
            P(),
            P(None, "chan"),
            P(None, "chan"),
            P(None, "chan"),
            P("chan", None),
            P(),
            P(None, "chan"),
            P(None, "chan"),
            P(None, "chan"),
            P("chan", None),
            P(),
            P(None, "chan"),
            P(None, "chan"),
            P(None, "chan"),
            P("chan", None),
            P(),
            P(None, "chan"),
            P(None, "chan"),
            P(None, "chan"),
        ),
        check_vma=False,
    )
```

profile of v0, /device:TPU:0, one launch (start us, length us, event | category | flops | bytes accessed | tf_op | source)
XLA Modules:
  0.0 1110.2 jit_solution(17724103384879078830)
XLA Ops:
  42.0 16.6 %all-reduce.58 = (f32[288]{0:T(512)S(1)}, f32[]{:T(128)}, f32[288]{0:T(512)S(1)}) all-reduce(f32[288]{0:T(512)S(1)} %get-tuple-element.96, f32[]{:T(128)} %convert_reduce_fusion.1, f32[288]{0:T(512)S(1)} %get-tuple-element.95), channel_id=1, replica_groups=mesh['dp'=8,'chan'=4] {'dp'}, use_global_device_ids=true, to_apply=%region_5.0 | all-reduce | flops 577 | bytes 4616 | tf_op jit(solution)/shard_map/psum | solution.py:78
  84.8 78.2 %multiply_reduce_fusion = (f32[288]{0:T(512)S(1)}, f32[288]{0:T(512)S(1)}, f32[16,16,16,288]{3,2,1,0:T(8,128)}) fusion(f32[16,16,16]{2,1,0:T(8,128)S(1)} %copy-done.28, f32[16,288]{1,0:T(8,128)S(1)} %copy-done.58, f32[16,288]{1,0:T(8,128)S(1)} %get-tuple-element.195, f32[16,288]{1,0:T(8,128)S(1)} %copy-done.33, f32[16,288]{1,0:T(8,128)S(1)} %copy-done.34, ...), kind=kLoop, calls=%fused_computation.30 | loop fusion | flops 62520768 | bytes 9916672 | tf_op jit(solution)/shard_map/reduce_sum | solution.py:76
  163.0 11.8 %all-reduce.57 = (f32[288]{0:T(512)S(1)}, f32[288]{0:T(512)S(1)}) all-reduce(f32[288]{0:T(512)S(1)} %get-tuple-element.88, f32[288]{0:T(512)S(1)} %get-tuple-element.87), channel_id=1, replica_groups=mesh['dp'=8,'chan'=4] {'dp'}, use_global_device_ids=true, to_apply=%region_9.10 | all-reduce | flops 576 | bytes 4608 | tf_op jit(solution)/shard_map/psum | solution.py:78
  192.2 12.4 %psum.224 = f32[16,48]{1,0:T(8,128)S(1)} all-reduce(f32[16,48]{1,0:T(8,128)S(1)} %fusion.119), channel_id=1, replica_groups=mesh['dp'=8,'chan'=4] {'chan'}, use_global_device_ids=true, to_apply=%region_10.11 | all-reduce | flops 768 | bytes 6144 | tf_op jit(solution)/shard_map/psum | solution.py:165
  224.3 88.6 %all-reduce.64.cloned.1.call-done = bf16[16,256,320]{1,2,0:T(8,128)(2,1)} async-done(((bf16[16,256,320]{1,2,0:T(8,128)(2,1)}), bf16[16,256,320]{1,2,0:T(8,128)(2,1)}) %all-reduce.64.cloned.1.call-update) | async-done | bytes 2621456 | tf_op jit(solution)/shard_map/psum | solution.py:190
  315.7 13.6 %all-reduce.56 = (f32[320]{0:T(512)S(1)}, f32[320]{0:T(512)S(1)}) all-reduce(f32[320]{0:T(512)S(1)} %get-tuple-element.104, f32[320]{0:T(512)S(1)} %get-tuple-element.103), channel_id=1, replica_groups=mesh['dp'=8,'chan'=4] {'dp'}, use_global_device_ids=true, to_apply=%region_15.16 | all-reduce | flops 640 | bytes 5120 | tf_op jit(solution)/shard_map/psum | solution.py:78
  346.2 13.0 %all-reduce.55 = (f32[320]{0:T(512)S(1)}, f32[320]{0:T(512)S(1)}, f32[]{:T(128)}) all-reduce(f32[320]{0:T(512)S(1)} %get-tuple-element.92, f32[320]{0:T(512)S(1)} %get-tuple-element.91, f32[]{:T(128)} %convert_reduce_fusion), channel_id=1, replica_groups=mesh['dp'=8,'chan'=4] {'dp'}, use_global_device_ids=true, to_apply=%region_19.20 | all-reduce | flops 641 | bytes 5128 | tf_op jit(solution)/shard_map/psum | solution.py:78
  370.8 17.2 %psum.230 = bf16[16,1000]{1,0:T(8,128)(2,1)S(1)} all-reduce(bf16[16,1000]{1,0:T(8,128)(2,1)S(1)} %fusion.86), channel_id=1, replica_groups=mesh['dp'=8,'chan'=4] {'chan'}, use_global_device_ids=true, to_apply=%region_20.21 | all-reduce | flops 16000 | bytes 64000 | tf_op jit(solution)/shard_map/psum | solution.py:206
  398.1 12.2 %all-reduce.54 = (f32[320]{0:T(512)S(1)}, f32[320]{0:T(512)S(1)}) all-reduce(f32[320]{0:T(512)S(1)} %multiply_multiply_fusion.13, f32[320]{0:T(512)S(1)} %neg.56), channel_id=1, replica_groups=mesh['dp'=8,'chan'=4] {'dp'}, use_global_device_ids=true, to_apply=%region_33.34 | all-reduce | flops 640 | bytes 5120 | tf_op jit(solution)/shard_map/psum | solution.py:95
  431.7 12.5 %fusion.107 = f32[16,8]{0,1:T(8,128)S(1)} fusion(f32[16,320,320]{1,0,2:T(8,128)} %copy.72, f32[16,8]{0,1:T(8,128)S(1)} %fusion.110, f32[320,2560]{0,1:T(8,128)} %copy.68), kind=kOutput, calls=%fused_computation.236 | convolution fusion | flops 157286784 | bytes 9831424 | tf_op jit(solution)/shard_map/bic,ice->be/dot_general | solution.py:236
  460.4 88.1 %all-reduce.66.cloned.1.call-done = bf16[16,256,320]{1,2,0:T(8,128)(2,1)} async-done(((bf16[16,256,320]{1,2,0:T(8,128)(2,1)}), bf16[16,256,320]{1,2,0:T(8,128)(2,1)}) %all-reduce.66.cloned.1.call-update) | async-done | bytes 2621456 | tf_op jit(solution)/shard_map/psum | solution.py:239
  553.7 13.6 %all-reduce.53 = (f32[320]{0:T(512)S(1)}, f32[320]{0:T(512)S(1)}) all-reduce(f32[320]{0:T(512)S(1)} %multiply_multiply_fusion.12, f32[320]{0:T(512)S(1)} %neg.57), channel_id=1, replica_groups=mesh['dp'=8,'chan'=4] {'dp'}, use_global_device_ids=true, to_apply=%region_38.39 | all-reduce | flops 640 | bytes 5120 | tf_op jit(solution)/shard_map/psum | solution.py:95
  600.3 12.0 %all-reduce.52 = (f32[288]{0:T(512)S(1)}, f32[288]{0:T(512)S(1)}) all-reduce(f32[288]{0:T(512)S(1)} %multiply_multiply_fusion.11, f32[288]{0:T(512)S(1)} %neg.58), channel_id=1, replica_groups=mesh['dp'=8,'chan'=4] {'dp'}, use_global_device_ids=true, to_apply=%region_44.45 | all-reduce | flops 576 | bytes 4608 | tf_op jit(solution)/shard_map/psum | solution.py:95
  627.3 16.7 %multiply_reduce_fusion.25 = (f32[16,288]{1,0:T(8,128)S(1)}, f32[16,288]{1,0:T(8,128)S(1)}, f32[16,288]{1,0:T(8,128)S(1)}, f32[16,288]{1,0:T(8,128)S(1)}, f32[16,288]{1,0:T(8,128)S(1)}, /*index=5*/f32[16,288]{1,0:T(8,128)S(1)}) fusion(f32[16,16,16,288]{3,2,1,0:T(8,128)} %bitcast.266, f32[16,256,288]{2,1,0:T(8,128)} %copy.75), kind=kLoop, calls=%fused_computation.72 | loop fusion | flops 14128128 | bytes 9547776 | tf_op jit(solution)/shard_map/transpose(jvp())/reduce_sum | solution.py:41
  644.1 52.5 %multiply_reduce_fusion.26 = (f32[16,288]{1,0:T(8,128)S(1)}, f32[16,288]{1,0:T(8,128)S(1)}, f32[16,288]{1,0:T(8,128)S(1)}, f32[16,288]{1,0:T(8,128)S(1)}, f32[16...) fusion(f32[16,16,16,288]{3,2,1,0:T(8,128)} %bitcast.267, ...), kind=kLoop, calls=%fused_computation.73 | loop fusion | flops 42384384 | bytes 9768960 | tf_op jit(solution)/shard_map/transpose(jvp())/reduce_sum | solution.py:41
  696.8 16.2 %broadcast_multiply_fusion.1 = (f32[16,16,16,288]{3,2,1,0:T(8,128)}, f32[16,16,16,288]{3,2,1,0:T(8,128)}, f32[16,16,16,288]{3,2,1,0:T(8,128)}, f32[16,16,16,288]...) fusion(f32[16,16,16,288]{3,2,1,0:T(8,128)} %bitcast.261, ...), kind=kLoop, calls=%fused_computation.163 | loop fusion | flops 8257536 | bytes 37877760 | tf_op jit(solution)/shard_map/transpose(jvp())/mul | solution.py:41
  713.1 37.0 %broadcast_multiply_fusion = (f32[16,16,16,288]{3,2,1,0:T(8,128)}, f32[16,16,16,288]{3,2,1,0:T(8,128)}, f32[16,16,16,288]{3,2,1,0:T(8,128)}, f32[16,16,16,288]{3...) fusion(f32[16,16,16,288]{3,2,1,0:T(8,128)} %bitcast.262, ...), kind=kLoop, calls=%fused_computation.162 | loop fusion | flops 21233664 | bytes 89985024 | tf_op jit(solution)/shard_map/transpose(jvp())/mul | solution.py:41
  763.0 42.3 %pad_add_fusion = f32[16,20,20,288]{3,2,1,0:T(8,128)} fusion(f32[16,16,16,288]{3,2,1,0:T(8,128)} %get-tuple-element.175, f32[16,16,16,288]{3,2,1,0:T(8,128)} %get-tuple-element.176, f32[16,16,16,288]{3,2,1,0:T(8,128)} %get-tuple-element.177, f32[16,16,16,288]{3,2,1,0:T(8,128)} %get-tuple-element.178, f32[16,16,16,288]{3,2,1,0:T(8,128)} %get-tuple-element.179, ...), kind=kLoop, calls=%fused_computation.24 | loop fusion | flops 33177600 | bytes 97026048 | tf_op jit(solution)/shard_map/transpose(jvp())/add_any | solution.py:42
  805.3 17.9 %pad_add_fusion.1 = f32[16,16,16,288]{3,2,1,0:T(8,128)} fusion(f32[16,16,16,288]{3,2,1,0:T(8,128)} %get-tuple-element.169, f32[16,16,16,288]{3,2,1,0:T(8,128)} %get-tuple-element.170, f32[16,16,16,288]{3,2,1,0:T(8,128)} %get-tuple-element.171, f32[16,16,16,288]{3,2,1,0:T(8,128)} %get-tuple-element.172, f32[16,16,16,288]{3,2,1,0:T(8,128)} %get-tuple-element.173, ...), kind=kLoop, calls=%fused_computation.44 | loop fusion | flops 7077888 | bytes 37748736 | tf_op jit(solution)/shard_map/transpose(jvp())/add_any | solution.py:42
  837.1 12.9 %all-reduce.51 = (f32[]{:T(128)}, f32[288]{0:T(512)S(1)}, f32[288]{0:T(512)S(1)}) all-reduce(f32[]{:T(128)} %select_reduce_fusion.1, f32[288]{0:T(512)S(1)} %multiply_multiply_fusion.10, f32[288]{0:T(512)S(1)} %neg.59), channel_id=1, replica_groups=mesh['dp'=8,'chan'=4] {'dp'}, use_global_device_ids=true, to_apply=%region_26.27 | all-reduce | flops 577 | bytes 4616 | tf_op jit(solution)/shard_map/psum | solution.py:219
  913.3 12.7 %fusion.99 = f32[16,8]{0,1:T(8,128)S(1)} fusion(f32[320,2304]{0,1:T(8,128)S(1)} %copy-done.5, f32[16,320,288]{1,2,0:T(8,128)} %fusion.114), kind=kOutput, calls=%fused_computation.230 | convolution fusion | flops 141557760 | bytes 8847872 | tf_op jit(solution)/shard_map/boc,oce->be/dot_general | solution.py:251
  927.6 38.6 %psum.248 = f32[5784]{0:T(1024)S(1)} all-reduce(f32[5784]{0:T(1024)S(1)} %concatenate.15), channel_id=1, replica_groups=mesh['dp'=8,'chan'=4] {'dp','chan'}, use_global_device_ids=true, to_apply=%region_98.99 | all-reduce | flops 5784 | bytes 46272 | tf_op jit(solution)/shard_map/psum | solution.py:302
  968.2 55.2 %all-reduce.68.cloned.1.call-done = (f32[537,2304]{1,0:T(8,128)}, f32[101,288]{1,0:T(8,128)}, f32[320,2560]{0,1:T(8,128)}, f32[320,1002]{1,0:T(8,128)}) async-done(((f32[537,2304]{1,0:T(8,128)}, f32[101,288]{1,0:T(8,128)}, f32[320,2560]{0,1:T(8,128)}, f32[320,1002]{1,0:T(8,128)}), (f32[537,2304]{1,0:T(8,128)}, f32[101,288]{1,0:T(8,128)}, f32[320,2560]{0,1:T(8,128)}, ...) | async-done | bytes 9624720 | tf_op jit(solution)/shard_map/psum | solution.py:301
  1038.5 12.0 %psum.247 = f32[8]{0:T(128)S(1)} all-reduce(f32[8]{0:T(128)S(1)} %stack.93), channel_id=1, replica_groups=mesh['dp'=8,'chan'=4] {'chan'}, use_global_device_ids=true, to_apply=%region_93.94 | all-reduce | flops 8 | bytes 64 | tf_op jit(solution)/shard_map/psum | solution.py:306
  (500 shorter events, 378.8 us)
Async XLA Ops:
  7.2 305.7 %all-reduce.64.cloned.1.call-start = ((), (), s32[]{:S(2)}) async-start(), calls=%async_computation | async-start | bytes 5242880 | tf_op jit(solution)/shard_map/psum | solution.py:190
  12.6 179.3 %copy-start.85 = (f32[16]{0:T(128)}, f32[16]{0:T(128)S(1)}, u32[]{:S(2)}) copy-start(f32[16]{0:T(128)S(1)} %maximum_convert_fusion) | copy-start | bytes 196
  20.5 54.2 %copy-start.89 = (f32[288]{0:T(512)}, f32[288]{0:T(512)S(1)}, u32[]{:S(2)}) copy-start(f32[288]{0:T(512)S(1)} %get-tuple-element.111) | copy-start | bytes 3460
  20.6 54.2 %copy-start.104 = (f32[288]{0:T(512)}, f32[288]{0:T(512)S(1)}, u32[]{:S(2)}) copy-start(f32[288]{0:T(512)S(1)} %get-tuple-element.110) | copy-start | bytes 3460
  212.4 336.2 %all-reduce.66.cloned.1.call-start = ((), (), s32[]{:S(2)}) async-start(), calls=%async_computation.1 | async-start | bytes 5242880 | tf_op jit(solution)/shard_map/psum | solution.py:239
  224.2 110.2 %copy-start.99 = (f32[320]{0:T(512)}, f32[320]{0:T(512)S(1)}, u32[]{:S(2)}) copy-start(f32[320]{0:T(512)S(1)} %get-tuple-element.219) | copy-start | bytes 3844
  224.2 110.2 %copy-start.86 = (f32[16]{0:T(128)S(1)}, f32[16]{0:T(128)}, u32[]{:S(2)}) copy-start(f32[16]{0:T(128)} %copy-done.85) | copy-start | bytes 196
  359.9 29.2 %copy-start.128 = (f32[16]{0:T(128)}, f32[16]{0:T(128)S(1)}, u32[]{:S(2)}) copy-start(f32[16]{0:T(128)S(1)} %get-tuple-element.246) | copy-start | bytes 196
  361.1 29.3 %copy-start.115 = (f32[320]{0:T(512)}, f32[320]{0:T(512)S(1)}, u32[]{:S(2)}) copy-start(f32[320]{0:T(512)S(1)} %get-tuple-element.232) | copy-start | bytes 3844
  447.9 575.5 %all-reduce.68.cloned.1.call-start = ((), (), s32[]{:S(2)}) async-start(), calls=%async_computation.2 | async-start | bytes 20832256 | tf_op jit(solution)/shard_map/psum | solution.py:301
  452.7 95.8 %copy-start.98 = (f32[320]{0:T(512)S(1)}, f32[320]{0:T(512)}, u32[]{:S(2)}) copy-start(f32[320]{0:T(512)} %copy-done.97) | copy-start | bytes 3844
  452.7 95.8 %copy-start.100 = (f32[320]{0:T(512)S(1)}, f32[320]{0:T(512)}, u32[]{:S(2)}) copy-start(f32[320]{0:T(512)} %copy-done.99) | copy-start | bytes 3844
  452.7 95.8 %copy-start.102 = (f32[320]{0:T(512)S(1)}, f32[320]{0:T(512)}, u32[]{:S(2)}) copy-start(f32[320]{0:T(512)} %copy-done.101) | copy-start | bytes 3844
  460.4 93.3 %copy-start.122 = (f32[320]{0:T(512)S(1)}, f32[320]{0:T(512)}, u32[]{:S(2)}) copy-start(f32[320]{0:T(512)} %copy-done.121) | copy-start | bytes 3844
  460.4 106.9 %copy-start.148 = (f32[320]{0:T(512)S(1)}, f32[320]{0:T(512)}, u32[]{:S(2)}) copy-start(f32[320]{0:T(512)} %copy-done.147) | copy-start | bytes 3844
  644.0 52.5 %copy-start.35 = (f32[16,288]{1,0:T(8,128)S(1)}, f32[16,288]{1,0:T(8,128)}, u32[]{:S(2)}) copy-start(f32[16,288]{1,0:T(8,128)} %get-tuple-element.197) | copy-start | bytes 55300
  644.0 52.5 %copy-start.37 = (f32[16,288]{1,0:T(8,128)S(1)}, f32[16,288]{1,0:T(8,128)}, u32[]{:S(2)}) copy-start(f32[16,288]{1,0:T(8,128)} %get-tuple-element.198) | copy-start | bytes 55300
  644.0 52.5 %copy-start.39 = (f32[16,288]{1,0:T(8,128)S(1)}, f32[16,288]{1,0:T(8,128)}, u32[]{:S(2)}) copy-start(f32[16,288]{1,0:T(8,128)} %get-tuple-element.199) | copy-start | bytes 55300
  644.0 52.5 %copy-start.41 = (f32[16,288]{1,0:T(8,128)S(1)}, f32[16,288]{1,0:T(8,128)}, u32[]{:S(2)}) copy-start(f32[16,288]{1,0:T(8,128)} %get-tuple-element.200) | copy-start | bytes 55300
  644.1 52.5 %copy-start.43 = (f32[16,288]{1,0:T(8,128)S(1)}, f32[16,288]{1,0:T(8,128)}, u32[]{:S(2)}) copy-start(f32[16,288]{1,0:T(8,128)} %get-tuple-element.201) | copy-start | bytes 55300
  913.3 54.2 %copy-start.113 = (f32[5784]{0:T(1024)S(1)}, f32[5784]{0:T(1024)}, u32[]{:S(2)}) copy-start(f32[5784]{0:T(1024)} %param.40) | copy-start | bytes 69412
  913.3 54.2 %copy-start.114 = (f32[5784]{0:T(1024)S(1)}, f32[5784]{0:T(1024)}, u32[]{:S(2)}) copy-start(f32[5784]{0:T(1024)} %param.35) | copy-start | bytes 69412
  1023.4 33.2 %copy-start.24 = (f32[101,288]{1,0:T(8,128)S(1)}, f32[101,288]{1,0:T(8,128)}, u32[]{:S(2)}) copy-start(f32[101,288]{1,0:T(8,128)} %copy.86) | copy-start | bytes 349060
  1023.4 33.2 %copy-start.25 = (f32[101,288]{1,0:T(8,128)S(1)}, f32[101,288]{1,0:T(8,128)}, u32[]{:S(2)}) copy-start(f32[101,288]{1,0:T(8,128)} %copy.92) | copy-start | bytes 349060
  (142 other events, 1358.0 us)
Sparse Core Ops, SparseCore 0:
  212.5 100.3 all-reduce.63
  448.0 100.4 all-reduce.65
  875.9 147.4 all-reduce.67
where the time goes:
time: 1120 us; the launch traced here: 1110 us
  other arithmetic  389 us (35%)
  waiting for transfers between devices  232 us (21%)
  blocking collectives  196 us (18%)
  matrix products  142 us (13%)
  local copies, waits for them, and re-layouts  123 us (11%)
  between operations  27.7 us (2%)
    psum x1, waiting for transfers between devices, body(): lax.psum(proj_part.astype(jnp.bfloat16), 'chan').astype(jnp.float32)  88.6 us
    psum x1, waiting for transfers between devices, body(): lax.psum(grad_proj_low.astype(jnp.bfloat16), 'chan').astype(jnp.float32)  88.1 us
    reduce_sum x2, other arithmetic, norm_forward(): first_sum = jnp.sum(mask_cols * values, axis=(0, 1))  81 us
    reduce_sum x3, other arithmetic, depthwise(): kernels[:, tap_index, None, None, :]  77.2 us
    add_any x2, other arithmetic, depthwise(): padded[:, row_off:row_off + MAP_SIDE, col_off:col_off + MAP_SIDE, :]  60.2 us
    psum x1, waiting for transfers between devices, body(): grads = lax.psum((grad_block, grad_side, grad_head_w, grad_hside), 'dp')  55.2 us
    psum x4, blocking collectives, norm_forward(): lax.psum((first_sum, second_sum, jnp.sum(pix_mask)), 'dp')  55 us
    mul x2, other arithmetic, depthwise(): kernels[:, tap_index, None, None, :]  53.2 us
  transfers between devices with their start and end apart: 3, of which 3 were waited for; matrix products, arithmetic and copies ran while one was open for 7% of the time, Pallas kernels for 0%

commit v1 on v0

v1 whole, which is shorter than its diff:
```python
import functools

import jax
import jax.numpy as jnp
from jax import lax
from jax.experimental import pallas as pl
from jax.experimental.pallas import tpu as pltpu
from jax.sharding import PartitionSpec as P

WIDTH_IN = 192
WIDTH_OUT = 320
SQUEEZE = 48
CLASSES = 1000
EXPERTS = 8
KERNEL = 5
MAP_SIDE = 16
TAPS = KERNEL * KERNEL
PIXELS = MAP_SIDE * MAP_SIDE
LANES = 128
CLASS_PAD = 1024
eps_norm = 0.001
highest = lax.Precision.HIGHEST
MESH = pl.DeviceIdType.MESH
f32 = jnp.float32
bf16 = jnp.bfloat16
VMEM = pltpu.VMEM
VLIMIT = 60 * 1024 * 1024


def dot(a, b, dims=((1,), (0,)), precision=None):
    return lax.dot_general(a, b, (dims, ((), ())), precision=precision, preferred_element_type=f32)


NN = ((1,), (0,))
NT = ((1,), (1,))
TN = ((0,), (0,))


def sig(x):
    return 0.5 * jnp.tanh(0.5 * x) + 0.5


def dsilu(n):
    s = sig(n)
    return s * (1.0 + n * (1.0 - s))


def rsum(x):
    return jnp.sum(x, axis=0, keepdims=True)


def split(x):
    high = x.astype(bf16)
    return jnp.concatenate([high, (x - high.astype(f32)).astype(bf16)], axis=0)


def greet(peers):
    barrier = pltpu.get_barrier_semaphore()
    for peer in peers:
        pl.semaphore_signal(barrier, inc=1, device_id=peer, device_id_type=MESH)
    pl.semaphore_wait(barrier, len(peers))


def sum_kernel(nd, nz, x_ref, o_ref, plane, depth, s1, r1, s2, r2):
    d = lax.axis_index("dp")
    z = lax.axis_index("chan")
    in_plane = [(lax.rem(d + k, nd), z) for k in range(1, nd)]
    along = [(d, lax.rem(z + k, nz)) for k in range(1, nz)]
    greet(in_plane + along)
    first = []
    for k, peer in enumerate(in_plane):
        first.append(
            pltpu.make_async_remote_copy(
                src_ref=x_ref,
                dst_ref=plane.at[d],
                send_sem=s1.at[k],
                recv_sem=r1.at[k],
                device_id=peer,
                device_id_type=MESH,
            )
        )
        first[-1].start()
    plane[d] = x_ref[...]
    for copy in first:
        copy.wait_recv()
    total = plane[0]
    for k in range(1, nd):
        total = total + plane[k]
    depth[z] = total
    second = []
    for k, peer in enumerate(along):
        second.append(
            pltpu.make_async_remote_copy(
                src_ref=depth.at[z],
                dst_ref=depth.at[z],
                send_sem=s2.at[k],
                recv_sem=r2.at[k],
                device_id=peer,
                device_id_type=MESH,
            )
        )
        second[-1].start()
    for copy in second:
        copy.wait_recv()
    total = depth[0]
    for k in range(1, nz):
        total = total + depth[k]
    o_ref[...] = total
    for copy in first + second:
        copy.wait_send()


def all_sum(x, nd, nz, ident):
    return pl.pallas_call(
        functools.partial(sum_kernel, nd, nz),
        out_shape=jax.ShapeDtypeStruct(x.shape, x.dtype),
        in_specs=[pl.BlockSpec(memory_space=VMEM)],
        out_specs=pl.BlockSpec(memory_space=VMEM),
        scratch_shapes=[
            VMEM((nd,) + x.shape, x.dtype),
            VMEM((nz,) + x.shape, x.dtype),
            pltpu.SemaphoreType.DMA((nd,)),
            pltpu.SemaphoreType.DMA((nd,)),
            pltpu.SemaphoreType.DMA((nz,)),
            pltpu.SemaphoreType.DMA((nz,)),
        ],
        compiler_params=pltpu.CompilerParams(collective_id=ident, has_side_effects=True),
        name="all_sum",
    )(x)


def by_column(width):
    return (width // 2) % LANES == 0


def pad_rows(rows, width, nd):
    unit = 16 * (nd // 2 if by_column(width) else nd)
    return -(-rows // unit) * unit


def core_block(rows, width, core):
    if by_column(width):
        return 0, rows, pl.multiple_of(core * (width // 2), LANES), width // 2
    return pl.multiple_of(core * (rows // 2), 16), rows // 2, 0, width


def part(rows, width, nd, core, place):
    row, count, col, cols = core_block(rows, width, core)
    unit = count // (nd // 2)
    return pl.multiple_of(row + place * unit, 16), unit, col, cols


def gather_kernel(nd, nz, shapes, side_count, *refs):
    n = len(shapes)
    ins, sides = refs[:n], refs[n : n + side_count]
    outs = refs[n + side_count : 2 * n + side_count]
    side_outs = refs[2 * n + side_count : 2 * (n + side_count)]
    send, recv, local = refs[2 * (n + side_count) :]
    d = lax.axis_index("dp")
    z = lax.axis_index("chan")
    core = lax.rem(d, 2)
    place = d // 2
    nxy = nd // 2
    along = [(d, lax.rem(z + k, nz)) for k in range(1, nz)]
    others = [lax.rem(place + k, nxy) for k in range(1, nxy)]
    twin = 1 - core
    greet(along + [(2 * o + core, z) for o in others] + [(2 * place + twin, z)])
    count = [0]

    def remote(src, dst, peer):
        k = count[0]
        count[0] += 1
        copy = pltpu.make_async_remote_copy(
            src_ref=src,
            dst_ref=dst,
            send_sem=send.at[k],
            recv_sem=recv.at[k],
            device_id=peer,
            device_id_type=MESH,
        )
        copy.start()
        return copy

    waits = []
    stage = []
    for q, (rows, width) in enumerate(shapes):
        row, unit, col, cols = part(rows, width, nd, core, place)
        mine = pl.ds(pl.multiple_of(z * width + col, LANES), cols)
        stage.append(
            [
                remote(ins[q].at[pl.ds(row, unit), pl.ds(col, cols)], outs[q].at[pl.ds(row, unit), mine], peer)
                for peer in along
            ]
        )
    side = []
    for q in range(side_count):
        side += [remote(sides[q], side_outs[q].at[z], peer) for peer in along]
    own = []
    for q, (rows, width) in enumerate(shapes):
        own.append(
            pltpu.make_async_copy(
                ins[q], outs[q].at[:, pl.ds(pl.multiple_of(z * width, LANES), width)], local.at[q]
            )
        )
        own[-1].start()
    for q in range(side_count):
        own.append(pltpu.make_async_copy(sides[q], side_outs[q].at[z], local.at[n + q]))
        own[-1].start()
    later = []
    for q, (rows, width) in enumerate(shapes):
        row, unit, col, cols = part(rows, width, nd, core, place)
        for copy in stage[q]:
            copy.wait_recv()
        waits += stage[q]
        group = []
        for k in range(1, nz):
            zz = lax.rem(z + k, nz)
            where = pl.ds(pl.multiple_of(zz * width + col, LANES), cols)
            block = outs[q].at[pl.ds(row, unit), where]
            group += [remote(block, block, (2 * o + core, z)) for o in others]
        later.append(group)
    last = []
    for q, (rows, width) in enumerate(shapes):
        row, unit, col, cols = core_block(rows, width, core)
        for copy in later[q]:
            copy.wait_recv()
        waits += later[q]
        for k in range(1, nz):
            zz = lax.rem(z + k, nz)
            where = pl.ds(pl.multiple_of(zz * width + col, LANES), cols)
            block = outs[q].at[pl.ds(row, unit), where]
            last.append(remote(block, block, (2 * place + twin, z)))
    for copy in last + side:
        copy.wait_recv()
    for copy in waits + last + side:
        copy.wait_send()
    for copy in own:
        copy.wait()


def gather(arrays, sides, nd, nz, ident):
    shapes = tuple(a.shape for a in arrays)
    nxy = nd // 2
    copies = len(arrays) * ((nz - 1) * (1 + (nxy - 1) + 1)) + len(sides) * (nz - 1)
    total = len(arrays) + len(sides)
    return pl.pallas_call(
        functools.partial(gather_kernel, nd, nz, shapes, len(sides)),
        out_shape=[jax.ShapeDtypeStruct((a.shape[0], nz * a.shape[1]), a.dtype) for a in arrays]
        + [jax.ShapeDtypeStruct((nz,) + a.shape, a.dtype) for a in sides],
        in_specs=[pl.BlockSpec(memory_space=pltpu.HBM)] * total,
        out_specs=[pl.BlockSpec(memory_space=pltpu.HBM)] * total,
        scratch_shapes=[
            pltpu.SemaphoreType.DMA((copies,)),
            pltpu.SemaphoreType.DMA((copies,)),
            pltpu.SemaphoreType.DMA((total,)),
        ],
        compiler_params=pltpu.CompilerParams(collective_id=ident, has_side_effects=True),
        name="weight_gather",
    )(*arrays, *sides)


def reduce_kernel(nd, nz, rows, width, g_ref, o_ref, twin_buf, half, plane_buf, sums, depth_buf, piece, send, recv):
    d = lax.axis_index("dp")
    z = lax.axis_index("chan")
    core = lax.rem(d, 2)
    place = d // 2
    nxy = nd // 2
    along = [(d, lax.rem(z + k, nz)) for k in range(1, nz)]
    others = [lax.rem(place + k, nxy) for k in range(1, nxy)]
    twin = (2 * place + 1 - core, z)
    greet(along + [(2 * o + core, z) for o in others] + [twin])
    count = [0]

    def remote(src, dst, peer):
        k = count[0]
        count[0] += 1
        copy = pltpu.make_async_remote_copy(
            src_ref=src,
            dst_ref=dst,
            send_sem=send.at[k],
            recv_sem=recv.at[k],
            device_id=peer,
            device_id_type=MESH,
        )
        copy.start()
        return copy

    row, unit, col, cols = core_block(rows, width, 1 - core)
    first = [
        remote(
            g_ref.at[pl.ds(row, unit), pl.ds(pl.multiple_of(k * width + col, LANES), cols)],
            twin_buf.at[k],
            twin,
        )
        for k in range(nz)
    ]
    row, unit, col, cols = core_block(rows, width, core)
    for k in range(nz):
        first[k].wait_recv()

        @pl.loop(0, unit // 16)
        def _(i):
            at = pl.ds(pl.multiple_of(i * 16, 16), 16)
            mine = g_ref[
                pl.ds(pl.multiple_of(row + i * 16, 16), 16),
                pl.ds(pl.multiple_of(k * width + col, LANES), cols),
            ]
            half[k, at, :] = (mine.astype(f32) + twin_buf[k, at, :].astype(f32)).astype(bf16)

    size = unit // nxy
    second = [
        remote(
            half.at[:, pl.ds(pl.multiple_of(o * size, 16), size), :],
            plane_buf.at[k],
            (2 * o + core, z),
        )
        for k, o in enumerate(others)
    ]
    for copy in second:
        copy.wait_recv()
    for k in range(nz):

        @pl.loop(0, size // 16)
        def _(i):
            at = pl.ds(pl.multiple_of(i * 16, 16), 16)
            total = half[k, pl.ds(pl.multiple_of(place * size + i * 16, 16), 16), :].astype(f32)
            for q in range(nxy - 1):
                total = total + plane_buf[q, k, at, :].astype(f32)
            sums[k, at, :] = total.astype(bf16)

    third = [remote(sums.at[peer[1]], depth_buf.at[k], peer) for k, peer in enumerate(along)]
    for copy in third:
        copy.wait_recv()

    @pl.loop(0, size // 16)
    def _(i):
        at = pl.ds(pl.multiple_of(i * 16, 16), 16)
        total = sums[z, at, :].astype(f32)
        for q in range(nz - 1):
            total = total + depth_buf[q, at, :].astype(f32)
        piece[at, :] = total.astype(bf16)
        o_ref[
            pl.ds(pl.multiple_of(row + place * size + i * 16, 16), 16), pl.ds(col, cols)
        ] = total.astype(bf16)

    block = o_ref.at[pl.ds(pl.multiple_of(row + place * size, 16), size), pl.ds(col, cols)]
    fourth = [remote(piece, block, (2 * o + core, z)) for o in others]
    for copy in fourth:
        copy.wait_recv()
    block = o_ref.at[pl.ds(row, unit), pl.ds(col, cols)]
    fifth = remote(block, block, twin)
    fifth.wait_recv()
    for copy in first + second + third + fourth + [fifth]:
        copy.wait_send()


def reduce_grad(g, nd, nz, ident):
    rows, width = g.shape[0], g.shape[1] // nz
    nxy = nd // 2
    unit, cols = (rows, width // 2) if by_column(width) else (rows // 2, width)
    size = unit // nxy
    copies = nz + (nxy - 1) + (nz - 1) + (nxy - 1) + 1
    return pl.pallas_call(
        functools.partial(reduce_kernel, nd, nz, rows, width),
        out_shape=jax.ShapeDtypeStruct((rows, width), bf16),
        in_specs=[pl.BlockSpec(memory_space=VMEM)],
        out_specs=pl.BlockSpec(memory_space=VMEM),
        scratch_shapes=[
            VMEM((nz, unit, cols), bf16),
            VMEM((nz, unit, cols), bf16),
            VMEM((nxy - 1, nz, size, cols), bf16),
            VMEM((nz, size, cols), bf16),
            VMEM((nz - 1, size, cols), bf16),
            VMEM((size, cols), bf16),
            pltpu.SemaphoreType.DMA((copies,)),
            pltpu.SemaphoreType.DMA((copies,)),
        ],
        compiler_params=pltpu.CompilerParams(
            collective_id=ident, has_side_effects=True, vmem_limit_bytes=VLIMIT
        ),
        name="grad_reduce",
    )(g)


def build_mix(gates, nb):
    deep = LANES * EXPERTS
    row = lax.broadcasted_iota(jnp.int32, (deep, EXPERTS), 0)
    col = lax.broadcasted_iota(jnp.int32, (deep, EXPERTS), 1)
    pick = jnp.where((row & (EXPERTS - 1)) == col, 1.0, 0.0).astype(f32)
    row = lax.broadcasted_iota(jnp.int32, (deep, LANES), 0)
    col = lax.broadcasted_iota(jnp.int32, (deep, LANES), 1)
    same = (row >> 3) == col
    out = []
    for b in range(nb):
        spread = jnp.broadcast_to(gates[b : b + 1, :], (LANES, EXPERTS))
        out.append(jnp.where(same, dot(pick, spread, NT, highest), 0.0).astype(bf16))
    return out


def gate_sums(rows):
    deep = LANES * EXPERTS
    row = lax.broadcasted_iota(jnp.int32, (deep, EXPERTS), 0)
    col = lax.broadcasted_iota(jnp.int32, (deep, EXPERTS), 1)
    pick = jnp.where((row & (EXPERTS - 1)) == col, 1.0, 0.0).astype(f32)
    return dot(rows, pick, NN, highest)


def gate_rows(grad, kernel_block):
    both = dot(grad, kernel_block, TN)
    row = lax.broadcasted_iota(jnp.int32, both.shape, 0)
    col = lax.broadcasted_iota(jnp.int32, both.shape, 1)
    return rsum(jnp.where(row == (col >> 3), both, 0.0))


def norm_rows(stats, chunk, chunks, total):
    mean = stats[pl.ds(chunk, 1), :] / total
    var = stats[pl.ds(chunks + chunk, 1), :] / total - mean * mean
    return mean, lax.rsqrt(var + eps_norm)


def image(b):
    return pl.ds(pl.multiple_of(b * PIXELS, PIXELS), PIXELS)


def expand_kernel(nb, chunks, kern_ref, images, mask, mask_rows, counts, route, pre, taps, stats, mix, gates, pooled):
    j = pl.program_id(0)

    @pl.when(j == 0)
    def _():
        stats[...] = jnp.zeros_like(stats)
        stats[2 * chunks : 2 * chunks + 1, :] = rsum(counts[...])
        stats[2 * chunks + 1 : 2 * chunks + 2, :] = rsum(jnp.where(counts[...] > 0.0, 1.0, 0.0))
        pool = dot(mask_rows[...], images[...]) / jnp.maximum(counts[:, 0:1], 1.0)
        pooled[...] = pool
        gate = sig(dot(pool, route[...], NN, highest))
        gates[...] = gate
        for b, block in enumerate(build_mix(gate, nb)):
            mix[:, b * LANES : (b + 1) * LANES] = block

    mixed = dot(kern_ref[...], mix[...])
    one = jnp.zeros((1, LANES), f32)
    two = jnp.zeros((1, LANES), f32)
    for b in range(nb):
        at = slice(b * PIXELS, (b + 1) * PIXELS)
        lane = slice(b * LANES, (b + 1) * LANES)
        taps[b] = mixed[WIDTH_IN : WIDTH_IN + 32, lane]
        value = dot(images[at, :], mixed[:WIDTH_IN, lane].astype(bf16))
        pre[at, :] = value
        masked = mask[at, :] * value
        one = one + rsum(masked)
        two = two + rsum(masked * value)
    stats[pl.ds(j, 1), :] = one
    stats[pl.ds(chunks + j, 1), :] = two


def whole(shape):
    return pl.BlockSpec(shape, lambda *_: (0,) * len(shape))


def expand(kern, images, mask, mask_rows, counts, route, nb, width):
    chunks = width // LANES
    rows = nb * PIXELS
    deep = LANES * EXPERTS
    return pl.pallas_call(
        functools.partial(expand_kernel, nb, chunks),
        grid=(chunks,),
        out_shape=[
            jax.ShapeDtypeStruct((rows, width), f32),
            jax.ShapeDtypeStruct((nb, 32, width), f32),
            jax.ShapeDtypeStruct((24, LANES), f32),
            jax.ShapeDtypeStruct((deep, nb * LANES), bf16),
            jax.ShapeDtypeStruct((8, EXPERTS), f32),
            jax.ShapeDtypeStruct((8, WIDTH_IN), f32),
        ],
        in_specs=[
            pl.BlockSpec((kern.shape[0], deep), lambda j: (0, j)),
            whole(images.shape),
            whole(mask.shape),
            whole(mask_rows.shape),
            whole(counts.shape),
            whole(route.shape),
        ],
        out_specs=[
            pl.BlockSpec((rows, LANES), lambda j: (0, j)),
            pl.BlockSpec((nb, 32, LANES), lambda j: (0, 0, j)),
            whole((24, LANES)),
            whole((deep, nb * LANES)),
            whole((8, EXPERTS)),
            whole((8, WIDTH_IN)),
        ],
        compiler_params=pltpu.CompilerParams(vmem_limit_bytes=VLIMIT),
        name="expand",
    )(kern, images, mask, mask_rows, counts, route)


def shifted(value, step):
    if step == 0:
        return value
    col = lax.broadcasted_iota(jnp.int32, value.shape, 0) & (MAP_SIDE - 1)
    moved = pltpu.roll(value, (-step) % PIXELS, 0)
    keep = (col + step >= 0) & (col + step < MAP_SIDE)
    return jnp.where(keep, moved, 0.0)


def depth_kernel(nb, chunks, pre, taps, mask, side, stats, kern, mix, out, mixed_out, sums, buf, held):
    j = pl.program_id(0)

    @pl.when(j == 0)
    def _():
        sums[...] = jnp.zeros_like(sums)

    mixed = dot(kern[...], mix[...])
    for b in range(nb):
        mixed_out[b] = mixed[:, b * LANES : (b + 1) * LANES].astype(bf16)
    mean, rstd = norm_rows(stats, j, chunks, stats[2 * chunks : 2 * chunks + 1, :])
    scale = rstd * side[2 * SQUEEZE : 2 * SQUEEZE + 1, :]
    bias = side[2 * SQUEEZE + 1 : 2 * SQUEEZE + 2, :]
    held[...] = jnp.zeros_like(held)

    @pl.loop(0, nb)
    def _(b):
        at = image(b)
        normed = (pre[at, :] - mean) * scale + bias
        act = normed * sig(normed) * mask[at, :]
        for s in range(KERNEL):
            buf[s] = shifted(act, s - KERNEL // 2)
        taps_now = [jnp.broadcast_to(taps[b, t : t + 1, :], (MAP_SIDE, LANES)) for t in range(TAPS)]
        acc = [None] * MAP_SIDE
        for y in range(MAP_SIDE):
            for s in range(KERNEL):
                x = buf[s, y * MAP_SIDE : (y + 1) * MAP_SIDE, :]
                for r in range(KERNEL):
                    i = y - r + KERNEL // 2
                    if 0 <= i < MAP_SIDE:
                        term = taps_now[r * KERNEL + s] * x
                        acc[i] = term if acc[i] is None else acc[i] + term
            done = [y - 2] if y < MAP_SIDE - 1 else [y - 2, y - 1, y]
            for i in done:
                if i >= 0:
                    out[pl.ds(pl.multiple_of(b * PIXELS + i * MAP_SIDE, MAP_SIDE), MAP_SIDE), :] = acc[i]
        value = out[at, :]
        masked = mask[at, :] * value
        held[0:1, :] += rsum(masked)
        held[1:2, :] += rsum(masked * value)

    sums[pl.ds(j, 1), :] = held[0:1, :]
    sums[pl.ds(chunks + j, 1), :] = held[1:2, :]


def depthwise(pre, taps, mask, side, stats, kern, mix, nb):
    rows, width = pre.shape
    chunks = width // LANES
    deep = LANES * EXPERTS
    wide = lambda j: (0, j)
    return pl.pallas_call(
        functools.partial(depth_kernel, nb, chunks),
        grid=(chunks,),
        out_shape=[
            jax.ShapeDtypeStruct((rows, width), f32),
            jax.ShapeDtypeStruct((nb, WIDTH_OUT, width), bf16),
            jax.ShapeDtypeStruct((24, LANES), f32),
        ],
        in_specs=[
            pl.BlockSpec((rows, LANES), wide),
            pl.BlockSpec((nb, 32, LANES), lambda j: (0, 0, j)),
            whole(mask.shape),
            pl.BlockSpec((side.shape[0], LANES), wide),
            whole(stats.shape),
            pl.BlockSpec((WIDTH_OUT, deep), wide),
            whole(mix.shape),
        ],
        out_specs=[
            pl.BlockSpec((rows, LANES), wide),
            pl.BlockSpec((nb, WIDTH_OUT, LANES), lambda j: (0, 0, j)),
            whole((24, LANES)),
        ],
        scratch_shapes=[VMEM((KERNEL, PIXELS, LANES), f32), VMEM((8, LANES), f32)],
        compiler_params=pltpu.CompilerParams(vmem_limit_bytes=VLIMIT),
        name="depthwise",
    )(pre, taps, mask, side, stats, kern, mix)


def store_wide(ref, row, value):
    width = value.shape[1]
    for k in range(-(-width // LANES)):
        lanes = min(LANES, width - k * LANES)
        ref[row + k : row + k + 1, :lanes] = value[:, k * LANES : k * LANES + lanes]


def load_wide(ref, row, width):
    parts = []
    for k in range(-(-width // LANES)):
        lanes = min(LANES, width - k * LANES)
        parts.append(ref[row + k : row + k + 1, :lanes])
    return jnp.concatenate(parts, axis=1)


OUT_CHUNKS = -(-WIDTH_OUT // LANES)


def project_kernel(nb, chunks, dpre, mask, side, stats, totals, counts, sq_bias, mixed, excited, proj, pooled, gate_out, squeezed, sums, act, exc):
    phase = pl.program_id(0)
    j = pl.program_id(1)
    total = totals[2 * chunks : 2 * chunks + 1, :]

    @pl.when((phase == 0) & (j == 0))
    def _():
        squeezed[...] = jnp.zeros_like(squeezed)
        pooled[...] = jnp.zeros_like(pooled)
        sums[...] = jnp.zeros_like(sums)

    lane = pl.ds(pl.multiple_of(j * LANES, LANES), LANES)

    @pl.when(phase == 0)
    def _():
        mean, rstd = norm_rows(stats, j, chunks, total)
        scale = rstd * side[2 * SQUEEZE + 2 : 2 * SQUEEZE + 3, :]
        bias = side[2 * SQUEEZE + 3 : 2 * SQUEEZE + 4, :]
        for b in range(nb):
            at = slice(b * PIXELS, (b + 1) * PIXELS)
            normed = (dpre[at, :] - mean) * scale + bias
            value = normed * sig(normed) * mask[at, :]
            act[j, at, :] = value
            pooled[b : b + 1, lane] = rsum(value) / jnp.maximum(counts[b : b + 1, :], 1.0)
        squeezed[...] += dot(pooled[:, lane], side[0:SQUEEZE, :], NT, highest)

    @pl.when(phase == 1)
    def _():
        before = squeezed[...] + sq_bias[...]
        gate = sig(
            dot(before * sig(before), side[SQUEEZE : 2 * SQUEEZE, :], NN, highest)
            + side[2 * SQUEEZE + 4 : 2 * SQUEEZE + 5, :]
        )
        gate_out[:, lane] = gate
        for b in range(nb):
            at = slice(b * PIXELS, (b + 1) * PIXELS)
            value = (act[j, at, :] * gate[b : b + 1, :]).astype(bf16)
            excited[at, :] = value
            exc[at, lane] = value

    @pl.when((phase == 1) & (j == chunks - 1))
    def _():
        one = jnp.zeros((1, WIDTH_OUT), f32)
        two = jnp.zeros((1, WIDTH_OUT), f32)
        for b in range(nb):
            at = slice(b * PIXELS, (b + 1) * PIXELS)
            value = dot(exc[at, :], mixed[b], NT)
            proj[at, :] = value
            masked = mask[at, 0:1] * value
            one = one + rsum(masked)
            two = two + rsum(masked * value)
        store_wide(sums, 0, one)
        store_wide(sums, OUT_CHUNKS, two)


def project(dpre, mask, side, stats, totals, counts, sq_bias, mixed, nb):
    rows, width = dpre.shape
    chunks = width // LANES
    return pl.pallas_call(
        functools.partial(project_kernel, nb, chunks),
        grid=(2, chunks),
        out_shape=[
            jax.ShapeDtypeStruct((rows, width), bf16),
            jax.ShapeDtypeStruct((rows, WIDTH_OUT), f32),
            jax.ShapeDtypeStruct((8, width), f32),
            jax.ShapeDtypeStruct((8, width), f32),
            jax.ShapeDtypeStruct((8, SQUEEZE), f32),
            jax.ShapeDtypeStruct((8, LANES), f32),
        ],
        in_specs=[
            pl.BlockSpec((rows, LANES), lambda p, j: (0, jnp.where(p == 0, j, chunks - 1))),
            whole(mask.shape),
            pl.BlockSpec((side.shape[0], LANES), lambda p, j: (0, j)),
            whole(stats.shape),
            whole(totals.shape),
            whole(counts.shape),
            whole(sq_bias.shape),
            whole(mixed.shape),
        ],
        out_specs=[
            pl.BlockSpec((rows, LANES), lambda p, j: (0, jnp.where(p == 0, 0, j))),
            whole((rows, WIDTH_OUT)),
            whole((8, width)),
            whole((8, width)),
            whole((8, SQUEEZE)),
            whole((8, LANES)),
        ],
        scratch_shapes=[VMEM((chunks, rows, LANES), f32), VMEM((rows, width), bf16)],
        compiler_params=pltpu.CompilerParams(vmem_limit_bytes=VLIMIT),
        name="project",
    )(dpre, mask, side, stats, totals, counts, sq_bias, mixed)


def out_norm(sums, total):
    mean = load_wide(sums, 0, WIDTH_OUT) / total
    var = load_wide(sums, OUT_CHUNKS, WIDTH_OUT) / total - mean * mean
    return mean, lax.rsqrt(var + eps_norm)


def head_kernel(nb, chunks, kern, proj, mask, mask_rows, counts, gain, route, stats, totals, low, pre, mixed_out, sums, mix_out, gates, pooled):
    j = pl.program_id(0)

    @pl.when(j == 0)
    def _():
        sums[...] = jnp.zeros_like(sums)
        mean, rstd = out_norm(stats, totals[TOTAL_ROW : TOTAL_ROW + 1, 0:1])
        scale = rstd * gain[0:1, :]
        for b in range(nb):
            at = slice(b * PIXELS, (b + 1) * PIXELS)
            low[at, :] = (((proj[at, :] - mean) * scale + gain[1:2, :]) * mask[at, 0:1]).astype(bf16)
        pool = dot(mask_rows[...], low[...]) / jnp.maximum(counts[:, 0:1], 1.0)
        pooled[...] = pool
        gate = sig(dot(pool, route[...], NN, highest))
        gates[...] = gate
        for b, block in enumerate(build_mix(gate, nb)):
            mix_out[:, b * LANES : (b + 1) * LANES] = block

    mixed = dot(kern[...], mix_out[...])
    one = jnp.zeros((1, LANES), f32)
    two = jnp.zeros((1, LANES), f32)
    for b in range(nb):
        at = slice(b * PIXELS, (b + 1) * PIXELS)
        weight = mixed[:, b * LANES : (b + 1) * LANES].astype(bf16)
        mixed_out[b] = weight
        value = dot(low[at, :], weight)
        pre[at, :] = value
        masked = mask[at, :] * value
        one = one + rsum(masked)
        two = two + rsum(masked * value)
    sums[pl.ds(j, 1), :] = one
    sums[pl.ds(chunks + j, 1), :] = two


TOTAL_ROW = 18


def head(kern, proj, mask, mask_rows, counts, gain, route, stats, totals, nb):
    rows = proj.shape[0]
    width = kern.shape[1] // EXPERTS
    chunks = width // LANES
    deep = LANES * EXPERTS
    wide = lambda j: (0, j)
    return pl.pallas_call(
        functools.partial(head_kernel, nb, chunks),
        grid=(chunks,),
        out_shape=[
            jax.ShapeDtypeStruct((rows, WIDTH_OUT), bf16),
            jax.ShapeDtypeStruct((rows, width), f32),
            jax.ShapeDtypeStruct((nb, WIDTH_OUT, width), bf16),
            jax.ShapeDtypeStruct((24, LANES), f32),
            jax.ShapeDtypeStruct((deep, nb * LANES), bf16),
            jax.ShapeDtypeStruct((8, EXPERTS), f32),
            jax.ShapeDtypeStruct((8, WIDTH_OUT), f32),
        ],
        in_specs=[
            pl.BlockSpec((WIDTH_OUT, deep), wide),
            whole(proj.shape),
            whole(mask.shape),
            whole(mask_rows.shape),
            whole(counts.shape),
            whole(gain.shape),
            whole(route.shape),
            whole(stats.shape),
            whole(totals.shape),
        ],
        out_specs=[
            whole((rows, WIDTH_OUT)),
            pl.BlockSpec((rows, LANES), wide),
            pl.BlockSpec((nb, WIDTH_OUT, LANES), lambda j: (0, 0, j)),
            whole((24, LANES)),
            whole((deep, nb * LANES)),
            whole((8, EXPERTS)),
            whole((8, WIDTH_OUT)),
        ],
        compiler_params=pltpu.CompilerParams(vmem_limit_bytes=VLIMIT),
        name="head",
    )(kern, proj, mask, mask_rows, counts, gain, route, stats, totals)


def loss_kernel(nb, chunks, pre, mask, counts, labels, bias, cls, gain, stats, totals, features, grad_logits, grad_features, sums, logits):
    phase = pl.program_id(0)
    j = pl.program_id(1)
    lane = pl.ds(pl.multiple_of(j * LANES, LANES), LANES)

    @pl.when((phase == 0) & (j == 0))
    def _():
        sums[...] = jnp.zeros_like(sums)
        features[...] = jnp.zeros_like(features)
        logits[...] = jnp.zeros_like(logits)

    mean, rstd = norm_rows(stats, j, chunks, totals[TOTAL_ROW : TOTAL_ROW + 1, :])
    scale = rstd * gain[0:1, :]

    @pl.when(phase == 0)
    def _():
        for b in range(nb):
            at = slice(b * PIXELS, (b + 1) * PIXELS)
            normed = (pre[at, :] - mean) * scale + gain[1:2, :]
            features[b : b + 1, lane] = rsum(normed * sig(normed) * mask[at, :]) / jnp.maximum(
                counts[b : b + 1, :], 1.0
            )
        both = dot(split(features[:, lane]), cls[lane, :])
        logits[...] += both[:8] + both[8:]

    @pl.when((phase == 1) & (j == 0))
    def _():
        col = lax.broadcasted_iota(jnp.int32, (8, CLASS_PAD), 1)
        inside = col < CLASSES
        scores = jnp.where(inside, logits[...] + bias[...], -1e30)
        top = jnp.max(scores, axis=1, keepdims=True)
        spread = jnp.where(inside, jnp.exp(scores - top), 0.0)
        mass = jnp.sum(spread, axis=1, keepdims=True)
        hot = jnp.where(col == labels[:, 0:1], 1.0, 0.0)
        shifted_scores = jnp.where(inside, scores - top - jnp.log(mass), 0.0)
        per_image = -(
            0.9 * jnp.sum(shifted_scores * hot, axis=1, keepdims=True)
            + (0.1 / CLASSES) * jnp.sum(shifted_scores, axis=1, keepdims=True)
        )
        valid = jnp.where(counts[:, 0:1] > 0.0, 1.0, 0.0)
        sums[2 * chunks : 2 * chunks + 1, :] = jnp.broadcast_to(rsum(per_image * valid), (1, LANES))
        weight = valid / totals[TOTAL_ROW + 1 : TOTAL_ROW + 2, 0:1]
        grad_logits[...] = weight * jnp.where(inside, spread / mass - 0.9 * hot - 0.1 / CLASSES, 0.0)

    @pl.when(phase == 1)
    def _():
        both = dot(split(grad_logits[...]), cls[lane, :], NT)
        grads = (both[:8] + both[8:]) / jnp.maximum(counts[...], 1.0)
        grad_features[:, lane] = grads
        one = jnp.zeros((1, LANES), f32)
        two = jnp.zeros((1, LANES), f32)
        for b in range(nb):
            at = slice(b * PIXELS, (b + 1) * PIXELS)
            hat = (pre[at, :] - mean) * rstd
            grad = mask[at, :] * dsilu(hat * gain[0:1, :] + gain[1:2, :]) * grads[b : b + 1, :]
            one = one + rsum(grad)
            two = two + rsum(grad * hat)
        sums[pl.ds(j, 1), :] = one
        sums[pl.ds(chunks + j, 1), :] = two


def loss_stage(pre, mask, counts, labels, bias, cls, gain, stats, totals, nb):
    rows, width = pre.shape
    chunks = width // LANES
    return pl.pallas_call(
        functools.partial(loss_kernel, nb, chunks),
        grid=(2, chunks),
        out_shape=[
            jax.ShapeDtypeStruct((8, width), f32),
            jax.ShapeDtypeStruct((8, CLASS_PAD), f32),
            jax.ShapeDtypeStruct((8, width), f32),
            jax.ShapeDtypeStruct((24, LANES), f32),
        ],
        in_specs=[
            pl.BlockSpec((rows, LANES), lambda p, j: (0, j)),
            whole(mask.shape),
            whole(counts.shape),
            whole(labels.shape),
            whole(bias.shape),
            whole(cls.shape),
            pl.BlockSpec((2, LANES), lambda p, j: (0, j)),
            whole(stats.shape),
            whole(totals.shape),
        ],
        out_specs=[whole((8, width)), whole((8, CLASS_PAD)), whole((8, width)), whole((24, LANES))],
        scratch_shapes=[VMEM((8, CLASS_PAD), f32)],
        compiler_params=pltpu.CompilerParams(vmem_limit_bytes=VLIMIT),
        name="loss_stage",
    )(pre, mask, counts, labels, bias, cls, gain, stats, totals)


def head_back_kernel(nb, chunks, pre, grad_features, mask, counts, gain, stats, sums_in, totals, low, kern, mixed, mix, gates, route, proj, proj_stats, grad_kern, grad_out, sums, dz_out, held, grads, gate_acc):
    j = pl.program_id(0)
    lane = pl.ds(pl.multiple_of(j * LANES, LANES), LANES)
    total = totals[TOTAL_ROW : TOTAL_ROW + 1, :]

    @pl.when(j == 0)
    def _():
        gate_acc[...] = jnp.zeros_like(gate_acc)
        sums[...] = jnp.zeros_like(sums)

    mean, rstd = norm_rows(stats, j, chunks, total)
    scale = rstd * gain[0:1, :]
    one = sums_in[pl.ds(j, 1), :] / total
    two = sums_in[pl.ds(chunks + j, 1), :] / total
    for b in range(nb):
        at = slice(b * PIXELS, (b + 1) * PIXELS)
        hat = (pre[at, :] - mean) * rstd
        grad = dsilu(hat * gain[0:1, :] + gain[1:2, :]) * grad_features[b : b + 1, :]
        value = (scale * mask[at, :] * (grad - one - hat * two)).astype(bf16)
        held[at, lane] = value
        grad_mixed = dot(low[at, :], value, TN).astype(bf16)
        grads[:, b * LANES : (b + 1) * LANES] = grad_mixed
        gate_acc[b : b + 1, :] += gate_rows(grad_mixed, kern[...])
    grad_kern[...] = dot(grads[...], mix[...], NT).astype(bf16)

    @pl.when(j == chunks - 1)
    def _():
        dz = gate_sums(gate_acc[...]) * gates[...] * (1.0 - gates[...])
        dz_out[...] = dz
        pool_grad = dot(dz, route[...], NT, highest) / jnp.maximum(counts[:, 0:1], 1.0)
        mean, rstd = out_norm(proj_stats, total[:, 0:1])
        one = jnp.zeros((1, WIDTH_OUT), f32)
        two = jnp.zeros((1, WIDTH_OUT), f32)
        for b in range(nb):
            at = slice(b * PIXELS, (b + 1) * PIXELS)
            value = (dot(held[at, :], mixed[b], NT) + pool_grad[b : b + 1, :]) * mask[at, 0:1]
            grad_out[at, :] = value
            one = one + rsum(value)
            two = two + rsum(value * ((proj[at, :] - mean) * rstd))
        store_wide(sums, 0, one)
        store_wide(sums, OUT_CHUNKS, two)


def head_back(pre, grad_features, mask, counts, gain, stats, sums_in, totals, low, kern, mixed, mix, gates, route, proj, proj_stats, nb):
    rows, width = pre.shape
    chunks = width // LANES
    deep = LANES * EXPERTS
    wide = lambda j: (0, j)
    return pl.pallas_call(
        functools.partial(head_back_kernel, nb, chunks),
        grid=(chunks,),
        out_shape=[
            jax.ShapeDtypeStruct((kern.shape[0], width * EXPERTS), bf16),
            jax.ShapeDtypeStruct((rows, WIDTH_OUT), f32),
            jax.ShapeDtypeStruct((8, LANES), f32),
            jax.ShapeDtypeStruct((8, EXPERTS), f32),
        ],
        in_specs=[
            pl.BlockSpec((rows, LANES), wide),
            pl.BlockSpec((8, LANES), wide),
            whole(mask.shape),
            whole(counts.shape),
            pl.BlockSpec((2, LANES), wide),
            whole(stats.shape),
            whole(sums_in.shape),
            whole(totals.shape),
            whole(low.shape),
            pl.BlockSpec((WIDTH_OUT, deep), wide),
            whole(mixed.shape),
            whole(mix.shape),
            whole(gates.shape),
            whole(route.shape),
            whole(proj.shape),
            whole(proj_stats.shape),
        ],
        out_specs=[
            pl.BlockSpec((WIDTH_OUT, deep), wide),
            whole((rows, WIDTH_OUT)),
            whole((8, LANES)),
            whole((8, EXPERTS)),
        ],
        scratch_shapes=[
            VMEM((rows, width), bf16),
            VMEM((WIDTH_OUT, nb * LANES), bf16),
            VMEM((8, deep), f32),
        ],
        compiler_params=pltpu.CompilerParams(vmem_limit_bytes=VLIMIT),
        name="head_back",
    )(pre, grad_features, mask, counts, gain, stats, sums_in, totals, low, kern, mixed, mix, gates, route, proj, proj_stats)


def project_back_kernel(nb, chunks, grad_in, proj, proj_stats, proj_sums, gain, mask, counts, totals, stats, side, dpre, excited, mixed, kern, mix, gate, pooled, squeezed, sq_bias, grad_kern, grad_norm, sums, grad_squeeze, gate_grad, dz_gate, low, held, grads, gate_acc):
    phase = pl.program_id(0)
    j = pl.program_id(1)
    lane = pl.ds(pl.multiple_of(j * LANES, LANES), LANES)
    total = totals[TOTAL_ROW : TOTAL_ROW + 1, :]

    @pl.when((phase == 0) & (j == 0))
    def _():
        gate_acc[...] = jnp.zeros_like(gate_acc)
        sums[...] = jnp.zeros_like(sums)
        grad_squeeze[...] = jnp.zeros_like(grad_squeeze)
        dz_gate[...] = jnp.zeros_like(dz_gate)
        mean, rstd = out_norm(proj_stats, total[:, 0:1])
        scale = rstd * gain[0:1, :]
        one = load_wide(proj_sums, 0, WIDTH_OUT) / total[:, 0:1]
        two = load_wide(proj_sums, OUT_CHUNKS, WIDTH_OUT) / total[:, 0:1]
        for b in range(nb):
            at = slice(b * PIXELS, (b + 1) * PIXELS)
            hat = (proj[at, :] - mean) * rstd
            low[at, :] = (scale * (grad_in[at, :] - mask[at, 0:1] * (one + hat * two))).astype(bf16)

    mean, rstd = norm_rows(stats, j, chunks, total)
    gain_now = side[2 * SQUEEZE + 2 : 2 * SQUEEZE + 3, :]
    bias_now = side[2 * SQUEEZE + 3 : 2 * SQUEEZE + 4, :]

    @pl.when(phase == 0)
    def _():
        for b in range(nb):
            at = slice(b * PIXELS, (b + 1) * PIXELS)
            grad_mixed = dot(low[at, :], excited[at, :], TN).astype(bf16)
            grads[:, b * LANES : (b + 1) * LANES] = grad_mixed
            gate_acc[b : b + 1, :] += gate_rows(grad_mixed, kern[...])
            value = dot(low[at, :], mixed[b])
            held[j, at, :] = value
            normed = (dpre[at, :] - mean) * (rstd * gain_now) + bias_now
            act = normed * sig(normed) * mask[at, :]
            now = gate[b : b + 1, :]
            dz_gate[b : b + 1, lane] = rsum(value * act) * now * (1.0 - now)
        grad_kern[...] = dot(grads[...], mix[...], NT).astype(bf16)
        grad_squeeze[...] += dot(dz_gate[:, lane], side[SQUEEZE : 2 * SQUEEZE, :], NT, highest)

    @pl.when((phase == 1) & (j == 0))
    def _():
        grad_squeeze[...] = grad_squeeze[...] * dsilu(squeezed[...] + sq_bias[...])
        gate_grad[...] = gate_sums(gate_acc[...])

    @pl.when(phase == 1)
    def _():
        pool_grad = dot(grad_squeeze[...], side[0:SQUEEZE, :], NN, highest) / jnp.maximum(counts[...], 1.0)
        one = jnp.zeros((1, LANES), f32)
        two = jnp.zeros((1, LANES), f32)
        for b in range(nb):
            at = slice(b * PIXELS, (b + 1) * PIXELS)
            hat = (dpre[at, :] - mean) * rstd
            grad = held[j, at, :] * gate[b : b + 1, :] + pool_grad[b : b + 1, :]
            value = mask[at, :] * grad * dsilu(hat * gain_now + bias_now)
            grad_norm[at, :] = value
            one = one + rsum(value)
            two = two + rsum(value * hat)
        sums[pl.ds(j, 1), :] = one
        sums[pl.ds(chunks + j, 1), :] = two


def project_back(grad_in, proj, proj_stats, proj_sums, gain, mask, counts, totals, stats, side, dpre, excited, mixed, kern, mix, gate, pooled, squeezed, sq_bias, nb):
    rows, width = dpre.shape
    chunks = width // LANES
    deep = LANES * EXPERTS
    wide = lambda p, j: (0, j)
    early = lambda p, j: (0, jnp.where(p == 0, j, chunks - 1))
    late = lambda p, j: (0, jnp.where(p == 0, 0, j))
    return pl.pallas_call(
        functools.partial(project_back_kernel, nb, chunks),
        grid=(2, chunks),
        out_shape=[
            jax.ShapeDtypeStruct((kern.shape[0], width * EXPERTS), bf16),
            jax.ShapeDtypeStruct((rows, width), f32),
            jax.ShapeDtypeStruct((24, LANES), f32),
            jax.ShapeDtypeStruct((8, SQUEEZE), f32),
            jax.ShapeDtypeStruct((8, EXPERTS), f32),
            jax.ShapeDtypeStruct((8, width), f32),
        ],
        in_specs=[
            whole(grad_in.shape),
            whole(proj.shape),
            whole(proj_stats.shape),
            whole(proj_sums.shape),
            whole(gain.shape),
            whole(mask.shape),
            whole(counts.shape),
            whole(totals.shape),
            whole(stats.shape),
            pl.BlockSpec((side.shape[0], LANES), wide),
            pl.BlockSpec((rows, LANES), wide),
            pl.BlockSpec((rows, LANES), early),
            pl.BlockSpec((nb, WIDTH_OUT, LANES), lambda p, j: (0, 0, jnp.where(p == 0, j, chunks - 1))),
            pl.BlockSpec((WIDTH_OUT, deep), early),
            whole(mix.shape),
            pl.BlockSpec((8, LANES), wide),
            pl.BlockSpec((8, LANES), wide),
            whole(squeezed.shape),
            whole(sq_bias.shape),
        ],
        out_specs=[
            pl.BlockSpec((WIDTH_OUT, deep), early),
            pl.BlockSpec((rows, LANES), late),
            whole((24, LANES)),
            whole((8, SQUEEZE)),
            whole((8, EXPERTS)),
            whole((8, width)),
        ],
        scratch_shapes=[
            VMEM((rows, WIDTH_OUT), bf16),
            VMEM((chunks, rows, LANES), f32),
            VMEM((WIDTH_OUT, nb * LANES), bf16),
            VMEM((8, deep), f32),
        ],
        compiler_params=pltpu.CompilerParams(vmem_limit_bytes=VLIMIT),
        name="project_back",
    )(grad_in, proj, proj_stats, proj_sums, gain, mask, counts, totals, stats, side, dpre, excited, mixed, kern, mix, gate, pooled, squeezed, sq_bias)


def depth_back_kernel(nb, chunks, grad_in, dpre, pre, taps, mask, side, stats_one, stats_two, sums_two, totals, grad_out, tap_grads, sums, buf, acts, held):
    j = pl.program_id(0)
    total = totals[TOTAL_ROW : TOTAL_ROW + 1, :]

    @pl.when(j == 0)
    def _():
        sums[...] = jnp.zeros_like(sums)

    mean_two, rstd_two = norm_rows(stats_two, j, chunks, total)
    scale_two = rstd_two * side[2 * SQUEEZE + 2 : 2 * SQUEEZE + 3, :]
    one_two = sums_two[pl.ds(j, 1), :] / total
    two_two = sums_two[pl.ds(chunks + j, 1), :] / total
    mean, rstd = norm_rows(stats_one, j, chunks, total)
    gain = side[2 * SQUEEZE : 2 * SQUEEZE + 1, :]
    bias = side[2 * SQUEEZE + 1 : 2 * SQUEEZE + 2, :]
    held[...] = jnp.zeros_like(held)
    reach = KERNEL // 2

    @pl.loop(0, nb)
    def _(b):
        at = image(b)
        hat = (dpre[at, :] - mean_two) * rstd_two
        grad = scale_two * (grad_in[at, :] - mask[at, :] * (one_two + hat * two_two))
        for s in range(KERNEL):
            buf[s] = shifted(grad, reach - s)
        hat = (pre[at, :] - mean) * rstd
        normed = hat * gain + bias
        acts[...] = normed * sig(normed) * mask[at, :]
        taps_now = [jnp.broadcast_to(taps[b, t : t + 1, :], (MAP_SIDE, LANES)) for t in range(TAPS)]
        acc = [None] * MAP_SIDE
        for q in range(MAP_SIDE):
            for s in range(KERNEL):
                x = buf[s, q * MAP_SIDE : (q + 1) * MAP_SIDE, :]
                for r in range(KERNEL):
                    y = q + r - reach
                    if 0 <= y < MAP_SIDE:
                        term = taps_now[r * KERNEL + s] * x
                        acc[y] = term if acc[y] is None else acc[y] + term
            done = [q - 2] if q < MAP_SIDE - 1 else [q - 2, q - 1, q]
            for i in done:
                if i >= 0:
                    grad_out[pl.ds(pl.multiple_of(b * PIXELS + i * MAP_SIDE, MAP_SIDE), MAP_SIDE), :] = acc[i]
        tap_acc = [None] * TAPS
        for q in range(MAP_SIDE):
            for s in range(KERNEL):
                x = buf[s, q * MAP_SIDE : (q + 1) * MAP_SIDE, :]
                for r in range(KERNEL):
                    y = q + r - reach
                    if 0 <= y < MAP_SIDE:
                        both = acts[y * MAP_SIDE : (y + 1) * MAP_SIDE, :] * x
                        term = both[:8] + both[8:]
                        t = r * KERNEL + s
                        tap_acc[t] = term if tap_acc[t] is None else tap_acc[t] + term
        tap_grads[b] = jnp.zeros((32, LANES), f32)
        for t in range(TAPS):
            tap_grads[b, t : t + 1, :] = rsum(tap_acc[t])
        hat = (pre[at, :] - mean) * rstd
        value = grad_out[at, :] * mask[at, :] * dsilu(hat * gain + bias)
        grad_out[at, :] = value
        held[0:1, :] += rsum(value)
        held[1:2, :] += rsum(value * hat)

    sums[pl.ds(j, 1), :] = held[0:1, :]
    sums[pl.ds(chunks + j, 1), :] = held[1:2, :]


def depth_back(grad_in, dpre, pre, taps, mask, side, stats_one, stats_two, sums_two, totals, nb):
    rows, width = pre.shape
    chunks = width // LANES
    wide = lambda j: (0, j)
    tall = pl.BlockSpec((rows, LANES), wide)
    return pl.pallas_call(
        functools.partial(depth_back_kernel, nb, chunks),
        grid=(chunks,),
        out_shape=[
            jax.ShapeDtypeStruct((rows, width), f32),
            jax.ShapeDtypeStruct((nb, 32, width), f32),
            jax.ShapeDtypeStruct((24, LANES), f32),
        ],
        in_specs=[
            tall,
            tall,
            tall,
            pl.BlockSpec((nb, 32, LANES), lambda j: (0, 0, j)),
            whole(mask.shape),
            pl.BlockSpec((side.shape[0], LANES), wide),
            whole(stats_one.shape),
            whole(stats_two.shape),
            whole(sums_two.shape),
            whole(totals.shape),
        ],
        out_specs=[tall, pl.BlockSpec((nb, 32, LANES), lambda j: (0, 0, j)), whole((24, LANES))],
        scratch_shapes=[
            VMEM((KERNEL, PIXELS, LANES), f32),
            VMEM((PIXELS, LANES), f32),
            VMEM((8, LANES), f32),
        ],
        compiler_params=pltpu.CompilerParams(vmem_limit_bytes=VLIMIT),
        name="depth_back",
    )(grad_in, dpre, pre, taps, mask, side, stats_one, stats_two, sums_two, totals)


def expand_back_kernel(nb, chunks, grad_in, pre, images, tap_grads, mask, side, stats, sums_in, totals, kern, mix, gates, gate_grad, grad_kern, dz_out, grads, gate_acc):
    j = pl.program_id(0)
    total = totals[TOTAL_ROW : TOTAL_ROW + 1, :]

    @pl.when(j == 0)
    def _():
        gate_acc[...] = jnp.zeros_like(gate_acc)
        grads[...] = jnp.zeros_like(grads)

    mean, rstd = norm_rows(stats, j, chunks, total)
    scale = rstd * side[2 * SQUEEZE : 2 * SQUEEZE + 1, :]
    one = sums_in[pl.ds(j, 1), :] / total
    two = sums_in[pl.ds(chunks + j, 1), :] / total
    for b in range(nb):
        at = slice(b * PIXELS, (b + 1) * PIXELS)
        lane = slice(b * LANES, (b + 1) * LANES)
        hat = (pre[at, :] - mean) * rstd
        value = (scale * (grad_in[at, :] - mask[at, :] * (one + hat * two))).astype(bf16)
        grads[0:WIDTH_IN, lane] = dot(images[at, :], value, TN).astype(bf16)
        grads[WIDTH_IN : WIDTH_IN + 32, lane] = tap_grads[b].astype(bf16)
        gate_acc[b : b + 1, :] += gate_rows(grads[:, lane], kern[...])
    grad_kern[...] = dot(grads[...], mix[...], NT).astype(bf16)

    @pl.when(j == chunks - 1)
    def _():
        dz_out[...] = (gate_sums(gate_acc[...]) + gate_grad[...]) * gates[...] * (1.0 - gates[...])


def expand_back(grad_in, pre, images, tap_grads, mask, side, stats, sums_in, totals, kern, mix, gates, gate_grad, nb):
    rows, width = pre.shape
    chunks = width // LANES
    deep = LANES * EXPERTS
    wide = lambda j: (0, j)
    tall = pl.BlockSpec((rows, LANES), wide)
    return pl.pallas_call(
        functools.partial(expand_back_kernel, nb, chunks),
        grid=(chunks,),
        out_shape=[
            jax.ShapeDtypeStruct(kern.shape, bf16),
            jax.ShapeDtypeStruct((8, EXPERTS), f32),
        ],
        in_specs=[
            tall,
            tall,
            whole(images.shape),
            pl.BlockSpec((nb, 32, LANES), lambda j: (0, 0, j)),
            whole(mask.shape),
            pl.BlockSpec((side.shape[0], LANES), wide),
            whole(stats.shape),
            whole(sums_in.shape),
            whole(totals.shape),
            pl.BlockSpec((kern.shape[0], deep), wide),
            whole(mix.shape),
            whole(gates.shape),
            whole(gate_grad.shape),
        ],
        out_specs=[pl.BlockSpec((kern.shape[0], deep), wide), whole((8, EXPERTS))],
        scratch_shapes=[VMEM((kern.shape[0], nb * LANES), bf16), VMEM((8, deep), f32)],
        compiler_params=pltpu.CompilerParams(vmem_limit_bytes=VLIMIT),
        name="expand_back",
    )(grad_in, pre, images, tap_grads, mask, side, stats, sums_in, totals, kern, mix, gates, gate_grad)


def update(weight, grad, moment, average, factor):
    scaled = grad * factor
    moment_new = 0.5 * moment + scaled
    weight_new = weight - 0.2 * (scaled + 0.5 * moment_new)
    average_new = 0.5 * average + 0.5 * weight_new
    return (weight_new, moment_new, average_new)


def grow(array, rows, cols=None):
    cols = array.shape[1] if cols is None else cols
    return jnp.pad(array, ((0, rows - array.shape[0]), (0, cols - array.shape[1])))


def square_sum(x):
    x = x.astype(f32)
    return jnp.sum(x * x)


def body(
    nd,
    nz,
    images,
    pixel_mask,
    counts,
    labels,
    block_w,
    chan_side,
    head_w,
    head_side,
    shared,
    block_mom,
    side_mom,
    head_mom,
    hside_mom,
    shared_mom,
    block_ema,
    side_ema,
    head_ema,
    hside_ema,
    shared_ema,
    chan_stats,
    head_stats,
    proj_stats,
):
    z = lax.axis_index("chan")
    nb = images.shape[0] // nz
    own = chan_side.shape[1]
    own_head = head_side.shape[0]
    width = own * nz
    head_width = own_head * nz
    end_route = WIDTH_IN * EXPERTS
    end_head = end_route + WIDTH_OUT * EXPERTS
    end_norm = end_head + 2 * WIDTH_OUT
    end_squeeze = end_norm + SQUEEZE
    route_in = shared[:end_route].reshape(WIDTH_IN, EXPERTS)
    route_head = shared[end_route:end_head].reshape(WIDTH_OUT, EXPERTS)
    gain_out = shared[end_head:end_norm].reshape(2, WIDTH_OUT)
    sq_bias = shared[None, end_norm:end_squeeze]
    class_bias = jnp.pad(shared[end_squeeze:], (0, CLASS_PAD - CLASSES))[None, :]

    def mine(x):
        return lax.dynamic_slice_in_dim(x, z * nb, nb, 0)

    image_rows = mine(images).reshape(nb * PIXELS, WIDTH_IN)
    mask_now = mine(pixel_mask).astype(f32)
    mask = jnp.broadcast_to(mask_now.reshape(-1, 1), (nb * PIXELS, LANES))
    mask_rows = jnp.pad(
        (jnp.eye(nb, dtype=f32)[:, :, None] * mask_now[None]).reshape(nb, nb * PIXELS).astype(bf16),
        ((0, 8 - nb), (0, 0)),
    )
    count_rows = jnp.broadcast_to(jnp.pad(mine(counts).astype(f32), (0, 8 - nb))[:, None], (8, LANES))
    label_rows = jnp.broadcast_to(jnp.pad(mine(labels), (0, 8 - nb))[:, None], (8, LANES))

    block_width = block_w.shape[1]
    first_rows = WIDTH_IN + TAPS
    rows_a = pad_rows(first_rows, block_width, nd)
    kern_a = grow(block_w[:first_rows].astype(bf16), rows_a)
    kern_b = grow(block_w[first_rows:].astype(bf16), pad_rows(WIDTH_OUT, block_width, nd))
    kern_h = grow(head_w.astype(bf16), pad_rows(WIDTH_OUT, head_w.shape[1], nd))
    cls = head_side[:, 2:].astype(bf16)
    cls_t = grow(cls, pad_rows(own_head, CLASS_PAD, nd), CLASS_PAD)
    head_gain = head_side[:, :2].T
    full_a, full_side = gather([kern_a], [chan_side], nd, nz, 1)
    full_b, full_h, full_c, full_gain = gather([kern_b, kern_h, cls_t], [head_gain], nd, nz, 2)
    side = full_side.transpose(1, 0, 2).reshape(chan_side.shape[0], width)
    gain_head = full_gain.transpose(1, 0, 2).reshape(2, head_width)
    cls_full = (
        full_c.reshape(full_c.shape[0], nz, CLASS_PAD)[:own_head].transpose(1, 0, 2).reshape(head_width, CLASS_PAD)
    )

    pre, taps, stats_one, mix, gates, pooled_in = expand(
        full_a, image_rows, mask, mask_rows, count_rows, route_in, nb, width
    )
    stats_one = all_sum(stats_one, nd, nz, 3)
    totals = stats_one
    dpre, mixed_proj, stats_two = depthwise(pre, taps, mask, side, stats_one, full_b, mix, nb)
    stats_two = all_sum(stats_two, nd, nz, 4)
    excited, proj, pooled, gate, squeezed, stats_three = project(
        dpre, mask, side, stats_two, totals, count_rows, sq_bias, mixed_proj, nb
    )
    stats_three = all_sum(stats_three, nd, nz, 5)
    low, head_pre, mixed_head, stats_four, mix_head, gates_head, head_pool = head(
        full_h, proj, mask, mask_rows, count_rows, gain_out, route_head, stats_three, totals, nb
    )
    stats_four = all_sum(stats_four, nd, nz, 6)
    features, grad_logits, grad_features, sums_four = loss_stage(
        head_pre, mask, count_rows, label_rows, class_bias, cls_full, gain_head, stats_four, totals, nb
    )
    sums_four = all_sum(sums_four, nd, nz, 7)
    grad_h, grad_proj, sums_three, dz_head = head_back(
        head_pre,
        grad_features,
        mask,
        count_rows,
        gain_head,
        stats_four,
        sums_four,
        totals,
        low,
        full_h,
        mixed_head,
        mix_head,
        gates_head,
        route_head,
        proj,
        stats_three,
        nb,
    )
    sums_three = all_sum(sums_three, nd, nz, 8)
    grad_b, grad_norm, sums_two, grad_squeeze, gate_grad, dz_gate = project_back(
        grad_proj,
        proj,
        stats_three,
        sums_three,
        gain_out,
        mask,
        count_rows,
        totals,
        stats_two,
        side,
        dpre,
        excited,
        mixed_proj,
        full_b,
        mix,
        gate,
        pooled,
        squeezed,
        sq_bias,
        nb,
    )
    before = squeezed + sq_bias
    rows = jnp.concatenate(
        [
            features,
            grad_logits,
            pooled,
            dz_gate,
            head_pool,
            pooled_in,
            grad_squeeze,
            before * sig(before),
            dz_head,
        ],
        axis=1,
    )[:nb]
    every = lax.all_gather(rows, ("dp", "chan"), tiled=True)
    sums_two = all_sum(sums_two, nd, nz, 9)
    grad_pre, tap_grads, sums_one = depth_back(
        grad_norm, dpre, pre, taps, mask, side, stats_one, stats_two, sums_two, totals, nb
    )
    sums_one = all_sum(sums_one, nd, nz, 10)
    grad_a, dz_in = expand_back(
        grad_pre,
        pre,
        image_rows,
        tap_grads,
        mask,
        side,
        stats_one,
        sums_one,
        totals,
        full_a,
        mix,
        gates,
        gate_grad,
        nb,
    )
    grad_h = reduce_grad(grad_h, nd, nz, 11)
    grad_b = reduce_grad(grad_b, nd, nz, 12)
    grad_a = reduce_grad(grad_a, nd, nz, 13)

    cuts = [0]
    for size in (head_width, CLASS_PAD, width, width, WIDTH_OUT, WIDTH_IN, SQUEEZE, SQUEEZE, EXPERTS):
        cuts.append(cuts[-1] + size)
    parts = [every[:, cuts[k] : cuts[k + 1]] for k in range(len(cuts) - 1)]
    features_all, logits_all, pooled_all, dz_gate_all, head_pool_all, pooled_in_all, grad_sq_all, sq_all, dz_head_all = parts

    def shard(x, size):
        return lax.dynamic_slice_in_dim(x, z * size, size, 1)

    grad_classifier = dot(shard(features_all, own_head), logits_all[:, :CLASSES], TN, highest)
    dz_own = shard(dz_gate_all, own)
    grad_reduce = dot(grad_sq_all, shard(pooled_all, own), TN, highest)
    grad_excite = dot(sq_all, dz_own, TN, highest)
    grad_route_head = dot(head_pool_all, dz_head_all, TN, highest)

    def channel_rows(stats, count):
        return stats[: 2 * count].reshape(2, count * LANES)

    chunks = width // LANES
    head_chunks = head_width // LANES
    sums_one = shard(channel_rows(sums_one, chunks), own)
    sums_two = shard(channel_rows(sums_two, chunks), own)
    loss_sum = sums_four[2 * head_chunks, 0]
    sums_four = shard(channel_rows(sums_four, head_chunks), own_head)
    grad_side = jnp.concatenate(
        [
            grad_reduce,
            grad_excite,
            sums_one[1:2],
            sums_one[0:1],
            sums_two[1:2],
            sums_two[0:1],
            jnp.sum(dz_own, axis=0, keepdims=True),
        ],
        axis=0,
    )
    grad_hside = jnp.concatenate([sums_four[1][:, None], sums_four[0][:, None], grad_classifier], axis=1)

    def out_rows(stats):
        return stats[: 2 * OUT_CHUNKS].reshape(2, OUT_CHUNKS * LANES)[:, :WIDTH_OUT]

    sums_three = out_rows(sums_three)

    grad_block = jnp.concatenate([grad_a[:first_rows], grad_b[:WIDTH_OUT]], axis=0)
    grad_head = grad_h[:WIDTH_OUT]
    weights = (block_w, chan_side, head_w, head_side)
    grads = (grad_block, grad_side, grad_head, grad_hside)
    squares = jnp.stack([square_sum(g) for g in grads] + [square_sum(w) for w in weights])
    me = lax.axis_index("dp") * nz + z
    images_all = nd * nz * nb
    slots = images_all * EXPERTS // LANES
    dz_flat = lax.dynamic_update_slice(
        jnp.zeros((images_all, EXPERTS), f32), dz_in[:nb], (me * nb, 0)
    ).reshape(slots, LANES)
    square_row = jnp.pad(squares / nd, (0, LANES - 8))[None]
    last = all_sum(grow(jnp.concatenate([dz_flat, square_row], axis=0), slots + 8), nd, nz, 14)
    dz_in_all = last[:slots].reshape(images_all, EXPERTS)
    squares = last[slots, :8]
    grad_route_in = dot(pooled_in_all, dz_in_all, TN, highest)
    grad_shared = jnp.concatenate(
        [
            grad_route_in.reshape(-1),
            grad_route_head.reshape(-1),
            sums_three[1],
            sums_three[0],
            jnp.sum(grad_sq_all, axis=0),
            jnp.sum(logits_all[:, :CLASSES], axis=0),
        ]
    )
    factors = [jnp.sqrt(squares[4 + k]) * lax.rsqrt(squares[k] + 1e-12) for k in range(4)]
    moments = (block_mom, side_mom, head_mom, hside_mom)
    averages = (block_ema, side_ema, head_ema, hside_ema)
    results = [
        update(weights[k], grads[k].astype(f32), moments[k], averages[k], factors[k]) for k in range(4)
    ]
    results.append(
        update(
            shared,
            grad_shared,
            shared_mom,
            shared_ema,
            jnp.sqrt(jnp.sum(shared * shared)) * lax.rsqrt(jnp.sum(grad_shared * grad_shared) + 1e-12),
        )
    )
    total = totals[2 * chunks, 0]
    loss = loss_sum / totals[2 * chunks + 1, 0]

    def moving(old, sums):
        mean = sums[0] / total
        var = sums[1] / total - mean * mean
        return 0.5 * old + 0.5 * jnp.stack([mean, var * (total / (total - 1.0))])

    new_chan = jnp.concatenate(
        [
            moving(chan_stats[0:2], shard(channel_rows(stats_one, chunks), own)),
            moving(chan_stats[2:4], shard(channel_rows(stats_two, chunks), own)),
        ]
    )
    new_head = moving(head_stats, shard(channel_rows(stats_four, head_chunks), own_head))
    new_proj = moving(proj_stats, shard(out_rows(stats_three), proj_stats.shape[1]))
    return (
        (loss,)
        + tuple(results[k][0] for k in range(5))
        + tuple(results[k][1] for k in range(5))
        + tuple(results[k][2] for k in range(5))
        + (new_chan, new_head, new_proj)
    )


def solution(mesh):
    nd, nz = mesh.shape["dp"], mesh.shape["chan"]
    cols = P(None, "chan")
    state = (cols, cols, cols, P("chan", None), P())
    return jax.shard_map(
        functools.partial(body, nd, nz),
        mesh=mesh,
        in_specs=(P("dp", None, None), P("dp", None), P("dp"), P("dp"))
        + state * 3
        + (cols, cols, cols),
        out_specs=(P(),) + state * 3 + (cols, cols, cols),
        check_vma=False,
    )
```

time: 1120 us -> 836 us (0.75)
  Pallas kernels: 0 us -> 682 us
  other arithmetic: 389 us -> 56.6 us
  waiting for transfers between devices: 232 us -> 0.02 us
  blocking collectives: 196 us -> 0 us
  matrix products: 142 us -> 7.4 us
  local copies, waits for them, and re-layouts: 123 us -> 57.1 us
    pallas_call x0 -> x23, Pallas kernels: none -> 682 us  [the longest x3 219 us: reduce_grad(): pl.pallas_call(functools.partial(reduce_kernel, nd, nz, rows, width), out...]
    psum x3 -> x0, waiting for transfers between devices: 232 us -> none  [the longest x1 88.6 us: body(): lax.psum(proj_part.astype(jnp.bfloat16), 'chan').astype(jnp.float32)]
    psum x13 -> x0, blocking collectives: 196 us -> none  [the longest x4 55 us: norm_forward(): lax.psum((first_sum, second_sum, jnp.sum(pix_mask)), 'dp')]
    reduce_sum x26 -> x12, other arithmetic: 211 us -> 20.6 us  [the longest x8 17.4 us: square_sum(): return jnp.sum(x * x)]
    dot_general x38 -> x5, matrix products: 142 us -> 7.4 us  [dot(): lax.dot_general(a, b, (dims, ((), ())), precision=precision, preferred_el...]
    mul x15 -> x3, other arithmetic: 65 us -> 1.39 us  [the longest x2 1.38 us: moving(): return 0.5 * old + 0.5 * jnp.stack([mean, var * (total / (total - 1.0))])]
    add_any x3 -> x0, other arithmetic: 60.3 us -> none  [the longest x2 60.2 us: depthwise(): padded[:, row_off:row_off + MAP_SIDE, col_off:col_off + MAP_SIDE, :]]
    unnamed x337 -> x102, local copies, waits for them, and re-layouts: 46.6 us -> 17.8 us
  transfers between devices with their start and end apart: 3 -> 1, of which waited for: 3 -> 0; matrix products, arithmetic and copies ran while one was open for 7% -> 3% of each run, Pallas kernels for 0% -> 35%
where the time goes in v1:
time: 836 us; the launch traced here: 829 us
  Pallas kernels  682 us (82%)
  local copies, waits for them, and re-layouts  57.1 us (7%)
  other arithmetic  56.6 us (7%)
  between operations  25.8 us (3%)
    pallas_call x3, Pallas kernels, reduce_grad(): pl.pallas_call(functools.partial(reduce_kernel, nd, nz, rows, width), out...  219 us
    pallas_call x2, Pallas kernels, gather(): pl.pallas_call(functools.partial(gather_kernel, nd, nz, shapes, len(sides...  165 us
    pallas_call x9, Pallas kernels, all_sum(): pl.pallas_call(functools.partial(sum_kernel, nd, nz), out_shape=jax.Shape...  102 us
    pallas_call x1, Pallas kernels, project_back(): pl.pallas_call(functools.partial(project_back_kernel, nb, chunks), grid=(...  34.5 us
    pallas_call x1, Pallas kernels, head_back(): pl.pallas_call(functools.partial(head_back_kernel, nb, chunks), grid=(chu...  29.1 us
    pallas_call x1, Pallas kernels, depth_back(): pl.pallas_call(functools.partial(depth_back_kernel, nb, chunks), grid=(ch...  27.6 us
    add x5, other arithmetic, update(): average_new = 0.5 * average + 0.5 * weight_new  25.5 us
    pallas_call x1, Pallas kernels, expand_back(): pl.pallas_call(functools.partial(expand_back_kernel, nb, chunks), grid=(c...  20.6 us
  transfers between devices with their start and end apart: 1, of which 0 were waited for; matrix products, arithmetic and copies ran while one was open for 3% of the time, Pallas kernels for 35%

profile of v1, /device:TPU:0, one launch (start us, length us, event | category | flops | bytes accessed | tf_op | source)
XLA Modules:
  0.0 829.1 jit_solution(1602298509697787882)
XLA Ops:
  31.3 47.1 %weight_gather.3 = (bf16[256,9216]{1,0:T(8,128)(2,1)}, f32[4,101,288]{2,1,0:T(8,128)}) custom-call(bf16[256,2304]{1,0:T(8,128)(2,1)} %slice_select_fusion.refs_0_, f32[101,288]{1,0:T(8,128)} %copy.70.refs_1_), custom_call_target="tpu_custom_call" | custom-call | tf_op jit(solution)/shard_map/weight_gather/pallas_call | solution.py:246
  82.4 13.2 %expand.1 = (f32[1024,1152]{1,0:T(8,128)}, f32[4,32,1152]{2,1,0:T(8,128)}, f32[24,128]{1,0:T(8,128)}, bf16[1024,512]{1,0:T(8,128)(2,1)}, f32[8,8]{1,0:T(8,128)}, /*index=5*/f32[8,192]{1,0:T(8,128)}) custom-call(bf16[256,9216]{1,0:T(8,128)(2,1)} %get-tuple-element.67.kern_ref.kern, bf16[1024,192]{1,0:T(8,128)(2,1)} %bitcast.53, ...), custom_call_target="tpu_custom_call" | custom-call | tf_op jit(solution)/shard_map/expand/pallas_call | solution.py:464
  95.6 13.8 %all_sum.9.stats.totals.stats_one = f32[24,128]{1,0:T(8,128)} custom-call(f32[24,128]{1,0:T(8,128)} %get-tuple-element.71.x_ref), custom_call_target="tpu_custom_call" | custom-call | tf_op jit(solution)/shard_map/all_sum/pallas_call | solution.py:114
  109.4 118.2 %weight_gather.2 = (bf16[320,9216]{1,0:T(8,128)(2,1)}, bf16[320,10240]{1,0:T(8,128)(2,1)}, bf16[320,4096]{1,0:T(8,128)(2,1)}, f32[4,2,320]{2,1,0:T(2,128)}) custom-call(bf16[320,2304]{1,0:T(8,128)(2,1)} %slice.283.refs_0_, bf16[320,2560]{1,0:T(8,128)(2,1)} %get-tuple-element.197.refs_1_, bf16[320,1024]{1,0:T(8,128)(2,1)} %pad.32.refs_2_, f32[2,320]{1,0:T(2,128)} %bitcast.70), custom_call_target="tpu_custom_call" | custom-call | tf_op jit(solution)/shard_map/weight_gather/pallas_call | solution.py:246
  227.6 20.4 %depthwise.1 = (f32[1024,1152]{1,0:T(8,128)}, bf16[4,320,1152]{2,1,0:T(8,128)(2,1)}, f32[24,128]{1,0:T(8,128)}) custom-call(f32[1024,1152]{1,0:T(8,128)} %get-tuple-element.68.pre, f32[4,32,1152]{2,1,0:T(8,128)} %get-tuple-element.69.taps, f32[1024,128]{1,0:T(8,128)} %broadcast_in_dim.37.mask, f32[101,1152]{1,0:T(8,128)} %reshape.171.side, ...), custom_call_target="tpu_custom_call" | custom-call | tf_op jit(solution)/shard_map/depthwise/pallas_call | solution.py:555
  248.1 10.4 %all_sum.10.stats.stats_two = f32[24,128]{1,0:T(8,128)} custom-call(f32[24,128]{1,0:T(8,128)} %get-tuple-element.75.x_ref), custom_call_target="tpu_custom_call" | custom-call | tf_op jit(solution)/shard_map/all_sum/pallas_call | solution.py:114
  260.0 16.4 %project.1 = (bf16[1024,1152]{1,0:T(8,128)(2,1)}, f32[1024,320]{1,0:T(8,128)}, f32[8,1152]{1,0:T(8,128)}, f32[8,1152]{1,0:T(8,128)}, f32[8,48]{1,0:T(8,128)}, /*index=5*/f32[8,128]{1,0:T(8,128)}) custom-call(f32[1024,1152]{1,0:T(8,128)} %get-tuple-element.74.dpre, f32[1024,128]{1,0:T(8,128)} %broadcast_in_dim.37.mask, f32[101,1152]{1,0:T(8,128)} %reshape.171.side, ...), custom_call_target="tpu_custom_call" | custom-call | tf_op jit(solution)/shard_map/project/pallas_call | solution.py:659
  276.4 10.0 %all_sum.11.stats.proj_stats = f32[8,128]{1,0:T(8,128)} custom-call(f32[8,128]{1,0:T(8,128)} %get-tuple-element.78.x_ref), custom_call_target="tpu_custom_call" | custom-call | tf_op jit(solution)/shard_map/all_sum/pallas_call | solution.py:114
  291.3 16.0 %head.1 = (bf16[1024,320]{1,0:T(8,128)(2,1)}, f32[1024,1280]{1,0:T(8,128)}, bf16[4,320,1280]{2,1,0:T(8,128)(2,1)}, f32[24,128]{1,0:T(8,128)}, bf16[1024,512]{1,0...) custom-call(bf16[320,10240]{1,0:T(8,128)(2,1)} %get-tuple-element.66.kern, f32[1024,320]{1,0:T(8,128)} %get-tuple-element.77.proj, ...), custom_call_target="tpu_custom_call" | custom-call | tf_op jit(solution)/shard_map/head/pallas_call | solution.py:743
  307.4 10.3 %all_sum.12.stats = f32[24,128]{1,0:T(8,128)} custom-call(f32[24,128]{1,0:T(8,128)} %get-tuple-element.82.x_ref), custom_call_target="tpu_custom_call" | custom-call | tf_op jit(solution)/shard_map/all_sum/pallas_call | solution.py:114
  318.3 17.5 %loss_stage.1 = (f32[8,1280]{1,0:T(8,128)}, f32[8,1024]{1,0:T(8,128)}, f32[8,1280]{1,0:T(8,128)}, f32[24,128]{1,0:T(8,128)}) custom-call(f32[1024,1280]{1,0:T(8,128)} %get-tuple-element.79.pre, f32[1024,128]{1,0:T(8,128)} %broadcast_in_dim.37.mask, f32[8,128]{1,0:T(8,128)} %broadcast_in_dim.38.counts, s32[8,128]{1,0:T(8,128)} %broadcast_in_dim.40.labels, ...), custom_call_target="tpu_custom_call" | custom-call | tf_op jit(solution)/shard_map/loss_stage/pallas_call | solution.py:844
  335.8 10.5 %all_sum.13.sums_in = f32[24,128]{1,0:T(8,128)} custom-call(f32[24,128]{1,0:T(8,128)} %get-tuple-element.83.x_ref), custom_call_target="tpu_custom_call" | custom-call | tf_op jit(solution)/shard_map/all_sum/pallas_call | solution.py:114
  346.4 29.1 %head_back.1 = (bf16[320,10240]{1,0:T(8,128)(2,1)}, f32[1024,320]{1,0:T(8,128)}, f32[8,128]{1,0:T(8,128)}, f32[8,8]{1,0:T(8,128)}) custom-call(f32[1024,1280]{1,0:T(8,128)} %get-tuple-element.79.pre, f32[8,1280]{1,0:T(8,128)} %get-tuple-element.84.grad_features, f32[1024,128]{1,0:T(8,128)} %broadcast_in_dim.37.mask, f32[8,128]{1,0:T(8,128)} %broadcast_in_dim.38.counts, ...), custom_call_target="tpu_custom_call" | custom-call | tf_op jit(solution)/shard_map/head_back/pallas_call | solution.py:919
  375.5 10.3 %all_sum.14.proj_sums = f32[8,128]{1,0:T(8,128)} custom-call(f32[8,128]{1,0:T(8,128)} %get-tuple-element.90.x_ref), custom_call_target="tpu_custom_call" | custom-call | tf_op jit(solution)/shard_map/all_sum/pallas_call | solution.py:114
  385.9 34.5 %project_back.1 = (bf16[320,9216]{1,0:T(8,128)(2,1)}, f32[1024,1152]{1,0:T(8,128)}, f32[24,128]{1,0:T(8,128)}, f32[8,48]{1,0:T(8,128)}, f32[8,8]{1,0:T(8,128)}, /*index=5*/f32[8,1152]{1,0:T(8,128)}) custom-call(f32[1024,320]{1,0:T(8,128)} %get-tuple-element.89.grad_in, f32[1024,320]{1,0:T(8,128)} %get-tuple-element.77.proj, ...), custom_call_target="tpu_custom_call" | custom-call | tf_op jit(solution)/shard_map/project_back/pallas_call | solution.py:1032
  422.6 79.5 %grad_reduce.4 = bf16[320,2304]{1,0:T(8,128)(2,1)} custom-call(bf16[320,9216]{1,0:T(8,128)(2,1)} %get-tuple-element.103.g_ref), custom_call_target="tpu_custom_call" | custom-call | tf_op jit(solution)/shard_map/grad_reduce/pallas_call | solution.py:363
  502.1 11.6 %all_sum.15.sums_two = f32[24,128]{1,0:T(8,128)} custom-call(f32[24,128]{1,0:T(8,128)} %get-tuple-element.96.x_ref), custom_call_target="tpu_custom_call" | custom-call | tf_op jit(solution)/shard_map/all_sum/pallas_call | solution.py:114
  513.7 27.6 %depth_back.1 = (f32[1024,1152]{1,0:T(8,128)}, f32[4,32,1152]{2,1,0:T(8,128)}, f32[24,128]{1,0:T(8,128)}) custom-call(f32[1024,1152]{1,0:T(8,128)} %get-tuple-element.95.grad_in, f32[1024,1152]{1,0:T(8,128)} %get-tuple-element.74.dpre, f32[1024,1152]{1,0:T(8,128)} %get-tuple-element.68.pre, f32[4,32,1152]{2,1,0:T(8,128)} %get-tuple-element.69.taps, ...), custom_call_target="tpu_custom_call" | custom-call | tf_op jit(solution)/shard_map/depth_back/pallas_call | solution.py:1154
  541.3 10.7 %all_sum.16.sums_in = f32[24,128]{1,0:T(8,128)} custom-call(f32[24,128]{1,0:T(8,128)} %get-tuple-element.99.x_ref), custom_call_target="tpu_custom_call" | custom-call | tf_op jit(solution)/shard_map/all_sum/pallas_call | solution.py:114
  552.0 20.6 %expand_back.1 = (bf16[256,9216]{1,0:T(8,128)(2,1)}, f32[8,8]{1,0:T(8,128)}) custom-call(f32[1024,1152]{1,0:T(8,128)} %get-tuple-element.97.grad_in, f32[1024,1152]{1,0:T(8,128)} %get-tuple-element.68.pre, bf16[1024,192]{1,0:T(8,128)(2,1)} %bitcast.54, f32[4,32,1152]{2,1,0:T(8,128)} %get-tuple-element.98.tap_grads, f32[1024,128]{1,0:T(8,128)} %broadcast_in_dim.37.mask, ...), custom_call_target="tpu_custom_call" | custom-call | tf_op jit(solution)/shard_map/expand_back/pallas_call | solution.py:1219
  572.6 59.1 %grad_reduce.3 = bf16[256,2304]{1,0:T(8,128)(2,1)} custom-call(bf16[256,9216]{1,0:T(8,128)(2,1)} %get-tuple-element.102.g_ref), custom_call_target="tpu_custom_call" | custom-call | tf_op jit(solution)/shard_map/grad_reduce/pallas_call | solution.py:363
  634.7 80.7 %grad_reduce.5 = bf16[320,2560]{1,0:T(8,128)(2,1)} custom-call(bf16[320,10240]{1,0:T(8,128)(2,1)} %get-tuple-element.112.g_ref), custom_call_target="tpu_custom_call" | custom-call | tf_op jit(solution)/shard_map/grad_reduce/pallas_call | solution.py:363
  757.2 14.5 %all_sum.17 = f32[16,128]{1,0:T(8,128)} custom-call(f32[16,128]{1,0:T(8,128)} %select_maximum_fusion.x_ref), custom_call_target="tpu_custom_call" | custom-call | tf_op jit(solution)/shard_map/all_sum/pallas_call | solution.py:114
  796.4 11.7 %add_multiply_fusion = (f32[537,2304]{1,0:T(8,128)}, f32[537,2304]{1,0:T(8,128)}, f32[537,2304]{1,0:T(8,128)}) fusion(f32[537,2304]{1,0:T(8,128)} %param.36, f32[537,2304]{1,0:T(8,128)} %param.26, f32[]{:T(128)} %bitcast.21, bf16[320,2304]{1,0:T(8,128)(2,1)S(1)} %copy-done.5, bf16[217,2304]{1,0:T(8,128)(2,1)} %slice.234, f32[537,2304]{1,0:T(8,128)} %param.31), kind=kLoop, calls=%fused_computation.7 | loop fusion | flops 16084224 | bytes 32168452 | tf_op jit(solution)/shard_map/add | solution.py:1252
  (205 shorter events, 109.5 us)
Async XLA Ops:
  7.2 19.9 %copy-start = (bf16[16,256,192]{1,2,0:T(8,128)(2,1)S(1)}, bf16[16,256,192]{1,2,0:T(8,128)(2,1)}, u32[]{:S(2)}) copy-start(bf16[16,256,192]{1,2,0:T(8,128)(2,1)} %param.22) | copy-start | bytes 4718596
  7.2 732.0 %all-gather.3.cloned.1.call-start = ((), (), s32[]{:S(2)}) async-start(), calls=%async_computation | async-start | bytes 2770944 | tf_op jit(solution)/shard_map/all_gather | solution.py:1414
  227.6 30.9 %slice-start.3 = ((f32[5784]{0:T(1024)}), f32[640]{0:T(1024)S(1)}, s32[]{:S(2)}) async-start(f32[5784]{0:T(1024)} %param.30), calls=%async_computation.4 | async-start | bytes 8192 | tf_op jit(solution)/shard_map/slice | solution.py:1304
  260.0 26.5 %copy-start.44 = (s32[16]{0:T(128)S(1)}, s32[16]{0:T(128)}, u32[]{:S(2)}) copy-start(s32[16]{0:T(128)} %param.25) | copy-start | bytes 196
  276.4 14.3 %copy-start.35 = (f32[4,2,320]{2,1,0:T(2,128)S(1)}, f32[4,2,320]{2,1,0:T(2,128)}, u32[]{:S(2)}) copy-start(f32[4,2,320]{2,1,0:T(2,128)} %get-tuple-element.81) | copy-start | bytes 30724
  346.4 39.4 %copy-start.33 = (f32[8,48]{1,0:T(8,128)S(1)}, f32[8,48]{1,0:T(8,128)}, u32[]{:S(2)}) copy-start(f32[8,48]{1,0:T(8,128)} %get-tuple-element.94.squeezed) | copy-start | bytes 4612
  385.8 34.6 %copy-start.23 = (f32[8,1152]{1,0:T(8,128)S(1)}, f32[8,1152]{1,0:T(8,128)}, u32[]{:S(2)}) copy-start(f32[8,1152]{1,0:T(8,128)} %get-tuple-element.93.pooled) | copy-start | bytes 110596
  385.8 34.6 %copy-start.28 = (f32[8,1280]{1,0:T(8,128)S(1)}, f32[8,1280]{1,0:T(8,128)}, u32[]{:S(2)}) copy-start(f32[8,1280]{1,0:T(8,128)} %get-tuple-element.105) | copy-start | bytes 122884
  385.9 34.6 %copy-start.30 = (f32[8,1024]{1,0:T(8,128)S(1)}, f32[8,1024]{1,0:T(8,128)}, u32[]{:S(2)}) copy-start(f32[8,1024]{1,0:T(8,128)} %get-tuple-element.106) | copy-start | bytes 98308
  385.9 34.6 %copy-start.34 = (f32[8,320]{1,0:T(8,128)S(1)}, f32[8,320]{1,0:T(8,128)}, u32[]{:S(2)}) copy-start(f32[8,320]{1,0:T(8,128)} %get-tuple-element.108) | copy-start | bytes 30724
  385.9 34.6 %copy-start.36 = (f32[8,192]{1,0:T(8,128)S(1)}, f32[8,192]{1,0:T(8,128)}, u32[]{:S(2)}) copy-start(f32[8,192]{1,0:T(8,128)} %get-tuple-element.109) | copy-start | bytes 18436
  385.9 34.6 %copy-start.39 = (f32[8,8]{1,0:T(8,128)S(1)}, f32[8,8]{1,0:T(8,128)}, u32[]{:S(2)}) copy-start(f32[8,8]{1,0:T(8,128)} %get-tuple-element.111) | copy-start | bytes 772
  385.9 36.1 %copy-start.24 = (f32[24,128]{1,0:T(8,128)S(1)}, f32[24,128]{1,0:T(8,128)}, u32[]{:S(2)}) copy-start(f32[24,128]{1,0:T(8,128)} %all_sum.13.sums_in) | copy-start | bytes 36868
  572.6 61.4 %copy-start.25 = (f32[24,128]{1,0:T(8,128)S(1)}, f32[24,128]{1,0:T(8,128)}, u32[]{:S(2)}) copy-start(f32[24,128]{1,0:T(8,128)} %all_sum.15.sums_two) | copy-start | bytes 36868
  572.6 61.4 %copy-start.26 = (f32[24,128]{1,0:T(8,128)S(1)}, f32[24,128]{1,0:T(8,128)}, u32[]{:S(2)}) copy-start(f32[24,128]{1,0:T(8,128)} %all_sum.16.sums_in) | copy-start | bytes 36868
  634.6 80.8 %copy-start.14 = (f32[24,128]{1,0:T(8,128)S(1)}, f32[24,128]{1,0:T(8,128)}, u32[]{:S(2)}) copy-start(f32[24,128]{1,0:T(8,128)} %all_sum.9.stats.totals.stats_one) | copy-start | bytes 36868
  634.6 82.6 %copy-start.22 = (f32[24,128]{1,0:T(8,128)S(1)}, f32[24,128]{1,0:T(8,128)}, u32[]{:S(2)}) copy-start(f32[24,128]{1,0:T(8,128)} %all_sum.12.stats) | copy-start | bytes 36868
  634.6 88.5 %copy-start.29 = (f32[8,128]{1,0:T(8,128)S(1)}, f32[8,128]{1,0:T(8,128)}, u32[]{:S(2)}) copy-start(f32[8,128]{1,0:T(8,128)} %all_sum.14.proj_sums) | copy-start | bytes 12292
  634.6 90.5 %copy-start.18 = (f32[24,128]{1,0:T(8,128)S(1)}, f32[24,128]{1,0:T(8,128)}, u32[]{:S(2)}) copy-start(f32[24,128]{1,0:T(8,128)} %all_sum.10.stats.stats_two) | copy-start | bytes 36868
  634.6 90.5 %copy-start.27 = (f32[8,128]{1,0:T(8,128)S(1)}, f32[8,128]{1,0:T(8,128)}, u32[]{:S(2)}) copy-start(f32[8,128]{1,0:T(8,128)} %all_sum.11.stats.proj_stats) | copy-start | bytes 12292
  634.6 97.1 %copy-start.4 = (bf16[320,2304]{1,0:T(8,128)(2,1)S(1)}, bf16[320,2304]{1,0:T(8,128)(2,1)}, u32[]{:S(2)}) copy-start(bf16[320,2304]{1,0:T(8,128)(2,1)} %grad_reduce.4) | copy-start | bytes 4423684
  715.4 20.5 %copy-start.2 = (bf16[320,2560]{1,0:T(8,128)(2,1)S(1)}, bf16[320,2560]{1,0:T(8,128)(2,1)}, u32[]{:S(2)}) copy-start(bf16[320,2560]{1,0:T(8,128)(2,1)} %grad_reduce.5) | copy-start | bytes 4915204
  750.3 46.1 %copy-start.5 = (bf16[320,2304]{1,0:T(8,128)(2,1)S(1)}, bf16[320,2304]{1,0:T(8,128)(2,1)}, u32[]{:S(2)}) copy-start(bf16[320,2304]{1,0:T(8,128)(2,1)} %grad_reduce.4) | copy-start | bytes 4423684
  791.7 16.4 %copy-start.20 = (f32[5784]{0:T(1024)}, f32[5784]{0:T(1024)S(1)}, u32[]{:S(2)}) copy-start(f32[5784]{0:T(1024)S(1)} %concatenate.26) | copy-start | bytes 69412
  (26 other events, 145.6 us)
Sparse Core Ops, SparseCore 0:
  422.2 83.8 all-gather.2

commit v2 on v1

v2 whole, which is shorter than its diff:
```python
import functools

import jax
import jax.numpy as jnp
from jax import lax
from jax.experimental import pallas as pl
from jax.experimental.pallas import tpu as pltpu
from jax.sharding import PartitionSpec as P

WIDTH_IN = 192
WIDTH_OUT = 320
SQUEEZE = 48
CLASSES = 1000
EXPERTS = 8
KERNEL = 5
MAP_SIDE = 16
TAPS = KERNEL * KERNEL
PIXELS = MAP_SIDE * MAP_SIDE
LANES = 128
CLASS_PAD = 1024
TOTAL_ROW = 18
eps_norm = 0.001
highest = lax.Precision.HIGHEST
MESH = pl.DeviceIdType.MESH
f32 = jnp.float32
bf16 = jnp.bfloat16
VMEM = pltpu.VMEM
VLIMIT = 60 * 1024 * 1024


def dot(a, b, dims=((1,), (0,)), precision=None):
    return lax.dot_general(a, b, (dims, ((), ())), precision=precision, preferred_element_type=f32)


NN = ((1,), (0,))
NT = ((1,), (1,))
TN = ((0,), (0,))


def sig(x):
    return 0.5 * jnp.tanh(0.5 * x) + 0.5


def dsilu(n):
    s = sig(n)
    return s * (1.0 + n * (1.0 - s))


def rsum(x):
    return jnp.sum(x, axis=0, keepdims=True)


def split(x):
    high = x.astype(bf16)
    return jnp.concatenate([high, (x - high.astype(f32)).astype(bf16)], axis=0)


def sum_peers(nd, nz):
    d = lax.axis_index("dp")
    z = lax.axis_index("chan")
    in_plane = [(lax.rem(d + k, nd), z) for k in range(1, nd)]
    along = [(d, lax.rem(z + k, nz)) for k in range(1, nz)]
    return in_plane, along


def signal(peers):
    barrier = pltpu.get_barrier_semaphore()
    for peer in peers:
        pl.semaphore_signal(barrier, inc=1, device_id=peer, device_id_type=MESH)


def sum_start(nd, nz):
    in_plane, along = sum_peers(nd, nz)
    signal(in_plane + along)


def met(nd, nz):
    pl.semaphore_wait(pltpu.get_barrier_semaphore(), nd + nz - 2)


def sum_finish(nd, nz, x_ref, o_ref, plane, depth, s1, r1, s2, r2):
    d = lax.axis_index("dp")
    z = lax.axis_index("chan")
    in_plane, along = sum_peers(nd, nz)
    first = []
    for k, peer in enumerate(in_plane):
        first.append(
            pltpu.make_async_remote_copy(
                src_ref=x_ref,
                dst_ref=plane.at[d],
                send_sem=s1.at[k],
                recv_sem=r1.at[k],
                device_id=peer,
                device_id_type=MESH,
            )
        )
        first[-1].start()
    plane[d] = x_ref[...]
    for copy in first:
        copy.wait_recv()
    total = plane[0]
    for k in range(1, nd):
        total = total + plane[k]
    depth[z] = total
    second = []
    for k, peer in enumerate(along):
        second.append(
            pltpu.make_async_remote_copy(
                src_ref=depth.at[z],
                dst_ref=depth.at[z],
                send_sem=s2.at[k],
                recv_sem=r2.at[k],
                device_id=peer,
                device_id_type=MESH,
            )
        )
        second[-1].start()
    for copy in second:
        copy.wait_recv()
    total = depth[0]
    for k in range(1, nz):
        total = total + depth[k]
    o_ref[...] = total
    for copy in first + second:
        copy.wait_send()


def sum_scratch(rows, nd, nz):
    return [
        VMEM((rows, LANES), f32),
        VMEM((nd, rows, LANES), f32),
        VMEM((nz, rows, LANES), f32),
        pltpu.SemaphoreType.DMA((nd,)),
        pltpu.SemaphoreType.DMA((nd,)),
        pltpu.SemaphoreType.DMA((nz,)),
        pltpu.SemaphoreType.DMA((nz,)),
    ]


def params(ident=None):
    if ident is None:
        return pltpu.CompilerParams(vmem_limit_bytes=VLIMIT)
    return pltpu.CompilerParams(vmem_limit_bytes=VLIMIT, collective_id=ident, has_side_effects=True)


def sum_kernel(nd, nz, x_ref, o_ref, *comm):
    sum_start(nd, nz)
    met(nd, nz)
    sum_finish(nd, nz, x_ref, o_ref, *comm)


def all_sum(x, nd, nz, ident):
    return pl.pallas_call(
        functools.partial(sum_kernel, nd, nz),
        out_shape=jax.ShapeDtypeStruct(x.shape, x.dtype),
        in_specs=[pl.BlockSpec(memory_space=VMEM)],
        out_specs=pl.BlockSpec(memory_space=VMEM),
        scratch_shapes=sum_scratch(x.shape[0], nd, nz)[1:],
        compiler_params=params(ident),
        name="all_sum",
    )(x)


def by_column(width):
    return (width // 2) % LANES == 0


def pad_rows(rows, width, nd):
    unit = 16 * (nd // 2 if by_column(width) else nd)
    return -(-rows // unit) * unit


def core_block(rows, width, core):
    if by_column(width):
        return 0, rows, pl.multiple_of(core * (width // 2), LANES), width // 2
    return pl.multiple_of(core * (rows // 2), 16), rows // 2, 0, width


def part(rows, width, nd, core, place):
    row, count, col, cols = core_block(rows, width, core)
    unit = count // (nd // 2)
    return pl.multiple_of(row + place * unit, 16), unit, col, cols


class Net:
    def __init__(self, nd, nz):
        self.nd, self.nz, self.nxy = nd, nz, nd // 2
        self.d = lax.axis_index("dp")
        self.z = lax.axis_index("chan")
        self.core = lax.rem(self.d, 2)
        self.place = self.d // 2
        self.far = [lax.rem(self.z + k, nz) for k in range(1, nz)]
        self.others = [lax.rem(self.place + k, self.nxy) for k in range(1, self.nxy)]
        self.along = [(self.d, zz) for zz in self.far]
        self.plane = [(2 * o + self.core, self.z) for o in self.others]
        self.twin = (2 * self.place + 1 - self.core, self.z)

    def copy(self, src, dst, sems, k, peer):
        return pltpu.make_async_remote_copy(
            src_ref=src,
            dst_ref=dst,
            send_sem=sems[0].at[k],
            recv_sem=sems[1].at[k],
            device_id=peer,
            device_id_type=MESH,
        )


def start(copies):
    for copy in copies:
        copy.start()


def arrived(copies):
    for copy in copies:
        copy.wait_recv()


def sent(copies):
    for copy in copies:
        copy.wait_send()


def pair(n):
    return [pltpu.SemaphoreType.DMA((n,)), pltpu.SemaphoreType.DMA((n,))]


def lanes(first, count):
    return pl.ds(pl.multiple_of(first, LANES), count)


def tall(first, count):
    return pl.ds(pl.multiple_of(first, 16), count)


def spot(ref, shape, zz, row, unit, col, cols):
    if len(ref.shape) == 3:
        return ref.at[zz, tall(row, unit), lanes(col, cols)]
    return ref.at[tall(row, unit), lanes(zz * shape[1] + col, cols)]


def shard_shape(full, nz):
    if len(full.shape) == 3:
        return full.shape[1:]
    return (full.shape[0], full.shape[1] // nz)


def own_copy(net, shape, src, dst, sem):
    return pltpu.make_async_copy(src, spot(dst, shape, net.z, 0, shape[0], 0, shape[1]), sem)


def gather_far(net, shape, src, dst, sems):
    rows, width = shape
    row, unit, col, cols = part(rows, width, net.nd, net.core, net.place)
    block = src.at[tall(row, unit), lanes(col, cols)]
    return [
        net.copy(block, spot(dst, shape, net.z, row, unit, col, cols), sems, k, peer)
        for k, peer in enumerate(net.along)
    ]


def gather_plane(net, shape, ref, sems, k):
    rows, width = shape
    row, unit, col, cols = part(rows, width, net.nd, net.core, net.place)
    block = spot(ref, shape, net.far[k], row, unit, col, cols)
    n = net.nxy - 1
    return [net.copy(block, block, sems, k * n + q, peer) for q, peer in enumerate(net.plane)]


def gather_twin(net, shape, ref, sems, k):
    rows, width = shape
    row, unit, col, cols = core_block(rows, width, net.core)
    block = spot(ref, shape, net.far[k], row, unit, col, cols)
    return [net.copy(block, block, sems, k, net.twin)]


def every(stage, net, shape, ref, sems):
    return [copy for k in range(net.nz - 1) for copy in stage(net, shape, ref, sems, k)]


def squares_of(ref, rows):
    step_rows = 16 if ref.dtype == bf16 else 8
    whole_rows = rows // step_rows * step_rows

    def step(i, total):
        value = ref[pl.ds(pl.multiple_of(i * step_rows, step_rows), step_rows), :].astype(f32)
        return total + value * value

    total = jnp.sum(lax.fori_loop(0, whole_rows // step_rows, step, jnp.zeros((step_rows, ref.shape[1]), f32)))
    if whole_rows < rows:
        last = ref[whole_rows:rows, :].astype(f32)
        total = total + jnp.sum(last * last)
    return total


def row_of(total):
    lane = lax.broadcasted_iota(jnp.int32, (1, LANES), 1)
    return jnp.where(lane == 0, total, 0.0)


def first_kernel(nd, nz, shape, shape_b, block_ref, head_ref, hside_ref, side_ref, full, full_b, side, gain, kb, kh, kc, squares, wide, tall_h, tall_s, low, side_buf, gain_buf, far_s, far_r, plane_s, plane_r, twin_s, twin_r, side_s, side_r, gain_s, gain_r, later_s, later_r, local):
    net = Net(nd, nz)
    signal(net.along + net.plane + [net.twin])
    rows = shape[0]
    total_rows = block_ref.shape[0]
    fetch = [
        pltpu.make_async_copy(block_ref.at[pl.ds(0, rows)], wide.at[pl.ds(0, rows)], local.at[0]),
        pltpu.make_async_copy(
            block_ref.at[pl.ds(rows, total_rows - rows)], wide.at[pl.ds(rows, total_rows - rows)], local.at[1]
        ),
        pltpu.make_async_copy(hside_ref, tall_s, local.at[2]),
        pltpu.make_async_copy(head_ref, tall_h, local.at[3]),
    ]
    fetch[0].start()
    fetch[0].wait()
    start(fetch[1:])

    @pl.loop(0, rows // 16)
    def _(i):
        at = tall(i * 16, 16)
        low[at, :] = wide[at, :].astype(bf16)

    own = own_copy(net, shape, low, full, local.at[4])
    own.start()
    pl.semaphore_wait(pltpu.get_barrier_semaphore(), nz - 1 + nd // 2)
    far = gather_far(net, shape, low, full, (far_s, far_r))
    start(far)
    side_buf[net.z] = jnp.transpose(side_ref[...])
    sides = [
        net.copy(side_buf.at[net.z], side_buf.at[net.z], (side_s, side_r), k, peer)
        for k, peer in enumerate(net.along)
    ]
    start(sides)
    fetch[2].wait()
    gain_buf[net.z] = jnp.transpose(tall_s[:, 0:LANES])[0:8]
    gains = [
        net.copy(gain_buf.at[net.z], gain_buf.at[net.z], (gain_s, gain_r), k, peer)
        for k, peer in enumerate(net.along)
    ]
    start(gains)
    fetch[1].wait()
    first = WIDTH_IN + TAPS
    for i in range(WIDTH_OUT // 16):
        kb[16 * i : 16 * (i + 1), :] = wide[first + 16 * i : first + 16 * (i + 1), :].astype(bf16)
    own_b = own_copy(net, shape_b, kb, full_b, local.at[5])
    own_b.start()
    planes = []
    for k in range(nz - 1):
        arrived([far[nz - 2 - k]])
        planes.append(gather_plane(net, shape, full, (plane_s, plane_r), k))
        start(planes[k])
    later = gather_far(net, shape_b, kb, full_b, (later_s, later_r))
    start(later)
    fetch[3].wait()

    @pl.loop(0, WIDTH_OUT // 16)
    def _(i):
        at = tall(i * 16, 16)
        kh[at, :] = tall_h[at, :].astype(bf16)

    for i in range(tall_s.shape[0] // 16):
        value = tall_s[16 * i : 16 * (i + 1), 2 : 2 + CLASSES]
        kc[16 * i : 16 * (i + 1), :] = jnp.concatenate(
            [value, jnp.zeros((16, CLASS_PAD - CLASSES), f32)], axis=1
        ).astype(bf16)
    squares[...] = jnp.zeros_like(squares)
    for k, (ref, count) in enumerate(
        ((wide, total_rows), (side_ref, side_ref.shape[0]), (tall_h, WIDTH_OUT), (tall_s, tall_s.shape[0]))
    ):
        squares[k : k + 1, :] = row_of(squares_of(ref, count))
    twins = []
    for k in range(nz - 1):
        arrived(planes[k])
        twins.append(gather_twin(net, shape, full, (twin_s, twin_r), k))
        start(twins[k])
    arrived(sides + gains)
    side[...] = jnp.zeros_like(side)
    side[0 : side_ref.shape[1], :] = jnp.concatenate([side_buf[k] for k in range(nz)], axis=1)
    gain[...] = jnp.concatenate([gain_buf[k] for k in range(nz)], axis=1)
    for k in range(nz - 1):
        arrived(twins[k])
    arrived(later)
    sent(far + sides + gains + later)
    for k in range(nz - 1):
        sent(planes[k] + twins[k])
    own.wait()
    own_b.wait()


def first_gather(block, head_w, head_side, side, nd, nz, ident):
    shape = (pad_rows(WIDTH_IN + TAPS, block.shape[1], nd), block.shape[1])
    shape_b = (pad_rows(WIDTH_OUT, block.shape[1], nd), block.shape[1])
    shape_h = (pad_rows(WIDTH_OUT, head_w.shape[1], nd), head_w.shape[1])
    shape_c = (pad_rows(head_side.shape[0], CLASS_PAD, nd), CLASS_PAD)
    hbm = pl.BlockSpec(memory_space=pltpu.HBM)
    vmem = pl.BlockSpec(memory_space=VMEM)
    own_head = head_side.shape[0]
    return pl.pallas_call(
        functools.partial(first_kernel, nd, nz, shape, shape_b),
        out_shape=[
            jax.ShapeDtypeStruct((shape[0], nz * shape[1]), bf16),
            jax.ShapeDtypeStruct((shape_b[0], nz * shape_b[1]), bf16),
            jax.ShapeDtypeStruct((104, nz * side.shape[0]), f32),
            jax.ShapeDtypeStruct((8, nz * own_head), f32),
            jax.ShapeDtypeStruct(shape_b, bf16),
            jax.ShapeDtypeStruct(shape_h, bf16),
            jax.ShapeDtypeStruct(shape_c, bf16),
            jax.ShapeDtypeStruct((8, LANES), f32),
        ],
        in_specs=[hbm, hbm, hbm, vmem],
        out_specs=[hbm, hbm] + [vmem] * 6,
        scratch_shapes=[
            VMEM(block.shape, f32),
            VMEM(head_w.shape, f32),
            VMEM(head_side.shape, f32),
            VMEM(shape, bf16),
            VMEM((nz, side.shape[1], side.shape[0]), f32),
            VMEM((nz, 8, own_head), f32),
        ]
        + pair(nz - 1)
        + pair((nz - 1) * (nd // 2 - 1))
        + pair(nz - 1)
        + pair(nz - 1) * 3
        + [pltpu.SemaphoreType.DMA((6,))],
        compiler_params=params(ident),
        name="first_gather",
    )(block, head_w, head_side, side)


def reduce_sizes(rows, width, nd):
    unit, cols = (rows, width // 2) if by_column(width) else (rows // 2, width)
    return unit, cols, unit // (nd // 2)


def reduce_twin(net, shape, g_ref, twin_buf, sems, k):
    row, unit, col, cols = core_block(shape[0], shape[1], 1 - net.core)
    return net.copy(
        g_ref.at[tall(row, unit), lanes(k * shape[1] + col, cols)], twin_buf.at[k], sems, k, net.twin
    )


def reduce_add(net, shape, g_ref, half, twin_buf, k):
    row, unit, col, cols = core_block(shape[0], shape[1], net.core)

    @pl.loop(0, unit // 16)
    def _(i):
        at = tall(i * 16, 16)
        mine = g_ref[tall(row + i * 16, 16), lanes(k * shape[1] + col, cols)]
        half[k, at, :] = (mine.astype(f32) + twin_buf[k, at, :].astype(f32)).astype(bf16)


def reduce_plane(net, shape, half, plane_buf, sems, k, base):
    size = reduce_sizes(*shape, net.nd)[2]
    n = net.nxy - 1
    return [
        net.copy(half.at[k, tall(o * size, size)], plane_buf.at[q, k - base], sems, (k - base) * n + q, net.plane[q])
        for q, o in enumerate(net.others)
    ]


def reduce_plane_sum(net, shape, half, plane_buf, out, k, base):
    size = reduce_sizes(*shape, net.nd)[2]

    @pl.loop(0, size // 16)
    def _(i):
        at = tall(i * 16, 16)
        total = half[k, tall(net.place * size + i * 16, 16), :].astype(f32)
        for q in range(net.nxy - 1):
            total = total + plane_buf[q, k - base, at, :].astype(f32)
        out[k, at, :] = total.astype(bf16)


def reduce_far(net, sums, depth_buf, sems):
    return [net.copy(sums.at[zz], depth_buf.at[k], sems, k, net.along[k]) for k, zz in enumerate(net.far)]


def reduce_far_sum(net, shape, sums, depth_buf, piece):
    @pl.loop(0, reduce_sizes(*shape, net.nd)[2] // 16)
    def _(i):
        at = tall(i * 16, 16)
        total = sums[net.z, at, :].astype(f32)
        for q in range(net.nz - 1):
            total = total + depth_buf[q, at, :].astype(f32)
        piece[at, :] = total.astype(bf16)


def spread_block(net, shape, out):
    row, unit, col, cols = part(shape[0], shape[1], net.nd, net.core, net.place)
    return out.at[tall(row, unit), lanes(col, cols)]


def spread_plane(net, shape, piece, out, sems):
    block = spread_block(net, shape, out)
    return [net.copy(piece, block, sems, q, peer) for q, peer in enumerate(net.plane)]


def spread_twin(net, shape, out, sems):
    row, unit, col, cols = core_block(shape[0], shape[1], net.core)
    block = out.at[tall(row, unit), lanes(col, cols)]
    return [net.copy(block, block, sems, 0, net.twin)]


def twin_scratch(shape, nd, nz):
    unit, cols, size = reduce_sizes(*shape, nd)
    return [VMEM((shape[0], nz * shape[1]), bf16), VMEM((nz, unit, cols), bf16)] + pair(nz)


def plane_scratch(shape, nd, count):
    unit, cols, size = reduce_sizes(*shape, nd)
    return [VMEM((nd // 2 - 1, count, size, cols), bf16)] + pair(count * (nd // 2 - 1))


def half_shape(shape, nd, nz):
    unit, cols, size = reduce_sizes(*shape, nd)
    return (nz, unit, cols)


def part_shape(shape, nd, nz):
    unit, cols, size = reduce_sizes(*shape, nd)
    return (nz, size, cols)


def ready(shape, k):
    return max(2, -(-(k + 1) * shape[1] // (LANES * EXPERTS)))


class Steps:
    def __init__(self):
        self.steps = {}

    def at(self, step, action):
        self.steps.setdefault(step, []).append(action)

    def emit(self, now, last):
        for step in sorted(self.steps):
            if step < last:

                @pl.when(now == step)
                def _(step=step):
                    for action in self.steps[step]:
                        action()

    def end(self, last):
        for step in sorted(self.steps):
            if step >= last:
                for action in self.steps[step]:
                    action()


def spread_scratch(shape, nd, nz):
    unit, cols, size = reduce_sizes(*shape, nd)
    return (
        [VMEM((nz - 1, size, cols), bf16), VMEM((size, cols), bf16), pltpu.SemaphoreType.DMA((1,))]
        + pair(nz - 1)
        + pair(nd // 2 - 1)
        + pair(1)
    )


class Twin:
    def __init__(self, net, shape, half, g_ref, twin_buf, ts, tr):
        self.net, self.shape, self.half, self.g, self.buf, self.sems = net, shape, half, g_ref, twin_buf, (ts, tr)

    def copy(self, k):
        return reduce_twin(self.net, self.shape, self.g, self.buf, self.sems, k)

    def begin(self, k):
        self.copy(k).start()

    def add(self, k):
        self.copy(k).wait_recv()
        reduce_add(self.net, self.shape, self.g, self.half, self.buf, k)

    def finish(self):
        for k in range(self.net.nz):
            self.copy(k).wait_send()


class Plane:
    def __init__(self, net, shape, half, out, base, count, buf, ps, pr):
        self.net, self.shape, self.half, self.out = net, shape, half, out
        self.shards, self.base, self.buf, self.sems = range(base, base + count), base, buf, (ps, pr)

    def copies(self, k):
        return reduce_plane(self.net, self.shape, self.half, self.buf, self.sems, k, self.base)

    def begin(self, k):
        start(self.copies(k))

    def add(self, then=None):
        for k in self.shards:
            arrived(self.copies(k))
            reduce_plane_sum(self.net, self.shape, self.half, self.buf, self.out, k, self.base)
            if then is not None:
                then(k)

    def finish(self):
        for k in self.shards:
            sent(self.copies(k))


class Spread:
    def __init__(self, net, shape, sums, out, depth_buf, piece, local, fs, fr, ps, pr, ts, tr):
        self.net, self.shape, self.sums, self.out = net, shape, sums, out
        self.depth_buf, self.piece, self.local = depth_buf, piece, local
        self.far_sems, self.plane_sems, self.twin_sems = (fs, fr), (ps, pr), (ts, tr)

    def far(self):
        return reduce_far(self.net, self.sums, self.depth_buf, self.far_sems)

    def own(self):
        return pltpu.make_async_copy(self.piece, spread_block(self.net, self.shape, self.out), self.local.at[0])

    def plane(self):
        return spread_plane(self.net, self.shape, self.piece, self.out, self.plane_sems)

    def twin(self):
        return spread_twin(self.net, self.shape, self.out, self.twin_sems)

    def send(self, k):
        net = self.net
        slot = lax.rem(k - net.z - 1 + net.nz, net.nz)

        @pl.when(net.z != k)
        def _():
            net.copy(self.sums.at[k], self.depth_buf.at[slot], self.far_sems, slot, (net.d, k)).start()

    def share(self):
        arrived(self.far())
        reduce_far_sum(self.net, self.shape, self.sums, self.depth_buf, self.piece)
        self.own().start()
        start(self.plane())

    def cross(self):
        arrived(self.plane())
        self.own().wait()
        start(self.twin())

    def finish(self):
        arrived(self.twin())
        sent(self.far() + self.plane() + self.twin())


def up_to(size):
    return -(-size // LANES) * LANES


def share_width(lines, nz):
    one = [0]
    for x in lines[0], lines[2], lines[3]:
        one.append(one[-1] + up_to(x.shape[1] // nz))
    for _ in range(3):
        one.append(one[-1] + LANES)
    two = [0]
    for x in lines[1], lines[4], lines[5]:
        two.append(two[-1] + up_to(x.shape[1]))
    return one, two, max(one[-1], two[-1])


def share_scratch(width, nd, nz):
    return (
        [VMEM((nz, 8, width), f32), pltpu.SemaphoreType.DMA((1,))]
        + pair(nz - 1)
        + pair(nd // 2 - 1)
        + pair(nd // 2)
    )


def fit(x, width):
    if x.shape[1] == width:
        return x
    return jnp.concatenate([x, jnp.zeros((x.shape[0], width - x.shape[1]), f32)], axis=1)


class Share:
    def __init__(self, net, rows_all, lines, local, fs, fr, ps, pr, ts, tr):
        self.net, self.rows, self.lines, self.local = net, rows_all, lines, local
        self.far_sems, self.plane_sems, self.twin_sems = (fs, fr), (ps, pr), (ts, tr)
        self.me = net.d * net.nz + net.z

    def fill(self, nb, cut, narrow, wide):
        width = self.lines.shape[2]
        self.lines[...] = jnp.zeros_like(self.lines)
        two = fit(jnp.concatenate([fit(x, up_to(x.shape[1])) for x in wide], axis=1), width)[:nb]
        last = [fit(x, LANES) for x in narrow]
        for k in range(self.net.nz):
            parts = []
            for x in cut:
                own = x.shape[1] // self.net.nz
                parts.append(fit(x[:, k * own : (k + 1) * own], up_to(own)))
            one = fit(jnp.concatenate(parts + last, axis=1), width)[:nb]
            self.lines[k, 0 : 2 * nb, :] = jnp.concatenate([one, two], axis=0)

    def far_copies(self):
        net = self.net
        return [
            net.copy(self.lines.at[zz], self.rows.at[self.me], self.far_sems, k, net.along[k])
            for k, zz in enumerate(net.far)
        ]

    def plane_copies(self):
        net = self.net
        block = self.rows.at[pl.ds(net.d * net.nz, net.nz)]
        return [net.copy(block, block, self.plane_sems, q, peer) for q, peer in enumerate(net.plane)]

    def twin_copies(self):
        net = self.net
        out = []
        for o in range(net.nxy):
            block = self.rows.at[pl.ds((2 * o + net.core) * net.nz, net.nz)]
            out.append(net.copy(block, block, self.twin_sems, o, net.twin))
        return out

    def far(self):
        start(self.far_copies())
        self.own().start()

    def own(self):
        return pltpu.make_async_copy(self.lines.at[self.net.z], self.rows.at[self.me], self.local.at[0])

    def plane(self):
        arrived(self.far_copies())
        self.own().wait()
        start(self.plane_copies())

    def twin(self):
        arrived(self.plane_copies())
        start(self.twin_copies())

    def finish(self):
        arrived(self.twin_copies())
        sent(self.far_copies() + self.plane_copies() + self.twin_copies())


def build_mix(gates, nb, ref):
    deep = LANES * EXPERTS
    row = lax.broadcasted_iota(jnp.int32, (deep, EXPERTS), 0)
    col = lax.broadcasted_iota(jnp.int32, (deep, EXPERTS), 1)
    pick = jnp.where((row & (EXPERTS - 1)) == col, 1.0, 0.0).astype(f32)
    row = lax.broadcasted_iota(jnp.int32, (deep, LANES), 0)
    col = lax.broadcasted_iota(jnp.int32, (deep, LANES), 1)
    same = (row >> 3) == col
    for b in range(nb):
        spread = jnp.broadcast_to(gates[b : b + 1, :], (LANES, EXPERTS))
        value = jnp.where(same, dot(pick, spread, NT, highest), 0.0)
        high = value.astype(bf16)
        ref[:, b * LANES : (b + 1) * LANES] = high
        ref[:, (nb + b) * LANES : (nb + b + 1) * LANES] = (value - high.astype(f32)).astype(bf16)


def mix_kernels(kernels, mix):
    both = dot(kernels, mix)
    half = both.shape[1] // 2
    return both[:, :half] + both[:, half:]


def gate_sums(rows):
    deep = LANES * EXPERTS
    row = lax.broadcasted_iota(jnp.int32, (deep, EXPERTS), 0)
    col = lax.broadcasted_iota(jnp.int32, (deep, EXPERTS), 1)
    pick = jnp.where((row & (EXPERTS - 1)) == col, 1.0, 0.0).astype(f32)
    return dot(rows, pick, NN, highest)


def gate_rows(grad, kernel_block):
    both = dot(grad, kernel_block, TN)
    row = lax.broadcasted_iota(jnp.int32, both.shape, 0)
    col = lax.broadcasted_iota(jnp.int32, both.shape, 1)
    return rsum(jnp.where(row == (col >> 3), both, 0.0))


def norm_rows(stats, chunk, chunks, total):
    mean = stats[pl.ds(chunk, 1), :] / total
    var = stats[pl.ds(chunks + chunk, 1), :] / total - mean * mean
    return mean, lax.rsqrt(var + eps_norm)


def whole(shape):
    return pl.BlockSpec(shape, lambda *_: (0,) * len(shape), pipeline_mode=pl.Buffered(1))


def image(b):
    return pl.ds(pl.multiple_of(b * PIXELS, PIXELS), PIXELS)


def expand_kernel(nd, nz, nb, chunks, shapes, kern_ref, images, mask, mask_rows, counts, route, in_b, kh, pre, taps, stats_all, mix, gates, pooled, full_b, full_h, stats, *comm):
    j = pl.program_id(0)
    sems = comm[6:]
    comm = comm[:6]
    net = Net(nd, nz)
    local = sems[4]

    def copies():
        return every(gather_plane, net, shapes[0], full_b, sems[0:2]) + gather_far(
            net, shapes[1], kh, full_h, sems[2:4]
        )

    def own():
        return [own_copy(net, shapes[1], kh, full_h, local.at[0])]

    @pl.when(j == 1)
    def _():
        met(nd, nz)
        start(copies() + own())

    @pl.when(j == 0)
    def _():
        sum_start(nd, nz)
        stats[...] = jnp.zeros_like(stats)
        stats[2 * chunks : 2 * chunks + 1, :] = rsum(counts[...])
        stats[2 * chunks + 1 : 2 * chunks + 2, :] = rsum(jnp.where(counts[...] > 0.0, 1.0, 0.0))
        pool = dot(mask_rows[...], images[...]) / jnp.maximum(counts[:, 0:1], 1.0)
        pooled[...] = pool
        gate = sig(dot(pool, route[...], NN, highest))
        gates[...] = gate
        build_mix(gate, nb, mix)

    mixed = mix_kernels(kern_ref[...], mix[...])
    one = jnp.zeros((1, LANES), f32)
    two = jnp.zeros((1, LANES), f32)
    for b in range(nb):
        at = slice(b * PIXELS, (b + 1) * PIXELS)
        lane = slice(b * LANES, (b + 1) * LANES)
        taps[b] = mixed[WIDTH_IN : WIDTH_IN + 32, lane]
        value = dot(images[at, :], mixed[:WIDTH_IN, lane].astype(bf16))
        pre[at, :] = value
        masked = mask[at, :] * value
        one = one + rsum(masked)
        two = two + rsum(masked * value)
    stats[pl.ds(j, 1), :] = one
    stats[pl.ds(chunks + j, 1), :] = two

    @pl.when(j == chunks - 1)
    def _():
        sum_finish(nd, nz, stats, stats_all, *comm)
        arrived(copies())
        sent(copies())
        for copy in own():
            copy.wait()


def expand(kern, images, mask, mask_rows, counts, route, full_b, kh, nb, width, nd, nz, ident):
    chunks = width // LANES
    rows = nb * PIXELS
    deep = LANES * EXPERTS
    shapes = ((full_b.shape[0], full_b.shape[1] // nz), kh.shape)
    hbm = pl.BlockSpec(memory_space=pltpu.HBM)
    return pl.pallas_call(
        functools.partial(expand_kernel, nd, nz, nb, chunks, shapes),
        grid=(chunks,),
        out_shape=[
            jax.ShapeDtypeStruct((rows, width), f32),
            jax.ShapeDtypeStruct((nb, 32, width), f32),
            jax.ShapeDtypeStruct((24, LANES), f32),
            jax.ShapeDtypeStruct((deep, 2 * nb * LANES), bf16),
            jax.ShapeDtypeStruct((8, EXPERTS), f32),
            jax.ShapeDtypeStruct((8, WIDTH_IN), f32),
        ]
        + [
            jax.ShapeDtypeStruct(full_b.shape, bf16),
            jax.ShapeDtypeStruct((kh.shape[0], nz * kh.shape[1]), bf16),
        ],
        in_specs=[
            pl.BlockSpec((kern.shape[0], deep), lambda j: (0, j)),
            whole(images.shape),
            whole(mask.shape),
            whole(mask_rows.shape),
            whole(counts.shape),
            whole(route.shape),
        ]
        + [hbm, whole(kh.shape)],
        out_specs=[
            pl.BlockSpec((rows, LANES), lambda j: (0, j)),
            pl.BlockSpec((nb, 32, LANES), lambda j: (0, 0, j)),
            whole((24, LANES)),
            whole((deep, 2 * nb * LANES)),
            whole((8, EXPERTS)),
            whole((8, WIDTH_IN)),
        ]
        + [hbm] * 2,
        scratch_shapes=sum_scratch(24, nd, nz)
        + pair((nz - 1) * (nd // 2 - 1))
        + pair(nz - 1)
        + [pltpu.SemaphoreType.DMA((1,))],
        input_output_aliases={6: 6},
        compiler_params=params(ident),
        name="expand",
    )(kern, images, mask, mask_rows, counts, route, full_b, kh)


def shifted(value, step):
    if step == 0:
        return value
    col = lax.broadcasted_iota(jnp.int32, value.shape, 0) & (MAP_SIDE - 1)
    moved = pltpu.roll(value, (-step) % PIXELS, 0)
    keep = (col + step >= 0) & (col + step < MAP_SIDE)
    return jnp.where(keep, moved, 0.0)


def depth_kernel(nd, nz, nb, chunks, shapes, pre, taps, mask, side, stats, in_b, in_h, kc, out, sums_all, full_b, full_h, full_c, buf, held, sums, *comm):
    j = pl.program_id(0)
    sems = comm[6:]
    comm = comm[:6]
    net = Net(nd, nz)

    def copies():
        return (
            every(gather_twin, net, shapes[0], full_b, sems[0:2])
            + every(gather_plane, net, shapes[1], full_h, sems[2:4])
            + gather_far(net, shapes[2], kc, full_c, sems[4:6])
        )

    def own():
        return own_copy(net, shapes[2], kc, full_c, sems[6].at[0])


    @pl.when(j == 0)
    def _():
        sum_start(nd, nz)

    @pl.when(j == 1)
    def _():
        met(nd, nz)
        start(copies())
        own().start()

    @pl.when(j == 0)
    def _():
        sums[...] = jnp.zeros_like(sums)

    mean, rstd = norm_rows(stats, j, chunks, stats[2 * chunks : 2 * chunks + 1, :])
    scale = rstd * side[2 * SQUEEZE : 2 * SQUEEZE + 1, :]
    bias = side[2 * SQUEEZE + 1 : 2 * SQUEEZE + 2, :]
    held[...] = jnp.zeros_like(held)

    @pl.loop(0, nb)
    def _(b):
        at = image(b)
        normed = (pre[at, :] - mean) * scale + bias
        act = normed * sig(normed) * mask[at, :]
        for s in range(KERNEL):
            buf[s] = shifted(act, s - KERNEL // 2)
        taps_now = [jnp.broadcast_to(taps[b, t : t + 1, :], (MAP_SIDE, LANES)) for t in range(TAPS)]
        acc = [None] * MAP_SIDE
        for y in range(MAP_SIDE):
            for s in range(KERNEL):
                x = buf[s, y * MAP_SIDE : (y + 1) * MAP_SIDE, :]
                for r in range(KERNEL):
                    i = y - r + KERNEL // 2
                    if 0 <= i < MAP_SIDE:
                        term = taps_now[r * KERNEL + s] * x
                        acc[i] = term if acc[i] is None else acc[i] + term
            done = [y - 2] if y < MAP_SIDE - 1 else [y - 2, y - 1, y]
            for i in done:
                if i >= 0:
                    out[pl.ds(pl.multiple_of(b * PIXELS + i * MAP_SIDE, MAP_SIDE), MAP_SIDE), :] = acc[i]
        value = out[at, :]
        masked = mask[at, :] * value
        held[0:1, :] += rsum(masked)
        held[1:2, :] += rsum(masked * value)

    sums[pl.ds(j, 1), :] = held[0:1, :]
    sums[pl.ds(chunks + j, 1), :] = held[1:2, :]

    @pl.when(j == chunks - 1)
    def _():
        sum_finish(nd, nz, sums, sums_all, *comm)
        arrived(copies())
        sent(copies())
        own().wait()


def depthwise(pre, taps, mask, side, stats, full_b, full_h, kc, nb, nd, nz, ident):
    rows, width = pre.shape
    chunks = width // LANES
    wide = lambda j: (0, j)
    later = (full_b, full_h)
    shapes = tuple(shard_shape(k, nz) for k in later) + (kc.shape,)
    hbm = pl.BlockSpec(memory_space=pltpu.HBM)
    planes = (nz - 1) * (nd // 2 - 1)
    return pl.pallas_call(
        functools.partial(depth_kernel, nd, nz, nb, chunks, shapes),
        grid=(chunks,),
        out_shape=[
            jax.ShapeDtypeStruct((rows, width), f32),
            jax.ShapeDtypeStruct((24, LANES), f32),
        ]
        + [jax.ShapeDtypeStruct(k.shape, bf16) for k in later]
        + [jax.ShapeDtypeStruct((nz,) + kc.shape, bf16)],
        in_specs=[
            pl.BlockSpec((rows, LANES), wide),
            pl.BlockSpec((nb, 32, LANES), lambda j: (0, 0, j)),
            whole(mask.shape),
            pl.BlockSpec((side.shape[0], LANES), wide),
            whole(stats.shape),
        ]
        + [hbm, hbm, whole(kc.shape)],
        out_specs=[pl.BlockSpec((rows, LANES), wide), whole((24, LANES))] + [hbm] * 3,
        scratch_shapes=[VMEM((KERNEL, PIXELS, LANES), f32), VMEM((8, LANES), f32)]
        + sum_scratch(24, nd, nz)
        + pair(nz - 1)
        + pair(planes)
        + pair(nz - 1)
        + [pltpu.SemaphoreType.DMA((1,))],
        input_output_aliases={5: 2, 6: 3},
        compiler_params=params(ident),
        name="depthwise",
    )(pre, taps, mask, side, stats, *later, kc)


def store_wide(ref, row, value):
    width = value.shape[1]
    for k in range(-(-width // LANES)):
        lanes = min(LANES, width - k * LANES)
        ref[row + k : row + k + 1, :lanes] = value[:, k * LANES : k * LANES + lanes]


def load_wide(ref, row, width):
    parts = []
    for k in range(-(-width // LANES)):
        lanes = min(LANES, width - k * LANES)
        parts.append(ref[row + k : row + k + 1, :lanes])
    return jnp.concatenate(parts, axis=1)


OUT_CHUNKS = -(-WIDTH_OUT // LANES)


def project_kernel(nd, nz, nb, chunks, shapes, dpre, mask, side, stats, totals, counts, sq_bias, kern, mix, in_h, in_c, excited, proj, pooled, gate_out, squeezed, sums_all, mixed, full_h, full_c, act, exc, sums, *comm):
    phase = pl.program_id(0)
    sems = comm[6:]
    comm = comm[:6]
    net = Net(nd, nz)

    def copies():
        return every(gather_twin, net, shapes[0], full_h, sems[0:2]) + every(
            gather_plane, net, shapes[1], full_c, sems[2:4]
        )

    j = pl.program_id(1)

    @pl.when((phase == 0) & (j == 0))
    def _():
        sum_start(nd, nz)

    @pl.when((phase == 0) & (j == 1))
    def _():
        met(nd, nz)
        start(copies())
    total = totals[2 * chunks : 2 * chunks + 1, :]

    @pl.when((phase == 0) & (j == 0))
    def _():
        squeezed[...] = jnp.zeros_like(squeezed)
        pooled[...] = jnp.zeros_like(pooled)
        sums[...] = jnp.zeros_like(sums)

    lane = pl.ds(pl.multiple_of(j * LANES, LANES), LANES)

    @pl.when(phase == 0)
    def _():
        both = mix_kernels(kern[...], mix[...])
        for b in range(nb):
            mixed[b, :, lane] = both[:, b * LANES : (b + 1) * LANES].astype(bf16)
        mean, rstd = norm_rows(stats, j, chunks, total)
        scale = rstd * side[2 * SQUEEZE + 2 : 2 * SQUEEZE + 3, :]
        bias = side[2 * SQUEEZE + 3 : 2 * SQUEEZE + 4, :]
        for b in range(nb):
            at = slice(b * PIXELS, (b + 1) * PIXELS)
            normed = (dpre[at, :] - mean) * scale + bias
            value = normed * sig(normed) * mask[at, :]
            act[j, at, :] = value
            pooled[b : b + 1, lane] = rsum(value) / jnp.maximum(counts[b : b + 1, :], 1.0)
        squeezed[...] += dot(pooled[:, lane], side[0:SQUEEZE, :], NT, highest)

    @pl.when(phase == 1)
    def _():
        before = squeezed[...] + sq_bias[...]
        gate = sig(
            dot(before * sig(before), side[SQUEEZE : 2 * SQUEEZE, :], NN, highest)
            + side[2 * SQUEEZE + 4 : 2 * SQUEEZE + 5, :]
        )
        gate_out[:, lane] = gate
        for b in range(nb):
            at = slice(b * PIXELS, (b + 1) * PIXELS)
            value = (act[j, at, :] * gate[b : b + 1, :]).astype(bf16)
            excited[at, :] = value
            exc[at, lane] = value

    @pl.when((phase == 1) & (j == chunks - 1))
    def _():
        one = jnp.zeros((1, WIDTH_OUT), f32)
        two = jnp.zeros((1, WIDTH_OUT), f32)
        for b in range(nb):
            at = slice(b * PIXELS, (b + 1) * PIXELS)
            value = dot(exc[at, :], mixed[b], NT)
            proj[at, :] = value
            masked = mask[at, 0:1] * value
            one = one + rsum(masked)
            two = two + rsum(masked * value)
        store_wide(sums, 0, one)
        store_wide(sums, OUT_CHUNKS, two)

    @pl.when((phase == 1) & (j == chunks - 1))
    def _():
        sum_finish(nd, nz, sums, sums_all, *comm)
        arrived(copies())
        sent(copies())


def project(dpre, mask, side, stats, totals, counts, sq_bias, full_b, mix, full_h, full_c, nb, nd, nz, ident):
    rows, width = dpre.shape
    chunks = width // LANES
    deep = LANES * EXPERTS
    later = (full_h, full_c)
    shapes = tuple(shard_shape(k, nz) for k in later)
    hbm = pl.BlockSpec(memory_space=pltpu.HBM)
    return pl.pallas_call(
        functools.partial(project_kernel, nd, nz, nb, chunks, shapes),
        grid=(2, chunks),
        out_shape=[
            jax.ShapeDtypeStruct((rows, width), bf16),
            jax.ShapeDtypeStruct((rows, WIDTH_OUT), f32),
            jax.ShapeDtypeStruct((8, width), f32),
            jax.ShapeDtypeStruct((8, width), f32),
            jax.ShapeDtypeStruct((8, SQUEEZE), f32),
            jax.ShapeDtypeStruct((8, LANES), f32),
            jax.ShapeDtypeStruct((nb, WIDTH_OUT, width), bf16),
        ]
        + [jax.ShapeDtypeStruct(k.shape, bf16) for k in later],
        in_specs=[
            pl.BlockSpec((rows, LANES), lambda p, j: (0, jnp.where(p == 0, j, chunks - 1))),
            whole(mask.shape),
            pl.BlockSpec((side.shape[0], LANES), lambda p, j: (0, j)),
            whole(stats.shape),
            whole(totals.shape),
            whole(counts.shape),
            whole(sq_bias.shape),
            pl.BlockSpec((WIDTH_OUT, deep), lambda p, j: (0, jnp.where(p == 0, j, chunks - 1))),
            whole(mix.shape),
        ]
        + [hbm] * 2,
        out_specs=[
            pl.BlockSpec((rows, LANES), lambda p, j: (0, jnp.where(p == 0, 0, j))),
            whole((rows, WIDTH_OUT)),
            whole((8, width)),
            whole((8, width)),
            whole((8, SQUEEZE)),
            whole((8, LANES)),
            whole((nb, WIDTH_OUT, width)),
        ]
        + [hbm] * 2,
        scratch_shapes=[VMEM((chunks, rows, LANES), f32), VMEM((rows, width), bf16)]
        + sum_scratch(8, nd, nz)
        + pair(nz - 1)
        + pair((nz - 1) * (nd // 2 - 1)),
        input_output_aliases={9: 7, 10: 8},
        compiler_params=params(ident),
        name="project",
    )(dpre, mask, side, stats, totals, counts, sq_bias, full_b, mix, *later)


def out_norm(sums, total):
    mean = load_wide(sums, 0, WIDTH_OUT) / total
    var = load_wide(sums, OUT_CHUNKS, WIDTH_OUT) / total - mean * mean
    return mean, lax.rsqrt(var + eps_norm)


def head_kernel(nd, nz, nb, chunks, shape, kern, proj, mask, mask_rows, counts, gain, route, stats, totals, in_c, low, pre, mixed_out, sums_all, mix_out, gates, pooled, full_c, sums, *comm):
    j = pl.program_id(0)
    sems = comm[6:]
    comm = comm[:6]
    net = Net(nd, nz)

    def copies():
        return every(gather_twin, net, shape, full_c, sems)


    @pl.when(j == 0)
    def _():
        sum_start(nd, nz)

    @pl.when(j == 1)
    def _():
        met(nd, nz)
        start(copies())

    @pl.when(j == 0)
    def _():
        sums[...] = jnp.zeros_like(sums)
        mean, rstd = out_norm(stats, totals[TOTAL_ROW : TOTAL_ROW + 1, 0:1])
        scale = rstd * gain[0:1, :]
        for b in range(nb):
            at = slice(b * PIXELS, (b + 1) * PIXELS)
            low[at, :] = (((proj[at, :] - mean) * scale + gain[1:2, :]) * mask[at, 0:1]).astype(bf16)
        pool = dot(mask_rows[...], low[...]) / jnp.maximum(counts[:, 0:1], 1.0)
        pooled[...] = pool
        gate = sig(dot(pool, route[...], NN, highest))
        gates[...] = gate
        build_mix(gate, nb, mix_out)

    mixed = mix_kernels(kern[...], mix_out[...])
    one = jnp.zeros((1, LANES), f32)
    two = jnp.zeros((1, LANES), f32)
    for b in range(nb):
        at = slice(b * PIXELS, (b + 1) * PIXELS)
        weight = mixed[:, b * LANES : (b + 1) * LANES].astype(bf16)
        mixed_out[b] = weight
        value = dot(low[at, :], weight)
        pre[at, :] = value
        masked = mask[at, :] * value
        one = one + rsum(masked)
        two = two + rsum(masked * value)
    sums[pl.ds(j, 1), :] = one
    sums[pl.ds(chunks + j, 1), :] = two


    @pl.when(j == chunks - 1)
    def _():
        sum_finish(nd, nz, sums, sums_all, *comm)
        arrived(copies())
        sent(copies())


def head(kern, proj, mask, mask_rows, counts, gain, route, stats, totals, full_c, nb, nd, nz, ident):
    rows = proj.shape[0]
    width = kern.shape[1] // EXPERTS
    chunks = width // LANES
    deep = LANES * EXPERTS
    wide = lambda j: (0, j)
    return pl.pallas_call(
        functools.partial(head_kernel, nd, nz, nb, chunks, shard_shape(full_c, nz)),
        grid=(chunks,),
        out_shape=[
            jax.ShapeDtypeStruct((rows, WIDTH_OUT), bf16),
            jax.ShapeDtypeStruct((rows, width), f32),
            jax.ShapeDtypeStruct((nb, WIDTH_OUT, width), bf16),
            jax.ShapeDtypeStruct((24, LANES), f32),
            jax.ShapeDtypeStruct((deep, 2 * nb * LANES), bf16),
            jax.ShapeDtypeStruct((8, EXPERTS), f32),
            jax.ShapeDtypeStruct((8, WIDTH_OUT), f32),
            jax.ShapeDtypeStruct(full_c.shape, bf16),
        ],
        in_specs=[
            pl.BlockSpec((WIDTH_OUT, deep), wide),
            whole(proj.shape),
            whole(mask.shape),
            whole(mask_rows.shape),
            whole(counts.shape),
            whole(gain.shape),
            whole(route.shape),
            whole(stats.shape),
            whole(totals.shape),
            pl.BlockSpec(memory_space=pltpu.HBM),
        ],
        out_specs=[
            whole((rows, WIDTH_OUT)),
            pl.BlockSpec((rows, LANES), wide),
            pl.BlockSpec((nb, WIDTH_OUT, LANES), lambda j: (0, 0, j)),
            whole((24, LANES)),
            whole((deep, 2 * nb * LANES)),
            whole((8, EXPERTS)),
            whole((8, WIDTH_OUT)),
            pl.BlockSpec(memory_space=pltpu.HBM),
        ],
        scratch_shapes=sum_scratch(24, nd, nz) + pair(nz - 1),
        input_output_aliases={9: 7},
        compiler_params=params(ident),
        name="head",
    )(kern, proj, mask, mask_rows, counts, gain, route, stats, totals, full_c)


def loss_kernel(nd, nz, nb, chunks, pre, mask, counts, labels, bias, cls, gain, stats, totals, features, grad_logits, grad_features, sums_all, logits, sums, *comm):
    phase = pl.program_id(0)
    j = pl.program_id(1)

    @pl.when((phase == 0) & (j == 0))
    def _():
        sum_start(nd, nz)

    @pl.when((phase == 0) & (j == 1))
    def _():
        met(nd, nz)
    lane = pl.ds(pl.multiple_of(j * LANES, LANES), LANES)

    @pl.when((phase == 0) & (j == 0))
    def _():
        sums[...] = jnp.zeros_like(sums)
        features[...] = jnp.zeros_like(features)
        logits[...] = jnp.zeros_like(logits)

    mean, rstd = norm_rows(stats, j, chunks, totals[TOTAL_ROW : TOTAL_ROW + 1, :])
    scale = rstd * gain[0:1, :]

    @pl.when(phase == 0)
    def _():
        for b in range(nb):
            at = slice(b * PIXELS, (b + 1) * PIXELS)
            normed = (pre[at, :] - mean) * scale + gain[1:2, :]
            features[b : b + 1, lane] = rsum(normed * sig(normed) * mask[at, :]) / jnp.maximum(
                counts[b : b + 1, :], 1.0
            )
        both = dot(split(features[:, lane]), cls[lane, :])
        logits[...] += both[:8] + both[8:]

    @pl.when((phase == 1) & (j == 0))
    def _():
        col = lax.broadcasted_iota(jnp.int32, (8, CLASS_PAD), 1)
        inside = col < CLASSES
        scores = jnp.where(inside, logits[...] + bias[...], -1e30)
        top = jnp.max(scores, axis=1, keepdims=True)
        spread = jnp.where(inside, jnp.exp(scores - top), 0.0)
        mass = jnp.sum(spread, axis=1, keepdims=True)
        hot = jnp.where(col == labels[:, 0:1], 1.0, 0.0)
        shifted_scores = jnp.where(inside, scores - top - jnp.log(mass), 0.0)
        per_image = -(
            0.9 * jnp.sum(shifted_scores * hot, axis=1, keepdims=True)
            + (0.1 / CLASSES) * jnp.sum(shifted_scores, axis=1, keepdims=True)
        )
        valid = jnp.where(counts[:, 0:1] > 0.0, 1.0, 0.0)
        sums[2 * chunks : 2 * chunks + 1, :] = jnp.broadcast_to(rsum(per_image * valid), (1, LANES))
        weight = valid / totals[TOTAL_ROW + 1 : TOTAL_ROW + 2, 0:1]
        grad_logits[...] = weight * jnp.where(inside, spread / mass - 0.9 * hot - 0.1 / CLASSES, 0.0)

    @pl.when(phase == 1)
    def _():
        both = dot(split(grad_logits[...]), cls[lane, :], NT)
        grads = (both[:8] + both[8:]) / jnp.maximum(counts[...], 1.0)
        grad_features[:, lane] = grads
        one = jnp.zeros((1, LANES), f32)
        two = jnp.zeros((1, LANES), f32)
        for b in range(nb):
            at = slice(b * PIXELS, (b + 1) * PIXELS)
            hat = (pre[at, :] - mean) * rstd
            grad = mask[at, :] * dsilu(hat * gain[0:1, :] + gain[1:2, :]) * grads[b : b + 1, :]
            one = one + rsum(grad)
            two = two + rsum(grad * hat)
        sums[pl.ds(j, 1), :] = one
        sums[pl.ds(chunks + j, 1), :] = two

    @pl.when((phase == 1) & (j == chunks - 1))
    def _():
        sum_finish(nd, nz, sums, sums_all, *comm)


def loss_stage(pre, mask, counts, labels, bias, cls, gain, stats, totals, nb, nd, nz, ident):
    rows, width = pre.shape
    chunks = width // LANES
    return pl.pallas_call(
        functools.partial(loss_kernel, nd, nz, nb, chunks),
        grid=(2, chunks),
        out_shape=[
            jax.ShapeDtypeStruct((8, width), f32),
            jax.ShapeDtypeStruct((8, CLASS_PAD), f32),
            jax.ShapeDtypeStruct((8, width), f32),
            jax.ShapeDtypeStruct((24, LANES), f32),
        ],
        in_specs=[
            pl.BlockSpec((rows, LANES), lambda p, j: (0, j)),
            whole(mask.shape),
            whole(counts.shape),
            whole(labels.shape),
            whole(bias.shape),
            whole(cls.shape),
            pl.BlockSpec((8, LANES), lambda p, j: (0, j)),
            whole(stats.shape),
            whole(totals.shape),
        ],
        out_specs=[whole((8, width)), whole((8, CLASS_PAD)), whole((8, width)), whole((24, LANES))],
        scratch_shapes=[VMEM((8, CLASS_PAD), f32)]
        + sum_scratch(24, nd, nz),
        compiler_params=params(ident),
        name="loss_stage",
    )(pre, mask, counts, labels, bias, cls, gain, stats, totals)


def head_back_kernel(nd, nz, nb, chunks, shape, pre, grad_features, mask, counts, gain, stats, sums_in, totals, low, kern, mixed, mix, gates, route, proj, proj_stats, grad_out, sums_all, dz_out, half, part, held, grads, gate_acc, sums, *comm):
    j = pl.program_id(0)
    net = Net(nd, nz)
    twin = Twin(net, shape, half, *comm[6:10])
    plane = Plane(net, shape, half, part, 0, nz // 2, *comm[10:13])
    made = comm[6]
    comm = comm[:6]
    steps = Steps()
    for k in range(nz):
        first = ready(shape, k)
        steps.at(first, functools.partial(twin.begin, k))
        steps.at(first + 2, functools.partial(twin.add, k))
        if k < nz // 2:
            steps.at(first + 2, functools.partial(plane.begin, k))

    @pl.when(j == 0)
    def _():
        sum_start(nd, nz)

    @pl.when(j == 1)
    def _():
        met(nd, nz)

    steps.emit(j, chunks)
    lane = pl.ds(pl.multiple_of(j * LANES, LANES), LANES)
    total = totals[TOTAL_ROW : TOTAL_ROW + 1, :]

    @pl.when(j == 0)
    def _():
        gate_acc[...] = jnp.zeros_like(gate_acc)
        sums[...] = jnp.zeros_like(sums)

    mean, rstd = norm_rows(stats, j, chunks, total)
    scale = rstd * gain[0:1, :]
    one = sums_in[pl.ds(j, 1), :] / total
    two = sums_in[pl.ds(chunks + j, 1), :] / total
    for b in range(nb):
        at = slice(b * PIXELS, (b + 1) * PIXELS)
        hat = (pre[at, :] - mean) * rstd
        grad = dsilu(hat * gain[0:1, :] + gain[1:2, :]) * grad_features[b : b + 1, :]
        value = (scale * mask[at, :] * (grad - one - hat * two)).astype(bf16)
        held[at, lane] = value
        grad_mixed = dot(low[at, :], value, TN).astype(bf16)
        grads[:, b * LANES : (b + 1) * LANES] = grad_mixed
        gate_acc[b : b + 1, :] += gate_rows(grad_mixed, kern[...])
    made[:WIDTH_OUT, lanes(j * LANES * EXPERTS, LANES * EXPERTS)] = dot(grads[...], mix[:, : nb * LANES], NT).astype(bf16)

    @pl.when(j == chunks - 1)
    def _():
        dz = gate_sums(gate_acc[...]) * gates[...] * (1.0 - gates[...])
        dz_out[...] = dz
        pool_grad = dot(dz, route[...], NT, highest) / jnp.maximum(counts[:, 0:1], 1.0)
        mean, rstd = out_norm(proj_stats, total[:, 0:1])
        one = jnp.zeros((1, WIDTH_OUT), f32)
        two = jnp.zeros((1, WIDTH_OUT), f32)
        for b in range(nb):
            at = slice(b * PIXELS, (b + 1) * PIXELS)
            value = (dot(held[at, :], mixed[b], NT) + pool_grad[b : b + 1, :]) * mask[at, 0:1]
            grad_out[at, :] = value
            one = one + rsum(value)
            two = two + rsum(value * ((proj[at, :] - mean) * rstd))
        store_wide(sums, 0, one)
        store_wide(sums, OUT_CHUNKS, two)

    @pl.when(j == chunks - 1)
    def _():
        late = [k for k in range(nz) if ready(shape, k) >= chunks]
        for k in late:
            twin.begin(k)
        sum_finish(nd, nz, sums, sums_all, *comm)
        for k in range(nz):
            if ready(shape, k) + 2 >= chunks:
                twin.add(k)
                if k < nz // 2:
                    plane.begin(k)
        plane.add()
        twin.finish()
        plane.finish()


def head_back(pre, grad_features, mask, counts, gain, stats, sums_in, totals, low, kern, mixed, mix, gates, route, proj, proj_stats, nb, nd, nz, ident):
    rows, width = pre.shape
    chunks = width // LANES
    deep = LANES * EXPERTS
    shape = (kern.shape[0], kern.shape[1] // nz)
    wide = lambda j: (0, j)
    return pl.pallas_call(
        functools.partial(head_back_kernel, nd, nz, nb, chunks, shape),
        grid=(chunks,),
        out_shape=[
            jax.ShapeDtypeStruct((rows, WIDTH_OUT), f32),
            jax.ShapeDtypeStruct((8, LANES), f32),
            jax.ShapeDtypeStruct((8, EXPERTS), f32),
            jax.ShapeDtypeStruct(half_shape(shape, nd, nz), bf16),
            jax.ShapeDtypeStruct(part_shape(shape, nd, nz // 2), bf16),
        ],
        in_specs=[
            pl.BlockSpec((rows, LANES), wide),
            pl.BlockSpec((8, LANES), wide),
            whole(mask.shape),
            whole(counts.shape),
            pl.BlockSpec((8, LANES), wide),
            whole(stats.shape),
            whole(sums_in.shape),
            whole(totals.shape),
            whole(low.shape),
            pl.BlockSpec((WIDTH_OUT, deep), wide),
            whole(mixed.shape),
            whole(mix.shape),
            whole(gates.shape),
            whole(route.shape),
            whole(proj.shape),
            whole(proj_stats.shape),
        ],
        out_specs=[
            whole((rows, WIDTH_OUT)),
            whole((8, LANES)),
            whole((8, EXPERTS)),
            whole(half_shape(shape, nd, nz)),
            whole(part_shape(shape, nd, nz // 2)),
        ],
        scratch_shapes=[
            VMEM((rows, width), bf16),
            VMEM((WIDTH_OUT, nb * LANES), bf16),
            VMEM((8, deep), f32),
        ]
        + sum_scratch(8, nd, nz)
        + twin_scratch(shape, nd, nz)
        + plane_scratch(shape, nd, nz // 2),
        compiler_params=params(ident),
        name="head_back",
    )(pre, grad_features, mask, counts, gain, stats, sums_in, totals, low, kern, mixed, mix, gates, route, proj, proj_stats)


def project_back_kernel(nd, nz, nb, chunks, shape_h, shape, half_h, part_h, grad_in, proj, proj_stats, proj_sums, gain, mask, counts, totals, stats, side, dpre, excited, mixed, kern, mix, gate, pooled, squeezed, sq_bias, grad_norm, sums_all, grad_squeeze, gate_grad, dz_gate, done_h, half, part, low, held, grads, gate_acc, sums_h, sums, *comm):
    phase = pl.program_id(0)
    net = Net(nd, nz)
    few = nz // 2
    cut_one = 9 + len(spread_scratch(shape_h, nd, nz))
    plane_h = Plane(net, shape_h, half_h, sums_h, few, nz - few, *comm[6:9])
    up = Spread(net, shape_h, sums_h, done_h, *comm[9:cut_one])
    twin = Twin(net, shape, half, *comm[cut_one : cut_one + 4])
    plane = Plane(net, shape, half, part, 0, few, *comm[cut_one + 4 : cut_one + 7])
    made = comm[cut_one]
    comm = comm[:6]
    steps = Steps()

    def begin():
        met(nd, nz)
        for k in plane_h.shards:
            plane_h.begin(k)
        sums_h[0:few] = part_h[...]
        for k in range(few):
            up.send(k)

    steps.at(1, begin)
    steps.at(chunks - 1, functools.partial(plane_h.add, up.send))
    steps.at(chunks + 3, up.share)
    steps.at(2 * chunks - 2, up.cross)
    for k in range(nz):
        first = ready(shape, k)
        steps.at(first, functools.partial(twin.begin, k))
        steps.at(first + 2, functools.partial(twin.add, k))
        if k < few:
            steps.at(first + 2, functools.partial(plane.begin, k))
    j = pl.program_id(1)

    @pl.when((phase == 0) & (j == 0))
    def _():
        sum_start(nd, nz)

    steps.emit(phase * chunks + j, 2 * chunks)
    lane = pl.ds(pl.multiple_of(j * LANES, LANES), LANES)
    total = totals[TOTAL_ROW : TOTAL_ROW + 1, :]

    @pl.when((phase == 0) & (j == 0))
    def _():
        gate_acc[...] = jnp.zeros_like(gate_acc)
        sums[...] = jnp.zeros_like(sums)
        grad_squeeze[...] = jnp.zeros_like(grad_squeeze)
        dz_gate[...] = jnp.zeros_like(dz_gate)
        mean, rstd = out_norm(proj_stats, total[:, 0:1])
        scale = rstd * gain[0:1, :]
        one = load_wide(proj_sums, 0, WIDTH_OUT) / total[:, 0:1]
        two = load_wide(proj_sums, OUT_CHUNKS, WIDTH_OUT) / total[:, 0:1]
        for b in range(nb):
            at = slice(b * PIXELS, (b + 1) * PIXELS)
            hat = (proj[at, :] - mean) * rstd
            low[at, :] = (scale * (grad_in[at, :] - mask[at, 0:1] * (one + hat * two))).astype(bf16)

    mean, rstd = norm_rows(stats, j, chunks, total)
    gain_now = side[2 * SQUEEZE + 2 : 2 * SQUEEZE + 3, :]
    bias_now = side[2 * SQUEEZE + 3 : 2 * SQUEEZE + 4, :]

    @pl.when(phase == 0)
    def _():
        for b in range(nb):
            at = slice(b * PIXELS, (b + 1) * PIXELS)
            grad_mixed = dot(low[at, :], excited[at, :], TN).astype(bf16)
            grads[:, b * LANES : (b + 1) * LANES] = grad_mixed
            gate_acc[b : b + 1, :] += gate_rows(grad_mixed, kern[...])
            value = dot(low[at, :], mixed[b])
            held[j, at, :] = value
            normed = (dpre[at, :] - mean) * (rstd * gain_now) + bias_now
            act = normed * sig(normed) * mask[at, :]
            now = gate[b : b + 1, :]
            dz_gate[b : b + 1, lane] = rsum(value * act) * now * (1.0 - now)
        made[:WIDTH_OUT, lanes(j * LANES * EXPERTS, LANES * EXPERTS)] = dot(grads[...], mix[:, : nb * LANES], NT).astype(bf16)
        grad_squeeze[...] += dot(dz_gate[:, lane], side[SQUEEZE : 2 * SQUEEZE, :], NT, highest)

    @pl.when((phase == 1) & (j == 0))
    def _():
        grad_squeeze[...] = grad_squeeze[...] * dsilu(squeezed[...] + sq_bias[...])
        gate_grad[...] = gate_sums(gate_acc[...])

    @pl.when(phase == 1)
    def _():
        pool_grad = dot(grad_squeeze[...], side[0:SQUEEZE, :], NN, highest) / jnp.maximum(counts[...], 1.0)
        one = jnp.zeros((1, LANES), f32)
        two = jnp.zeros((1, LANES), f32)
        for b in range(nb):
            at = slice(b * PIXELS, (b + 1) * PIXELS)
            hat = (dpre[at, :] - mean) * rstd
            grad = held[j, at, :] * gate[b : b + 1, :] + pool_grad[b : b + 1, :]
            value = mask[at, :] * grad * dsilu(hat * gain_now + bias_now)
            grad_norm[at, :] = value
            one = one + rsum(value)
            two = two + rsum(value * hat)
        sums[pl.ds(j, 1), :] = one
        sums[pl.ds(chunks + j, 1), :] = two

    @pl.when((phase == 1) & (j == chunks - 1))
    def _():
        sum_finish(nd, nz, sums, sums_all, *comm)
        plane.add()
        up.finish()
        twin.finish()
        plane.finish()
        plane_h.finish()


def project_back(half_h, part_h, shape_h, grad_in, proj, proj_stats, proj_sums, gain, mask, counts, totals, stats, side, dpre, excited, mixed, kern, mix, gate, pooled, squeezed, sq_bias, nb, nd, nz, ident):
    rows, width = dpre.shape
    shape = (kern.shape[0], kern.shape[1] // nz)
    few = nz // 2
    chunks = width // LANES
    deep = LANES * EXPERTS
    wide = lambda p, j: (0, j)
    early = lambda p, j: (0, jnp.where(p == 0, j, chunks - 1))
    late = lambda p, j: (0, jnp.where(p == 0, 0, j))
    return pl.pallas_call(
        functools.partial(project_back_kernel, nd, nz, nb, chunks, shape_h, shape),
        grid=(2, chunks),
        out_shape=[
            jax.ShapeDtypeStruct((rows, width), f32),
            jax.ShapeDtypeStruct((24, LANES), f32),
            jax.ShapeDtypeStruct((8, SQUEEZE), f32),
            jax.ShapeDtypeStruct((8, EXPERTS), f32),
            jax.ShapeDtypeStruct((8, width), f32),
            jax.ShapeDtypeStruct(shape_h, bf16),
            jax.ShapeDtypeStruct(half_shape(shape, nd, nz), bf16),
            jax.ShapeDtypeStruct(part_shape(shape, nd, few), bf16),
        ],
        in_specs=[
            whole(half_h.shape),
            whole(part_h.shape),
            whole(grad_in.shape),
            whole(proj.shape),
            whole(proj_stats.shape),
            whole(proj_sums.shape),
            whole(gain.shape),
            whole(mask.shape),
            whole(counts.shape),
            whole(totals.shape),
            whole(stats.shape),
            pl.BlockSpec((side.shape[0], LANES), wide),
            pl.BlockSpec((rows, LANES), wide),
            pl.BlockSpec((rows, LANES), early),
            pl.BlockSpec((nb, WIDTH_OUT, LANES), lambda p, j: (0, 0, jnp.where(p == 0, j, chunks - 1))),
            pl.BlockSpec((WIDTH_OUT, deep), early),
            whole(mix.shape),
            pl.BlockSpec((8, LANES), wide),
            pl.BlockSpec((8, LANES), wide),
            whole(squeezed.shape),
            whole(sq_bias.shape),
        ],
        out_specs=[
            pl.BlockSpec((rows, LANES), late),
            whole((24, LANES)),
            whole((8, SQUEEZE)),
            whole((8, EXPERTS)),
            whole((8, width)),
            pl.BlockSpec(memory_space=pltpu.HBM),
            whole(half_shape(shape, nd, nz)),
            whole(part_shape(shape, nd, few)),
        ],
        scratch_shapes=[
            VMEM((rows, WIDTH_OUT), bf16),
            VMEM((chunks, rows, LANES), f32),
            VMEM((WIDTH_OUT, nb * LANES), bf16),
            VMEM((8, deep), f32),
            VMEM(part_shape(shape_h, nd, nz), bf16),
        ]
        + sum_scratch(24, nd, nz)
        + plane_scratch(shape_h, nd, nz - few)
        + spread_scratch(shape_h, nd, nz)
        + twin_scratch(shape, nd, nz)
        + plane_scratch(shape, nd, few),
        compiler_params=params(ident),
        name="project_back",
    )(half_h, part_h, grad_in, proj, proj_stats, proj_sums, gain, mask, counts, totals, stats, side, dpre, excited, mixed, kern, mix, gate, pooled, squeezed, sq_bias)


def depth_back_kernel(nd, nz, nb, chunks, shape, half, part, grad_in, dpre, pre, taps, mask, side, stats_one, stats_two, sums_two, totals, features, logits, pooled, dz_gate, head_pool, pooled_in, grad_sq, before, sq_bias, dz_head, grad_out, tap_grads, sums_all, done, rows_all, buf, acts, held, sums_b, sums, *comm):
    j = pl.program_id(0)
    net = Net(nd, nz)
    few = nz // 2
    plane = Plane(net, shape, half, sums_b, few, nz - few, *comm[6:9])
    up = Spread(net, shape, sums_b, done, *comm[9 : 9 + len(spread_scratch(shape, nd, nz))])
    share = Share(net, rows_all, *comm[9 + len(spread_scratch(shape, nd, nz)) :])
    comm = comm[:6]
    steps = Steps()

    def begin():
        met(nd, nz)
        for k in plane.shards:
            plane.begin(k)
        sums_b[0:few] = part[...]
        for k in range(few):
            up.send(k)

    steps.at(1, begin)
    steps.at(2, share.far)
    steps.at(4, functools.partial(plane.add, up.send))
    steps.at(4, share.plane)
    steps.at(chunks - 3, up.share)
    steps.at(chunks - 3, share.twin)
    steps.at(chunks - 1, up.cross)

    @pl.when(j == 0)
    def _():
        sum_start(nd, nz)

    steps.emit(j, chunks)

    @pl.when(j == 0)
    def _():
        total_before = before[...] + sq_bias[...]
        squeezed = total_before * sig(total_before)
        share.fill(
            nb,
            [features, pooled, dz_gate],
            [grad_sq[...], squeezed, dz_head[...]],
            [logits[...], head_pool[...], pooled_in[...]],
        )

    total = totals[TOTAL_ROW : TOTAL_ROW + 1, :]

    @pl.when(j == 0)
    def _():
        sums[...] = jnp.zeros_like(sums)

    mean_two, rstd_two = norm_rows(stats_two, j, chunks, total)
    scale_two = rstd_two * side[2 * SQUEEZE + 2 : 2 * SQUEEZE + 3, :]
    one_two = sums_two[pl.ds(j, 1), :] / total
    two_two = sums_two[pl.ds(chunks + j, 1), :] / total
    mean, rstd = norm_rows(stats_one, j, chunks, total)
    gain = side[2 * SQUEEZE : 2 * SQUEEZE + 1, :]
    bias = side[2 * SQUEEZE + 1 : 2 * SQUEEZE + 2, :]
    held[...] = jnp.zeros_like(held)
    reach = KERNEL // 2

    @pl.loop(0, nb)
    def _(b):
        at = image(b)
        hat = (dpre[at, :] - mean_two) * rstd_two
        grad = scale_two * (grad_in[at, :] - mask[at, :] * (one_two + hat * two_two))
        for s in range(KERNEL):
            buf[s] = shifted(grad, reach - s)
        hat = (pre[at, :] - mean) * rstd
        normed = hat * gain + bias
        acts[...] = normed * sig(normed) * mask[at, :]
        taps_now = [jnp.broadcast_to(taps[b, t : t + 1, :], (MAP_SIDE, LANES)) for t in range(TAPS)]
        acc = [None] * MAP_SIDE
        for q in range(MAP_SIDE):
            for s in range(KERNEL):
                x = buf[s, q * MAP_SIDE : (q + 1) * MAP_SIDE, :]
                for r in range(KERNEL):
                    y = q + r - reach
                    if 0 <= y < MAP_SIDE:
                        term = taps_now[r * KERNEL + s] * x
                        acc[y] = term if acc[y] is None else acc[y] + term
            done = [q - 2] if q < MAP_SIDE - 1 else [q - 2, q - 1, q]
            for i in done:
                if i >= 0:
                    grad_out[pl.ds(pl.multiple_of(b * PIXELS + i * MAP_SIDE, MAP_SIDE), MAP_SIDE), :] = acc[i]
        tap_acc = [None] * TAPS
        for q in range(MAP_SIDE):
            for s in range(KERNEL):
                x = buf[s, q * MAP_SIDE : (q + 1) * MAP_SIDE, :]
                for r in range(KERNEL):
                    y = q + r - reach
                    if 0 <= y < MAP_SIDE:
                        both = acts[y * MAP_SIDE : (y + 1) * MAP_SIDE, :] * x
                        term = both[:8] + both[8:]
                        t = r * KERNEL + s
                        tap_acc[t] = term if tap_acc[t] is None else tap_acc[t] + term
        tap_grads[b] = jnp.zeros((32, LANES), f32)
        for t in range(TAPS):
            tap_grads[b, t : t + 1, :] = rsum(tap_acc[t])
        hat = (pre[at, :] - mean) * rstd
        value = grad_out[at, :] * mask[at, :] * dsilu(hat * gain + bias)
        grad_out[at, :] = value
        held[0:1, :] += rsum(value)
        held[1:2, :] += rsum(value * hat)

    sums[pl.ds(j, 1), :] = held[0:1, :]
    sums[pl.ds(chunks + j, 1), :] = held[1:2, :]

    @pl.when(j == chunks - 1)
    def _():
        sum_finish(nd, nz, sums, sums_all, *comm)
        share.finish()
        up.finish()
        plane.finish()


def depth_back(half, part, shape, grad_in, dpre, pre, taps, mask, side, stats_one, stats_two, sums_two, totals, lines, nb, nd, nz, ident):
    rows, width = pre.shape
    chunks = width // LANES
    wide = lambda j: (0, j)
    tall = pl.BlockSpec((rows, LANES), wide)
    hbm = pl.BlockSpec(memory_space=pltpu.HBM)
    return pl.pallas_call(
        functools.partial(depth_back_kernel, nd, nz, nb, chunks, shape),
        grid=(chunks,),
        out_shape=[
            jax.ShapeDtypeStruct((rows, width), f32),
            jax.ShapeDtypeStruct((nb, 32, width), f32),
            jax.ShapeDtypeStruct((24, LANES), f32),
            jax.ShapeDtypeStruct(shape, bf16),
            jax.ShapeDtypeStruct((nd * nz, 8, share_width(lines, nz)[-1]), f32),
        ],
        in_specs=[
            whole(half.shape),
            whole(part.shape),
            tall,
            tall,
            tall,
            pl.BlockSpec((nb, 32, LANES), lambda j: (0, 0, j)),
            whole(mask.shape),
            pl.BlockSpec((side.shape[0], LANES), wide),
            whole(stats_one.shape),
            whole(stats_two.shape),
            whole(sums_two.shape),
            whole(totals.shape),
        ]
        + [whole(x.shape) for x in lines],
        out_specs=[tall, pl.BlockSpec((nb, 32, LANES), lambda j: (0, 0, j)), whole((24, LANES)), hbm, hbm],
        scratch_shapes=[
            VMEM((KERNEL, PIXELS, LANES), f32),
            VMEM((PIXELS, LANES), f32),
            VMEM((8, LANES), f32),
            VMEM(part_shape(shape, nd, nz), bf16),
        ]
        + sum_scratch(24, nd, nz)
        + plane_scratch(shape, nd, nz - nz // 2)
        + spread_scratch(shape, nd, nz)
        + share_scratch(share_width(lines, nz)[-1], nd, nz),
        compiler_params=params(ident),
        name="depth_back",
    )(half, part, grad_in, dpre, pre, taps, mask, side, stats_one, stats_two, sums_two, totals, *lines)


def expand_back_kernel(nd, nz, nb, chunks, shape, cuts_one, cuts_two, grad_in, pre, images, tap_grads, mask, side, stats, sums_in, totals, kern, mix, gates, gate_grad, rows_all, grad_b, grad_h, squares_w, stats_two, stats_three, stats_four, sums_two, sums_four, chan_old, head_old, proj_old, done, grad_cls, grad_side_out, factors, route_in, route_head, sq_bias, class_bias, chan_new, head_new, proj_new, loss, grads, gate_acc, grad_side, every_sum, half, sums, *comm):
    j = pl.program_id(0)
    net = Net(nd, nz)
    low = comm[0]
    sum_comm = comm[1:7]
    comm = comm[7:]
    twin = Twin(net, shape, half, *comm[0:4])
    plane = Plane(net, shape, half, sums, 0, nz, *comm[4:7])
    up = Spread(net, shape, sums, done, *comm[7:])
    made = comm[0]
    steps = Steps()
    for k in range(nz):
        first = ready(shape, k)
        steps.at(first, functools.partial(twin.begin, k))
        steps.at(first + 1, functools.partial(twin.add, k))
        steps.at(first + 1, functools.partial(plane.begin, k))

    @pl.when(j == 0)
    def _():
        sum_start(nd, nz)

    @pl.when(j == 1)
    def _():
        met(nd, nz)

    steps.emit(j, chunks)

    total = totals[TOTAL_ROW : TOTAL_ROW + 1, :]

    @pl.when(j == 0)
    def _():
        gate_acc[...] = jnp.zeros_like(gate_acc)
        grads[...] = jnp.zeros_like(grads)

    mean, rstd = norm_rows(stats, j, chunks, total)
    scale = rstd * side[2 * SQUEEZE : 2 * SQUEEZE + 1, :]
    one = sums_in[pl.ds(j, 1), :] / total
    two = sums_in[pl.ds(chunks + j, 1), :] / total
    for b in range(nb):
        at = slice(b * PIXELS, (b + 1) * PIXELS)
        lane = slice(b * LANES, (b + 1) * LANES)
        hat = (pre[at, :] - mean) * rstd
        value = (scale * (grad_in[at, :] - mask[at, :] * (one + hat * two))).astype(bf16)
        grads[0:WIDTH_IN, lane] = dot(images[at, :], value, TN).astype(bf16)
        grads[WIDTH_IN : WIDTH_IN + 32, lane] = tap_grads[b].astype(bf16)
        gate_acc[b : b + 1, :] += gate_rows(grads[:, lane], kern[...])
    made[:, lanes(j * LANES * EXPERTS, LANES * EXPERTS)] = dot(grads[...], mix[:, : nb * LANES], NT).astype(bf16)

    @pl.when(j == chunks - 1)
    def _():
        dz = (gate_sums(gate_acc[...]) + gate_grad[...]) * gates[...] * (1.0 - gates[...])
        steps.end(chunks)
        z = net.z
        me = net.d * nz + z
        devices = nd * nz
        own = chan_old.shape[1]
        own_head = head_old.shape[1]
        own_proj = proj_old.shape[1]
        width = own * nz
        head_width = own_head * nz
        head_chunks = head_width // LANES
        count = devices * 8
        row = lax.broadcasted_iota(jnp.int32, (count, 1), 0)
        keep = jnp.where((row & 7) < nb, 1.0, 0.0)

        def one(k, size):
            return rows_all[:, :, cuts_one[k] : cuts_one[k] + size].reshape(count, size) * keep

        def two(k, size):
            return pltpu.roll(rows_all[:, :, cuts_two[k] : cuts_two[k] + size].reshape(count, size), count - nb, 0)

        features = one(0, own_head)
        logits = two(0, CLASS_PAD)
        pooled = one(1, own)
        dz_gate = one(2, own)
        grad_sq = one(3, SQUEEZE)
        grad_cls[...] = dot(features, logits, TN, highest)
        grad_side[...] = jnp.zeros_like(grad_side)
        grad_side[0:SQUEEZE, :own] = dot(grad_sq, pooled, TN, highest)
        grad_side[SQUEEZE : 2 * SQUEEZE, :own] = dot(one(4, SQUEEZE), dz_gate, TN, highest)

        def channel(ref, at, n, size, own_size):
            return turn(load_wide(ref, at, size), z * own_size)[:, :own_size]

        at = 2 * SQUEEZE
        grad_side[at : at + 1, :own] = channel(sums_in, chunks, chunks, width, own)
        grad_side[at + 1 : at + 2, :own] = channel(sums_in, 0, chunks, width, own)
        grad_side[at + 2 : at + 3, :own] = channel(sums_two, chunks, chunks, width, own)
        grad_side[at + 3 : at + 4, :own] = channel(sums_two, 0, chunks, width, own)
        grad_side[at + 4 : at + 5, :own] = rsum(dz_gate)
        route_head[...] = dot(two(1, WIDTH_OUT), one(5, EXPERTS), TN, highest)
        sq_bias[...] = rsum(grad_sq)
        class_bias[...] = rsum(logits * keep)
        head_gain = channel(sums_four, head_chunks, head_chunks, head_width, own_head)
        head_bias = channel(sums_four, 0, head_chunks, head_width, own_head)
        totals = stats[TOTAL_ROW : TOTAL_ROW + 1, 0:1]
        loss[...] = jnp.broadcast_to(
            sums_four[2 * head_chunks : 2 * head_chunks + 1, :] / stats[TOTAL_ROW + 1 : TOTAL_ROW + 2, :], (8, LANES)
        )

        def moving(new, old, ref, at, n, size, own_size):
            mean = load_wide(ref, 0, size) / totals
            var = (load_wide(ref, n, size) / totals - mean * mean) * (totals / (totals - 1.0))
            new[at : at + 1, :] = 0.5 * old[at : at + 1, :] + 0.5 * turn(mean, z * own_size)[:, :own_size]
            new[at + 1 : at + 2, :] = 0.5 * old[at + 1 : at + 2, :] + 0.5 * turn(var, z * own_size)[:, :own_size]

        moving(chan_new, chan_old, stats, 0, chunks, width, own)
        moving(chan_new, chan_old, stats_two, 2, chunks, width, own)
        moving(head_new, head_old, stats_four, 0, head_chunks, head_width, own_head)
        moving(proj_new, proj_old, stats_three, 0, OUT_CHUNKS, WIDTH_OUT, own_proj)
        low[...] = jnp.zeros_like(low)
        low[pl.ds(me, 1), 0 : nb * EXPERTS] = jnp.concatenate([dz[b : b + 1, :] for b in range(nb)], axis=1)
        share = 1.0 / nd
        g_hside = jnp.sum(grad_cls[...] * grad_cls[...]) + jnp.sum(head_gain * head_gain) + jnp.sum(head_bias * head_bias)
        sums = (
            squares_of(grad_b, WIDTH_OUT),
            squares_of(grad_side, 104),
            squares_of(grad_h, WIDTH_OUT),
            g_hside,
        )
        for k in range(4):
            low[devices + k : devices + k + 1, :] = row_of(sums[k] * share)
            low[devices + 4 + k : devices + 5 + k, :] = squares_w[k : k + 1, :] * share
        plane.add(up.send)
        up.share()
        low[devices : devices + 1, :] += row_of(squares_of(up.piece, up.piece.shape[0]))
        sum_finish(nd, nz, low, every_sum, *sum_comm)
        up.cross()
        for k in range(4):
            grad_sq_sum = jnp.sum(every_sum[devices + k : devices + k + 1, :], axis=1, keepdims=True)
            weight_sq = jnp.sum(every_sum[devices + 4 + k : devices + 5 + k, :], axis=1, keepdims=True)
            factors[k : k + 1, :] = jnp.broadcast_to(
                jnp.sqrt(weight_sq) * lax.rsqrt(grad_sq_sum + 1e-12), (1, LANES)
            )
        row = lax.broadcasted_iota(jnp.int32, (count, devices), 0)
        col = lax.broadcasted_iota(jnp.int32, (count, devices), 1)
        spread = dot(jnp.where((row >> 3) == col, 1.0, 0.0), every_sum[0:devices, :], NN, highest)
        row = lax.broadcasted_iota(jnp.int32, (count, LANES), 0)
        col = lax.broadcasted_iota(jnp.int32, (count, LANES), 1)
        spread = jnp.where((col >> 3) == (row & 7) - nb, spread, 0.0)
        row = lax.broadcasted_iota(jnp.int32, (LANES, EXPERTS), 0)
        col = lax.broadcasted_iota(jnp.int32, (LANES, EXPERTS), 1)
        dz_rows = dot(spread, jnp.where((row & (EXPERTS - 1)) == col, 1.0, 0.0), NN, highest)
        pooled_in = rows_all[:, :, cuts_two[2] : cuts_two[2] + 256].reshape(count, 256)
        route_in[...] = dot(pooled_in, dz_rows, TN, highest)[:WIDTH_IN]
        grad_side_out[...] = jnp.transpose(grad_side[...])[:own]
        values = grad_cls[:, :CLASSES]
        both = jnp.concatenate([head_gain, head_bias] + [jnp.zeros((6, own_head), f32)], axis=0)
        grad_cls[...] = jnp.concatenate(
            [jnp.transpose(both)[:, 0:2], values, jnp.zeros((own_head, CLASS_PAD - CLASSES - 2), f32)], axis=1
        )
        up.finish()
        twin.finish()
        plane.finish()


def expand_back(grad_in, pre, images, tap_grads, mask, side, stats, sums_in, totals, kern, mix, gates, gate_grad, small, cuts, nb, nd, nz, ident):
    rows, width = pre.shape
    chunks = width // LANES
    deep = LANES * EXPERTS
    wide = lambda j: (0, j)
    tall = pl.BlockSpec((rows, LANES), wide)
    shape = (kern.shape[0], kern.shape[1] // nz)
    devices = nd * nz
    chan_old, head_old, proj_old = small[-3:]
    own, own_head = chan_old.shape[1], head_old.shape[1]
    outs = [(own_head, CLASS_PAD), (own, 104), (8, LANES)]
    outs += [(WIDTH_IN, EXPERTS), (WIDTH_OUT, EXPERTS), (1, SQUEEZE), (1, CLASS_PAD)]
    outs += [chan_old.shape, head_old.shape, proj_old.shape, (8, LANES)]
    return pl.pallas_call(
        functools.partial(expand_back_kernel, nd, nz, nb, chunks, shape, *cuts),
        grid=(chunks,),
        out_shape=[
            jax.ShapeDtypeStruct(shape, bf16),
        ]
        + [jax.ShapeDtypeStruct(x, f32) for x in outs],
        in_specs=[
            tall,
            tall,
            whole(images.shape),
            pl.BlockSpec((nb, 32, LANES), lambda j: (0, 0, j)),
            whole(mask.shape),
            pl.BlockSpec((side.shape[0], LANES), wide),
            whole(stats.shape),
            whole(sums_in.shape),
            whole(totals.shape),
            pl.BlockSpec((kern.shape[0], deep), wide),
            whole(mix.shape),
            whole(gates.shape),
            whole(gate_grad.shape),
        ]
        + [whole(x.shape) for x in small],
        out_specs=[pl.BlockSpec(memory_space=pltpu.HBM)] + [whole(x) for x in outs],
        scratch_shapes=[VMEM((kern.shape[0], nb * LANES), bf16), VMEM((8, deep), f32)]
        + [VMEM((104, up_to(own)), f32)]
        + sum_scratch(devices + 8, nd, nz)[:1]
        + [VMEM(half_shape(shape, nd, nz), bf16), VMEM(part_shape(shape, nd, nz), bf16)]
        + sum_scratch(devices + 8, nd, nz)
        + twin_scratch(shape, nd, nz)
        + plane_scratch(shape, nd, nz)
        + spread_scratch(shape, nd, nz),
        compiler_params=params(ident),
        name="expand_back",
    )(grad_in, pre, images, tap_grads, mask, side, stats, sums_in, totals, kern, mix, gates, gate_grad, *small)


def update(weight, grad, moment, average, factor):
    scaled = grad * factor
    moment_new = 0.5 * moment + scaled
    weight_new = weight - 0.2 * (scaled + 0.5 * moment_new)
    average_new = 0.5 * average + 0.5 * weight_new
    return (weight_new, moment_new, average_new)


BLOCK_STEP = 64
HEAD_STEP = 32


def turn(x, shift):
    width = x.shape[1]
    return pltpu.roll(x, lax.rem(width - shift, width), 1)


def apply_kernel(
    factors,
    grad_side,
    side_w,
    side_m,
    side_e,
    grad_a,
    grad_b,
    block_w,
    block_m,
    block_e,
    grad_h,
    head_w,
    head_m,
    head_e,
    grad_cls,
    hside_w,
    hside_m,
    hside_e,
    side_wo,
    side_mo,
    side_eo,
    block_wo,
    block_mo,
    block_eo,
    head_wo,
    head_mo,
    head_eo,
    hside_wo,
    hside_mo,
    hside_eo,
    grad_block,
):
    @pl.when(pl.program_id(0) == 0)
    def _():
        fresh = update(side_w[...], grad_side[:, : side_w.shape[1]], side_m[...], side_e[...], factors[1:2, 0:1])
        side_wo[...], side_mo[...], side_eo[...] = fresh
        first = WIDTH_IN + TAPS
        whole_rows = first // 16 * 16

        @pl.loop(0, whole_rows // 16)
        def _(i):
            here = tall(i * 16, 16)
            grad_block[here, :] = grad_a[here, :].astype(f32)

        grad_block[whole_rows:first, :] = grad_a[whole_rows : whole_rows + 16, :].astype(f32)[: first - whole_rows]
        for i in range(WIDTH_OUT // 16):
            grad_block[first + 16 * i : first + 16 * (i + 1), :] = grad_b[16 * i : 16 * (i + 1), :].astype(f32)
        grad_block[first + WIDTH_OUT :, :] = jnp.zeros(
            (grad_block.shape[0] - first - WIDTH_OUT, grad_block.shape[1]), f32
        )

    here = pl.multiple_of(jnp.minimum(pl.program_id(0), grad_block.shape[0] // BLOCK_STEP - 1) * BLOCK_STEP, BLOCK_STEP)

    for k in range(0, BLOCK_STEP, 16):
        rows = slice(k, k + 16)
        fresh = update(
            block_w[rows, :], grad_block[pl.ds(here + k, 16), :], block_m[rows, :], block_e[rows, :], factors[0:1, 0:1]
        )
        block_wo[rows, :], block_mo[rows, :], block_eo[rows, :] = fresh
    for k in range(0, HEAD_STEP, 16):
        rows = slice(k, k + 16)
        fresh = update(
            head_w[rows, :], grad_h[rows, :].astype(f32), head_m[rows, :], head_e[rows, :], factors[2:3, 0:1]
        )
        head_wo[rows, :], head_mo[rows, :], head_eo[rows, :] = fresh
    fresh = update(hside_w[...], grad_cls[:, : hside_w.shape[1]], hside_m[...], hside_e[...], factors[3:4, 0:1])
    hside_wo[...], hside_mo[...], hside_eo[...] = fresh


def apply(factors, side, grads, block, head_arrays, hside):
    def stepped(array, size):
        last = -(-array.shape[0] // size) - 1
        return pl.BlockSpec((size, array.shape[1]), lambda j: (jnp.minimum(j, last), 0))

    steps = max(-(-block[0].shape[0] // BLOCK_STEP), -(-WIDTH_OUT // HEAD_STEP))
    blocks = (
        [whole(x.shape) for x in side]
        + [whole(x.shape) for x in grads]
        + [stepped(x, BLOCK_STEP) for x in block]
        + [stepped(x, HEAD_STEP) for x in head_arrays]
        + [stepped(x, HEAD_STEP) for x in hside]
    )
    arrays = side + grads + block + head_arrays + hside
    keep = [k for k in range(17) if k not in (0, 4, 5, 9, 13)]
    return pl.pallas_call(
        apply_kernel,
        grid=(steps,),
        out_shape=[jax.ShapeDtypeStruct(arrays[k].shape, f32) for k in keep],
        in_specs=[whole(factors.shape)] + blocks,
        out_specs=[blocks[k] for k in keep],
        scratch_shapes=[VMEM((-(-block[0].shape[0] // BLOCK_STEP) * BLOCK_STEP, block[0].shape[1]), f32)],
        compiler_params=params(),
        name="apply",
    )(factors, *arrays)


def body(
    nd,
    nz,
    images,
    pixel_mask,
    counts,
    labels,
    block_w,
    chan_side,
    head_w,
    head_side,
    shared,
    block_mom,
    side_mom,
    head_mom,
    hside_mom,
    shared_mom,
    block_ema,
    side_ema,
    head_ema,
    hside_ema,
    shared_ema,
    chan_stats,
    head_stats,
    proj_stats,
):
    z = lax.axis_index("chan")
    nb = images.shape[0] // nz
    own = chan_side.shape[1]
    own_head = head_side.shape[0]
    width = own * nz
    head_width = own_head * nz
    end_route = WIDTH_IN * EXPERTS
    end_head = end_route + WIDTH_OUT * EXPERTS
    end_norm = end_head + 2 * WIDTH_OUT
    end_squeeze = end_norm + SQUEEZE
    route_in = shared[:end_route].reshape(WIDTH_IN, EXPERTS)
    route_head = shared[end_route:end_head].reshape(WIDTH_OUT, EXPERTS)
    gain_out = shared[end_head:end_norm].reshape(2, WIDTH_OUT)
    sq_bias = shared[None, end_norm:end_squeeze]
    class_bias = jnp.pad(shared[end_squeeze:], (0, CLASS_PAD - CLASSES))[None, :]

    def mine(x):
        return lax.dynamic_slice_in_dim(x, z * nb, nb, 0)

    image_rows = mine(images).reshape(nb * PIXELS, WIDTH_IN)
    mask_now = mine(pixel_mask).astype(f32)
    mask = jnp.broadcast_to(mask_now.reshape(-1, 1), (nb * PIXELS, LANES))
    mask_rows = jnp.pad(
        (jnp.eye(nb, dtype=f32)[:, :, None] * mask_now[None]).reshape(nb, nb * PIXELS).astype(bf16),
        ((0, 8 - nb), (0, 0)),
    )
    count_rows = jnp.broadcast_to(jnp.pad(mine(counts).astype(f32), (0, 8 - nb))[:, None], (8, LANES))
    label_rows = jnp.broadcast_to(jnp.pad(mine(labels), (0, 8 - nb))[:, None], (8, LANES))

    full_a, full_b, side, gain_head, kern_b, kern_h, kern_c, squares = first_gather(
        block_w, head_w, head_side, chan_side.T, nd, nz, 1
    )
    pre, taps, stats_one, mix, gates, pooled_in, full_b, full_h = expand(
        full_a, image_rows, mask, mask_rows, count_rows, route_in, full_b, kern_h, nb, width, nd, nz, 3
    )
    totals = stats_one
    dpre, stats_two, full_b, full_h, full_c = depthwise(
        pre, taps, mask, side, stats_one, full_b, full_h, kern_c, nb, nd, nz, 4
    )
    excited, proj, pooled, gate, squeezed, stats_three, mixed_proj, full_h, full_c = project(
        dpre, mask, side, stats_two, totals, count_rows, sq_bias, full_b, mix, full_h, full_c, nb, nd, nz, 5
    )
    low, head_pre, mixed_head, stats_four, mix_head, gates_head, head_pool, full_c = head(
        full_h, proj, mask, mask_rows, count_rows, gain_out, route_head, stats_three, totals, full_c, nb, nd, nz, 6
    )
    cls_full = full_c[:, :own_head].reshape(head_width, CLASS_PAD)
    features, grad_logits, grad_features, sums_four = loss_stage(
        head_pre, mask, count_rows, label_rows, class_bias, cls_full, gain_head, stats_four, totals, nb, nd, nz, 7
    )
    grad_proj, sums_three, dz_head, half_h, part_h = head_back(
        head_pre,
        grad_features,
        mask,
        count_rows,
        gain_head,
        stats_four,
        sums_four,
        totals,
        low,
        full_h,
        mixed_head,
        mix_head,
        gates_head,
        route_head,
        proj,
        stats_three,
        nb,
        nd,
        nz,
        8,
    )
    shape_h, shape_b = kern_h.shape, kern_b.shape
    grad_norm, sums_two, grad_squeeze, gate_grad, dz_gate, grad_h, half_b, part_b = project_back(
        half_h,
        part_h,
        shape_h,
        grad_proj,
        proj,
        stats_three,
        sums_three,
        gain_out,
        mask,
        count_rows,
        totals,
        stats_two,
        side,
        dpre,
        excited,
        mixed_proj,
        full_b,
        mix,
        gate,
        pooled,
        squeezed,
        sq_bias,
        nb,
        nd,
        nz,
        9,
    )
    lines = [features, grad_logits, pooled, dz_gate, head_pool, pooled_in, grad_squeeze, squeezed, sq_bias, dz_head]
    grad_pre, tap_grads, sums_one, grad_b, rows_all = depth_back(
        half_b, part_b, shape_b, grad_norm, dpre, pre, taps, mask, side, stats_one, stats_two, sums_two, totals, lines, nb, nd, nz, 10
    )
    small = [rows_all, grad_b, grad_h, squares, stats_two, stats_three, stats_four, sums_two, sums_four]
    small += [chan_stats, head_stats, proj_stats]
    grad_a, grad_cls, grad_side, factors, *rest = expand_back(
        grad_pre,
        pre,
        image_rows,
        tap_grads,
        mask,
        side,
        stats_one,
        sums_one,
        totals,
        full_a,
        mix,
        gates,
        gate_grad,
        small,
        share_width(lines, nz)[:2],
        nb,
        nd,
        nz,
        11,
    )
    grad_route_in, grad_route_head, grad_sq_bias, grad_class_bias, new_chan, new_head_stats, new_proj, loss = rest
    results = apply(
        factors,
        [grad_side, chan_side.T, side_mom.T, side_ema.T],
        [grad_a, grad_b],
        [block_w, block_mom, block_ema],
        [grad_h, head_w, head_mom, head_ema],
        [grad_cls, head_side, hside_mom, hside_ema],
    )
    new_side, new_block, new_head, new_hside = (results[3 * k : 3 * k + 3] for k in range(4))
    new_side = [x.T for x in new_side]

    def out_row(first):
        return sums_three[first : first + OUT_CHUNKS].reshape(-1)[:WIDTH_OUT]

    grad_shared = jnp.concatenate(
        [
            grad_route_in.reshape(-1),
            grad_route_head.reshape(-1),
            out_row(OUT_CHUNKS),
            out_row(0),
            grad_sq_bias[0],
            grad_class_bias[0, :CLASSES],
        ]
    )
    new_shared = update(
        shared,
        grad_shared,
        shared_mom,
        shared_ema,
        jnp.sqrt(jnp.sum(shared * shared)) * lax.rsqrt(jnp.sum(grad_shared * grad_shared) + 1e-12),
    )
    groups = (new_block, new_side, new_head, new_hside, new_shared)
    return (
        (loss[0, 0],)
        + tuple(group[k] for k in range(3) for group in groups)
        + (new_chan, new_head_stats, new_proj)
    )


def solution(mesh):
    nd, nz = mesh.shape["dp"], mesh.shape["chan"]
    cols = P(None, "chan")
    state = (cols, cols, cols, P("chan", None), P())
    return jax.shard_map(
        functools.partial(body, nd, nz),
        mesh=mesh,
        in_specs=(P("dp", None, None), P("dp", None), P("dp"), P("dp"))
        + state * 3
        + (cols, cols, cols),
        out_specs=(P(),) + state * 3 + (cols, cols, cols),
        check_vma=False,
    )
```

time: 836 us -> 491 us (0.59)
  Pallas kernels: 682 us -> 471 us
  other arithmetic: 56.6 us -> 3.41 us
  local copies, waits for them, and re-layouts: 57.1 us -> 13.3 us
  between operations: 25.8 us -> 2.27 us
    pallas_call x23 -> x11, Pallas kernels: 682 us -> 471 us  [the longest x1 68.9 us: expand_back(): pl.pallas_call(functools.partial(expand_back_kernel, nd, nz, nb, chunks,...]
    add x5 -> x1, other arithmetic: 25.5 us -> 0.64 us  [update(): average_new = 0.5 * average + 0.5 * weight_new]
    reduce_sum x11 -> x0, other arithmetic: 20 us -> none  [the longest x8 17.4 us: square_sum(): return jnp.sum(x * x)]
    unnamed x102 -> x26, local copies, waits for them, and re-layouts: 17.8 us -> 1.87 us
    slice x15 -> x1, local copies, waits for them, and re-layouts: 12.8 us -> 1.19 us  [body(): loss[0, 0]]
  transfers between devices with their start and end apart: 1 -> 0, of which waited for: 0 -> 0; matrix products, arithmetic and copies ran while one was open for 3% -> 0% of each run, Pallas kernels for 35% -> 0%
where the time goes in v2:
time: 491 us; the launch traced here: 489 us
  Pallas kernels  471 us (96%)
  local copies, waits for them, and re-layouts  13.3 us (3%)
    pallas_call x1, Pallas kernels, expand_back(): pl.pallas_call(functools.partial(expand_back_kernel, nd, nz, nb, chunks,...  68.9 us
    pallas_call x1, Pallas kernels, project_back(): pl.pallas_call(functools.partial(project_back_kernel, nd, nz, nb, chunks,...  66.6 us
    pallas_call x1, Pallas kernels, depth_back(): pl.pallas_call(functools.partial(depth_back_kernel, nd, nz, nb, chunks, s...  56.9 us
    pallas_call x1, Pallas kernels, first_gather(): pl.pallas_call(functools.partial(first_kernel, nd, nz, shape, shape_b), o...  50.8 us
    pallas_call x1, Pallas kernels, head_back(): pl.pallas_call(functools.partial(head_back_kernel, nd, nz, nb, chunks, sh...  42.7 us
    pallas_call x1, Pallas kernels, expand(): pl.pallas_call(functools.partial(expand_kernel, nd, nz, nb, chunks, shape...  40.4 us
    pallas_call x1, Pallas kernels, depthwise(): pl.pallas_call(functools.partial(depth_kernel, nd, nz, nb, chunks, shapes...  37.6 us
    pallas_call x1, Pallas kernels, project(): pl.pallas_call(functools.partial(project_kernel, nd, nz, nb, chunks, shap...  29 us

profile of v2, /device:TPU:0, one launch (start us, length us, event | category | flops | bytes accessed | tf_op | source)
XLA Modules:
  0.0 489.5 jit_solution(14347469097049970668)
XLA Ops:
  0.7 0.8 convert_bitcast_fusion
  1.5 1.0 broadcast_in_dim.13.mask
  2.5 0.7 dynamic-slice_convert_fusion
  3.2 0.7 broadcast_in_dim.14.counts
  4.6 1.0 copy.48
  5.7 50.8 %first_gather.1 = (bf16[256,9216]{1,0:T(8,128)(2,1)}, bf16[320,9216]{1,0:T(8,128)(2,1)}, f32[104,1152]{1,0:T(8,128)}, f32[8,1280]{1,0:T(8,128)}, bf16[320,2304]{...) custom-call(f32[537,2304]{1,0:T(8,128)} %block_w.1, ...), custom_call_target="tpu_custom_call" | custom-call | tf_op jit(solution)/shard_map/first_gather/pallas_call | solution.py:398
  56.5 0.7 reshape.99.route
  57.2 40.4 %expand.1 = (f32[1024,1152]{1,0:T(8,128)}, f32[4,32,1152]{2,1,0:T(8,128)}, f32[24,128]{1,0:T(8,128)}, bf16[1024,1024]{1,0:T(8,128)(2,1)}, f32[8,8]{1,0:T(8,128)}...) custom-call(bf16[256,9216]{1,0:T(8,128)(2,1)} %get-tuple-element.102, ...), custom_call_target="tpu_custom_call", output_to_operand_aliasing={{6}: (6, {})} | custom-call | tf_op jit(solution)/shard_map/expand/pallas_call | solution.py:848
  97.7 37.6 %depthwise.1 = (f32[1024,1152]{1,0:T(8,128)}, f32[24,128]{1,0:T(8,128)}, bf16[320,9216]{1,0:T(8,128)(2,1)}, bf16[320,10240]{1,0:T(8,128)(2,1)}, bf16[4,320,1024]{2,1,0:T(8,128)(2,1)}) custom-call(f32[1024,1152]{1,0:T(8,128)} %get-tuple-element.105.pre, f32[4,32,1152]{2,1,0:T(8,128)} %get-tuple-element.106.taps, ...), custom_call_target="tpu_custom_call", output_to_operand_aliasing={{2}: (5, {}), {3}: (6, {})} | custom-call | tf_op jit(solution)/shard_map/depthwise/pallas_call | solution.py:981
  135.8 29.0 %project.1 = (bf16[1024,1152]{1,0:T(8,128)(2,1)}, f32[1024,320]{1,0:T(8,128)}, f32[8,1152]{1,0:T(8,128)}, f32[8,1152]{1,0:T(8,128)}, f32[8,48]{1,0:T(8,128)}, /*...) custom-call(f32[1024,1152]{1,0:T(8,128)} %get-tuple-element.112.dpre, ...), custom_call_target="tpu_custom_call", output_to_operand_aliasing={{7}: (9, {}), {8}: (10, {})} | custom-call | tf_op jit(solution)/shard_map/project/pallas_call | solution.py:1118
  164.9 0.8 reshape.101.route
  165.7 0.7 reshape.100.gain
  166.3 27.1 %head.1 = (bf16[1024,320]{1,0:T(8,128)(2,1)}, f32[1024,1280]{1,0:T(8,128)}, bf16[4,320,1280]{2,1,0:T(8,128)(2,1)}, f32[24,128]{1,0:T(8,128)}, bf16[1024,1024]{1,...) custom-call(bf16[320,10240]{1,0:T(8,128)(2,1)} %get-tuple-element.11, ...), custom_call_target="tpu_custom_call", output_to_operand_aliasing={{7}: (9, {})} | custom-call | tf_op jit(solution)/shard_map/head/pallas_call | solution.py:1231
  193.5 0.7 broadcast_in_dim.31.labels
  194.9 25.7 %loss_stage.1 = (f32[8,1280]{1,0:T(8,128)}, f32[8,1024]{1,0:T(8,128)}, f32[8,1280]{1,0:T(8,128)}, f32[24,128]{1,0:T(8,128)}) custom-call(f32[1024,1280]{1,0:T(8,128)} %get-tuple-element.122.pre, f32[1024,128]{1,0:T(8,128)} %broadcast_in_dim.13.mask, f32[8,128]{1,0:T(8,128)} %broadcast_in_dim.14.counts, s32[8,128]{1,0:T(8,128)} %broadcast_in_dim.31.labels, ...), custom_call_target="tpu_custom_call" | custom-call | tf_op jit(solution)/shard_map/loss_stage/pallas_call | solution.py:1349
  220.6 42.7 %head_back.1 = (f32[1024,320]{1,0:T(8,128)}, f32[8,128]{1,0:T(8,128)}, f32[8,8]{1,0:T(8,128)}, bf16[4,320,1280]{2,1,0:T(8,128)(2,1)}, bf16[2,80,1280]{2,1,0:T(8,128)(2,1)}) custom-call(f32[1024,1280]{1,0:T(8,128)} %get-tuple-element.122.pre, f32[8,1280]{1,0:T(8,128)} %get-tuple-element.126.grad_features, f32[1024,128]{1,0:T(8,128)} %broadcast_in_dim.13.mask, ...), custom_call_target="tpu_custom_call" | custom-call | tf_op jit(solution)/shard_map/head_back/pallas_call | solution.py:1463
  263.2 66.6 %project_back.1 = (f32[1024,1152]{1,0:T(8,128)}, f32[24,128]{1,0:T(8,128)}, f32[8,48]{1,0:T(8,128)}, f32[8,8]{1,0:T(8,128)}, f32[8,1152]{1,0:T(8,128)}, /*index=...) custom-call(bf16[4,320,1280]{2,1,0:T(8,128)(2,1)} %get-tuple-element.132.half_h, ...), custom_call_target="tpu_custom_call" | custom-call | tf_op jit(solution)/shard_map/project_back/pallas_call | solution.py:1627
  329.8 56.9 %depth_back.1 = (f32[1024,1152]{1,0:T(8,128)}, f32[4,32,1152]{2,1,0:T(8,128)}, f32[24,128]{1,0:T(8,128)}, bf16[320,2304]{1,0:T(8,128)(2,1)}, f32[32,8,1664]{2,1,0:T(8,128)}) custom-call(bf16[4,320,1152]{2,1,0:T(8,128)(2,1)} %get-tuple-element.141.half, bf16[2,80,1152]{2,1,0:T(8,128)(2,1)} %get-tuple-element.142.part, ...), custom_call_target="tpu_custom_call" | custom-call | tf_op jit(solution)/shard_map/depth_back/pallas_call | solution.py:1810
  386.7 68.9 %expand_back.1 = (bf16[256,2304]{1,0:T(8,128)(2,1)}, f32[320,1024]{1,0:T(8,128)}, f32[288,104]{1,0:T(8,128)}, f32[8,128]{1,0:T(8,128)}, f32[192,8]{1,0:T(8,128)}...) custom-call(f32[1024,1152]{1,0:T(8,128)} %get-tuple-element.152.grad, ...), custom_call_target="tpu_custom_call" | custom-call | tf_op jit(solution)/shard_map/expand_back/pallas_call | solution.py:2020
  455.7 1.0 reshape.104
  456.7 1.0 reshape.103
  457.7 0.8 concatenate.3
  461.7 24.8 %apply.1 = (f32[288,101]{1,0:T(8,128)}, f32[288,101]{1,0:T(8,128)}, f32[288,101]{1,0:T(8,128)}, f32[537,2304]{1,0:T(8,128)}, f32[537,2304]{1,0:T(8,128)}, /*inde...) custom-call(f32[8,128]{1,0:T(8,128)} %get-tuple-element.162.factors,, ...), custom_call_target="tpu_custom_call" | custom-call | tf_op jit(solution)/shard_map/apply/pallas_call | solution.py:2159
  486.5 1.2 slice.54
  (45 shorter events, 5.7 us)
Async XLA Ops:
  0.7 4.0 copy-start
  5.6 50.8 %slice-start = ((f32[5784]{0:T(1024)}), f32[1536]{0:T(1024)S(1)}, s32[]{:S(2)}) async-start(f32[5784]{0:T(1024)} %param.30), calls=%async_computation | async-start | bytes 16384 | tf_op jit(solution)/shard_map/slice | solution.py:2207
  97.6 37.6 %copy-start.2 = (f32[5784]{0:T(1024)S(1)}, f32[5784]{0:T(1024)}, u32[]{:S(2)}) copy-start(f32[5784]{0:T(1024)} %param.30) | copy-start | bytes 69412
  135.8 29.8 %slice-start.1 = ((f32[5784]{0:T(1024)}), f32[640]{0:T(1024)S(1)}, s32[]{:S(2)}) async-start(f32[5784]{0:T(1024)} %param.30), calls=%async_computation.1 | async-start | bytes 8192 | tf_op jit(solution)/shard_map/slice | solution.py:2209
  166.3 27.1 %copy-start.9 = (s32[16]{0:T(128)S(1)}, s32[16]{0:T(128)}, u32[]{:S(2)}) copy-start(s32[16]{0:T(128)} %param.25) | copy-start | bytes 196
  386.7 71.0 %copy-start.5 = (f32[8,128]{1,0:T(8,128)S(1)}, f32[8,128]{1,0:T(8,128)}, u32[]{:S(2)}) copy-start(f32[8,128]{1,0:T(8,128)} %get-tuple-element.135.proj_sums) | copy-start | bytes 12292
  386.7 74.4 %copy-start.3 = (f32[5784]{0:T(1024)S(1)}, f32[5784]{0:T(1024)}, u32[]{:S(2)}) copy-start(f32[5784]{0:T(1024)} %param.40) | copy-start | bytes 69412
  386.7 74.4 %copy-start.4 = (f32[5784]{0:T(1024)S(1)}, f32[5784]{0:T(1024)}, u32[]{:S(2)}) copy-start(f32[5784]{0:T(1024)} %param.35) | copy-start | bytes 69412
  461.7 26.0 %copy-start.6 = (f32[4,288]{1,0:T(4,128)S(1)}, f32[4,288]{1,0:T(4,128)}, u32[]{:S(2)}) copy-start(f32[4,288]{1,0:T(4,128)} %get-tuple-element.225) | copy-start | bytes 13828
  461.7 26.6 %copy-start.7 = (f32[2,320]{1,0:T(2,128)S(1)}, f32[2,320]{1,0:T(2,128)}, u32[]{:S(2)}) copy-start(f32[2,320]{1,0:T(2,128)} %get-tuple-element.226) | copy-start | bytes 7684
  461.7 27.2 %copy-start.8 = (f32[2,80]{1,0:T(2,128)S(1)}, f32[2,80]{1,0:T(2,128)}, u32[]{:S(2)}) copy-start(f32[2,80]{1,0:T(2,128)} %get-tuple-element.227) | copy-start | bytes 1924
  461.7 27.7 %copy-start.1 = (bf16[16,256,192]{1,2,0:T(8,128)(2,1)S(1)}, bf16[16,256,192]{1,2,0:T(8,128)(2,1)}, u32[]{:S(2)}) copy-start(bf16[16,256,192]{1,2,0:T(8,128)(2,1)} %param.22) | copy-start | bytes 4718596

commit v3 on v2

--- a/solution.py
+++ b/solution.py
@@ -78,51 +78,50 @@
     pl.semaphore_wait(pltpu.get_barrier_semaphore(), nd + nz - 2)
 
 
-def sum_finish(nd, nz, x_ref, o_ref, plane, depth, s1, r1, s2, r2):
+def sum_copies(nd, nz, x_ref, plane, depth, s1, r1, s2, r2):
     d = lax.axis_index("dp")
     z = lax.axis_index("chan")
     in_plane, along = sum_peers(nd, nz)
-    first = []
-    for k, peer in enumerate(in_plane):
-        first.append(
-            pltpu.make_async_remote_copy(
-                src_ref=x_ref,
-                dst_ref=plane.at[d],
-                send_sem=s1.at[k],
-                recv_sem=r1.at[k],
-                device_id=peer,
-                device_id_type=MESH,
-            )
+
+    def copy(src, dst, send, recv, peer):
+        return pltpu.make_async_remote_copy(
+            src_ref=src, dst_ref=dst, send_sem=send, recv_sem=recv, device_id=peer, device_id_type=MESH
         )
-        first[-1].start()
-    plane[d] = x_ref[...]
-    for copy in first:
-        copy.wait_recv()
+
+    first = [copy(x_ref, plane.at[d], s1.at[k], r1.at[k], peer) for k, peer in enumerate(in_plane)]
+    second = [copy(depth.at[z], depth.at[z], s2.at[k], r2.at[k], peer) for k, peer in enumerate(along)]
+    return first, second
+
+
+def sum_first(nd, nz, x_ref, plane, *comm):
+    start(sum_copies(nd, nz, x_ref, plane, *comm)[0])
+    plane[lax.axis_index("dp")] = x_ref[...]
+
+
+def sum_second(nd, nz, x_ref, plane, depth, *sems):
+    first, second = sum_copies(nd, nz, x_ref, plane, depth, *sems)
+    arrived(first)
     total = plane[0]
     for k in range(1, nd):
         total = total + plane[k]
-    depth[z] = total
-    second = []
-    for k, peer in enumerate(along):
-        second.append(
-            pltpu.make_async_remote_copy(
-                src_ref=depth.at[z],
-                dst_ref=depth.at[z],
-                send_sem=s2.at[k],
-                recv_sem=r2.at[k],
-                device_id=peer,
-                device_id_type=MESH,
-            )
-        )
-        second[-1].start()
-    for copy in second:
-        copy.wait_recv()
+    depth[lax.axis_index("chan")] = total
+    start(second)
+
+
+def sum_third(nd, nz, x_ref, plane, depth, *sems):
+    first, second = sum_copies(nd, nz, x_ref, plane, depth, *sems)
+    arrived(second)
     total = depth[0]
     for k in range(1, nz):
         total = total + depth[k]
-    o_ref[...] = total
-    for copy in first + second:
-        copy.wait_send()
+    sent(first + second)
+    return total
+
+
+def sum_finish(nd, nz, x_ref, o_ref, *comm):
+    sum_first(nd, nz, x_ref, *comm)
+    sum_second(nd, nz, x_ref, *comm)
+    o_ref[...] = sum_third(nd, nz, x_ref, *comm)
 
 
 def sum_scratch(rows, nd, nz):
@@ -137,10 +136,10 @@
     ]
 
 
-def params(ident=None):
+def params(ident=None, limit=VLIMIT):
     if ident is None:
         return pltpu.CompilerParams(vmem_limit_bytes=VLIMIT)
-    return pltpu.CompilerParams(vmem_limit_bytes=VLIMIT, collective_id=ident, has_side_effects=True)
+    return pltpu.CompilerParams(vmem_limit_bytes=limit, collective_id=ident, has_side_effects=True)
 
 
 def sum_kernel(nd, nz, x_ref, o_ref, *comm):
@@ -274,6 +273,14 @@
     return [net.copy(block, block, sems, k, net.twin)]
 
 
+def late_count(nz):
+    return max(1, (nz - 1) // 3)
+
+
+def some(stage, net, shape, ref, sems, shards):
+    return [copy for k in shards for copy in stage(net, shape, ref, sems, k)]
+
+
 def every(stage, net, shape, ref, sems):
     return [copy for k in range(net.nz - 1) for copy in stage(net, shape, ref, sems, k)]
 
@@ -298,7 +305,7 @@
     return jnp.where(lane == 0, total, 0.0)
 
 
-def first_kernel(nd, nz, shape, shape_b, block_ref, head_ref, hside_ref, side_ref, full, full_b, side, gain, kb, kh, kc, squares, wide, tall_h, tall_s, low, side_buf, gain_buf, far_s, far_r, plane_s, plane_r, twin_s, twin_r, side_s, side_r, gain_s, gain_r, later_s, later_r, local):
+def first_kernel(nd, nz, shape, shape_b, block_ref, head_ref, hside_ref, side_ref, full, full_b, side, gain, kh, kc, squares, wide, tall_h, tall_s, kb, low, side_buf, gain_buf, far_s, far_r, plane_s, plane_r, twin_s, twin_r, side_s, side_r, gain_s, gain_r, later_s, later_r, local):
     net = Net(nd, nz)
     signal(net.along + net.plane + [net.twin])
     rows = shape[0]
@@ -402,17 +409,17 @@
             jax.ShapeDtypeStruct((shape_b[0], nz * shape_b[1]), bf16),
             jax.ShapeDtypeStruct((104, nz * side.shape[0]), f32),
             jax.ShapeDtypeStruct((8, nz * own_head), f32),
-            jax.ShapeDtypeStruct(shape_b, bf16),
             jax.ShapeDtypeStruct(shape_h, bf16),
             jax.ShapeDtypeStruct(shape_c, bf16),
             jax.ShapeDtypeStruct((8, LANES), f32),
         ],
         in_specs=[hbm, hbm, hbm, vmem],
-        out_specs=[hbm, hbm] + [vmem] * 6,
+        out_specs=[hbm] * 2 + [vmem] * 5,
         scratch_shapes=[
             VMEM(block.shape, f32),
             VMEM(head_w.shape, f32),
             VMEM(head_side.shape, f32),
+            VMEM(shape_b, bf16),
             VMEM(shape, bf16),
             VMEM((nz, side.shape[1], side.shape[0]), f32),
             VMEM((nz, 8, own_head), f32),
@@ -449,22 +456,22 @@
         half[k, at, :] = (mine.astype(f32) + twin_buf[k, at, :].astype(f32)).astype(bf16)
 
 
-def reduce_plane(net, shape, half, plane_buf, sems, k, base):
+def reduce_plane(net, shape, half, plane_buf, sems, k, base, shift):
     size = reduce_sizes(*shape, net.nd)[2]
     n = net.nxy - 1
     return [
-        net.copy(half.at[k, tall(o * size, size)], plane_buf.at[q, k - base], sems, (k - base) * n + q, net.plane[q])
+        net.copy(half.at[k - shift, tall(o * size, size)], plane_buf.at[q, k - base], sems, (k - base) * n + q, net.plane[q])
         for q, o in enumerate(net.others)
     ]
 
 
-def reduce_plane_sum(net, shape, half, plane_buf, out, k, base):
+def reduce_plane_sum(net, shape, half, plane_buf, out, k, base, shift):
     size = reduce_sizes(*shape, net.nd)[2]
 
     @pl.loop(0, size // 16)
     def _(i):
         at = tall(i * 16, 16)
-        total = half[k, tall(net.place * size + i * 16, 16), :].astype(f32)
+        total = half[k - shift, tall(net.place * size + i * 16, 16), :].astype(f32)
         for q in range(net.nxy - 1):
             total = total + plane_buf[q, k - base, at, :].astype(f32)
         out[k, at, :] = total.astype(bf16)
@@ -547,14 +554,18 @@
                     action()
 
 
+def far_scratch(shape, nd, nz):
+    unit, cols, size = reduce_sizes(*shape, nd)
+    return [VMEM((nz - 1, size, cols), bf16)] + pair(nz - 1)
+
+
 def spread_scratch(shape, nd, nz):
+    return [pltpu.SemaphoreType.DMA((1,))] + pair(nd // 2 - 1) + pair(1)
+
+
+def piece_shape(shape, nd):
     unit, cols, size = reduce_sizes(*shape, nd)
-    return (
-        [VMEM((nz - 1, size, cols), bf16), VMEM((size, cols), bf16), pltpu.SemaphoreType.DMA((1,))]
-        + pair(nz - 1)
-        + pair(nd // 2 - 1)
-        + pair(1)
-    )
+    return (size, cols)
 
 
 class Twin:
@@ -577,12 +588,13 @@
 
 
 class Plane:
-    def __init__(self, net, shape, half, out, base, count, buf, ps, pr):
+    def __init__(self, net, shape, half, out, base, count, buf, ps, pr, shift=0):
         self.net, self.shape, self.half, self.out = net, shape, half, out
         self.shards, self.base, self.buf, self.sems = range(base, base + count), base, buf, (ps, pr)
+        self.shift = shift
 
     def copies(self, k):
-        return reduce_plane(self.net, self.shape, self.half, self.buf, self.sems, k, self.base)
+        return reduce_plane(self.net, self.shape, self.half, self.buf, self.sems, k, self.base, self.shift)
 
     def begin(self, k):
         start(self.copies(k))
@@ -590,7 +602,7 @@
     def add(self, then=None):
         for k in self.shards:
             arrived(self.copies(k))
-            reduce_plane_sum(self.net, self.shape, self.half, self.buf, self.out, k, self.base)
+            reduce_plane_sum(self.net, self.shape, self.half, self.buf, self.out, k, self.base, self.shift)
             if then is not None:
                 then(k)
 
@@ -599,23 +611,12 @@
             sent(self.copies(k))
 
 
-class Spread:
-    def __init__(self, net, shape, sums, out, depth_buf, piece, local, fs, fr, ps, pr, ts, tr):
-        self.net, self.shape, self.sums, self.out = net, shape, sums, out
-        self.depth_buf, self.piece, self.local = depth_buf, piece, local
-        self.far_sems, self.plane_sems, self.twin_sems = (fs, fr), (ps, pr), (ts, tr)
-
-    def far(self):
-        return reduce_far(self.net, self.sums, self.depth_buf, self.far_sems)
-
-    def own(self):
-        return pltpu.make_async_copy(self.piece, spread_block(self.net, self.shape, self.out), self.local.at[0])
-
-    def plane(self):
-        return spread_plane(self.net, self.shape, self.piece, self.out, self.plane_sems)
-
-    def twin(self):
-        return spread_twin(self.net, self.shape, self.out, self.twin_sems)
+class Far:
+    def __init__(self, net, shape, sums, piece, buf, fs, fr):
+        self.net, self.shape, self.sums, self.piece, self.buf, self.sems = net, shape, sums, piece, buf, (fs, fr)
+
+    def copies(self):
+        return reduce_far(self.net, self.sums, self.buf, self.sems)
 
     def send(self, k):
         net = self.net
@@ -623,11 +624,31 @@
 
         @pl.when(net.z != k)
         def _():
-            net.copy(self.sums.at[k], self.depth_buf.at[slot], self.far_sems, slot, (net.d, k)).start()
-
-    def share(self):
-        arrived(self.far())
-        reduce_far_sum(self.net, self.shape, self.sums, self.depth_buf, self.piece)
+            net.copy(self.sums.at[k], self.buf.at[slot], self.sems, slot, (net.d, k)).start()
+
+    def add(self):
+        arrived(self.copies())
+        reduce_far_sum(self.net, self.shape, self.sums, self.buf, self.piece)
+
+    def finish(self):
+        sent(self.copies())
+
+
+class Spread:
+    def __init__(self, net, shape, piece, out, local, ps, pr, ts, tr):
+        self.net, self.shape, self.piece, self.out, self.local = net, shape, piece, out, local
+        self.plane_sems, self.twin_sems = (ps, pr), (ts, tr)
+
+    def own(self):
+        return pltpu.make_async_copy(self.piece, spread_block(self.net, self.shape, self.out), self.local.at[0])
+
+    def plane(self):
+        return spread_plane(self.net, self.shape, self.piece, self.out, self.plane_sems)
+
+    def twin(self):
+        return spread_twin(self.net, self.shape, self.out, self.twin_sems)
+
+    def begin(self):
         self.own().start()
         start(self.plane())
 
@@ -638,7 +659,7 @@
 
     def finish(self):
         arrived(self.twin())
-        sent(self.far() + self.plane() + self.twin())
+        sent(self.plane() + self.twin())
 
 
 def up_to(size):
@@ -783,111 +804,6 @@
     return pl.ds(pl.multiple_of(b * PIXELS, PIXELS), PIXELS)
 
 
-def expand_kernel(nd, nz, nb, chunks, shapes, kern_ref, images, mask, mask_rows, counts, route, in_b, kh, pre, taps, stats_all, mix, gates, pooled, full_b, full_h, stats, *comm):
-    j = pl.program_id(0)
-    sems = comm[6:]
-    comm = comm[:6]
-    net = Net(nd, nz)
-    local = sems[4]
-
-    def copies():
-        return every(gather_plane, net, shapes[0], full_b, sems[0:2]) + gather_far(
-            net, shapes[1], kh, full_h, sems[2:4]
-        )
-
-    def own():
-        return [own_copy(net, shapes[1], kh, full_h, local.at[0])]
-
-    @pl.when(j == 1)
-    def _():
-        met(nd, nz)
-        start(copies() + own())
-
-    @pl.when(j == 0)
-    def _():
-        sum_start(nd, nz)
-        stats[...] = jnp.zeros_like(stats)
-        stats[2 * chunks : 2 * chunks + 1, :] = rsum(counts[...])
-        stats[2 * chunks + 1 : 2 * chunks + 2, :] = rsum(jnp.where(counts[...] > 0.0, 1.0, 0.0))
-        pool = dot(mask_rows[...], images[...]) / jnp.maximum(counts[:, 0:1], 1.0)
-        pooled[...] = pool
-        gate = sig(dot(pool, route[...], NN, highest))
-        gates[...] = gate
-        build_mix(gate, nb, mix)
-
-    mixed = mix_kernels(kern_ref[...], mix[...])
-    one = jnp.zeros((1, LANES), f32)
-    two = jnp.zeros((1, LANES), f32)
-    for b in range(nb):
-        at = slice(b * PIXELS, (b + 1) * PIXELS)
-        lane = slice(b * LANES, (b + 1) * LANES)
-        taps[b] = mixed[WIDTH_IN : WIDTH_IN + 32, lane]
-        value = dot(images[at, :], mixed[:WIDTH_IN, lane].astype(bf16))
-        pre[at, :] = value
-        masked = mask[at, :] * value
-        one = one + rsum(masked)
-        two = two + rsum(masked * value)
-    stats[pl.ds(j, 1), :] = one
-    stats[pl.ds(chunks + j, 1), :] = two
-
-    @pl.when(j == chunks - 1)
-    def _():
-        sum_finish(nd, nz, stats, stats_all, *comm)
-        arrived(copies())
-        sent(copies())
-        for copy in own():
-            copy.wait()
-
-
-def expand(kern, images, mask, mask_rows, counts, route, full_b, kh, nb, width, nd, nz, ident):
-    chunks = width // LANES
-    rows = nb * PIXELS
-    deep = LANES * EXPERTS
-    shapes = ((full_b.shape[0], full_b.shape[1] // nz), kh.shape)
-    hbm = pl.BlockSpec(memory_space=pltpu.HBM)
-    return pl.pallas_call(
-        functools.partial(expand_kernel, nd, nz, nb, chunks, shapes),
-        grid=(chunks,),
-        out_shape=[
-            jax.ShapeDtypeStruct((rows, width), f32),
-            jax.ShapeDtypeStruct((nb, 32, width), f32),
-            jax.ShapeDtypeStruct((24, LANES), f32),
-            jax.ShapeDtypeStruct((deep, 2 * nb * LANES), bf16),
-            jax.ShapeDtypeStruct((8, EXPERTS), f32),
-            jax.ShapeDtypeStruct((8, WIDTH_IN), f32),
-        ]
-        + [
-            jax.ShapeDtypeStruct(full_b.shape, bf16),
-            jax.ShapeDtypeStruct((kh.shape[0], nz * kh.shape[1]), bf16),
-        ],
-        in_specs=[
-            pl.BlockSpec((kern.shape[0], deep), lambda j: (0, j)),
-            whole(images.shape),
-            whole(mask.shape),
-            whole(mask_rows.shape),
-            whole(counts.shape),
-            whole(route.shape),
-        ]
-        + [hbm, whole(kh.shape)],
-        out_specs=[
-            pl.BlockSpec((rows, LANES), lambda j: (0, j)),
-            pl.BlockSpec((nb, 32, LANES), lambda j: (0, 0, j)),
-            whole((24, LANES)),
-            whole((deep, 2 * nb * LANES)),
-            whole((8, EXPERTS)),
-            whole((8, WIDTH_IN)),
-        ]
-        + [hbm] * 2,
-        scratch_shapes=sum_scratch(24, nd, nz)
-        + pair((nz - 1) * (nd // 2 - 1))
-        + pair(nz - 1)
-        + [pltpu.SemaphoreType.DMA((1,))],
-        input_output_aliases={6: 6},
-        compiler_params=params(ident),
-        name="expand",
-    )(kern, images, mask, mask_rows, counts, route, full_b, kh)
-
-
 def shifted(value, step):
     if step == 0:
         return value
@@ -897,115 +813,276 @@
     return jnp.where(keep, moved, 0.0)
 
 
-def depth_kernel(nd, nz, nb, chunks, shapes, pre, taps, mask, side, stats, in_b, in_h, kc, out, sums_all, full_b, full_h, full_c, buf, held, sums, *comm):
-    j = pl.program_id(0)
-    sems = comm[6:]
-    comm = comm[:6]
+def stage_kernel(
+    nd,
+    nz,
+    nb,
+    chunks,
+    shapes,
+    kern_ref,
+    images,
+    mask,
+    mask_rows,
+    counts,
+    route,
+    side,
+    in_b,
+    kh,
+    kc,
+    pre_out,
+    taps_out,
+    out,
+    stats_all,
+    sums_all,
+    mix,
+    gates,
+    pooled,
+    full_b,
+    full_h,
+    full_c,
+    pre,
+    taps,
+    buf,
+    held,
+    early,
+    late,
+    sums,
+    *comm,
+):
+    step = pl.program_id(0)
+    comm_early, comm_late, comm_two, sems = comm[0:6], comm[6:12], comm[12:18], comm[18:]
     net = Net(nd, nz)
-
-    def copies():
-        return (
-            every(gather_twin, net, shapes[0], full_b, sems[0:2])
-            + every(gather_plane, net, shapes[1], full_h, sems[2:4])
-            + gather_far(net, shapes[2], kc, full_c, sems[4:6])
-        )
+    few = late_count(nz)
+    cut = chunks // 2
+    groups = [[k for k in range(nz - 1) if 3 * k // (nz - 1) == g] for g in range(3)]
+
+    def far_h():
+        return gather_far(net, shapes[1], kh, full_h, sems[0:2])
+
+    def far_c():
+        return gather_far(net, shapes[2], kc, full_c, sems[2:4])
+
+    def planes_b(k):
+        return gather_plane(net, shapes[0], full_b, sems[4:6], k)
+
+    def planes_h():
+        return some(gather_plane, net, shapes[1], full_h, sems[6:8], range(few))
+
+    def twins_b(k):
+        return gather_twin(net, shapes[0], full_b, sems[8:10], k)
 
     def own():
-        return own_copy(net, shapes[2], kc, full_c, sems[6].at[0])
-
-
-    @pl.when(j == 0)
+        return [
+            own_copy(net, shapes[1], kh, full_h, sems[10].at[0]),
+            own_copy(net, shapes[2], kc, full_c, sems[10].at[1]),
+        ]
+
+    def b_planes(group):
+        for k in groups[group]:
+            start(planes_b(k))
+
+    def begin():
+        met(nd, nz)
+        b_planes(0)
+        start(far_h() + own())
+
+    def early_sum():
+        sum_first(nd, nz, early, *comm_early)
+
+    def early_second():
+        sum_second(nd, nz, early, *comm_early)
+
+    def early_third():
+        stats_all[...] = sum_third(nd, nz, early, *comm_early)
+        sum_first(nd, nz, late, *comm_late)
+
+    def late_second():
+        sum_second(nd, nz, late, *comm_late)
+
+    def late_third():
+        stats_all[...] += sum_third(nd, nz, late, *comm_late)
+
+    def h_planes():
+        arrived(far_h())
+        start(planes_h() + far_c())
+
+    def b_twins():
+        for k in range(nz - 1):
+            arrived(planes_b(k))
+            start(twins_b(k))
+
+    @pl.when(step == 0)
     def _():
         sum_start(nd, nz)
-
-    @pl.when(j == 1)
-    def _():
-        met(nd, nz)
-        start(copies())
-        own().start()
-
-    @pl.when(j == 0)
-    def _():
+        early[...] = jnp.zeros_like(early)
+        late[...] = jnp.zeros_like(late)
         sums[...] = jnp.zeros_like(sums)
-
-    mean, rstd = norm_rows(stats, j, chunks, stats[2 * chunks : 2 * chunks + 1, :])
-    scale = rstd * side[2 * SQUEEZE : 2 * SQUEEZE + 1, :]
-    bias = side[2 * SQUEEZE + 1 : 2 * SQUEEZE + 2, :]
-    held[...] = jnp.zeros_like(held)
-
-    @pl.loop(0, nb)
-    def _(b):
-        at = image(b)
-        normed = (pre[at, :] - mean) * scale + bias
-        act = normed * sig(normed) * mask[at, :]
-        for s in range(KERNEL):
-            buf[s] = shifted(act, s - KERNEL // 2)
-        taps_now = [jnp.broadcast_to(taps[b, t : t + 1, :], (MAP_SIDE, LANES)) for t in range(TAPS)]
-        acc = [None] * MAP_SIDE
-        for y in range(MAP_SIDE):
+        early[2 * chunks : 2 * chunks + 1, :] = rsum(counts[...])
+        early[2 * chunks + 1 : 2 * chunks + 2, :] = rsum(jnp.where(counts[...] > 0.0, 1.0, 0.0))
+        pool = dot(mask_rows[...], images[...]) / jnp.maximum(counts[:, 0:1], 1.0)
+        pooled[...] = pool
+        gate = sig(dot(pool, route[...], NN, highest))
+        gates[...] = gate
+        build_mix(gate, nb, mix)
+
+    steps = Steps()
+    steps.at(1, begin)
+    steps.at(cut, early_sum)
+    steps.at(cut + 2, early_second)
+    steps.at(cut + 3, functools.partial(b_planes, 1))
+    steps.at(chunks, early_third)
+    steps.at(chunks + 2, late_second)
+    steps.at(chunks + 2, functools.partial(b_planes, 2))
+    steps.at(chunks + cut, late_third)
+    steps.at(chunks + cut, h_planes)
+    steps.at(2 * chunks - 2, b_twins)
+    steps.emit(step, 2 * chunks)
+
+    @pl.when(step < chunks)
+    def _():
+        j = step
+        mixed = mix_kernels(kern_ref[...], mix[...])
+        one = jnp.zeros((1, LANES), f32)
+        two = jnp.zeros((1, LANES), f32)
+        for b in range(nb):
+            at = slice(b * PIXELS, (b + 1) * PIXELS)
+            lane = slice(b * LANES, (b + 1) * LANES)
+            taps[j, b] = mixed[WIDTH_IN : WIDTH_IN + 32, lane]
+            taps_out[b] = mixed[WIDTH_IN : WIDTH_IN + 32, lane]
+            value = dot(images[at, :], mixed[:WIDTH_IN, lane].astype(bf16))
+            pre[j, at, :] = value
+            pre_out[at, :] = value
+            masked = mask[at, :] * value
+            one = one + rsum(masked)
+            two = two + rsum(masked * value)
+
+        @pl.when(j < cut)
+        def _():
+            early[pl.ds(j, 1), :] = one
+            early[pl.ds(chunks + j, 1), :] = two
+
+        @pl.when(j >= cut)
+        def _():
+            late[pl.ds(j, 1), :] = one
+            late[pl.ds(chunks + j, 1), :] = two
+
+    @pl.when(step >= chunks)
+    def _():
+        j = step - chunks
+        mean, rstd = norm_rows(stats_all, j, chunks, stats_all[2 * chunks : 2 * chunks + 1, :])
+        scale = rstd * side[2 * SQUEEZE : 2 * SQUEEZE + 1, :]
+        bias = side[2 * SQUEEZE + 1 : 2 * SQUEEZE + 2, :]
+        held[...] = jnp.zeros_like(held)
+
+        @pl.loop(0, nb)
+        def _(b):
+            at = image(b)
+            normed = (pre[j, at, :] - mean) * scale + bias
+            act = normed * sig(normed) * mask[at, :]
             for s in range(KERNEL):
-                x = buf[s, y * MAP_SIDE : (y + 1) * MAP_SIDE, :]
-                for r in range(KERNEL):
-                    i = y - r + KERNEL // 2
-                    if 0 <= i < MAP_SIDE:
-                        term = taps_now[r * KERNEL + s] * x
-                        acc[i] = term if acc[i] is None else acc[i] + term
-            done = [y - 2] if y < MAP_SIDE - 1 else [y - 2, y - 1, y]
-            for i in done:
-                if i >= 0:
-                    out[pl.ds(pl.multiple_of(b * PIXELS + i * MAP_SIDE, MAP_SIDE), MAP_SIDE), :] = acc[i]
-        value = out[at, :]
-        masked = mask[at, :] * value
-        held[0:1, :] += rsum(masked)
-        held[1:2, :] += rsum(masked * value)
-
-    sums[pl.ds(j, 1), :] = held[0:1, :]
-    sums[pl.ds(chunks + j, 1), :] = held[1:2, :]
-
-    @pl.when(j == chunks - 1)
-    def _():
-        sum_finish(nd, nz, sums, sums_all, *comm)
-        arrived(copies())
-        sent(copies())
-        own().wait()
-
-
-def depthwise(pre, taps, mask, side, stats, full_b, full_h, kc, nb, nd, nz, ident):
-    rows, width = pre.shape
+                buf[s] = shifted(act, s - KERNEL // 2)
+            taps_now = [jnp.broadcast_to(taps[j, b, t : t + 1, :], (MAP_SIDE, LANES)) for t in range(TAPS)]
+            acc = [None] * MAP_SIDE
+            for y in range(MAP_SIDE):
+                for s in range(KERNEL):
+                    x = buf[s, y * MAP_SIDE : (y + 1) * MAP_SIDE, :]
+                    for r in range(KERNEL):
+                        i = y - r + KERNEL // 2
+                        if 0 <= i < MAP_SIDE:
+                            term = taps_now[r * KERNEL + s] * x
+                            acc[i] = term if acc[i] is None else acc[i] + term
+                done = [y - 2] if y < MAP_SIDE - 1 else [y - 2, y - 1, y]
+                for i in done:
+                    if i >= 0:
+                        out[pl.ds(pl.multiple_of(b * PIXELS + i * MAP_SIDE, MAP_SIDE), MAP_SIDE), :] = acc[i]
+            value = out[at, :]
+            masked = mask[at, :] * value
+            held[0:1, :] += rsum(masked)
+            held[1:2, :] += rsum(masked * value)
+
+        sums[pl.ds(j, 1), :] = held[0:1, :]
+        sums[pl.ds(chunks + j, 1), :] = held[1:2, :]
+
+    @pl.when(step == 2 * chunks - 1)
+    def _():
+        sum_finish(nd, nz, sums, sums_all, *comm_two)
+        for k in range(nz - 1):
+            arrived(twins_b(k))
+            sent(planes_b(k) + twins_b(k))
+        arrived(planes_h() + far_c())
+        sent(far_h() + planes_h() + far_c())
+        for copy in own():
+            copy.wait()
+
+
+def first_stage(kern, images, mask, mask_rows, counts, route, side, full_b, kh, kc, nb, width, nd, nz, ident):
     chunks = width // LANES
-    wide = lambda j: (0, j)
-    later = (full_b, full_h)
-    shapes = tuple(shard_shape(k, nz) for k in later) + (kc.shape,)
+    rows = nb * PIXELS
+    deep = LANES * EXPERTS
+    planes = (nz - 1) * (nd // 2 - 1)
+    shapes = (shard_shape(full_b, nz), kh.shape, kc.shape)
     hbm = pl.BlockSpec(memory_space=pltpu.HBM)
-    planes = (nz - 1) * (nd // 2 - 1)
+    before = lambda t: jnp.minimum(t, chunks - 1)
+    after = lambda t: jnp.maximum(t - chunks, 0)
     return pl.pallas_call(
-        functools.partial(depth_kernel, nd, nz, nb, chunks, shapes),
-        grid=(chunks,),
+        functools.partial(stage_kernel, nd, nz, nb, chunks, shapes),
+        grid=(2 * chunks,),
         out_shape=[
             jax.ShapeDtypeStruct((rows, width), f32),
+            jax.ShapeDtypeStruct((nb, 32, width), f32),
+            jax.ShapeDtypeStruct((rows, width), f32),
             jax.ShapeDtypeStruct((24, LANES), f32),
+            jax.ShapeDtypeStruct((24, LANES), f32),
+            jax.ShapeDtypeStruct((deep, 2 * nb * LANES), bf16),
+            jax.ShapeDtypeStruct((8, EXPERTS), f32),
+            jax.ShapeDtypeStruct((8, WIDTH_IN), f32),
+            jax.ShapeDtypeStruct(full_b.shape, bf16),
+            jax.ShapeDtypeStruct((kh.shape[0], nz * kh.shape[1]), bf16),
+            jax.ShapeDtypeStruct((nz,) + kc.shape, bf16),
+        ],
+        in_specs=[
+            pl.BlockSpec((kern.shape[0], deep), lambda t: (0, before(t))),
+            whole(images.shape),
+            whole(mask.shape),
+            whole(mask_rows.shape),
+            whole(counts.shape),
+            whole(route.shape),
+            pl.BlockSpec((side.shape[0], LANES), lambda t: (0, after(t))),
+            hbm,
+            whole(kh.shape),
+            whole(kc.shape),
+        ],
+        out_specs=[
+            pl.BlockSpec((rows, LANES), lambda t: (0, before(t))),
+            pl.BlockSpec((nb, 32, LANES), lambda t: (0, 0, before(t))),
+            pl.BlockSpec((rows, LANES), lambda t: (0, after(t))),
+            whole((24, LANES)),
+            whole((24, LANES)),
+            whole((deep, 2 * nb * LANES)),
+            whole((8, EXPERTS)),
+            whole((8, WIDTH_IN)),
+            hbm,
+            hbm,
+            hbm,
+        ],
+        scratch_shapes=[
+            VMEM((chunks, rows, LANES), f32),
+            VMEM((chunks, nb, 32, LANES), f32),
+            VMEM((KERNEL, PIXELS, LANES), f32),
+            VMEM((8, LANES), f32),
+            VMEM((24, LANES), f32),
+            VMEM((24, LANES), f32),
+            VMEM((24, LANES), f32),
         ]
-        + [jax.ShapeDtypeStruct(k.shape, bf16) for k in later]
-        + [jax.ShapeDtypeStruct((nz,) + kc.shape, bf16)],
-        in_specs=[
-            pl.BlockSpec((rows, LANES), wide),
-            pl.BlockSpec((nb, 32, LANES), lambda j: (0, 0, j)),
-            whole(mask.shape),
-            pl.BlockSpec((side.shape[0], LANES), wide),
-            whole(stats.shape),
-        ]
-        + [hbm, hbm, whole(kc.shape)],
-        out_specs=[pl.BlockSpec((rows, LANES), wide), whole((24, LANES))] + [hbm] * 3,
-        scratch_shapes=[VMEM((KERNEL, PIXELS, LANES), f32), VMEM((8, LANES), f32)]
-        + sum_scratch(24, nd, nz)
+        + sum_scratch(24, nd, nz)[1:] * 3
+        + pair(nz - 1) * 2
+        + pair(planes) * 2
         + pair(nz - 1)
-        + pair(planes)
-        + pair(nz - 1)
-        + [pltpu.SemaphoreType.DMA((1,))],
-        input_output_aliases={5: 2, 6: 3},
+        + [pltpu.SemaphoreType.DMA((2,))],
+        input_output_aliases={7: 8},
         compiler_params=params(ident),
-        name="depthwise",
-    )(pre, taps, mask, side, stats, *later, kc)
+        name="first_stage",
+    )(kern, images, mask, mask_rows, counts, route, side, full_b, kh, kc)
 
 
 def store_wide(ref, row, value):
@@ -1026,18 +1103,21 @@
 OUT_CHUNKS = -(-WIDTH_OUT // LANES)
 
 
-def project_kernel(nd, nz, nb, chunks, shapes, dpre, mask, side, stats, totals, counts, sq_bias, kern, mix, in_h, in_c, excited, proj, pooled, gate_out, squeezed, sums_all, mixed, full_h, full_c, act, exc, sums, *comm):
+def project_kernel(nd, nz, nb, chunks, shapes, dpre, mask, side, stats, totals, counts, sq_bias, kern, mix, in_h, excited, proj, pooled, gate_out, squeezed, sums_all, mixed, full_h, act, exc, sums, *comm):
     phase = pl.program_id(0)
+    j = pl.program_id(1)
     sems = comm[6:]
     comm = comm[:6]
     net = Net(nd, nz)
 
-    def copies():
-        return every(gather_twin, net, shapes[0], full_h, sems[0:2]) + every(
-            gather_plane, net, shapes[1], full_c, sems[2:4]
-        )
-
-    j = pl.program_id(1)
+    few = late_count(nz)
+
+    def twins(shards):
+        return some(gather_twin, net, shapes[0], full_h, sems[0:2], shards)
+
+    def planes():
+        return some(gather_plane, net, shapes[0], full_h, sems[2:4], range(few, nz - 1))
+
 
     @pl.when((phase == 0) & (j == 0))
     def _():
@@ -1046,7 +1126,12 @@
     @pl.when((phase == 0) & (j == 1))
     def _():
         met(nd, nz)
-        start(copies())
+        start(planes() + twins(range(few)))
+
+    @pl.when((phase == 1) & (j == chunks - 2))
+    def _():
+        arrived(planes())
+        start(twins(range(few, nz - 1)))
     total = totals[2 * chunks : 2 * chunks + 1, :]
 
     @pl.when((phase == 0) & (j == 0))
@@ -1104,15 +1189,15 @@
     @pl.when((phase == 1) & (j == chunks - 1))
     def _():
         sum_finish(nd, nz, sums, sums_all, *comm)
-        arrived(copies())
-        sent(copies())
-
-
-def project(dpre, mask, side, stats, totals, counts, sq_bias, full_b, mix, full_h, full_c, nb, nd, nz, ident):
+        arrived(twins(range(nz - 1)))
+        sent(planes() + twins(range(nz - 1)))
+
+
+def project(dpre, mask, side, stats, totals, counts, sq_bias, full_b, mix, full_h, nb, nd, nz, ident):
     rows, width = dpre.shape
     chunks = width // LANES
     deep = LANES * EXPERTS
-    later = (full_h, full_c)
+    later = (full_h,)
     shapes = tuple(shard_shape(k, nz) for k in later)
     hbm = pl.BlockSpec(memory_space=pltpu.HBM)
     return pl.pallas_call(
@@ -1139,7 +1224,7 @@
             pl.BlockSpec((WIDTH_OUT, deep), lambda p, j: (0, jnp.where(p == 0, j, chunks - 1))),
             whole(mix.shape),
         ]
-        + [hbm] * 2,
+        + [hbm],
         out_specs=[
             pl.BlockSpec((rows, LANES), lambda p, j: (0, jnp.where(p == 0, 0, j))),
             whole((rows, WIDTH_OUT)),
@@ -1149,12 +1234,12 @@
             whole((8, LANES)),
             whole((nb, WIDTH_OUT, width)),
         ]
-        + [hbm] * 2,
+        + [hbm],
         scratch_shapes=[VMEM((chunks, rows, LANES), f32), VMEM((rows, width), bf16)]
         + sum_scratch(8, nd, nz)
         + pair(nz - 1)
         + pair((nz - 1) * (nd // 2 - 1)),
-        input_output_aliases={9: 7, 10: 8},
+        input_output_aliases={9: 7},
         compiler_params=params(ident),
         name="project",
     )(dpre, mask, side, stats, totals, counts, sq_bias, full_b, mix, *later)
@@ -1172,8 +1257,11 @@
     comm = comm[:6]
     net = Net(nd, nz)
 
-    def copies():
-        return every(gather_twin, net, shape, full_c, sems)
+    def planes():
+        return every(gather_plane, net, shape, full_c, sems[0:2])
+
+    def twins():
+        return every(gather_twin, net, shape, full_c, sems[2:4])
 
 
     @pl.when(j == 0)
@@ -1183,7 +1271,12 @@
     @pl.when(j == 1)
     def _():
         met(nd, nz)
-        start(copies())
+        start(planes())
+
+    @pl.when(j == chunks - 2)
+    def _():
+        arrived(planes())
+        start(twins())
 
     @pl.when(j == 0)
     def _():
@@ -1218,8 +1311,8 @@
     @pl.when(j == chunks - 1)
     def _():
         sum_finish(nd, nz, sums, sums_all, *comm)
-        arrived(copies())
-        sent(copies())
+        arrived(twins())
+        sent(planes() + twins())
 
 
 def head(kern, proj, mask, mask_rows, counts, gain, route, stats, totals, full_c, nb, nd, nz, ident):
@@ -1263,33 +1356,116 @@
             whole((8, WIDTH_OUT)),
             pl.BlockSpec(memory_space=pltpu.HBM),
         ],
-        scratch_shapes=sum_scratch(24, nd, nz) + pair(nz - 1),
+        scratch_shapes=sum_scratch(24, nd, nz)
+        + pair((nz - 1) * (nd // 2 - 1))
+        + pair(nz - 1),
         input_output_aliases={9: 7},
         compiler_params=params(ident),
         name="head",
     )(kern, proj, mask, mask_rows, counts, gain, route, stats, totals, full_c)
 
 
-def loss_kernel(nd, nz, nb, chunks, pre, mask, counts, labels, bias, cls, gain, stats, totals, features, grad_logits, grad_features, sums_all, logits, sums, *comm):
-    phase = pl.program_id(0)
-    j = pl.program_id(1)
-
-    @pl.when((phase == 0) & (j == 0))
+def store_sums(early, late, cut, chunks, j, one, two):
+    @pl.when(j < cut)
+    def _():
+        early[pl.ds(j, 1), :] = one
+        early[pl.ds(chunks + j, 1), :] = two
+
+    @pl.when(j >= cut)
+    def _():
+        late[pl.ds(j, 1), :] = one
+        late[pl.ds(chunks + j, 1), :] = two
+
+
+def split_sum(nd, nz, steps, at, early, late, out, comm_early, comm_late):
+    def early_third():
+        out[...] = sum_third(nd, nz, early, *comm_early)
+
+    def late_third():
+        out[...] += sum_third(nd, nz, late, *comm_late)
+
+    steps.at(at[0], lambda: sum_first(nd, nz, early, *comm_early))
+    steps.at(at[1], lambda: sum_second(nd, nz, early, *comm_early))
+    steps.at(at[2], early_third)
+    steps.at(at[3], lambda: sum_first(nd, nz, late, *comm_late))
+    steps.at(at[4], lambda: sum_second(nd, nz, late, *comm_late))
+    steps.at(at[5], late_third)
+
+
+def head_back_kernel(
+    nd,
+    nz,
+    nb,
+    chunks,
+    shape,
+    pre,
+    mask,
+    counts,
+    labels,
+    bias,
+    cls,
+    gain,
+    stats,
+    totals,
+    low,
+    kern,
+    mixed,
+    mix,
+    gates,
+    route,
+    proj,
+    proj_stats,
+    features,
+    grad_logits,
+    sums_four,
+    grad_out,
+    sums_all,
+    dz_out,
+    half,
+    part,
+    logits,
+    grad_features,
+    held,
+    grads,
+    gate_acc,
+    early,
+    late,
+    sums,
+    *comm,
+):
+    step = pl.program_id(0)
+    phase = step // chunks
+    j = lax.rem(step, chunks)
+    net = Net(nd, nz)
+    comm_early, comm_late, comm_two, comm = comm[0:6], comm[6:12], comm[12:18], comm[18:]
+    twin = Twin(net, shape, half, *comm[0:4])
+    plane = Plane(net, shape, half, part, 0, nz // 2, *comm[4:7])
+    made = comm[0]
+    cut = chunks // 3
+    base = 2 * chunks
+    steps = Steps()
+    steps.at(1, lambda: met(nd, nz))
+    places = (chunks + cut, chunks + cut + 3, base, base, base + 1, base + cut)
+    split_sum(nd, nz, steps, places, early, late, sums_four, comm_early, comm_late)
+    for k in range(nz):
+        first = base + ready(shape, k)
+        steps.at(first, functools.partial(twin.begin, k))
+        steps.at(first + 2, functools.partial(twin.add, k))
+        if k < nz // 2:
+            steps.at(first + 2, functools.partial(plane.begin, k))
+
+    @pl.when(step == 0)
     def _():
         sum_start(nd, nz)
-
-    @pl.when((phase == 0) & (j == 1))
-    def _():
-        met(nd, nz)
+        for ref in (sums, early, late, features, logits, gate_acc):
+            ref[...] = jnp.zeros_like(ref)
+        if shape[0] > WIDTH_OUT:
+            made[WIDTH_OUT:, :] = jnp.zeros((shape[0] - WIDTH_OUT, made.shape[1]), bf16)
+
+    steps.emit(step, 3 * chunks)
     lane = pl.ds(pl.multiple_of(j * LANES, LANES), LANES)
-
-    @pl.when((phase == 0) & (j == 0))
-    def _():
-        sums[...] = jnp.zeros_like(sums)
-        features[...] = jnp.zeros_like(features)
-        logits[...] = jnp.zeros_like(logits)
-
-    mean, rstd = norm_rows(stats, j, chunks, totals[TOTAL_ROW : TOTAL_ROW + 1, :])
+    total = totals[TOTAL_ROW : TOTAL_ROW + 1, :]
+    mean, rstd = norm_rows(stats, j, chunks, total)
     scale = rstd * gain[0:1, :]
 
     @pl.when(phase == 0)
@@ -1318,7 +1494,7 @@
             + (0.1 / CLASSES) * jnp.sum(shifted_scores, axis=1, keepdims=True)
         )
         valid = jnp.where(counts[:, 0:1] > 0.0, 1.0, 0.0)
-        sums[2 * chunks : 2 * chunks + 1, :] = jnp.broadcast_to(rsum(per_image * valid), (1, LANES))
+        early[2 * chunks : 2 * chunks + 1, :] = jnp.broadcast_to(rsum(per_image * valid), (1, LANES))
         weight = valid / totals[TOTAL_ROW + 1 : TOTAL_ROW + 2, 0:1]
         grad_logits[...] = weight * jnp.where(inside, spread / mass - 0.9 * hot - 0.1 / CLASSES, 0.0)
 
@@ -1335,93 +1511,24 @@
             grad = mask[at, :] * dsilu(hat * gain[0:1, :] + gain[1:2, :]) * grads[b : b + 1, :]
             one = one + rsum(grad)
             two = two + rsum(grad * hat)
-        sums[pl.ds(j, 1), :] = one
-        sums[pl.ds(chunks + j, 1), :] = two
-
-    @pl.when((phase == 1) & (j == chunks - 1))
-    def _():
-        sum_finish(nd, nz, sums, sums_all, *comm)
-
-
-def loss_stage(pre, mask, counts, labels, bias, cls, gain, stats, totals, nb, nd, nz, ident):
-    rows, width = pre.shape
-    chunks = width // LANES
-    return pl.pallas_call(
-        functools.partial(loss_kernel, nd, nz, nb, chunks),
-        grid=(2, chunks),
-        out_shape=[
-            jax.ShapeDtypeStruct((8, width), f32),
-            jax.ShapeDtypeStruct((8, CLASS_PAD), f32),
-            jax.ShapeDtypeStruct((8, width), f32),
-            jax.ShapeDtypeStruct((24, LANES), f32),
-        ],
-        in_specs=[
-            pl.BlockSpec((rows, LANES), lambda p, j: (0, j)),
-            whole(mask.shape),
-            whole(counts.shape),
-            whole(labels.shape),
-            whole(bias.shape),
-            whole(cls.shape),
-            pl.BlockSpec((8, LANES), lambda p, j: (0, j)),
-            whole(stats.shape),
-            whole(totals.shape),
-        ],
-        out_specs=[whole((8, width)), whole((8, CLASS_PAD)), whole((8, width)), whole((24, LANES))],
-        scratch_shapes=[VMEM((8, CLASS_PAD), f32)]
-        + sum_scratch(24, nd, nz),
-        compiler_params=params(ident),
-        name="loss_stage",
-    )(pre, mask, counts, labels, bias, cls, gain, stats, totals)
-
-
-def head_back_kernel(nd, nz, nb, chunks, shape, pre, grad_features, mask, counts, gain, stats, sums_in, totals, low, kern, mixed, mix, gates, route, proj, proj_stats, grad_out, sums_all, dz_out, half, part, held, grads, gate_acc, sums, *comm):
-    j = pl.program_id(0)
-    net = Net(nd, nz)
-    twin = Twin(net, shape, half, *comm[6:10])
-    plane = Plane(net, shape, half, part, 0, nz // 2, *comm[10:13])
-    made = comm[6]
-    comm = comm[:6]
-    steps = Steps()
-    for k in range(nz):
-        first = ready(shape, k)
-        steps.at(first, functools.partial(twin.begin, k))
-        steps.at(first + 2, functools.partial(twin.add, k))
-        if k < nz // 2:
-            steps.at(first + 2, functools.partial(plane.begin, k))
-
-    @pl.when(j == 0)
-    def _():
-        sum_start(nd, nz)
-
-    @pl.when(j == 1)
-    def _():
-        met(nd, nz)
-
-    steps.emit(j, chunks)
-    lane = pl.ds(pl.multiple_of(j * LANES, LANES), LANES)
-    total = totals[TOTAL_ROW : TOTAL_ROW + 1, :]
-
-    @pl.when(j == 0)
-    def _():
-        gate_acc[...] = jnp.zeros_like(gate_acc)
-        sums[...] = jnp.zeros_like(sums)
-
-    mean, rstd = norm_rows(stats, j, chunks, total)
-    scale = rstd * gain[0:1, :]
-    one = sums_in[pl.ds(j, 1), :] / total
-    two = sums_in[pl.ds(chunks + j, 1), :] / total
-    for b in range(nb):
-        at = slice(b * PIXELS, (b + 1) * PIXELS)
-        hat = (pre[at, :] - mean) * rstd
-        grad = dsilu(hat * gain[0:1, :] + gain[1:2, :]) * grad_features[b : b + 1, :]
-        value = (scale * mask[at, :] * (grad - one - hat * two)).astype(bf16)
-        held[at, lane] = value
-        grad_mixed = dot(low[at, :], value, TN).astype(bf16)
-        grads[:, b * LANES : (b + 1) * LANES] = grad_mixed
-        gate_acc[b : b + 1, :] += gate_rows(grad_mixed, kern[...])
-    made[:WIDTH_OUT, lanes(j * LANES * EXPERTS, LANES * EXPERTS)] = dot(grads[...], mix[:, : nb * LANES], NT).astype(bf16)
-
-    @pl.when(j == chunks - 1)
+        store_sums(early, late, cut, chunks, j, one, two)
+
+    @pl.when(phase == 2)
+    def _():
+        one = sums_four[pl.ds(j, 1), :] / total
+        two = sums_four[pl.ds(chunks + j, 1), :] / total
+        for b in range(nb):
+            at = slice(b * PIXELS, (b + 1) * PIXELS)
+            hat = (pre[at, :] - mean) * rstd
+            grad = dsilu(hat * gain[0:1, :] + gain[1:2, :]) * grad_features[b : b + 1, lane]
+            value = (scale * mask[at, :] * (grad - one - hat * two)).astype(bf16)
+            held[at, lane] = value
+            grad_mixed = dot(low[at, :], value, TN).astype(bf16)
+            grads[:, b * LANES : (b + 1) * LANES] = grad_mixed
+            gate_acc[b : b + 1, :] += gate_rows(grad_mixed, kern[...])
+        made[:WIDTH_OUT, lanes(j * LANES * EXPERTS, LANES * EXPERTS)] = dot(grads[...], mix[:, : nb * LANES], NT).astype(bf16)
+
+    @pl.when(step == 3 * chunks - 1)
     def _():
         dz = gate_sums(gate_acc[...]) * gates[...] * (1.0 - gates[...])
         dz_out[...] = dz
@@ -1437,13 +1544,10 @@
             two = two + rsum(value * ((proj[at, :] - mean) * rstd))
         store_wide(sums, 0, one)
         store_wide(sums, OUT_CHUNKS, two)
-
-    @pl.when(j == chunks - 1)
-    def _():
-        late = [k for k in range(nz) if ready(shape, k) >= chunks]
-        for k in late:
+        last = [k for k in range(nz) if ready(shape, k) >= chunks]
+        for k in last:
             twin.begin(k)
-        sum_finish(nd, nz, sums, sums_all, *comm)
+        sum_finish(nd, nz, sums, sums_all, *comm_two)
         for k in range(nz):
             if ready(shape, k) + 2 >= chunks:
                 twin.add(k)
@@ -1454,16 +1558,19 @@
         plane.finish()
 
 
-def head_back(pre, grad_features, mask, counts, gain, stats, sums_in, totals, low, kern, mixed, mix, gates, route, proj, proj_stats, nb, nd, nz, ident):
+def head_back(pre, mask, counts, labels, bias, cls, gain, stats, totals, low, kern, mixed, mix, gates, route, proj, proj_stats, nb, nd, nz, ident):
     rows, width = pre.shape
     chunks = width // LANES
     deep = LANES * EXPERTS
     shape = (kern.shape[0], kern.shape[1] // nz)
-    wide = lambda j: (0, j)
+    wide = lambda t: (0, lax.rem(t, chunks))
     return pl.pallas_call(
         functools.partial(head_back_kernel, nd, nz, nb, chunks, shape),
-        grid=(chunks,),
+        grid=(3 * chunks,),
         out_shape=[
+            jax.ShapeDtypeStruct((8, width), f32),
+            jax.ShapeDtypeStruct((8, CLASS_PAD), f32),
+            jax.ShapeDtypeStruct((24, LANES), f32),
             jax.ShapeDtypeStruct((rows, WIDTH_OUT), f32),
             jax.ShapeDtypeStruct((8, LANES), f32),
             jax.ShapeDtypeStruct((8, EXPERTS), f32),
@@ -1472,15 +1579,16 @@
         ],
         in_specs=[
             pl.BlockSpec((rows, LANES), wide),
-            pl.BlockSpec((8, LANES), wide),
             whole(mask.shape),
             whole(counts.shape),
+            whole(labels.shape),
+            whole(bias.shape),
+            whole(cls.shape),
             pl.BlockSpec((8, LANES), wide),
             whole(stats.shape),
-            whole(sums_in.shape),
             whole(totals.shape),
             whole(low.shape),
-            pl.BlockSpec((WIDTH_OUT, deep), wide),
+            pl.BlockSpec((WIDTH_OUT, deep), lambda t: (0, jnp.maximum(t - 2 * chunks, 0))),
             whole(mixed.shape),
             whole(mix.shape),
             whole(gates.shape),
@@ -1489,6 +1597,9 @@
             whole(proj_stats.shape),
         ],
         out_specs=[
+            whole((8, width)),
+            whole((8, CLASS_PAD)),
+            whole((24, LANES)),
             whole((rows, WIDTH_OUT)),
             whole((8, LANES)),
             whole((8, EXPERTS)),
@@ -1496,25 +1607,31 @@
             whole(part_shape(shape, nd, nz // 2)),
         ],
         scratch_shapes=[
+            VMEM((8, CLASS_PAD), f32),
+            VMEM((8, width), f32),
             VMEM((rows, width), bf16),
             VMEM((WIDTH_OUT, nb * LANES), bf16),
             VMEM((8, deep), f32),
+            VMEM((24, LANES), f32),
+            VMEM((24, LANES), f32),
+            VMEM((8, LANES), f32),
         ]
-        + sum_scratch(8, nd, nz)
+        + sum_scratch(24, nd, nz)[1:] * 2
+        + sum_scratch(8, nd, nz)[1:]
         + twin_scratch(shape, nd, nz)
         + plane_scratch(shape, nd, nz // 2),
         compiler_params=params(ident),
         name="head_back",
-    )(pre, grad_features, mask, counts, gain, stats, sums_in, totals, low, kern, mixed, mix, gates, route, proj, proj_stats)
-
-
-def project_back_kernel(nd, nz, nb, chunks, shape_h, shape, half_h, part_h, grad_in, proj, proj_stats, proj_sums, gain, mask, counts, totals, stats, side, dpre, excited, mixed, kern, mix, gate, pooled, squeezed, sq_bias, grad_norm, sums_all, grad_squeeze, gate_grad, dz_gate, done_h, half, part, low, held, grads, gate_acc, sums_h, sums, *comm):
+    )(pre, mask, counts, labels, bias, cls, gain, stats, totals, low, kern, mixed, mix, gates, route, proj, proj_stats)
+
+
+def project_back_kernel(nd, nz, nb, chunks, shape_h, shape, half_h, part_h, grad_in, proj, proj_stats, proj_sums, gain, mask, counts, totals, stats, side, dpre, excited, mixed, kern, mix, gate, pooled, squeezed, sq_bias, grad_norm, sums_all, grad_squeeze, gate_grad, dz_gate, piece_h, half, part, low, held, grads, gate_acc, sums_h, sums, *comm):
     phase = pl.program_id(0)
     net = Net(nd, nz)
     few = nz // 2
-    cut_one = 9 + len(spread_scratch(shape_h, nd, nz))
+    cut_one = 12
     plane_h = Plane(net, shape_h, half_h, sums_h, few, nz - few, *comm[6:9])
-    up = Spread(net, shape_h, sums_h, done_h, *comm[9:cut_one])
+    far = Far(net, shape_h, sums_h, piece_h, *comm[9:cut_one])
     twin = Twin(net, shape, half, *comm[cut_one : cut_one + 4])
     plane = Plane(net, shape, half, part, 0, few, *comm[cut_one + 4 : cut_one + 7])
     made = comm[cut_one]
@@ -1527,18 +1644,16 @@
             plane_h.begin(k)
         sums_h[0:few] = part_h[...]
         for k in range(few):
-            up.send(k)
+            far.send(k)
 
     steps.at(1, begin)
-    steps.at(chunks - 1, functools.partial(plane_h.add, up.send))
-    steps.at(chunks + 3, up.share)
-    steps.at(2 * chunks - 2, up.cross)
+    steps.at(chunks + 3, functools.partial(plane_h.add, far.send))
     for k in range(nz):
         first = ready(shape, k)
         steps.at(first, functools.partial(twin.begin, k))
-        steps.at(first + 2, functools.partial(twin.add, k))
+        steps.at(first + 3, functools.partial(twin.add, k))
         if k < few:
-            steps.at(first + 2, functools.partial(plane.begin, k))
+            steps.at(first + 3, functools.partial(plane.begin, k))
     j = pl.program_id(1)
 
     @pl.when((phase == 0) & (j == 0))
@@ -1552,6 +1667,8 @@
     @pl.when((phase == 0) & (j == 0))
     def _():
         gate_acc[...] = jnp.zeros_like(gate_acc)
+        if shape[0] > WIDTH_OUT:
+            made[WIDTH_OUT:, :] = jnp.zeros((shape[0] - WIDTH_OUT, made.shape[1]), bf16)
         sums[...] = jnp.zeros_like(sums)
         grad_squeeze[...] = jnp.zeros_like(grad_squeeze)
         dz_gate[...] = jnp.zeros_like(dz_gate)
@@ -1608,8 +1725,9 @@
     @pl.when((phase == 1) & (j == chunks - 1))
     def _():
         sum_finish(nd, nz, sums, sums_all, *comm)
+        far.add()
         plane.add()
-        up.finish()
+        far.finish()
         twin.finish()
         plane.finish()
         plane_h.finish()
@@ -1633,7 +1751,7 @@
             jax.ShapeDtypeStruct((8, SQUEEZE), f32),
             jax.ShapeDtypeStruct((8, EXPERTS), f32),
             jax.ShapeDtypeStruct((8, width), f32),
-            jax.ShapeDtypeStruct(shape_h, bf16),
+            jax.ShapeDtypeStruct(piece_shape(shape_h, nd), bf16),
             jax.ShapeDtypeStruct(half_shape(shape, nd, nz), bf16),
             jax.ShapeDtypeStruct(part_shape(shape, nd, few), bf16),
         ],
@@ -1666,7 +1784,7 @@
             whole((8, SQUEEZE)),
             whole((8, EXPERTS)),
             whole((8, width)),
-            pl.BlockSpec(memory_space=pltpu.HBM),
+            whole(piece_shape(shape_h, nd)),
             whole(half_shape(shape, nd, nz)),
             whole(part_shape(shape, nd, few)),
         ],
@@ -1679,7 +1797,7 @@
         ]
         + sum_scratch(24, nd, nz)
         + plane_scratch(shape_h, nd, nz - few)
-        + spread_scratch(shape_h, nd, nz)
+        + far_scratch(shape_h, nd, nz)
         + twin_scratch(shape, nd, nz)
         + plane_scratch(shape, nd, few),
         compiler_params=params(ident),
@@ -1687,41 +1805,158 @@
     )(half_h, part_h, grad_in, proj, proj_stats, proj_sums, gain, mask, counts, totals, stats, side, dpre, excited, mixed, kern, mix, gate, pooled, squeezed, sq_bias)
 
 
-def depth_back_kernel(nd, nz, nb, chunks, shape, half, part, grad_in, dpre, pre, taps, mask, side, stats_one, stats_two, sums_two, totals, features, logits, pooled, dz_gate, head_pool, pooled_in, grad_sq, before, sq_bias, dz_head, grad_out, tap_grads, sums_all, done, rows_all, buf, acts, held, sums_b, sums, *comm):
-    j = pl.program_id(0)
+def dz_slots(nb, devices):
+    per = max(1, min(devices, LANES // (nb * EXPERTS)))
+    return per, -(-devices // (per * 8)) * 8
+
+
+def stage_back_kernel(
+    nd,
+    nz,
+    nb,
+    chunks,
+    shape,
+    shape_b,
+    shape_h,
+    cuts_one,
+    cuts_two,
+    half_b,
+    part_b,
+    piece_h,
+    grad_in,
+    dpre,
+    pre,
+    taps,
+    mask,
+    side,
+    stats_one,
+    stats_two,
+    sums_two,
+    totals,
+    features,
+    logits,
+    pooled,
+    dz_gate,
+    head_pool,
+    pooled_in,
+    grad_sq,
+    before,
+    sq_bias_in,
+    dz_head,
+    images,
+    kern,
+    mix,
+    gates,
+    gate_grad,
+    squares_w,
+    stats_three,
+    stats_four,
+    sums_four,
+    chan_old,
+    head_old,
+    proj_old,
+    done,
+    done_b,
+    done_h,
+    grad_cls,
+    grad_side_out,
+    factors,
+    route_in,
+    route_head,
+    sq_bias,
+    class_bias,
+    chan_new,
+    head_new,
+    proj_new,
+    loss,
+    made_norm,
+    tap_grads,
+    buf,
+    acts,
+    held,
+    early,
+    late,
+    sums_one,
+    sums_b,
+    piece_b,
+    rows_all,
+    grads,
+    gate_acc,
+    grad_side,
+    every_sum,
+    low,
+    half,
+    sums,
+    piece,
+    *comm,
+):
+    step = pl.program_id(0)
     net = Net(nd, nz)
     few = nz // 2
-    plane = Plane(net, shape, half, sums_b, few, nz - few, *comm[6:9])
-    up = Spread(net, shape, sums_b, done, *comm[9 : 9 + len(spread_scratch(shape, nd, nz))])
-    share = Share(net, rows_all, *comm[9 + len(spread_scratch(shape, nd, nz)) :])
-    comm = comm[:6]
+    cut = 2 * chunks // 3
+    comm_early, comm_late, comm_two, comm = comm[0:6], comm[6:12], comm[12:18], comm[18:]
+    plane_b = Plane(net, shape_b, half_b, sums_b, few, nz - few, *comm[0:3], shift=few)
+    far_b = Far(net, shape_b, sums_b, piece_b, *comm[3:6])
+    up_b = Spread(net, shape_b, piece_b, done_b, *comm[6:11])
+    up_h = Spread(net, shape_h, piece_h, done_h, *comm[11:16])
+    share = Share(net, rows_all, *comm[16:24])
+    comm = comm[24:]
+    twin = Twin(net, shape, half, *comm[0:4])
+    made = comm[0]
+    plane = Plane(net, shape, half, sums, 0, nz, *comm[4:7])
+    far = Far(net, shape, sums, piece, *comm[7:10])
+    up = Spread(net, shape, piece, done, *comm[10:15])
     steps = Steps()
+    first_planes = range(few, few + (nz - few + 1) // 2)
+    last_planes = range(first_planes.stop, nz)
 
     def begin():
         met(nd, nz)
-        for k in plane.shards:
-            plane.begin(k)
-        sums_b[0:few] = part[...]
+        up_h.begin()
+        for k in first_planes:
+            plane_b.begin(k)
+        sums_b[0:few] = part_b[...]
         for k in range(few):
-            up.send(k)
+            far_b.send(k)
+        share.far()
+
+    def more_planes():
+        for k in last_planes:
+            plane_b.begin(k)
+
+    def far_end():
+        far_b.add()
+        up_b.begin()
 
     steps.at(1, begin)
-    steps.at(2, share.far)
-    steps.at(4, functools.partial(plane.add, up.send))
-    steps.at(4, share.plane)
-    steps.at(chunks - 3, up.share)
-    steps.at(chunks - 3, share.twin)
-    steps.at(chunks - 1, up.cross)
-
-    @pl.when(j == 0)
+    steps.at(4, up_h.cross)
+    split_sum(
+        nd,
+        nz,
+        steps,
+        (cut, cut + 2, chunks, chunks, chunks + 2, chunks + cut - 1),
+        early,
+        late,
+        sums_one,
+        comm_early,
+        comm_late,
+    )
+    steps.at(cut + 1, more_planes)
+    steps.at(cut + 2, share.plane)
+    steps.at(chunks + 1, functools.partial(plane_b.add, far_b.send))
+    steps.at(chunks + 2, share.twin)
+    steps.at(chunks + 3, far_end)
+    for k in range(nz):
+        first = chunks + ready(shape, k)
+        steps.at(first, functools.partial(twin.begin, k))
+        steps.at(first + 1, functools.partial(twin.add, k))
+        steps.at(first + 1, functools.partial(plane.begin, k))
+    steps.at(2 * chunks - 2, up_b.cross)
+
+    @pl.when(step == 0)
     def _():
         sum_start(nd, nz)
-
-    steps.emit(j, chunks)
-
-    @pl.when(j == 0)
-    def _():
-        total_before = before[...] + sq_bias[...]
+        total_before = before[...] + sq_bias_in[...]
         squeezed = total_before * sig(total_before)
         share.fill(
             nb,
@@ -1729,177 +1964,92 @@
             [grad_sq[...], squeezed, dz_head[...]],
             [logits[...], head_pool[...], pooled_in[...]],
         )
-
+        for ref in (early, late, gate_acc, grads):
+            ref[...] = jnp.zeros_like(ref)
+
+    steps.emit(step, 2 * chunks)
     total = totals[TOTAL_ROW : TOTAL_ROW + 1, :]
 
-    @pl.when(j == 0)
-    def _():
-        sums[...] = jnp.zeros_like(sums)
-
-    mean_two, rstd_two = norm_rows(stats_two, j, chunks, total)
-    scale_two = rstd_two * side[2 * SQUEEZE + 2 : 2 * SQUEEZE + 3, :]
-    one_two = sums_two[pl.ds(j, 1), :] / total
-    two_two = sums_two[pl.ds(chunks + j, 1), :] / total
-    mean, rstd = norm_rows(stats_one, j, chunks, total)
-    gain = side[2 * SQUEEZE : 2 * SQUEEZE + 1, :]
-    bias = side[2 * SQUEEZE + 1 : 2 * SQUEEZE + 2, :]
-    held[...] = jnp.zeros_like(held)
-    reach = KERNEL // 2
-
-    @pl.loop(0, nb)
-    def _(b):
-        at = image(b)
-        hat = (dpre[at, :] - mean_two) * rstd_two
-        grad = scale_two * (grad_in[at, :] - mask[at, :] * (one_two + hat * two_two))
-        for s in range(KERNEL):
-            buf[s] = shifted(grad, reach - s)
-        hat = (pre[at, :] - mean) * rstd
-        normed = hat * gain + bias
-        acts[...] = normed * sig(normed) * mask[at, :]
-        taps_now = [jnp.broadcast_to(taps[b, t : t + 1, :], (MAP_SIDE, LANES)) for t in range(TAPS)]
-        acc = [None] * MAP_SIDE
-        for q in range(MAP_SIDE):
+    @pl.when(step < chunks)
+    def _():
+        j = step
+        mean_two, rstd_two = norm_rows(stats_two, j, chunks, total)
+        scale_two = rstd_two * side[2 * SQUEEZE + 2 : 2 * SQUEEZE + 3, :]
+        one_two = sums_two[pl.ds(j, 1), :] / total
+        two_two = sums_two[pl.ds(chunks + j, 1), :] / total
+        mean, rstd = norm_rows(stats_one, j, chunks, total)
+        gain = side[2 * SQUEEZE : 2 * SQUEEZE + 1, :]
+        bias = side[2 * SQUEEZE + 1 : 2 * SQUEEZE + 2, :]
+        held[...] = jnp.zeros_like(held)
+        reach = KERNEL // 2
+
+        @pl.loop(0, nb)
+        def _(b):
+            at = image(b)
+            hat = (dpre[at, :] - mean_two) * rstd_two
+            grad = scale_two * (grad_in[at, :] - mask[at, :] * (one_two + hat * two_two))
             for s in range(KERNEL):
-                x = buf[s, q * MAP_SIDE : (q + 1) * MAP_SIDE, :]
-                for r in range(KERNEL):
-                    y = q + r - reach
-                    if 0 <= y < MAP_SIDE:
-                        term = taps_now[r * KERNEL + s] * x
-                        acc[y] = term if acc[y] is None else acc[y] + term
-            done = [q - 2] if q < MAP_SIDE - 1 else [q - 2, q - 1, q]
-            for i in done:
-                if i >= 0:
-                    grad_out[pl.ds(pl.multiple_of(b * PIXELS + i * MAP_SIDE, MAP_SIDE), MAP_SIDE), :] = acc[i]
-        tap_acc = [None] * TAPS
-        for q in range(MAP_SIDE):
-            for s in range(KERNEL):
-                x = buf[s, q * MAP_SIDE : (q + 1) * MAP_SIDE, :]
-                for r in range(KERNEL):
-                    y = q + r - reach
-                    if 0 <= y < MAP_SIDE:
-                        both = acts[y * MAP_SIDE : (y + 1) * MAP_SIDE, :] * x
-                        term = both[:8] + both[8:]
-                        t = r * KERNEL + s
-                        tap_acc[t] = term if tap_acc[t] is None else tap_acc[t] + term
-        tap_grads[b] = jnp.zeros((32, LANES), f32)
-        for t in range(TAPS):
-            tap_grads[b, t : t + 1, :] = rsum(tap_acc[t])
-        hat = (pre[at, :] - mean) * rstd
-        value = grad_out[at, :] * mask[at, :] * dsilu(hat * gain + bias)
-        grad_out[at, :] = value
-        held[0:1, :] += rsum(value)
-        held[1:2, :] += rsum(value * hat)
-
-    sums[pl.ds(j, 1), :] = held[0:1, :]
-    sums[pl.ds(chunks + j, 1), :] = held[1:2, :]
-
-    @pl.when(j == chunks - 1)
-    def _():
-        sum_finish(nd, nz, sums, sums_all, *comm)
-        share.finish()
-        up.finish()
-        plane.finish()
-
-
-def depth_back(half, part, shape, grad_in, dpre, pre, taps, mask, side, stats_one, stats_two, sums_two, totals, lines, nb, nd, nz, ident):
-    rows, width = pre.shape
-    chunks = width // LANES
-    wide = lambda j: (0, j)
-    tall = pl.BlockSpec((rows, LANES), wide)
-    hbm = pl.BlockSpec(memory_space=pltpu.HBM)
-    return pl.pallas_call(
-        functools.partial(depth_back_kernel, nd, nz, nb, chunks, shape),
-        grid=(chunks,),
-        out_shape=[
-            jax.ShapeDtypeStruct((rows, width), f32),
-            jax.ShapeDtypeStruct((nb, 32, width), f32),
-            jax.ShapeDtypeStruct((24, LANES), f32),
-            jax.ShapeDtypeStruct(shape, bf16),
-            jax.ShapeDtypeStruct((nd * nz, 8, share_width(lines, nz)[-1]), f32),
-        ],
-        in_specs=[
-            whole(half.shape),
-            whole(part.shape),
-            tall,
-            tall,
-            tall,
-            pl.BlockSpec((nb, 32, LANES), lambda j: (0, 0, j)),
-            whole(mask.shape),
-            pl.BlockSpec((side.shape[0], LANES), wide),
-            whole(stats_one.shape),
-            whole(stats_two.shape),
-            whole(sums_two.shape),
-            whole(totals.shape),
-        ]
-        + [whole(x.shape) for x in lines],
-        out_specs=[tall, pl.BlockSpec((nb, 32, LANES), lambda j: (0, 0, j)), whole((24, LANES)), hbm, hbm],
-        scratch_shapes=[
-            VMEM((KERNEL, PIXELS, LANES), f32),
-            VMEM((PIXELS, LANES), f32),
-            VMEM((8, LANES), f32),
-            VMEM(part_shape(shape, nd, nz), bf16),
-        ]
-        + sum_scratch(24, nd, nz)
-        + plane_scratch(shape, nd, nz - nz // 2)
-        + spread_scratch(shape, nd, nz)
-        + share_scratch(share_width(lines, nz)[-1], nd, nz),
-        compiler_params=params(ident),
-        name="depth_back",
-    )(half, part, grad_in, dpre, pre, taps, mask, side, stats_one, stats_two, sums_two, totals, *lines)
-
-
-def expand_back_kernel(nd, nz, nb, chunks, shape, cuts_one, cuts_two, grad_in, pre, images, tap_grads, mask, side, stats, sums_in, totals, kern, mix, gates, gate_grad, rows_all, grad_b, grad_h, squares_w, stats_two, stats_three, stats_four, sums_two, sums_four, chan_old, head_old, proj_old, done, grad_cls, grad_side_out, factors, route_in, route_head, sq_bias, class_bias, chan_new, head_new, proj_new, loss, grads, gate_acc, grad_side, every_sum, half, sums, *comm):
-    j = pl.program_id(0)
-    net = Net(nd, nz)
-    low = comm[0]
-    sum_comm = comm[1:7]
-    comm = comm[7:]
-    twin = Twin(net, shape, half, *comm[0:4])
-    plane = Plane(net, shape, half, sums, 0, nz, *comm[4:7])
-    up = Spread(net, shape, sums, done, *comm[7:])
-    made = comm[0]
-    steps = Steps()
-    for k in range(nz):
-        first = ready(shape, k)
-        steps.at(first, functools.partial(twin.begin, k))
-        steps.at(first + 1, functools.partial(twin.add, k))
-        steps.at(first + 1, functools.partial(plane.begin, k))
-
-    @pl.when(j == 0)
-    def _():
-        sum_start(nd, nz)
-
-    @pl.when(j == 1)
-    def _():
-        met(nd, nz)
-
-    steps.emit(j, chunks)
-
-    total = totals[TOTAL_ROW : TOTAL_ROW + 1, :]
-
-    @pl.when(j == 0)
-    def _():
-        gate_acc[...] = jnp.zeros_like(gate_acc)
-        grads[...] = jnp.zeros_like(grads)
-
-    mean, rstd = norm_rows(stats, j, chunks, total)
-    scale = rstd * side[2 * SQUEEZE : 2 * SQUEEZE + 1, :]
-    one = sums_in[pl.ds(j, 1), :] / total
-    two = sums_in[pl.ds(chunks + j, 1), :] / total
-    for b in range(nb):
-        at = slice(b * PIXELS, (b + 1) * PIXELS)
-        lane = slice(b * LANES, (b + 1) * LANES)
-        hat = (pre[at, :] - mean) * rstd
-        value = (scale * (grad_in[at, :] - mask[at, :] * (one + hat * two))).astype(bf16)
-        grads[0:WIDTH_IN, lane] = dot(images[at, :], value, TN).astype(bf16)
-        grads[WIDTH_IN : WIDTH_IN + 32, lane] = tap_grads[b].astype(bf16)
-        gate_acc[b : b + 1, :] += gate_rows(grads[:, lane], kern[...])
-    made[:, lanes(j * LANES * EXPERTS, LANES * EXPERTS)] = dot(grads[...], mix[:, : nb * LANES], NT).astype(bf16)
-
-    @pl.when(j == chunks - 1)
+                buf[s] = shifted(grad, reach - s)
+            hat = (pre[at, :] - mean) * rstd
+            normed = hat * gain + bias
+            acts[...] = normed * sig(normed) * mask[at, :]
+            taps_now = [jnp.broadcast_to(taps[b, t : t + 1, :], (MAP_SIDE, LANES)) for t in range(TAPS)]
+            acc = [None] * MAP_SIDE
+            for q in range(MAP_SIDE):
+                for s in range(KERNEL):
+                    x = buf[s, q * MAP_SIDE : (q + 1) * MAP_SIDE, :]
+                    for r in range(KERNEL):
+                        y = q + r - reach
+                        if 0 <= y < MAP_SIDE:
+                            term = taps_now[r * KERNEL + s] * x
+                            acc[y] = term if acc[y] is None else acc[y] + term
+                done = [q - 2] if q < MAP_SIDE - 1 else [q - 2, q - 1, q]
+                for i in done:
+                    if i >= 0:
+                        made_norm[j, pl.ds(pl.multiple_of(b * PIXELS + i * MAP_SIDE, MAP_SIDE), MAP_SIDE), :] = acc[i]
+            tap_acc = [None] * TAPS
+            for q in range(MAP_SIDE):
+                for s in range(KERNEL):
+                    x = buf[s, q * MAP_SIDE : (q + 1) * MAP_SIDE, :]
+                    for r in range(KERNEL):
+                        y = q + r - reach
+                        if 0 <= y < MAP_SIDE:
+                            both = acts[y * MAP_SIDE : (y + 1) * MAP_SIDE, :] * x
+                            term = both[:8] + both[8:]
+                            t = r * KERNEL + s
+                            tap_acc[t] = term if tap_acc[t] is None else tap_acc[t] + term
+            tap_grads[j, b] = jnp.zeros((32, LANES), f32)
+            for t in range(TAPS):
+                tap_grads[j, b, t : t + 1, :] = rsum(tap_acc[t])
+            hat = (pre[at, :] - mean) * rstd
+            value = made_norm[j, at, :] * mask[at, :] * dsilu(hat * gain + bias)
+            made_norm[j, at, :] = value
+            held[0:1, :] += rsum(value)
+            held[1:2, :] += rsum(value * hat)
+
+        store_sums(early, late, cut, chunks, j, held[0:1, :], held[1:2, :])
+
+    @pl.when(step >= chunks)
+    def _():
+        j = step - chunks
+        mean, rstd = norm_rows(stats_one, j, chunks, total)
+        scale = rstd * side[2 * SQUEEZE : 2 * SQUEEZE + 1, :]
+        one = sums_one[pl.ds(j, 1), :] / total
+        two = sums_one[pl.ds(chunks + j, 1), :] / total
+        for b in range(nb):
+            at = slice(b * PIXELS, (b + 1) * PIXELS)
+            lane = slice(b * LANES, (b + 1) * LANES)
+            hat = (pre[at, :] - mean) * rstd
+            value = (scale * (made_norm[j, at, :] - mask[at, :] * (one + hat * two))).astype(bf16)
+            grads[0:WIDTH_IN, lane] = dot(images[at, :], value, TN).astype(bf16)
+            grads[WIDTH_IN : WIDTH_IN + 32, lane] = tap_grads[j, b].astype(bf16)
+            gate_acc[b : b + 1, :] += gate_rows(grads[:, lane], kern[...])
+        made[:, lanes(j * LANES * EXPERTS, LANES * EXPERTS)] = dot(grads[...], mix[:, : nb * LANES], NT).astype(bf16)
+
+    @pl.when(step == 2 * chunks - 1)
     def _():
         dz = (gate_sums(gate_acc[...]) + gate_grad[...]) * gates[...] * (1.0 - gates[...])
-        steps.end(chunks)
+        steps.end(2 * chunks)
         z = net.z
         me = net.d * nz + z
         devices = nd * nz
@@ -1909,7 +2059,9 @@
         width = own * nz
         head_width = own_head * nz
         head_chunks = head_width // LANES
+        share.finish()
         count = devices * 8
+        per, slots = dz_slots(nb, devices)
         row = lax.broadcasted_iota(jnp.int32, (count, 1), 0)
         keep = jnp.where((row & 7) < nb, 1.0, 0.0)
 
@@ -1933,8 +2085,8 @@
             return turn(load_wide(ref, at, size), z * own_size)[:, :own_size]
 
         at = 2 * SQUEEZE
-        grad_side[at : at + 1, :own] = channel(sums_in, chunks, chunks, width, own)
-        grad_side[at + 1 : at + 2, :own] = channel(sums_in, 0, chunks, width, own)
+        grad_side[at : at + 1, :own] = channel(sums_one, chunks, chunks, width, own)
+        grad_side[at + 1 : at + 2, :own] = channel(sums_one, 0, chunks, width, own)
         grad_side[at + 2 : at + 3, :own] = channel(sums_two, chunks, chunks, width, own)
         grad_side[at + 3 : at + 4, :own] = channel(sums_two, 0, chunks, width, own)
         grad_side[at + 4 : at + 5, :own] = rsum(dz_gate)
@@ -1943,9 +2095,9 @@
         class_bias[...] = rsum(logits * keep)
         head_gain = channel(sums_four, head_chunks, head_chunks, head_width, own_head)
         head_bias = channel(sums_four, 0, head_chunks, head_width, own_head)
-        totals = stats[TOTAL_ROW : TOTAL_ROW + 1, 0:1]
+        totals = stats_one[TOTAL_ROW : TOTAL_ROW + 1, 0:1]
         loss[...] = jnp.broadcast_to(
-            sums_four[2 * head_chunks : 2 * head_chunks + 1, :] / stats[TOTAL_ROW + 1 : TOTAL_ROW + 2, :], (8, LANES)
+            sums_four[2 * head_chunks : 2 * head_chunks + 1, :] / stats_one[TOTAL_ROW + 1 : TOTAL_ROW + 2, :], (8, LANES)
         )
 
         def moving(new, old, ref, at, n, size, own_size):
@@ -1954,40 +2106,45 @@
             new[at : at + 1, :] = 0.5 * old[at : at + 1, :] + 0.5 * turn(mean, z * own_size)[:, :own_size]
             new[at + 1 : at + 2, :] = 0.5 * old[at + 1 : at + 2, :] + 0.5 * turn(var, z * own_size)[:, :own_size]
 
-        moving(chan_new, chan_old, stats, 0, chunks, width, own)
+        moving(chan_new, chan_old, stats_one, 0, chunks, width, own)
         moving(chan_new, chan_old, stats_two, 2, chunks, width, own)
         moving(head_new, head_old, stats_four, 0, head_chunks, head_width, own_head)
         moving(proj_new, proj_old, stats_three, 0, OUT_CHUNKS, WIDTH_OUT, own_proj)
         low[...] = jnp.zeros_like(low)
-        low[pl.ds(me, 1), 0 : nb * EXPERTS] = jnp.concatenate([dz[b : b + 1, :] for b in range(nb)], axis=1)
-        share = 1.0 / nd
+        own_dz = fit(jnp.concatenate([dz[b : b + 1, :] for b in range(nb)], axis=1), LANES)
+        low[pl.ds(me // per, 1), :] = pltpu.roll(own_dz, lax.rem(me, per) * (nb * EXPERTS), 1)
+        fraction = 1.0 / nd
         g_hside = jnp.sum(grad_cls[...] * grad_cls[...]) + jnp.sum(head_gain * head_gain) + jnp.sum(head_bias * head_bias)
         sums = (
-            squares_of(grad_b, WIDTH_OUT),
+            0.0,
             squares_of(grad_side, 104),
-            squares_of(grad_h, WIDTH_OUT),
+            squares_of(piece_h, piece_h.shape[0]) * nd,
             g_hside,
         )
         for k in range(4):
-            low[devices + k : devices + k + 1, :] = row_of(sums[k] * share)
-            low[devices + 4 + k : devices + 5 + k, :] = squares_w[k : k + 1, :] * share
-        plane.add(up.send)
-        up.share()
-        low[devices : devices + 1, :] += row_of(squares_of(up.piece, up.piece.shape[0]))
-        sum_finish(nd, nz, low, every_sum, *sum_comm)
+            low[slots + k : slots + k + 1, :] = row_of(sums[k] * fraction)
+            low[slots + 4 + k : slots + 5 + k, :] = squares_w[k : k + 1, :] * fraction
+        plane.add(far.send)
+        far.add()
+        up.begin()
+        low[slots : slots + 1, :] = row_of(
+            squares_of(piece, piece.shape[0]) + squares_of(piece_b, piece_b.shape[0])
+        )
+        sum_finish(nd, nz, low, every_sum, *comm_two)
         up.cross()
         for k in range(4):
-            grad_sq_sum = jnp.sum(every_sum[devices + k : devices + k + 1, :], axis=1, keepdims=True)
-            weight_sq = jnp.sum(every_sum[devices + 4 + k : devices + 5 + k, :], axis=1, keepdims=True)
+            grad_sq_sum = jnp.sum(every_sum[slots + k : slots + k + 1, :], axis=1, keepdims=True)
+            weight_sq = jnp.sum(every_sum[slots + 4 + k : slots + 5 + k, :], axis=1, keepdims=True)
             factors[k : k + 1, :] = jnp.broadcast_to(
                 jnp.sqrt(weight_sq) * lax.rsqrt(grad_sq_sum + 1e-12), (1, LANES)
             )
-        row = lax.broadcasted_iota(jnp.int32, (count, devices), 0)
-        col = lax.broadcasted_iota(jnp.int32, (count, devices), 1)
-        spread = dot(jnp.where((row >> 3) == col, 1.0, 0.0), every_sum[0:devices, :], NN, highest)
+        row = lax.broadcasted_iota(jnp.int32, (count, slots), 0)
+        col = lax.broadcasted_iota(jnp.int32, (count, slots), 1)
+        spread = dot(jnp.where((row >> 3) // per == col, 1.0, 0.0), every_sum[0:slots, :], NN, highest)
         row = lax.broadcasted_iota(jnp.int32, (count, LANES), 0)
         col = lax.broadcasted_iota(jnp.int32, (count, LANES), 1)
-        spread = jnp.where((col >> 3) == (row & 7) - nb, spread, 0.0)
+        place = lax.rem(row >> 3, per) * nb + (row & 7) - nb
+        spread = jnp.where(((col >> 3) == place) & ((row & 7) >= nb), spread, 0.0)
         row = lax.broadcasted_iota(jnp.int32, (LANES, EXPERTS), 0)
         col = lax.broadcasted_iota(jnp.int32, (LANES, EXPERTS), 1)
         dz_rows = dot(spread, jnp.where((row & (EXPERTS - 1)) == col, 1.0, 0.0), NN, highest)
@@ -2000,58 +2157,100 @@
             [jnp.transpose(both)[:, 0:2], values, jnp.zeros((own_head, CLASS_PAD - CLASSES - 2), f32)], axis=1
         )
         up.finish()
+        up_b.finish()
+        up_h.finish()
+        plane_b.finish()
+        far_b.finish()
+        far.finish()
         twin.finish()
         plane.finish()
 
 
-def expand_back(grad_in, pre, images, tap_grads, mask, side, stats, sums_in, totals, kern, mix, gates, gate_grad, small, cuts, nb, nd, nz, ident):
+def stage_back(half_b, part_b, piece_h, grad_in, dpre, pre, taps, mask, side, stats_one, stats_two, sums_two, totals, lines, images, kern, mix, gates, gate_grad, small, shape_b, shape_h, nb, nd, nz, ident):
     rows, width = pre.shape
     chunks = width // LANES
     deep = LANES * EXPERTS
-    wide = lambda j: (0, j)
-    tall = pl.BlockSpec((rows, LANES), wide)
+    before = lambda t: jnp.minimum(t, chunks - 1)
+    after = lambda t: jnp.maximum(t - chunks, 0)
     shape = (kern.shape[0], kern.shape[1] // nz)
     devices = nd * nz
+    slots = dz_slots(nb, devices)[1]
+    few = nz // 2
     chan_old, head_old, proj_old = small[-3:]
     own, own_head = chan_old.shape[1], head_old.shape[1]
     outs = [(own_head, CLASS_PAD), (own, 104), (8, LANES)]
     outs += [(WIDTH_IN, EXPERTS), (WIDTH_OUT, EXPERTS), (1, SQUEEZE), (1, CLASS_PAD)]
     outs += [chan_old.shape, head_old.shape, proj_old.shape, (8, LANES)]
+    cuts_one, cuts_two, wide = share_width(lines, nz)
+    hbm = pl.BlockSpec(memory_space=pltpu.HBM)
+    tall_before = pl.BlockSpec((rows, LANES), lambda t: (0, before(t)))
     return pl.pallas_call(
-        functools.partial(expand_back_kernel, nd, nz, nb, chunks, shape, *cuts),
-        grid=(chunks,),
-        out_shape=[
-            jax.ShapeDtypeStruct(shape, bf16),
-        ]
+        functools.partial(stage_back_kernel, nd, nz, nb, chunks, shape, shape_b, shape_h, cuts_one, cuts_two),
+        grid=(2 * chunks,),
+        out_shape=[jax.ShapeDtypeStruct(x, bf16) for x in (shape, shape_b, shape_h)]
         + [jax.ShapeDtypeStruct(x, f32) for x in outs],
         in_specs=[
-            tall,
-            tall,
+            pl.BlockSpec(
+                (nz - few,) + half_b.shape[1:], lambda t: (1, 0, 0), pipeline_mode=pl.Buffered(1)
+            ),
+            whole(part_b.shape),
+            whole(piece_h.shape),
+            tall_before,
+            tall_before,
+            pl.BlockSpec((rows, LANES), lambda t: (0, lax.rem(t, chunks))),
+            pl.BlockSpec((nb, 32, LANES), lambda t: (0, 0, before(t))),
+            whole(mask.shape),
+            pl.BlockSpec((side.shape[0], LANES), lambda t: (0, lax.rem(t, chunks))),
+            whole(stats_one.shape),
+            whole(stats_two.shape),
+            whole(sums_two.shape),
+            whole(totals.shape),
+        ]
+        + [whole(x.shape) for x in lines]
+        + [
             whole(images.shape),
-            pl.BlockSpec((nb, 32, LANES), lambda j: (0, 0, j)),
-            whole(mask.shape),
-            pl.BlockSpec((side.shape[0], LANES), wide),
-            whole(stats.shape),
-            whole(sums_in.shape),
-            whole(totals.shape),
-            pl.BlockSpec((kern.shape[0], deep), wide),
+            pl.BlockSpec((kern.shape[0], deep), lambda t: (0, after(t))),
             whole(mix.shape),
             whole(gates.shape),
             whole(gate_grad.shape),
         ]
         + [whole(x.shape) for x in small],
-        out_specs=[pl.BlockSpec(memory_space=pltpu.HBM)] + [whole(x) for x in outs],
-        scratch_shapes=[VMEM((kern.shape[0], nb * LANES), bf16), VMEM((8, deep), f32)]
-        + [VMEM((104, up_to(own)), f32)]
-        + sum_scratch(devices + 8, nd, nz)[:1]
-        + [VMEM(half_shape(shape, nd, nz), bf16), VMEM(part_shape(shape, nd, nz), bf16)]
-        + sum_scratch(devices + 8, nd, nz)
+        out_specs=[hbm] * 3 + [whole(x) for x in outs],
+        scratch_shapes=[
+            VMEM((chunks, rows, LANES), f32),
+            VMEM((chunks, nb, 32, LANES), f32),
+            VMEM((KERNEL, PIXELS, LANES), f32),
+            VMEM((PIXELS, LANES), f32),
+            VMEM((8, LANES), f32),
+            VMEM((24, LANES), f32),
+            VMEM((24, LANES), f32),
+            VMEM((24, LANES), f32),
+            VMEM(part_shape(shape_b, nd, nz), bf16),
+            VMEM(piece_shape(shape_b, nd), bf16),
+            VMEM((devices, 8, wide), f32),
+            VMEM((kern.shape[0], nb * LANES), bf16),
+            VMEM((8, deep), f32),
+            VMEM((104, up_to(own)), f32),
+            VMEM((slots + 8, LANES), f32),
+            VMEM((slots + 8, LANES), f32),
+            VMEM(half_shape(shape, nd, nz), bf16),
+            VMEM(part_shape(shape, nd, nz), bf16),
+            VMEM(piece_shape(shape, nd), bf16),
+        ]
+        + sum_scratch(24, nd, nz)[1:] * 2
+        + sum_scratch(slots + 8, nd, nz)[1:]
+        + plane_scratch(shape_b, nd, nz - nz // 2)
+        + far_scratch(shape_b, nd, nz)
+        + spread_scratch(shape_b, nd, nz)
+        + spread_scratch(shape_h, nd, nz)
+        + share_scratch(wide, nd, nz)
         + twin_scratch(shape, nd, nz)
         + plane_scratch(shape, nd, nz)
+        + far_scratch(shape, nd, nz)
         + spread_scratch(shape, nd, nz),
-        compiler_params=params(ident),
-        name="expand_back",
-    )(grad_in, pre, images, tap_grads, mask, side, stats, sums_in, totals, kern, mix, gates, gate_grad, *small)
+        compiler_params=params(ident, 62 * 1024 * 1024),
+        name="stage_back",
+    )(half_b, part_b, piece_h, grad_in, dpre, pre, taps, mask, side, stats_one, stats_two, sums_two, totals, *lines, images, kern, mix, gates, gate_grad, *small)
 
 
 def update(weight, grad, moment, average, factor):
@@ -2223,34 +2422,43 @@
     count_rows = jnp.broadcast_to(jnp.pad(mine(counts).astype(f32), (0, 8 - nb))[:, None], (8, LANES))
     label_rows = jnp.broadcast_to(jnp.pad(mine(labels), (0, 8 - nb))[:, None], (8, LANES))
 
-    full_a, full_b, side, gain_head, kern_b, kern_h, kern_c, squares = first_gather(
+    full_a, full_b, side, gain_head, kern_h, kern_c, squares = first_gather(
         block_w, head_w, head_side, chan_side.T, nd, nz, 1
     )
-    pre, taps, stats_one, mix, gates, pooled_in, full_b, full_h = expand(
-        full_a, image_rows, mask, mask_rows, count_rows, route_in, full_b, kern_h, nb, width, nd, nz, 3
+    pre, taps, dpre, stats_one, stats_two, mix, gates, pooled_in, full_b, full_h, full_c = first_stage(
+        full_a,
+        image_rows,
+        mask,
+        mask_rows,
+        count_rows,
+        route_in,
+        side,
+        full_b,
+        kern_h,
+        kern_c,
+        nb,
+        width,
+        nd,
+        nz,
+        3,
     )
     totals = stats_one
-    dpre, stats_two, full_b, full_h, full_c = depthwise(
-        pre, taps, mask, side, stats_one, full_b, full_h, kern_c, nb, nd, nz, 4
-    )
-    excited, proj, pooled, gate, squeezed, stats_three, mixed_proj, full_h, full_c = project(
-        dpre, mask, side, stats_two, totals, count_rows, sq_bias, full_b, mix, full_h, full_c, nb, nd, nz, 5
+    excited, proj, pooled, gate, squeezed, stats_three, mixed_proj, full_h = project(
+        dpre, mask, side, stats_two, totals, count_rows, sq_bias, full_b, mix, full_h, nb, nd, nz, 5
     )
     low, head_pre, mixed_head, stats_four, mix_head, gates_head, head_pool, full_c = head(
         full_h, proj, mask, mask_rows, count_rows, gain_out, route_head, stats_three, totals, full_c, nb, nd, nz, 6
     )
     cls_full = full_c[:, :own_head].reshape(head_width, CLASS_PAD)
-    features, grad_logits, grad_features, sums_four = loss_stage(
-        head_pre, mask, count_rows, label_rows, class_bias, cls_full, gain_head, stats_four, totals, nb, nd, nz, 7
-    )
-    grad_proj, sums_three, dz_head, half_h, part_h = head_back(
+    features, grad_logits, sums_four, grad_proj, sums_three, dz_head, half_h, part_h = head_back(
         head_pre,
-        grad_features,
         mask,
         count_rows,
+        label_rows,
+        class_bias,
+        cls_full,
         gain_head,
         stats_four,
-        sums_four,
         totals,
         low,
         full_h,
@@ -2265,8 +2473,8 @@
         nz,
         8,
     )
-    shape_h, shape_b = kern_h.shape, kern_b.shape
-    grad_norm, sums_two, grad_squeeze, gate_grad, dz_gate, grad_h, half_b, part_b = project_back(
+    shape_h, shape_b = shard_shape(full_h, nz), shard_shape(full_b, nz)
+    grad_norm, sums_two, grad_squeeze, gate_grad, dz_gate, piece_h, half_b, part_b = project_back(
         half_h,
         part_h,
         shape_h,
@@ -2295,27 +2503,30 @@
         9,
     )
     lines = [features, grad_logits, pooled, dz_gate, head_pool, pooled_in, grad_squeeze, squeezed, sq_bias, dz_head]
-    grad_pre, tap_grads, sums_one, grad_b, rows_all = depth_back(
-        half_b, part_b, shape_b, grad_norm, dpre, pre, taps, mask, side, stats_one, stats_two, sums_two, totals, lines, nb, nd, nz, 10
-    )
-    small = [rows_all, grad_b, grad_h, squares, stats_two, stats_three, stats_four, sums_two, sums_four]
-    small += [chan_stats, head_stats, proj_stats]
-    grad_a, grad_cls, grad_side, factors, *rest = expand_back(
-        grad_pre,
+    small = [squares, stats_three, stats_four, sums_four, chan_stats, head_stats, proj_stats]
+    grad_a, grad_b, grad_h, grad_cls, grad_side, factors, *rest = stage_back(
+        half_b,
+        part_b,
+        piece_h,
+        grad_norm,
+        dpre,
         pre,
-        image_rows,
-        tap_grads,
+        taps,
         mask,
         side,
         stats_one,
-        sums_one,
+        stats_two,
+        sums_two,
         totals,
+        lines,
+        image_rows,
         full_a,
         mix,
         gates,
         gate_grad,
         small,
-        share_width(lines, nz)[:2],
+        shape_b,
+        shape_h,
         nb,
         nd,
         nz,

time: 491 us -> 451 us (0.919)
  Pallas kernels: 471 us -> 430 us
    pallas_call x5 -> x2, Pallas kernels: 230 us -> 175 us  [the longest x1 116 us: stage_back(): pl.pallas_call(functools.partial(stage_back_kernel, nd, nz, nb, chunks, s...]
    pallas_call x1, Pallas kernels: 42.7 us -> 63.5 us  [head_back(): pl.pallas_call(functools.partial(head_back_kernel, nd, nz, nb, chunks, sh...]
    pallas_call x1, Pallas kernels: 66.6 us -> 50.7 us  [project_back(): pl.pallas_call(functools.partial(project_back_kernel, nd, nz, nb, chunks,...]
    pallas_call x1, Pallas kernels: 29 us -> 35 us  [project(): pl.pallas_call(functools.partial(project_kernel, nd, nz, nb, chunks, shap...]
where the time goes in v3:
time: 451 us; the launch traced here: 449 us
  Pallas kernels  430 us (95%)
  local copies, waits for them, and re-layouts  13.3 us (3%)
    pallas_call x1, Pallas kernels, stage_back(): pl.pallas_call(functools.partial(stage_back_kernel, nd, nz, nb, chunks, s...  116 us
    pallas_call x1, Pallas kernels, head_back(): pl.pallas_call(functools.partial(head_back_kernel, nd, nz, nb, chunks, sh...  63.5 us
    pallas_call x1, Pallas kernels, first_stage(): pl.pallas_call(functools.partial(stage_kernel, nd, nz, nb, chunks, shapes...  59 us
    pallas_call x1, Pallas kernels, project_back(): pl.pallas_call(functools.partial(project_back_kernel, nd, nz, nb, chunks,...  50.7 us
    pallas_call x1, Pallas kernels, first_gather(): pl.pallas_call(functools.partial(first_kernel, nd, nz, shape, shape_b), o...  50.4 us
    pallas_call x1, Pallas kernels, project(): pl.pallas_call(functools.partial(project_kernel, nd, nz, nb, chunks, shap...  35 us
    pallas_call x1, Pallas kernels, head(): pl.pallas_call(functools.partial(head_kernel, nd, nz, nb, chunks, shard_s...  30.8 us
    pallas_call x1, Pallas kernels, apply(): pl.pallas_call(apply_kernel, grid=(steps,), out_shape=[jax.ShapeDtypeStru...  24.8 us

profile of v3, /device:TPU:0, one launch (start us, length us, event | category | flops | bytes accessed | tf_op | source)
XLA Modules:
  0.0 448.9 jit_solution(11901104390962005202)
XLA Ops:
  0.7 0.8 convert_bitcast_fusion
  1.5 1.0 broadcast_in_dim.13.mask
  2.5 0.7 dynamic-slice_convert_fusion
  3.2 0.7 broadcast_in_dim.14.counts
  4.0 0.6 pad.16.mask_rows
  4.6 50.4 %first_gather.1 = (bf16[256,9216]{1,0:T(8,128)(2,1)}, bf16[320,9216]{1,0:T(8,128)(2,1)}, f32[104,1152]{1,0:T(8,128)}, f32[8,1280]{1,0:T(8,128)}, bf16[320,2560]{...) custom-call(f32[537,2304]{1,0:T(8,128)} %block_w.1, f32[320,2560]{1,0:T(8,128)} %head_w.1, ...), custom_call_target="tpu_custom_call" | custom-call | tf_op jit(solution)/shard_map/first_gather/pallas_call | solution.py:405
  55.1 1.0 copy.45
  56.1 0.7 reshape.99.route
  56.8 59.0 %first_stage.1 = (f32[1024,1152]{1,0:T(8,128)}, f32[4,32,1152]{2,1,0:T(8,128)}, f32[1024,1152]{1,0:T(8,128)}, f32[24,128]{1,0:T(8,128)}, f32[24,128]{1,0:T(8,128...) custom-call(bf16[256,9216]{1,0:T(8,128)(2,1)} %get-tuple-element.95., ...), custom_call_target="tpu_custom_call", output_to_operand_aliasing={{8}: (7, {})} | custom-call | tf_op jit(solution)/shard_map/first_stage/pallas_call | solution.py:1027
  116.3 35.0 %project.1 = (bf16[1024,1152]{1,0:T(8,128)(2,1)}, f32[1024,320]{1,0:T(8,128)}, f32[8,1152]{1,0:T(8,128)}, f32[8,1152]{1,0:T(8,128)}, f32[8,48]{1,0:T(8,128)}, /*...) custom-call(f32[1024,1152]{1,0:T(8,128)} %get-tuple-element.100.dpre, ...), custom_call_target="tpu_custom_call", output_to_operand_aliasing={{7}: (9, {})} | custom-call | tf_op jit(solution)/shard_map/project/pallas_call | solution.py:1203
  151.3 0.8 reshape.101.route
  152.1 0.7 reshape.100.gain
  152.8 30.8 %head.1 = (bf16[1024,320]{1,0:T(8,128)(2,1)}, f32[1024,1280]{1,0:T(8,128)}, bf16[4,320,1280]{2,1,0:T(8,128)(2,1)}, f32[24,128]{1,0:T(8,128)}, bf16[1024,1024]{1,...) custom-call(bf16[320,10240]{1,0:T(8,128)(2,1)} %get-tuple-element.10, ...), custom_call_target="tpu_custom_call", output_to_operand_aliasing={{7}: (9, {})} | custom-call | tf_op jit(solution)/shard_map/head/pallas_call | solution.py:1324
  183.7 0.7 broadcast_in_dim.31.labels
  185.0 63.5 %head_back.1 = (f32[8,1280]{1,0:T(8,128)}, f32[8,1024]{1,0:T(8,128)}, f32[24,128]{1,0:T(8,128)}, f32[1024,320]{1,0:T(8,128)}, f32[8,128]{1,0:T(8,128)}, /*index=...) custom-call(f32[1024,1280]{1,0:T(8,128)} %get-tuple-element.110.pre, ...), custom_call_target="tpu_custom_call" | custom-call | tf_op jit(solution)/shard_map/head_back/pallas_call | solution.py:1567
  248.6 50.7 %project_back.1 = (f32[1024,1152]{1,0:T(8,128)}, f32[24,128]{1,0:T(8,128)}, f32[8,48]{1,0:T(8,128)}, f32[8,8]{1,0:T(8,128)}, f32[8,1152]{1,0:T(8,128)}, /*index=...) custom-call(bf16[4,320,1280]{2,1,0:T(8,128)(2,1)} %get-tuple-element.118.half_h, ...), custom_call_target="tpu_custom_call" | custom-call | tf_op jit(solution)/shard_map/project_back/pallas_call | solution.py:1745
  299.3 115.8 %stage_back.1 = (bf16[256,2304]{1,0:T(8,128)(2,1)}, bf16[320,2304]{1,0:T(8,128)(2,1)}, bf16[320,2560]{1,0:T(8,128)(2,1)}, f32[320,1024]{1,0:T(8,128)}, f32[288,1...) custom-call(bf16[4,320,1152]{2,1,0:T(8,128)(2,1)} %get-tuple-element, ...), custom_call_target="tpu_custom_call" | custom-call | tf_op jit(solution)/shard_map/stage_back/pallas_call | solution.py:2187
  415.1 1.0 reshape.104
  416.2 1.0 reshape.103
  417.2 0.8 concatenate.3
  417.9 0.6 multiply_reduce_fusion
  420.5 0.6 add_multiply_fusion
  421.2 24.8 %apply.1 = (f32[288,101]{1,0:T(8,128)}, f32[288,101]{1,0:T(8,128)}, f32[288,101]{1,0:T(8,128)}, f32[537,2304]{1,0:T(8,128)}, f32[537,2304]{1,0:T(8,128)}, /*inde...) custom-call(f32[8,128]{1,0:T(8,128)} %get-tuple-element.146.factors,, ...), custom_call_target="tpu_custom_call" | custom-call | tf_op jit(solution)/shard_map/apply/pallas_call | solution.py:2358
  446.0 1.2 slice.54
  (42 shorter events, 3.8 us)
Async XLA Ops:
  0.7 54.4 %copy-start = (bf16[16,256,192]{1,2,0:T(8,128)(2,1)S(1)}, bf16[16,256,192]{1,2,0:T(8,128)(2,1)}, u32[]{:S(2)}) copy-start(bf16[16,256,192]{1,2,0:T(8,128)(2,1)} %param.22) | copy-start | bytes 4718596
  4.6 51.4 %slice-start = ((f32[5784]{0:T(1024)}), f32[1536]{0:T(1024)S(1)}, s32[]{:S(2)}) async-start(f32[5784]{0:T(1024)} %param.30), calls=%async_computation | async-start | bytes 16384 | tf_op jit(solution)/shard_map/slice | solution.py:2406
  56.8 59.0 %copy-start.2 = (f32[5784]{0:T(1024)S(1)}, f32[5784]{0:T(1024)}, u32[]{:S(2)}) copy-start(f32[5784]{0:T(1024)} %param.30) | copy-start | bytes 69412
  116.3 35.8 %slice-start.1 = ((f32[5784]{0:T(1024)}), f32[640]{0:T(1024)S(1)}, s32[]{:S(2)}) async-start(f32[5784]{0:T(1024)} %param.30), calls=%async_computation.1 | async-start | bytes 8192 | tf_op jit(solution)/shard_map/slice | solution.py:2408
  152.8 30.8 %copy-start.9 = (s32[16]{0:T(128)S(1)}, s32[16]{0:T(128)}, u32[]{:S(2)}) copy-start(s32[16]{0:T(128)} %param.25) | copy-start | bytes 196
  299.3 117.9 %copy-start.5 = (f32[8,128]{1,0:T(8,128)S(1)}, f32[8,128]{1,0:T(8,128)}, u32[]{:S(2)}) copy-start(f32[8,128]{1,0:T(8,128)} %get-tuple-element.121.proj_sums) | copy-start | bytes 12292
  299.3 121.3 %copy-start.3 = (f32[5784]{0:T(1024)S(1)}, f32[5784]{0:T(1024)}, u32[]{:S(2)}) copy-start(f32[5784]{0:T(1024)} %param.40) | copy-start | bytes 69412
  299.3 121.2 %copy-start.4 = (f32[5784]{0:T(1024)S(1)}, f32[5784]{0:T(1024)}, u32[]{:S(2)}) copy-start(f32[5784]{0:T(1024)} %param.35) | copy-start | bytes 69412
  421.2 26.0 %copy-start.6 = (f32[4,288]{1,0:T(4,128)S(1)}, f32[4,288]{1,0:T(4,128)}, u32[]{:S(2)}) copy-start(f32[4,288]{1,0:T(4,128)} %get-tuple-element.211) | copy-start | bytes 13828
  421.2 26.6 %copy-start.7 = (f32[2,320]{1,0:T(2,128)S(1)}, f32[2,320]{1,0:T(2,128)}, u32[]{:S(2)}) copy-start(f32[2,320]{1,0:T(2,128)} %get-tuple-element.212) | copy-start | bytes 7684
  421.2 27.2 %copy-start.8 = (f32[2,80]{1,0:T(2,128)S(1)}, f32[2,80]{1,0:T(2,128)}, u32[]{:S(2)}) copy-start(f32[2,80]{1,0:T(2,128)} %get-tuple-element.213) | copy-start | bytes 1924
  421.2 27.7 %copy-start.1 = (bf16[16,256,192]{1,2,0:T(8,128)(2,1)S(1)}, bf16[16,256,192]{1,2,0:T(8,128)(2,1)}, u32[]{:S(2)}) copy-start(bf16[16,256,192]{1,2,0:T(8,128)(2,1)} %param.22) | copy-start | bytes 4718596

commit v4 on v3

--- a/solution.py
+++ b/solution.py
@@ -601,10 +601,13 @@
 
     def add(self, then=None):
         for k in self.shards:
-            arrived(self.copies(k))
-            reduce_plane_sum(self.net, self.shape, self.half, self.buf, self.out, k, self.base, self.shift)
-            if then is not None:
-                then(k)
+            self.add_one(k, then)
+
+    def add_one(self, k, then=None):
+        arrived(self.copies(k))
+        reduce_plane_sum(self.net, self.shape, self.half, self.buf, self.out, k, self.base, self.shift)
+        if then is not None:
+            then(k)
 
     def finish(self):
         for k in self.shards:
@@ -826,6 +829,7 @@
     counts,
     route,
     side,
+    sq_bias,
     in_b,
     kh,
     kc,
@@ -837,6 +841,13 @@
     mix,
     gates,
     pooled,
+    excited,
+    proj,
+    pool_out,
+    gate_out,
+    squeezed,
+    last_all,
+    mixed,
     full_b,
     full_h,
     full_c,
@@ -846,11 +857,18 @@
     held,
     early,
     late,
-    sums,
+    early_two,
+    late_two,
+    sums_three,
+    dpre,
+    exc,
+    kern_buf,
     *comm,
 ):
     step = pl.program_id(0)
     comm_early, comm_late, comm_two, sems = comm[0:6], comm[6:12], comm[12:18], comm[18:]
+    two_early, two_late, sems = sems[0:6], sems[6:12], sems[12:]
+    cut_two = chunks // 2
     net = Net(nd, nz)
     few = late_count(nz)
     cut = chunks // 2
@@ -866,7 +884,7 @@
         return gather_plane(net, shapes[0], full_b, sems[4:6], k)
 
     def planes_h():
-        return some(gather_plane, net, shapes[1], full_h, sems[6:8], range(few))
+        return every(gather_plane, net, shapes[1], full_h, sems[6:8])
 
     def twins_b(k):
         return gather_twin(net, shapes[0], full_b, sems[8:10], k)
@@ -902,12 +920,30 @@
     def late_third():
         stats_all[...] += sum_third(nd, nz, late, *comm_late)
 
-    def h_planes():
-        arrived(far_h())
-        start(planes_h() + far_c())
-
-    def b_twins():
+    def h_planes(k):
+        start(gather_plane(net, shapes[1], full_h, sems[6:8], k))
+
+    def twins_h(k):
+        return gather_twin(net, shapes[1], full_h, sems[11:13], k)
+
+    def h_twin(k):
+        arrived(gather_plane(net, shapes[1], full_h, sems[6:8], k))
+        start(twins_h(k))
+
+    def load(k):
+        return pltpu.make_async_copy(
+            full_b.at[pl.ds(0, WIDTH_OUT), lanes(k * LANES * EXPERTS, LANES * EXPERTS)],
+            kern_buf.at[lax.rem(k, 2)],
+            sems[13].at[lax.rem(k, 2)],
+        )
+
+    def b_whole():
         for k in range(nz - 1):
+            arrived(twins_b(k))
+        load(0).start()
+
+    def b_twins(group):
+        for k in groups[group]:
             arrived(planes_b(k))
             start(twins_b(k))
 
@@ -916,7 +952,8 @@
         sum_start(nd, nz)
         early[...] = jnp.zeros_like(early)
         late[...] = jnp.zeros_like(late)
-        sums[...] = jnp.zeros_like(sums)
+        for ref in (early_two, late_two, sums_three, squeezed, pool_out):
+            ref[...] = jnp.zeros_like(ref)
         early[2 * chunks : 2 * chunks + 1, :] = rsum(counts[...])
         early[2 * chunks + 1 : 2 * chunks + 2, :] = rsum(jnp.where(counts[...] > 0.0, 1.0, 0.0))
         pool = dot(mask_rows[...], images[...]) / jnp.maximum(counts[:, 0:1], 1.0)
@@ -934,9 +971,20 @@
     steps.at(chunks + 2, late_second)
     steps.at(chunks + 2, functools.partial(b_planes, 2))
     steps.at(chunks + cut, late_third)
-    steps.at(chunks + cut, h_planes)
-    steps.at(2 * chunks - 2, b_twins)
-    steps.emit(step, 2 * chunks)
+    steps.at(chunks + cut, lambda: arrived(far_h()))
+    steps.at(chunks + cut, lambda: start(far_c()))
+    places = (chunks + cut_two, chunks + cut_two + 2, 2 * chunks, 2 * chunks, 2 * chunks + 2, 2 * chunks + cut_two)
+    split_sum(nd, nz, steps, places, early_two, late_two, sums_all, two_early, two_late)
+    later_steps = (chunks + cut_two + 1, 2 * chunks + 1, 2 * chunks + cut_two)
+    for k in range(nz - 1):
+        group = 3 * k // (nz - 1)
+        steps.at(later_steps[group], functools.partial(h_planes, k))
+        steps.at((2 * chunks + 2, 3 * chunks, 4 * chunks - 3)[group], functools.partial(h_twin, k))
+    steps.at(2 * chunks - 1, b_whole)
+    steps.at(chunks - 1, functools.partial(b_twins, 0))
+    steps.at(chunks + 3, functools.partial(b_twins, 1))
+    steps.at(2 * chunks - 3, functools.partial(b_twins, 2))
+    steps.emit(step, 4 * chunks)
 
     @pl.when(step < chunks)
     def _():
@@ -966,7 +1014,7 @@
             late[pl.ds(j, 1), :] = one
             late[pl.ds(chunks + j, 1), :] = two
 
-    @pl.when(step >= chunks)
+    @pl.when((step >= chunks) & (step < 2 * chunks))
     def _():
         j = step - chunks
         mean, rstd = norm_rows(stats_all, j, chunks, stats_all[2 * chunks : 2 * chunks + 1, :])
@@ -996,26 +1044,79 @@
                     if i >= 0:
                         out[pl.ds(pl.multiple_of(b * PIXELS + i * MAP_SIDE, MAP_SIDE), MAP_SIDE), :] = acc[i]
             value = out[at, :]
+            dpre[j, at, :] = value
             masked = mask[at, :] * value
             held[0:1, :] += rsum(masked)
             held[1:2, :] += rsum(masked * value)
 
-        sums[pl.ds(j, 1), :] = held[0:1, :]
-        sums[pl.ds(chunks + j, 1), :] = held[1:2, :]
-
-    @pl.when(step == 2 * chunks - 1)
+        store_sums(early_two, late_two, cut_two, chunks, j, held[0:1, :], held[1:2, :])
+
+    total = stats_all[2 * chunks : 2 * chunks + 1, :]
+
+    @pl.when((step >= 2 * chunks) & (step < 3 * chunks))
     def _():
-        sum_finish(nd, nz, sums, sums_all, *comm_two)
+        j = step - 2 * chunks
+        lane = pl.ds(pl.multiple_of(j * LANES, LANES), LANES)
+        load(j).wait()
+
+        @pl.when(j + 1 < chunks)
+        def _():
+            load(j + 1).start()
+
+        both = mix_kernels(kern_buf[lax.rem(j, 2)], mix[...])
+        for b in range(nb):
+            mixed[b, :, lane] = both[:, b * LANES : (b + 1) * LANES].astype(bf16)
+        mean, rstd = norm_rows(sums_all, j, chunks, total)
+        scale = rstd * side[2 * SQUEEZE + 2 : 2 * SQUEEZE + 3, :]
+        bias = side[2 * SQUEEZE + 3 : 2 * SQUEEZE + 4, :]
+        for b in range(nb):
+            at = slice(b * PIXELS, (b + 1) * PIXELS)
+            normed = (dpre[j, at, :] - mean) * scale + bias
+            value = normed * sig(normed) * mask[at, :]
+            dpre[j, at, :] = value
+            pool_out[b : b + 1, lane] = rsum(value) / jnp.maximum(counts[b : b + 1, :], 1.0)
+        squeezed[...] += dot(pool_out[:, lane], side[0:SQUEEZE, :], NT, highest)
+
+    @pl.when(step >= 3 * chunks)
+    def _():
+        j = step - 3 * chunks
+        lane = pl.ds(pl.multiple_of(j * LANES, LANES), LANES)
+        before = squeezed[...] + sq_bias[...]
+        gate = sig(
+            dot(before * sig(before), side[SQUEEZE : 2 * SQUEEZE, :], NN, highest)
+            + side[2 * SQUEEZE + 4 : 2 * SQUEEZE + 5, :]
+        )
+        gate_out[:, lane] = gate
+        for b in range(nb):
+            at = slice(b * PIXELS, (b + 1) * PIXELS)
+            value = (dpre[j, at, :] * gate[b : b + 1, :]).astype(bf16)
+            excited[at, :] = value
+            exc[at, lane] = value
+
+    @pl.when(step == 4 * chunks - 1)
+    def _():
+        one = jnp.zeros((1, WIDTH_OUT), f32)
+        two = jnp.zeros((1, WIDTH_OUT), f32)
+        for b in range(nb):
+            at = slice(b * PIXELS, (b + 1) * PIXELS)
+            value = dot(exc[at, :], mixed[b], NT)
+            proj[at, :] = value
+            masked = mask[at, 0:1] * value
+            one = one + rsum(masked)
+            two = two + rsum(masked * value)
+        store_wide(sums_three, 0, one)
+        store_wide(sums_three, OUT_CHUNKS, two)
+        sum_finish(nd, nz, sums_three, last_all, *comm_two)
         for k in range(nz - 1):
-            arrived(twins_b(k))
-            sent(planes_b(k) + twins_b(k))
-        arrived(planes_h() + far_c())
+            arrived(twins_h(k))
+            sent(planes_b(k) + twins_b(k) + twins_h(k))
+        arrived(far_c())
         sent(far_h() + planes_h() + far_c())
         for copy in own():
             copy.wait()
 
 
-def first_stage(kern, images, mask, mask_rows, counts, route, side, full_b, kh, kc, nb, width, nd, nz, ident):
+def first_stage(kern, images, mask, mask_rows, counts, route, side, sq_bias, full_b, kh, kc, nb, width, nd, nz, ident):
     chunks = width // LANES
     rows = nb * PIXELS
     deep = LANES * EXPERTS
@@ -1023,10 +1124,11 @@
     shapes = (shard_shape(full_b, nz), kh.shape, kc.shape)
     hbm = pl.BlockSpec(memory_space=pltpu.HBM)
     before = lambda t: jnp.minimum(t, chunks - 1)
-    after = lambda t: jnp.maximum(t - chunks, 0)
+    after = lambda t: jnp.clip(t - chunks, 0, chunks - 1)
+    cycled = lambda t: lax.rem(t, chunks)
     return pl.pallas_call(
         functools.partial(stage_kernel, nd, nz, nb, chunks, shapes),
-        grid=(2 * chunks,),
+        grid=(4 * chunks,),
         out_shape=[
             jax.ShapeDtypeStruct((rows, width), f32),
             jax.ShapeDtypeStruct((nb, 32, width), f32),
@@ -1036,6 +1138,13 @@
             jax.ShapeDtypeStruct((deep, 2 * nb * LANES), bf16),
             jax.ShapeDtypeStruct((8, EXPERTS), f32),
             jax.ShapeDtypeStruct((8, WIDTH_IN), f32),
+            jax.ShapeDtypeStruct((rows, width), bf16),
+            jax.ShapeDtypeStruct((rows, WIDTH_OUT), f32),
+            jax.ShapeDtypeStruct((8, width), f32),
+            jax.ShapeDtypeStruct((8, width), f32),
+            jax.ShapeDtypeStruct((8, SQUEEZE), f32),
+            jax.ShapeDtypeStruct((8, LANES), f32),
+            jax.ShapeDtypeStruct((nb, WIDTH_OUT, width), bf16),
             jax.ShapeDtypeStruct(full_b.shape, bf16),
             jax.ShapeDtypeStruct((kh.shape[0], nz * kh.shape[1]), bf16),
             jax.ShapeDtypeStruct((nz,) + kc.shape, bf16),
@@ -1047,7 +1156,8 @@
             whole(mask_rows.shape),
             whole(counts.shape),
             whole(route.shape),
-            pl.BlockSpec((side.shape[0], LANES), lambda t: (0, after(t))),
+            pl.BlockSpec((side.shape[0], LANES), lambda t: (0, cycled(t))),
+            whole(sq_bias.shape),
             hbm,
             whole(kh.shape),
             whole(kc.shape),
@@ -1061,6 +1171,13 @@
             whole((deep, 2 * nb * LANES)),
             whole((8, EXPERTS)),
             whole((8, WIDTH_IN)),
+            pl.BlockSpec((rows, LANES), lambda t: (0, jnp.maximum(t - 3 * chunks, 0))),
+            whole((rows, WIDTH_OUT)),
+            whole((8, width)),
+            whole((8, width)),
+            whole((8, SQUEEZE)),
+            whole((8, LANES)),
+            whole((nb, WIDTH_OUT, width)),
             hbm,
             hbm,
             hbm,
@@ -1073,16 +1190,25 @@
             VMEM((24, LANES), f32),
             VMEM((24, LANES), f32),
             VMEM((24, LANES), f32),
+            VMEM((24, LANES), f32),
+            VMEM((8, LANES), f32),
+            VMEM((chunks, rows, LANES), f32),
+            VMEM((rows, width), bf16),
+            VMEM((2, WIDTH_OUT, deep), bf16),
         ]
-        + sum_scratch(24, nd, nz)[1:] * 3
+        + sum_scratch(24, nd, nz)[1:] * 2
+        + sum_scratch(8, nd, nz)[1:]
+        + sum_scratch(24, nd, nz)[1:] * 2
         + pair(nz - 1) * 2
         + pair(planes) * 2
         + pair(nz - 1)
+        + [pltpu.SemaphoreType.DMA((2,))]
+        + pair(nz - 1)
         + [pltpu.SemaphoreType.DMA((2,))],
-        input_output_aliases={7: 8},
+        input_output_aliases={8: 15},
         compiler_params=params(ident),
         name="first_stage",
-    )(kern, images, mask, mask_rows, counts, route, side, full_b, kh, kc)
+    )(kern, images, mask, mask_rows, counts, route, side, sq_bias, full_b, kh, kc)
 
 
 def store_wide(ref, row, value):
@@ -1103,266 +1229,10 @@
 OUT_CHUNKS = -(-WIDTH_OUT // LANES)
 
 
-def project_kernel(nd, nz, nb, chunks, shapes, dpre, mask, side, stats, totals, counts, sq_bias, kern, mix, in_h, excited, proj, pooled, gate_out, squeezed, sums_all, mixed, full_h, act, exc, sums, *comm):
-    phase = pl.program_id(0)
-    j = pl.program_id(1)
-    sems = comm[6:]
-    comm = comm[:6]
-    net = Net(nd, nz)
-
-    few = late_count(nz)
-
-    def twins(shards):
-        return some(gather_twin, net, shapes[0], full_h, sems[0:2], shards)
-
-    def planes():
-        return some(gather_plane, net, shapes[0], full_h, sems[2:4], range(few, nz - 1))
-
-
-    @pl.when((phase == 0) & (j == 0))
-    def _():
-        sum_start(nd, nz)
-
-    @pl.when((phase == 0) & (j == 1))
-    def _():
-        met(nd, nz)
-        start(planes() + twins(range(few)))
-
-    @pl.when((phase == 1) & (j == chunks - 2))
-    def _():
-        arrived(planes())
-        start(twins(range(few, nz - 1)))
-    total = totals[2 * chunks : 2 * chunks + 1, :]
-
-    @pl.when((phase == 0) & (j == 0))
-    def _():
-        squeezed[...] = jnp.zeros_like(squeezed)
-        pooled[...] = jnp.zeros_like(pooled)
-        sums[...] = jnp.zeros_like(sums)
-
-    lane = pl.ds(pl.multiple_of(j * LANES, LANES), LANES)
-
-    @pl.when(phase == 0)
-    def _():
-        both = mix_kernels(kern[...], mix[...])
-        for b in range(nb):
-            mixed[b, :, lane] = both[:, b * LANES : (b + 1) * LANES].astype(bf16)
-        mean, rstd = norm_rows(stats, j, chunks, total)
-        scale = rstd * side[2 * SQUEEZE + 2 : 2 * SQUEEZE + 3, :]
-        bias = side[2 * SQUEEZE + 3 : 2 * SQUEEZE + 4, :]
-        for b in range(nb):
-            at = slice(b * PIXELS, (b + 1) * PIXELS)
-            normed = (dpre[at, :] - mean) * scale + bias
-            value = normed * sig(normed) * mask[at, :]
-            act[j, at, :] = value
-            pooled[b : b + 1, lane] = rsum(value) / jnp.maximum(counts[b : b + 1, :], 1.0)
-        squeezed[...] += dot(pooled[:, lane], side[0:SQUEEZE, :], NT, highest)
-
-    @pl.when(phase == 1)
-    def _():
-        before = squeezed[...] + sq_bias[...]
-        gate = sig(
-            dot(before * sig(before), side[SQUEEZE : 2 * SQUEEZE, :], NN, highest)
-            + side[2 * SQUEEZE + 4 : 2 * SQUEEZE + 5, :]
-        )
-        gate_out[:, lane] = gate
-        for b in range(nb):
-            at = slice(b * PIXELS, (b + 1) * PIXELS)
-            value = (act[j, at, :] * gate[b : b + 1, :]).astype(bf16)
-            excited[at, :] = value
-            exc[at, lane] = value
-
-    @pl.when((phase == 1) & (j == chunks - 1))
-    def _():
-        one = jnp.zeros((1, WIDTH_OUT), f32)
-        two = jnp.zeros((1, WIDTH_OUT), f32)
-        for b in range(nb):
-            at = slice(b * PIXELS, (b + 1) * PIXELS)
-            value = dot(exc[at, :], mixed[b], NT)
-            proj[at, :] = value
-            masked = mask[at, 0:1] * value
-            one = one + rsum(masked)
-            two = two + rsum(masked * value)
-        store_wide(sums, 0, one)
-        store_wide(sums, OUT_CHUNKS, two)
-
-    @pl.when((phase == 1) & (j == chunks - 1))
-    def _():
-        sum_finish(nd, nz, sums, sums_all, *comm)
-        arrived(twins(range(nz - 1)))
-        sent(planes() + twins(range(nz - 1)))
-
-
-def project(dpre, mask, side, stats, totals, counts, sq_bias, full_b, mix, full_h, nb, nd, nz, ident):
-    rows, width = dpre.shape
-    chunks = width // LANES
-    deep = LANES * EXPERTS
-    later = (full_h,)
-    shapes = tuple(shard_shape(k, nz) for k in later)
-    hbm = pl.BlockSpec(memory_space=pltpu.HBM)
-    return pl.pallas_call(
-        functools.partial(project_kernel, nd, nz, nb, chunks, shapes),
-        grid=(2, chunks),
-        out_shape=[
-            jax.ShapeDtypeStruct((rows, width), bf16),
-            jax.ShapeDtypeStruct((rows, WIDTH_OUT), f32),
-            jax.ShapeDtypeStruct((8, width), f32),
-            jax.ShapeDtypeStruct((8, width), f32),
-            jax.ShapeDtypeStruct((8, SQUEEZE), f32),
-            jax.ShapeDtypeStruct((8, LANES), f32),
-            jax.ShapeDtypeStruct((nb, WIDTH_OUT, width), bf16),
-        ]
-        + [jax.ShapeDtypeStruct(k.shape, bf16) for k in later],
-        in_specs=[
-            pl.BlockSpec((rows, LANES), lambda p, j: (0, jnp.where(p == 0, j, chunks - 1))),
-            whole(mask.shape),
-            pl.BlockSpec((side.shape[0], LANES), lambda p, j: (0, j)),
-            whole(stats.shape),
-            whole(totals.shape),
-            whole(counts.shape),
-            whole(sq_bias.shape),
-            pl.BlockSpec((WIDTH_OUT, deep), lambda p, j: (0, jnp.where(p == 0, j, chunks - 1))),
-            whole(mix.shape),
-        ]
-        + [hbm],
-        out_specs=[
-            pl.BlockSpec((rows, LANES), lambda p, j: (0, jnp.where(p == 0, 0, j))),
-            whole((rows, WIDTH_OUT)),
-            whole((8, width)),
-            whole((8, width)),
-            whole((8, SQUEEZE)),
-            whole((8, LANES)),
-            whole((nb, WIDTH_OUT, width)),
-        ]
-        + [hbm],
-        scratch_shapes=[VMEM((chunks, rows, LANES), f32), VMEM((rows, width), bf16)]
-        + sum_scratch(8, nd, nz)
-        + pair(nz - 1)
-        + pair((nz - 1) * (nd // 2 - 1)),
-        input_output_aliases={9: 7},
-        compiler_params=params(ident),
-        name="project",
-    )(dpre, mask, side, stats, totals, counts, sq_bias, full_b, mix, *later)
-
-
 def out_norm(sums, total):
     mean = load_wide(sums, 0, WIDTH_OUT) / total
     var = load_wide(sums, OUT_CHUNKS, WIDTH_OUT) / total - mean * mean
     return mean, lax.rsqrt(var + eps_norm)
-
-
-def head_kernel(nd, nz, nb, chunks, shape, kern, proj, mask, mask_rows, counts, gain, route, stats, totals, in_c, low, pre, mixed_out, sums_all, mix_out, gates, pooled, full_c, sums, *comm):
-    j = pl.program_id(0)
-    sems = comm[6:]
-    comm = comm[:6]
-    net = Net(nd, nz)
-
-    def planes():
-        return every(gather_plane, net, shape, full_c, sems[0:2])
-
-    def twins():
-        return every(gather_twin, net, shape, full_c, sems[2:4])
-
-
-    @pl.when(j == 0)
-    def _():
-        sum_start(nd, nz)
-
-    @pl.when(j == 1)
-    def _():
-        met(nd, nz)
-        start(planes())
-
-    @pl.when(j == chunks - 2)
-    def _():
-        arrived(planes())
-        start(twins())
-
-    @pl.when(j == 0)
-    def _():
-        sums[...] = jnp.zeros_like(sums)
-        mean, rstd = out_norm(stats, totals[TOTAL_ROW : TOTAL_ROW + 1, 0:1])
-        scale = rstd * gain[0:1, :]
-        for b in range(nb):
-            at = slice(b * PIXELS, (b + 1) * PIXELS)
-            low[at, :] = (((proj[at, :] - mean) * scale + gain[1:2, :]) * mask[at, 0:1]).astype(bf16)
-        pool = dot(mask_rows[...], low[...]) / jnp.maximum(counts[:, 0:1], 1.0)
-        pooled[...] = pool
-        gate = sig(dot(pool, route[...], NN, highest))
-        gates[...] = gate
-        build_mix(gate, nb, mix_out)
-
-    mixed = mix_kernels(kern[...], mix_out[...])
-    one = jnp.zeros((1, LANES), f32)
-    two = jnp.zeros((1, LANES), f32)
-    for b in range(nb):
-        at = slice(b * PIXELS, (b + 1) * PIXELS)
-        weight = mixed[:, b * LANES : (b + 1) * LANES].astype(bf16)
-        mixed_out[b] = weight
-        value = dot(low[at, :], weight)
-        pre[at, :] = value
-        masked = mask[at, :] * value
-        one = one + rsum(masked)
-        two = two + rsum(masked * value)
-    sums[pl.ds(j, 1), :] = one
-    sums[pl.ds(chunks + j, 1), :] = two
-
-
-    @pl.when(j == chunks - 1)
-    def _():
-        sum_finish(nd, nz, sums, sums_all, *comm)
-        arrived(twins())
-        sent(planes() + twins())
-
-
-def head(kern, proj, mask, mask_rows, counts, gain, route, stats, totals, full_c, nb, nd, nz, ident):
-    rows = proj.shape[0]
-    width = kern.shape[1] // EXPERTS
-    chunks = width // LANES
-    deep = LANES * EXPERTS
-    wide = lambda j: (0, j)
-    return pl.pallas_call(
-        functools.partial(head_kernel, nd, nz, nb, chunks, shard_shape(full_c, nz)),
-        grid=(chunks,),
-        out_shape=[
-            jax.ShapeDtypeStruct((rows, WIDTH_OUT), bf16),
-            jax.ShapeDtypeStruct((rows, width), f32),
-            jax.ShapeDtypeStruct((nb, WIDTH_OUT, width), bf16),
-            jax.ShapeDtypeStruct((24, LANES), f32),
-            jax.ShapeDtypeStruct((deep, 2 * nb * LANES), bf16),
-            jax.ShapeDtypeStruct((8, EXPERTS), f32),
-            jax.ShapeDtypeStruct((8, WIDTH_OUT), f32),
-            jax.ShapeDtypeStruct(full_c.shape, bf16),
-        ],
-        in_specs=[
-            pl.BlockSpec((WIDTH_OUT, deep), wide),
-            whole(proj.shape),
-            whole(mask.shape),
-            whole(mask_rows.shape),
-            whole(counts.shape),
-            whole(gain.shape),
-            whole(route.shape),
-            whole(stats.shape),
-            whole(totals.shape),
-            pl.BlockSpec(memory_space=pltpu.HBM),
-        ],
-        out_specs=[
-            whole((rows, WIDTH_OUT)),
-            pl.BlockSpec((rows, LANES), wide),
-            pl.BlockSpec((nb, WIDTH_OUT, LANES), lambda j: (0, 0, j)),
-            whole((24, LANES)),
-            whole((deep, 2 * nb * LANES)),
-            whole((8, EXPERTS)),
-            whole((8, WIDTH_OUT)),
-            pl.BlockSpec(memory_space=pltpu.HBM),
-        ],
-        scratch_shapes=sum_scratch(24, nd, nz)
-        + pair((nz - 1) * (nd // 2 - 1))
-        + pair(nz - 1),
-        input_output_aliases={9: 7},
-        compiler_params=params(ident),
-        name="head",
-    )(kern, proj, mask, mask_rows, counts, gain, route, stats, totals, full_c)
 
 
 def store_sums(early, late, cut, chunks, j, one, two):
@@ -1398,23 +1268,22 @@
     nb,
     chunks,
     shape,
-    pre,
+    shape_c,
     mask,
+    mask_rows,
     counts,
     labels,
     bias,
-    cls,
     gain,
-    stats,
     totals,
-    low,
+    gain_out,
     kern,
-    mixed,
-    mix,
-    gates,
     route,
     proj,
     proj_stats,
+    in_c,
+    head_pool,
+    stats,
     features,
     grad_logits,
     sums_four,
@@ -1423,6 +1292,15 @@
     dz_out,
     half,
     part,
+    full_c,
+    pre_all,
+    low,
+    mixed,
+    mix,
+    gates,
+    cls,
+    early_head,
+    late_head,
     logits,
     grad_features,
     held,
@@ -1438,14 +1316,53 @@
     j = lax.rem(step, chunks)
     net = Net(nd, nz)
     comm_early, comm_late, comm_two, comm = comm[0:6], comm[6:12], comm[12:18], comm[18:]
+    head_early, head_late, sems, comm = comm[0:6], comm[6:12], comm[12:17], comm[17:]
     twin = Twin(net, shape, half, *comm[0:4])
     plane = Plane(net, shape, half, part, 0, nz // 2, *comm[4:7])
     made = comm[0]
     cut = chunks // 3
-    base = 2 * chunks
+    head_cut = 2 * chunks // 3
+    base = 3 * chunks
     steps = Steps()
-    steps.at(1, lambda: met(nd, nz))
-    places = (chunks + cut, chunks + cut + 3, base, base, base + 1, base + cut)
+
+    def planes():
+        return every(gather_plane, net, shape_c, full_c, sems[0:2])
+
+    def twins():
+        return every(gather_twin, net, shape_c, full_c, sems[2:4])
+
+    def load():
+        own_rows = cls.shape[0] // nz
+        return [
+            pltpu.make_async_copy(
+                full_c.at[k, pl.ds(0, own_rows)], cls.at[pl.ds(k * own_rows, own_rows)], sems[4].at[k]
+            )
+            for k in range(nz)
+        ]
+
+    def begin():
+        met(nd, nz)
+        start(planes())
+
+    def cross():
+        arrived(planes())
+        start(twins())
+
+    def fetch():
+        arrived(twins())
+        start(load())
+
+    def loaded():
+        for copy in load():
+            copy.wait()
+
+    steps.at(1, begin)
+    steps.at(head_cut - 1, cross)
+    steps.at(chunks - 1, fetch)
+    steps.at(chunks, loaded)
+    places = (head_cut, head_cut + 2, chunks, chunks, chunks + 2, chunks + head_cut)
+    split_sum(nd, nz, steps, places, early_head, late_head, stats, head_early, head_late)
+    places = (2 * chunks + cut, 2 * chunks + cut + 3, base, base, base + 1, base + cut)
     split_sum(nd, nz, steps, places, early, late, sums_four, comm_early, comm_late)
     for k in range(nz):
         first = base + ready(shape, k)
@@ -1457,18 +1374,47 @@
     @pl.when(step == 0)
     def _():
         sum_start(nd, nz)
-        for ref in (sums, early, late, features, logits, gate_acc):
+        for ref in (sums, early, late, early_head, late_head, features, logits, gate_acc):
             ref[...] = jnp.zeros_like(ref)
+        mean, rstd = out_norm(proj_stats, totals[TOTAL_ROW : TOTAL_ROW + 1, 0:1])
+        scale = rstd * gain_out[0:1, :]
+        for b in range(nb):
+            at = slice(b * PIXELS, (b + 1) * PIXELS)
+            low[at, :] = (((proj[at, :] - mean) * scale + gain_out[1:2, :]) * mask[at, 0:1]).astype(bf16)
+        pool = dot(mask_rows[...], low[...]) / jnp.maximum(counts[:, 0:1], 1.0)
+        head_pool[...] = pool
+        gate = sig(dot(pool, route[...], NN, highest))
+        gates[...] = gate
+        build_mix(gate, nb, mix)
         if shape[0] > WIDTH_OUT:
             made[WIDTH_OUT:, :] = jnp.zeros((shape[0] - WIDTH_OUT, made.shape[1]), bf16)
 
-    steps.emit(step, 3 * chunks)
+    steps.emit(step, 4 * chunks)
+    pre = pre_all.at[j]
+
+    @pl.when(phase == 0)
+    def _():
+        lane = pl.ds(pl.multiple_of(j * LANES, LANES), LANES)
+        both = mix_kernels(kern[...], mix[...])
+        one = jnp.zeros((1, LANES), f32)
+        two = jnp.zeros((1, LANES), f32)
+        for b in range(nb):
+            at = slice(b * PIXELS, (b + 1) * PIXELS)
+            weight = both[:, b * LANES : (b + 1) * LANES].astype(bf16)
+            mixed[b, :, lane] = weight
+            value = dot(low[at, :], weight)
+            pre[at, :] = value
+            masked = mask[at, :] * value
+            one = one + rsum(masked)
+            two = two + rsum(masked * value)
+        store_sums(early_head, late_head, head_cut, chunks, j, one, two)
+
     lane = pl.ds(pl.multiple_of(j * LANES, LANES), LANES)
     total = totals[TOTAL_ROW : TOTAL_ROW + 1, :]
     mean, rstd = norm_rows(stats, j, chunks, total)
     scale = rstd * gain[0:1, :]
 
-    @pl.when(phase == 0)
+    @pl.when(phase == 1)
     def _():
         for b in range(nb):
             at = slice(b * PIXELS, (b + 1) * PIXELS)
@@ -1479,7 +1425,7 @@
         both = dot(split(features[:, lane]), cls[lane, :])
         logits[...] += both[:8] + both[8:]
 
-    @pl.when((phase == 1) & (j == 0))
+    @pl.when((phase == 2) & (j == 0))
     def _():
         col = lax.broadcasted_iota(jnp.int32, (8, CLASS_PAD), 1)
         inside = col < CLASSES
@@ -1498,7 +1444,7 @@
         weight = valid / totals[TOTAL_ROW + 1 : TOTAL_ROW + 2, 0:1]
         grad_logits[...] = weight * jnp.where(inside, spread / mass - 0.9 * hot - 0.1 / CLASSES, 0.0)
 
-    @pl.when(phase == 1)
+    @pl.when(phase == 2)
     def _():
         both = dot(split(grad_logits[...]), cls[lane, :], NT)
         grads = (both[:8] + both[8:]) / jnp.maximum(counts[...], 1.0)
@@ -1513,7 +1459,7 @@
             two = two + rsum(grad * hat)
         store_sums(early, late, cut, chunks, j, one, two)
 
-    @pl.when(phase == 2)
+    @pl.when(phase == 3)
     def _():
         one = sums_four[pl.ds(j, 1), :] / total
         two = sums_four[pl.ds(chunks + j, 1), :] / total
@@ -1528,7 +1474,7 @@
             gate_acc[b : b + 1, :] += gate_rows(grad_mixed, kern[...])
         made[:WIDTH_OUT, lanes(j * LANES * EXPERTS, LANES * EXPERTS)] = dot(grads[...], mix[:, : nb * LANES], NT).astype(bf16)
 
-    @pl.when(step == 3 * chunks - 1)
+    @pl.when(step == 4 * chunks - 1)
     def _():
         dz = gate_sums(gate_acc[...]) * gates[...] * (1.0 - gates[...])
         dz_out[...] = dz
@@ -1545,9 +1491,11 @@
         store_wide(sums, 0, one)
         store_wide(sums, OUT_CHUNKS, two)
         last = [k for k in range(nz) if ready(shape, k) >= chunks]
+        sum_first(nd, nz, sums, *comm_two)
         for k in last:
             twin.begin(k)
-        sum_finish(nd, nz, sums, sums_all, *comm_two)
+        sum_second(nd, nz, sums, *comm_two)
+        sums_all[...] = sum_third(nd, nz, sums, *comm_two)
         for k in range(nz):
             if ready(shape, k) + 2 >= chunks:
                 twin.add(k)
@@ -1556,18 +1504,23 @@
         plane.add()
         twin.finish()
         plane.finish()
-
-
-def head_back(pre, mask, counts, labels, bias, cls, gain, stats, totals, low, kern, mixed, mix, gates, route, proj, proj_stats, nb, nd, nz, ident):
-    rows, width = pre.shape
+        sent(planes() + twins())
+
+
+def head_stage(mask, mask_rows, counts, labels, bias, gain, totals, gain_out, kern, route, proj, proj_stats, full_c, nb, nd, nz, ident):
+    rows = proj.shape[0]
+    width = kern.shape[1] // EXPERTS
     chunks = width // LANES
     deep = LANES * EXPERTS
     shape = (kern.shape[0], kern.shape[1] // nz)
-    wide = lambda t: (0, lax.rem(t, chunks))
+    hbm = pl.BlockSpec(memory_space=pltpu.HBM)
+    kept = lambda t: (0, jnp.where(t < chunks, t, jnp.maximum(t - 3 * chunks, 0)))
     return pl.pallas_call(
-        functools.partial(head_back_kernel, nd, nz, nb, chunks, shape),
-        grid=(3 * chunks,),
+        functools.partial(head_back_kernel, nd, nz, nb, chunks, shape, shard_shape(full_c, nz)),
+        grid=(4 * chunks,),
         out_shape=[
+            jax.ShapeDtypeStruct((8, WIDTH_OUT), f32),
+            jax.ShapeDtypeStruct((24, LANES), f32),
             jax.ShapeDtypeStruct((8, width), f32),
             jax.ShapeDtypeStruct((8, CLASS_PAD), f32),
             jax.ShapeDtypeStruct((24, LANES), f32),
@@ -1576,27 +1529,26 @@
             jax.ShapeDtypeStruct((8, EXPERTS), f32),
             jax.ShapeDtypeStruct(half_shape(shape, nd, nz), bf16),
             jax.ShapeDtypeStruct(part_shape(shape, nd, nz // 2), bf16),
+            jax.ShapeDtypeStruct(full_c.shape, bf16),
         ],
         in_specs=[
-            pl.BlockSpec((rows, LANES), wide),
             whole(mask.shape),
+            whole(mask_rows.shape),
             whole(counts.shape),
             whole(labels.shape),
             whole(bias.shape),
-            whole(cls.shape),
-            pl.BlockSpec((8, LANES), wide),
-            whole(stats.shape),
+            pl.BlockSpec((8, LANES), lambda t: (0, lax.rem(t, chunks))),
             whole(totals.shape),
-            whole(low.shape),
-            pl.BlockSpec((WIDTH_OUT, deep), lambda t: (0, jnp.maximum(t - 2 * chunks, 0))),
-            whole(mixed.shape),
-            whole(mix.shape),
-            whole(gates.shape),
+            whole(gain_out.shape),
+            pl.BlockSpec((WIDTH_OUT, deep), kept),
             whole(route.shape),
             whole(proj.shape),
             whole(proj_stats.shape),
+            hbm,
         ],
         out_specs=[
+            whole((8, WIDTH_OUT)),
+            whole((24, LANES)),
             whole((8, width)),
             whole((8, CLASS_PAD)),
             whole((24, LANES)),
@@ -1605,8 +1557,17 @@
             whole((8, EXPERTS)),
             whole(half_shape(shape, nd, nz)),
             whole(part_shape(shape, nd, nz // 2)),
+            hbm,
         ],
         scratch_shapes=[
+            VMEM((chunks, rows, LANES), f32),
+            VMEM((rows, WIDTH_OUT), bf16),
+            VMEM((nb, WIDTH_OUT, width), bf16),
+            VMEM((deep, 2 * nb * LANES), bf16),
+            VMEM((8, EXPERTS), f32),
+            VMEM((width, CLASS_PAD), bf16),
+            VMEM((24, LANES), f32),
+            VMEM((24, LANES), f32),
             VMEM((8, CLASS_PAD), f32),
             VMEM((8, width), f32),
             VMEM((rows, width), bf16),
@@ -1618,11 +1579,16 @@
         ]
         + sum_scratch(24, nd, nz)[1:] * 2
         + sum_scratch(8, nd, nz)[1:]
+        + sum_scratch(24, nd, nz)[1:] * 2
+        + pair((nz - 1) * (nd // 2 - 1))
+        + pair(nz - 1)
+        + [pltpu.SemaphoreType.DMA((nz,))]
         + twin_scratch(shape, nd, nz)
         + plane_scratch(shape, nd, nz // 2),
+        input_output_aliases={12: 10},
         compiler_params=params(ident),
-        name="head_back",
-    )(pre, mask, counts, labels, bias, cls, gain, stats, totals, low, kern, mixed, mix, gates, route, proj, proj_stats)
+        name="head_stage",
+    )(mask, mask_rows, counts, labels, bias, gain, totals, gain_out, kern, route, proj, proj_stats, full_c)
 
 
 def project_back_kernel(nd, nz, nb, chunks, shape_h, shape, half_h, part_h, grad_in, proj, proj_stats, proj_sums, gain, mask, counts, totals, stats, side, dpre, excited, mixed, kern, mix, gate, pooled, squeezed, sq_bias, grad_norm, sums_all, grad_squeeze, gate_grad, dz_gate, piece_h, half, part, low, held, grads, gate_acc, sums_h, sums, *comm):
@@ -1951,6 +1917,8 @@
         steps.at(first, functools.partial(twin.begin, k))
         steps.at(first + 1, functools.partial(twin.add, k))
         steps.at(first + 1, functools.partial(plane.begin, k))
+        if first + 4 < 2 * chunks:
+            steps.at(first + 4, functools.partial(plane.add_one, k, far.send))
     steps.at(2 * chunks - 2, up_b.cross)
 
     @pl.when(step == 0)
@@ -2124,14 +2092,18 @@
         for k in range(4):
             low[slots + k : slots + k + 1, :] = row_of(sums[k] * fraction)
             low[slots + 4 + k : slots + 5 + k, :] = squares_w[k : k + 1, :] * fraction
-        plane.add(far.send)
+        for k in range(nz):
+            if chunks + ready(shape, k) + 4 >= 2 * chunks:
+                plane.add_one(k, far.send)
         far.add()
-        up.begin()
         low[slots : slots + 1, :] = row_of(
             squares_of(piece, piece.shape[0]) + squares_of(piece_b, piece_b.shape[0])
         )
-        sum_finish(nd, nz, low, every_sum, *comm_two)
+        sum_first(nd, nz, low, *comm_two)
+        up.begin()
+        sum_second(nd, nz, low, *comm_two)
         up.cross()
+        every_sum[...] = sum_third(nd, nz, low, *comm_two)
         for k in range(4):
             grad_sq_sum = jnp.sum(every_sum[slots + k : slots + k + 1, :], axis=1, keepdims=True)
             weight_sq = jnp.sum(every_sum[slots + 4 + k : slots + 5 + k, :], axis=1, keepdims=True)
@@ -2425,7 +2397,26 @@
     full_a, full_b, side, gain_head, kern_h, kern_c, squares = first_gather(
         block_w, head_w, head_side, chan_side.T, nd, nz, 1
     )
-    pre, taps, dpre, stats_one, stats_two, mix, gates, pooled_in, full_b, full_h, full_c = first_stage(
+    (
+        pre,
+        taps,
+        dpre,
+        stats_one,
+        stats_two,
+        mix,
+        gates,
+        pooled_in,
+        excited,
+        proj,
+        pooled,
+        gate,
+        squeezed,
+        stats_three,
+        mixed_proj,
+        full_b,
+        full_h,
+        full_c,
+    ) = first_stage(
         full_a,
         image_rows,
         mask,
@@ -2433,6 +2424,7 @@
         count_rows,
         route_in,
         side,
+        sq_bias,
         full_b,
         kern_h,
         kern_c,
@@ -2443,31 +2435,20 @@
         3,
     )
     totals = stats_one
-    excited, proj, pooled, gate, squeezed, stats_three, mixed_proj, full_h = project(
-        dpre, mask, side, stats_two, totals, count_rows, sq_bias, full_b, mix, full_h, nb, nd, nz, 5
-    )
-    low, head_pre, mixed_head, stats_four, mix_head, gates_head, head_pool, full_c = head(
-        full_h, proj, mask, mask_rows, count_rows, gain_out, route_head, stats_three, totals, full_c, nb, nd, nz, 6
-    )
-    cls_full = full_c[:, :own_head].reshape(head_width, CLASS_PAD)
-    features, grad_logits, sums_four, grad_proj, sums_three, dz_head, half_h, part_h = head_back(
-        head_pre,
+    head_pool, stats_four, features, grad_logits, sums_four, grad_proj, sums_three, dz_head, half_h, part_h, _ = head_stage(
         mask,
+        mask_rows,
         count_rows,
         label_rows,
         class_bias,
-        cls_full,
         gain_head,
-        stats_four,
         totals,
-        low,
+        gain_out,
         full_h,
-        mixed_head,
-        mix_head,
-        gates_head,
         route_head,
         proj,
         stats_three,
+        full_c,
         nb,
         nd,
         nz,

time: 451 us -> 435 us (0.965)
  Pallas kernels: 430 us -> 414 us
    pallas_call x3 -> x1, Pallas kernels: 129 us -> 88.2 us  [head_stage(): pl.pallas_call(functools.partial(head_back_kernel, nd, nz, nb, chunks, sh...]
    pallas_call x1, Pallas kernels: 59 us -> 88.2 us  [first_stage(): pl.pallas_call(functools.partial(stage_kernel, nd, nz, nb, chunks, shapes...]
where the time goes in v4:
time: 435 us; the launch traced here: 432 us
  Pallas kernels  414 us (95%)
  local copies, waits for them, and re-layouts  13.3 us (3%)
    pallas_call x1, Pallas kernels, stage_back(): pl.pallas_call(functools.partial(stage_back_kernel, nd, nz, nb, chunks, s...  112 us
    pallas_call x1, Pallas kernels, first_stage(): pl.pallas_call(functools.partial(stage_kernel, nd, nz, nb, chunks, shapes...  88.2 us
    pallas_call x1, Pallas kernels, head_stage(): pl.pallas_call(functools.partial(head_back_kernel, nd, nz, nb, chunks, sh...  88.2 us
    pallas_call x1, Pallas kernels, first_gather(): pl.pallas_call(functools.partial(first_kernel, nd, nz, shape, shape_b), o...  50.4 us
    pallas_call x1, Pallas kernels, project_back(): pl.pallas_call(functools.partial(project_back_kernel, nd, nz, nb, chunks,...  50.1 us
    pallas_call x1, Pallas kernels, apply(): pl.pallas_call(apply_kernel, grid=(steps,), out_shape=[jax.ShapeDtypeStru...  24.8 us

profile of v4, /device:TPU:0, one launch (start us, length us, event | category | flops | bytes accessed | tf_op | source)
XLA Modules:
  0.0 432.4 jit_solution(1159261274484404502)
XLA Ops:
  0.7 0.8 convert_bitcast_fusion
  1.5 1.0 broadcast_in_dim.13.mask
  2.6 0.6 pad.16.mask_rows
  3.2 0.7 dynamic-slice_convert_fusion
  4.0 0.7 broadcast_in_dim.14.counts
  4.6 1.0 copy.44
  5.7 50.4 %first_gather.1 = (bf16[256,9216]{1,0:T(8,128)(2,1)}, bf16[320,9216]{1,0:T(8,128)(2,1)}, f32[104,1152]{1,0:T(8,128)}, f32[8,1280]{1,0:T(8,128)}, bf16[320,2560]{...) custom-call(f32[537,2304]{1,0:T(8,128)} %block_w.1, f32[320,2560]{1,0:T(8,128)} %head_w.1, ...), custom_call_target="tpu_custom_call" | custom-call | tf_op jit(solution)/shard_map/first_gather/pallas_call | solution.py:405
  56.5 0.7 reshape.96.route
  57.3 88.2 %first_stage.1 = (f32[1024,1152]{1,0:T(8,128)}, f32[4,32,1152]{2,1,0:T(8,128)}, f32[1024,1152]{1,0:T(8,128)}, f32[24,128]{1,0:T(8,128)}, f32[24,128]{1,0:T(8,128...) custom-call(bf16[256,9216]{1,0:T(8,128)(2,1)} %get-tuple-element.89., ...), custom_call_target="tpu_custom_call", output_to_operand_aliasing={{15}: (8, {})} | custom-call | tf_op jit(solution)/shard_map/first_stage/pallas_call | solution.py:1129
  145.6 0.7 broadcast_in_dim.30.labels
  146.3 0.7 reshape.97.gain_out.gain
  146.9 0.8 reshape.98.route
  147.8 0.6 pad.19
  148.4 88.2 %head_stage.1 = (f32[8,320]{1,0:T(8,128)}, f32[24,128]{1,0:T(8,128)}, f32[8,1280]{1,0:T(8,128)}, f32[8,1024]{1,0:T(8,128)}, f32[24,128]{1,0:T(8,128)}, /*index=5...) custom-call(f32[1024,128]{1,0:T(8,128)} %broadcast_in_dim.13.mask, ...), custom_call_target="tpu_custom_call", output_to_operand_aliasing={{10}: (12, {})} | custom-call | tf_op jit(solution)/shard_map/head_stage/pallas_call | solution.py:1518
  236.6 50.1 %project_back.1 = (f32[1024,1152]{1,0:T(8,128)}, f32[24,128]{1,0:T(8,128)}, f32[8,48]{1,0:T(8,128)}, f32[8,8]{1,0:T(8,128)}, f32[8,1152]{1,0:T(8,128)}, /*index=...) custom-call(bf16[4,320,1280]{2,1,0:T(8,128)(2,1)} %get-tuple-element.99.half_h, ...), custom_call_target="tpu_custom_call" | custom-call | tf_op jit(solution)/shard_map/project_back/pallas_call | solution.py:1711
  286.7 111.9 %stage_back.1 = (bf16[256,2304]{1,0:T(8,128)(2,1)}, bf16[320,2304]{1,0:T(8,128)(2,1)}, bf16[320,2560]{1,0:T(8,128)(2,1)}, f32[320,1024]{1,0:T(8,128)}, f32[288,1...) custom-call(bf16[4,320,1152]{2,1,0:T(8,128)(2,1)} %get-tuple-element, ...), custom_call_target="tpu_custom_call" | custom-call | tf_op jit(solution)/shard_map/stage_back/pallas_call | solution.py:2159
  398.6 1.0 reshape.100
  399.7 1.0 reshape.99
  400.7 0.8 concatenate.3
  401.5 0.6 multiply_reduce_fusion
  402.7 0.6 multiply_reduce_fusion.1
  404.1 0.6 add_multiply_fusion
  404.7 24.8 %apply.1 = (f32[288,101]{1,0:T(8,128)}, f32[288,101]{1,0:T(8,128)}, f32[288,101]{1,0:T(8,128)}, f32[537,2304]{1,0:T(8,128)}, f32[537,2304]{1,0:T(8,128)}, /*inde...) custom-call(f32[8,128]{1,0:T(8,128)} %get-tuple-element.132.factors,, ...), custom_call_target="tpu_custom_call" | custom-call | tf_op jit(solution)/shard_map/apply/pallas_call | solution.py:2330
  429.5 1.2 slice.54
  (40 shorter events, 2.6 us)
Async XLA Ops:
  0.7 4.0 copy-start
  5.6 50.4 %copy-start.2 = (f32[5784]{0:T(1024)S(1)}, f32[5784]{0:T(1024)}, u32[]{:S(2)}) copy-start(f32[5784]{0:T(1024)} %param.30) | copy-start | bytes 69412
  5.7 50.9 %slice-start = ((f32[5784]{0:T(1024)}), f32[1536]{0:T(1024)S(1)}, s32[]{:S(2)}) async-start(f32[5784]{0:T(1024)} %param.30), calls=%async_computation | async-start | bytes 16384 | tf_op jit(solution)/shard_map/slice | solution.py:2378
  57.3 88.2 %copy-start.9 = (s32[16]{0:T(128)S(1)}, s32[16]{0:T(128)}, u32[]{:S(2)}) copy-start(s32[16]{0:T(128)} %param.25) | copy-start | bytes 196
  57.3 89.0 %slice-start.1 = ((f32[5784]{0:T(1024)}), f32[640]{0:T(1024)S(1)}, s32[]{:S(2)}) async-start(f32[5784]{0:T(1024)} %param.30), calls=%async_computation.1 | async-start | bytes 8192 | tf_op jit(solution)/shard_map/slice | solution.py:2380
  286.6 114.0 %copy-start.5 = (f32[8,128]{1,0:T(8,128)S(1)}, f32[8,128]{1,0:T(8,128)}, u32[]{:S(2)}) copy-start(f32[8,128]{1,0:T(8,128)} %get-tuple-element.102.proj_sums) | copy-start | bytes 12292
  286.7 117.4 %copy-start.3 = (f32[5784]{0:T(1024)S(1)}, f32[5784]{0:T(1024)}, u32[]{:S(2)}) copy-start(f32[5784]{0:T(1024)} %param.40) | copy-start | bytes 69412
  286.7 117.4 %copy-start.4 = (f32[5784]{0:T(1024)S(1)}, f32[5784]{0:T(1024)}, u32[]{:S(2)}) copy-start(f32[5784]{0:T(1024)} %param.35) | copy-start | bytes 69412
  404.7 26.0 %copy-start.6 = (f32[4,288]{1,0:T(4,128)S(1)}, f32[4,288]{1,0:T(4,128)}, u32[]{:S(2)}) copy-start(f32[4,288]{1,0:T(4,128)} %get-tuple-element.197) | copy-start | bytes 13828
  404.7 26.6 %copy-start.7 = (f32[2,320]{1,0:T(2,128)S(1)}, f32[2,320]{1,0:T(2,128)}, u32[]{:S(2)}) copy-start(f32[2,320]{1,0:T(2,128)} %get-tuple-element.198) | copy-start | bytes 7684
  404.7 27.2 %copy-start.8 = (f32[2,80]{1,0:T(2,128)S(1)}, f32[2,80]{1,0:T(2,128)}, u32[]{:S(2)}) copy-start(f32[2,80]{1,0:T(2,128)} %get-tuple-element.199) | copy-start | bytes 1924
  404.7 27.7 %copy-start.1 = (bf16[16,256,192]{1,2,0:T(8,128)(2,1)S(1)}, bf16[16,256,192]{1,2,0:T(8,128)(2,1)}, u32[]{:S(2)}) copy-start(bf16[16,256,192]{1,2,0:T(8,128)(2,1)} %param.22) | copy-start | bytes 4718596

commit v5 on v4

--- a/solution.py
+++ b/solution.py
@@ -786,11 +786,21 @@
     return dot(rows, pick, NN, highest)
 
 
-def gate_rows(grad, kernel_block):
-    both = dot(grad, kernel_block, TN)
-    row = lax.broadcasted_iota(jnp.int32, both.shape, 0)
-    col = lax.broadcasted_iota(jnp.int32, both.shape, 1)
-    return rsum(jnp.where(row == (col >> 3), both, 0.0))
+def gate_rows(grads, kernel_block, nb):
+    both = dot(grads, kernel_block, TN)
+    channels = LANES // EXPERTS
+    row = lax.broadcasted_iota(jnp.int32, (channels, LANES), 0)
+    col = lax.broadcasted_iota(jnp.int32, (channels, LANES), 1)
+    same = row == (col >> 3)
+    out = []
+    for b in range(nb):
+        parts = []
+        for m in range(EXPERTS):
+            first = b * LANES + m * channels
+            block = both[first : first + channels, m * LANES : (m + 1) * LANES]
+            parts.append(rsum(jnp.where(same, block, 0.0)))
+        out.append(jnp.concatenate(parts, axis=1))
+    return jnp.concatenate(out, axis=0)
 
 
 def norm_rows(stats, chunk, chunks, total):
@@ -1295,6 +1305,7 @@
     full_c,
     pre_all,
     low,
+    low_t,
     mixed,
     mix,
     gates,
@@ -1381,6 +1392,7 @@
         for b in range(nb):
             at = slice(b * PIXELS, (b + 1) * PIXELS)
             low[at, :] = (((proj[at, :] - mean) * scale + gain_out[1:2, :]) * mask[at, 0:1]).astype(bf16)
+            low_t[b] = jnp.transpose(low[at, :])
         pool = dot(mask_rows[...], low[...]) / jnp.maximum(counts[:, 0:1], 1.0)
         head_pool[...] = pool
         gate = sig(dot(pool, route[...], NN, highest))
@@ -1469,9 +1481,8 @@
             grad = dsilu(hat * gain[0:1, :] + gain[1:2, :]) * grad_features[b : b + 1, lane]
             value = (scale * mask[at, :] * (grad - one - hat * two)).astype(bf16)
             held[at, lane] = value
-            grad_mixed = dot(low[at, :], value, TN).astype(bf16)
-            grads[:, b * LANES : (b + 1) * LANES] = grad_mixed
-            gate_acc[b : b + 1, :] += gate_rows(grad_mixed, kern[...])
+            grads[:, b * LANES : (b + 1) * LANES] = dot(low_t[b], value).astype(bf16)
+        gate_acc[0:nb, :] += gate_rows(grads[...], kern[...], nb)
         made[:WIDTH_OUT, lanes(j * LANES * EXPERTS, LANES * EXPERTS)] = dot(grads[...], mix[:, : nb * LANES], NT).astype(bf16)
 
     @pl.when(step == 4 * chunks - 1)
@@ -1562,6 +1573,7 @@
         scratch_shapes=[
             VMEM((chunks, rows, LANES), f32),
             VMEM((rows, WIDTH_OUT), bf16),
+            VMEM((nb, WIDTH_OUT, PIXELS), bf16),
             VMEM((nb, WIDTH_OUT, width), bf16),
             VMEM((deep, 2 * nb * LANES), bf16),
             VMEM((8, EXPERTS), f32),
@@ -1591,7 +1603,7 @@
     )(mask, mask_rows, counts, labels, bias, gain, totals, gain_out, kern, route, proj, proj_stats, full_c)
 
 
-def project_back_kernel(nd, nz, nb, chunks, shape_h, shape, half_h, part_h, grad_in, proj, proj_stats, proj_sums, gain, mask, counts, totals, stats, side, dpre, excited, mixed, kern, mix, gate, pooled, squeezed, sq_bias, grad_norm, sums_all, grad_squeeze, gate_grad, dz_gate, piece_h, half, part, low, held, grads, gate_acc, sums_h, sums, *comm):
+def project_back_kernel(nd, nz, nb, chunks, shape_h, shape, half_h, part_h, grad_in, proj, proj_stats, proj_sums, gain, mask, counts, totals, stats, side, dpre, excited, mixed, kern, mix, gate, pooled, squeezed, sq_bias, grad_norm, sums_all, grad_squeeze, gate_grad, dz_gate, piece_h, half, part, low, low_t, held, grads, gate_acc, sums_h, sums, *comm):
     phase = pl.program_id(0)
     net = Net(nd, nz)
     few = nz // 2
@@ -1646,6 +1658,7 @@
             at = slice(b * PIXELS, (b + 1) * PIXELS)
             hat = (proj[at, :] - mean) * rstd
             low[at, :] = (scale * (grad_in[at, :] - mask[at, 0:1] * (one + hat * two))).astype(bf16)
+            low_t[b] = jnp.transpose(low[at, :])
 
     mean, rstd = norm_rows(stats, j, chunks, total)
     gain_now = side[2 * SQUEEZE + 2 : 2 * SQUEEZE + 3, :]
@@ -1655,15 +1668,14 @@
     def _():
         for b in range(nb):
             at = slice(b * PIXELS, (b + 1) * PIXELS)
-            grad_mixed = dot(low[at, :], excited[at, :], TN).astype(bf16)
-            grads[:, b * LANES : (b + 1) * LANES] = grad_mixed
-            gate_acc[b : b + 1, :] += gate_rows(grad_mixed, kern[...])
+            grads[:, b * LANES : (b + 1) * LANES] = dot(low_t[b], excited[at, :]).astype(bf16)
             value = dot(low[at, :], mixed[b])
             held[j, at, :] = value
             normed = (dpre[at, :] - mean) * (rstd * gain_now) + bias_now
             act = normed * sig(normed) * mask[at, :]
             now = gate[b : b + 1, :]
             dz_gate[b : b + 1, lane] = rsum(value * act) * now * (1.0 - now)
+        gate_acc[0:nb, :] += gate_rows(grads[...], kern[...], nb)
         made[:WIDTH_OUT, lanes(j * LANES * EXPERTS, LANES * EXPERTS)] = dot(grads[...], mix[:, : nb * LANES], NT).astype(bf16)
         grad_squeeze[...] += dot(dz_gate[:, lane], side[SQUEEZE : 2 * SQUEEZE, :], NT, highest)
 
@@ -1756,6 +1768,7 @@
         ],
         scratch_shapes=[
             VMEM((rows, WIDTH_OUT), bf16),
+            VMEM((nb, WIDTH_OUT, PIXELS), bf16),
             VMEM((chunks, rows, LANES), f32),
             VMEM((WIDTH_OUT, nb * LANES), bf16),
             VMEM((8, deep), f32),
@@ -1846,6 +1859,7 @@
     sums_b,
     piece_b,
     rows_all,
+    images_t,
     grads,
     gate_acc,
     grad_side,
@@ -1932,6 +1946,8 @@
             [grad_sq[...], squeezed, dz_head[...]],
             [logits[...], head_pool[...], pooled_in[...]],
         )
+        for b in range(nb):
+            images_t[b] = jnp.transpose(images[b * PIXELS : (b + 1) * PIXELS, :])
         for ref in (early, late, gate_acc, grads):
             ref[...] = jnp.zeros_like(ref)
 
@@ -2009,9 +2025,9 @@
             lane = slice(b * LANES, (b + 1) * LANES)
             hat = (pre[at, :] - mean) * rstd
             value = (scale * (made_norm[j, at, :] - mask[at, :] * (one + hat * two))).astype(bf16)
-            grads[0:WIDTH_IN, lane] = dot(images[at, :], value, TN).astype(bf16)
+            grads[0:WIDTH_IN, lane] = dot(images_t[b], value).astype(bf16)
             grads[WIDTH_IN : WIDTH_IN + 32, lane] = tap_grads[j, b].astype(bf16)
-            gate_acc[b : b + 1, :] += gate_rows(grads[:, lane], kern[...])
+        gate_acc[0:nb, :] += gate_rows(grads[...], kern[...], nb)
         made[:, lanes(j * LANES * EXPERTS, LANES * EXPERTS)] = dot(grads[...], mix[:, : nb * LANES], NT).astype(bf16)
 
     @pl.when(step == 2 * chunks - 1)
@@ -2200,6 +2216,7 @@
             VMEM(part_shape(shape_b, nd, nz), bf16),
             VMEM(piece_shape(shape_b, nd), bf16),
             VMEM((devices, 8, wide), f32),
+            VMEM((nb, WIDTH_IN, PIXELS), bf16),
             VMEM((kern.shape[0], nb * LANES), bf16),
             VMEM((8, deep), f32),
             VMEM((104, up_to(own)), f32),

time: 435 us -> 427 us (0.982)
  Pallas kernels: 414 us -> 406 us
    pallas_call x1, Pallas kernels: 112 us -> 107 us  [stage_back(): pl.pallas_call(functools.partial(stage_back_kernel, nd, nz, nb, chunks, s...]
where the time goes in v5:
time: 427 us; the launch traced here: 425 us
  Pallas kernels  406 us (95%)
  local copies, waits for them, and re-layouts  13.3 us (3%)
    pallas_call x1, Pallas kernels, stage_back(): pl.pallas_call(functools.partial(stage_back_kernel, nd, nz, nb, chunks, s...  107 us
    pallas_call x1, Pallas kernels, first_stage(): pl.pallas_call(functools.partial(stage_kernel, nd, nz, nb, chunks, shapes...  88.2 us
    pallas_call x1, Pallas kernels, head_stage(): pl.pallas_call(functools.partial(head_back_kernel, nd, nz, nb, chunks, sh...  86.2 us
    pallas_call x1, Pallas kernels, first_gather(): pl.pallas_call(functools.partial(first_kernel, nd, nz, shape, shape_b), o...  50.4 us
    pallas_call x1, Pallas kernels, project_back(): pl.pallas_call(functools.partial(project_back_kernel, nd, nz, nb, chunks,...  49.6 us
    pallas_call x1, Pallas kernels, apply(): pl.pallas_call(apply_kernel, grid=(steps,), out_shape=[jax.ShapeDtypeStru...  24.8 us

profile of v5, /device:TPU:0, one launch (start us, length us, event | category | flops | bytes accessed | tf_op | source)
XLA Modules:
  0.0 424.7 jit_solution(15810299498663355870)
XLA Ops:
  0.7 0.8 convert_bitcast_fusion
  1.5 1.0 broadcast_in_dim.13.mask
  2.6 0.6 pad.16.mask_rows
  3.2 0.7 dynamic-slice_convert_fusion
  4.0 0.7 broadcast_in_dim.14.counts
  4.6 1.0 copy.44
  5.7 50.4 %first_gather.1 = (bf16[256,9216]{1,0:T(8,128)(2,1)}, bf16[320,9216]{1,0:T(8,128)(2,1)}, f32[104,1152]{1,0:T(8,128)}, f32[8,1280]{1,0:T(8,128)}, bf16[320,2560]{...) custom-call(f32[537,2304]{1,0:T(8,128)} %block_w.1, f32[320,2560]{1,0:T(8,128)} %head_w.1, ...), custom_call_target="tpu_custom_call" | custom-call | tf_op jit(solution)/shard_map/first_gather/pallas_call | solution.py:405
  56.5 0.7 reshape.96.route
  57.3 88.2 %first_stage.1 = (f32[1024,1152]{1,0:T(8,128)}, f32[4,32,1152]{2,1,0:T(8,128)}, f32[1024,1152]{1,0:T(8,128)}, f32[24,128]{1,0:T(8,128)}, f32[24,128]{1,0:T(8,128...) custom-call(bf16[256,9216]{1,0:T(8,128)(2,1)} %get-tuple-element.89., ...), custom_call_target="tpu_custom_call", output_to_operand_aliasing={{15}: (8, {})} | custom-call | tf_op jit(solution)/shard_map/first_stage/pallas_call | solution.py:1139
  145.6 0.7 broadcast_in_dim.30.labels
  146.3 0.7 reshape.97.gain_out.gain
  146.9 0.8 reshape.98.route
  147.8 0.6 pad.19
  148.4 86.2 %head_stage.1 = (f32[8,320]{1,0:T(8,128)}, f32[24,128]{1,0:T(8,128)}, f32[8,1280]{1,0:T(8,128)}, f32[8,1024]{1,0:T(8,128)}, f32[24,128]{1,0:T(8,128)}, /*index=5...) custom-call(f32[1024,128]{1,0:T(8,128)} %broadcast_in_dim.13.mask, ...), custom_call_target="tpu_custom_call", output_to_operand_aliasing={{10}: (12, {})} | custom-call | tf_op jit(solution)/shard_map/head_stage/pallas_call | solution.py:1529
  234.6 49.6 %project_back.1 = (f32[1024,1152]{1,0:T(8,128)}, f32[24,128]{1,0:T(8,128)}, f32[8,48]{1,0:T(8,128)}, f32[8,8]{1,0:T(8,128)}, f32[8,1152]{1,0:T(8,128)}, /*index=...) custom-call(bf16[4,320,1280]{2,1,0:T(8,128)(2,1)} %get-tuple-element.99.half_h, ...), custom_call_target="tpu_custom_call" | custom-call | tf_op jit(solution)/shard_map/project_back/pallas_call | solution.py:1723
  284.2 106.7 %stage_back.1 = (bf16[256,2304]{1,0:T(8,128)(2,1)}, bf16[320,2304]{1,0:T(8,128)(2,1)}, bf16[320,2560]{1,0:T(8,128)(2,1)}, f32[320,1024]{1,0:T(8,128)}, f32[288,1...) custom-call(bf16[4,320,1152]{2,1,0:T(8,128)(2,1)} %get-tuple-element, ...), custom_call_target="tpu_custom_call" | custom-call | tf_op jit(solution)/shard_map/stage_back/pallas_call | solution.py:2175
  390.9 1.0 reshape.100
  391.9 1.0 reshape.99
  392.9 0.8 concatenate.3
  393.7 0.6 multiply_reduce_fusion
  395.0 0.6 multiply_reduce_fusion.1
  396.3 0.6 add_multiply_fusion
  397.0 24.8 %apply.1 = (f32[288,101]{1,0:T(8,128)}, f32[288,101]{1,0:T(8,128)}, f32[288,101]{1,0:T(8,128)}, f32[537,2304]{1,0:T(8,128)}, f32[537,2304]{1,0:T(8,128)}, /*inde...) custom-call(f32[8,128]{1,0:T(8,128)} %get-tuple-element.132.factors,, ...), custom_call_target="tpu_custom_call" | custom-call | tf_op jit(solution)/shard_map/apply/pallas_call | solution.py:2347
  421.8 1.2 slice.54
  (40 shorter events, 2.6 us)
Async XLA Ops:
  0.7 4.0 copy-start
  5.6 50.4 %copy-start.2 = (f32[5784]{0:T(1024)S(1)}, f32[5784]{0:T(1024)}, u32[]{:S(2)}) copy-start(f32[5784]{0:T(1024)} %param.30) | copy-start | bytes 69412
  5.7 50.9 %slice-start = ((f32[5784]{0:T(1024)}), f32[1536]{0:T(1024)S(1)}, s32[]{:S(2)}) async-start(f32[5784]{0:T(1024)} %param.30), calls=%async_computation | async-start | bytes 16384 | tf_op jit(solution)/shard_map/slice | solution.py:2395
  57.3 88.2 %copy-start.9 = (s32[16]{0:T(128)S(1)}, s32[16]{0:T(128)}, u32[]{:S(2)}) copy-start(s32[16]{0:T(128)} %param.25) | copy-start | bytes 196
  57.3 89.0 %slice-start.1 = ((f32[5784]{0:T(1024)}), f32[640]{0:T(1024)S(1)}, s32[]{:S(2)}) async-start(f32[5784]{0:T(1024)} %param.30), calls=%async_computation.1 | async-start | bytes 8192 | tf_op jit(solution)/shard_map/slice | solution.py:2397
  284.1 108.8 %copy-start.5 = (f32[8,128]{1,0:T(8,128)S(1)}, f32[8,128]{1,0:T(8,128)}, u32[]{:S(2)}) copy-start(f32[8,128]{1,0:T(8,128)} %get-tuple-element.102.proj_sums) | copy-start | bytes 12292
  284.1 112.1 %copy-start.3 = (f32[5784]{0:T(1024)S(1)}, f32[5784]{0:T(1024)}, u32[]{:S(2)}) copy-start(f32[5784]{0:T(1024)} %param.40) | copy-start | bytes 69412
  284.2 112.1 %copy-start.4 = (f32[5784]{0:T(1024)S(1)}, f32[5784]{0:T(1024)}, u32[]{:S(2)}) copy-start(f32[5784]{0:T(1024)} %param.35) | copy-start | bytes 69412
  396.9 26.0 %copy-start.6 = (f32[4,288]{1,0:T(4,128)S(1)}, f32[4,288]{1,0:T(4,128)}, u32[]{:S(2)}) copy-start(f32[4,288]{1,0:T(4,128)} %get-tuple-element.197) | copy-start | bytes 13828
  397.0 26.6 %copy-start.7 = (f32[2,320]{1,0:T(2,128)S(1)}, f32[2,320]{1,0:T(2,128)}, u32[]{:S(2)}) copy-start(f32[2,320]{1,0:T(2,128)} %get-tuple-element.198) | copy-start | bytes 7684
  397.0 27.2 %copy-start.8 = (f32[2,80]{1,0:T(2,128)S(1)}, f32[2,80]{1,0:T(2,128)}, u32[]{:S(2)}) copy-start(f32[2,80]{1,0:T(2,128)} %get-tuple-element.199) | copy-start | bytes 1924
  397.0 27.7 %copy-start.1 = (bf16[16,256,192]{1,2,0:T(8,128)(2,1)S(1)}, bf16[16,256,192]{1,2,0:T(8,128)(2,1)}, u32[]{:S(2)}) copy-start(bf16[16,256,192]{1,2,0:T(8,128)(2,1)} %param.22) | copy-start | bytes 4718596

commit v6 on v5

--- a/solution.py
+++ b/solution.py
@@ -1921,11 +1921,11 @@
         comm_early,
         comm_late,
     )
-    steps.at(cut + 1, more_planes)
+    steps.at(2, more_planes)
     steps.at(cut + 2, share.plane)
-    steps.at(chunks + 1, functools.partial(plane_b.add, far_b.send))
+    steps.at(chunks - 2, functools.partial(plane_b.add, far_b.send))
     steps.at(chunks + 2, share.twin)
-    steps.at(chunks + 3, far_end)
+    steps.at(chunks, far_end)
     for k in range(nz):
         first = chunks + ready(shape, k)
         steps.at(first, functools.partial(twin.begin, k))

time: 427 us -> 424 us (level)
  no operation moved by 1% of the time
where the time goes in v6:
time: 424 us; the launch traced here: 423 us
  Pallas kernels  404 us (95%)
  local copies, waits for them, and re-layouts  13.3 us (3%)
    pallas_call x1, Pallas kernels, stage_back(): pl.pallas_call(functools.partial(stage_back_kernel, nd, nz, nb, chunks, s...  105 us
    pallas_call x1, Pallas kernels, first_stage(): pl.pallas_call(functools.partial(stage_kernel, nd, nz, nb, chunks, shapes...  88.2 us
    pallas_call x1, Pallas kernels, head_stage(): pl.pallas_call(functools.partial(head_back_kernel, nd, nz, nb, chunks, sh...  86.2 us
    pallas_call x1, Pallas kernels, first_gather(): pl.pallas_call(functools.partial(first_kernel, nd, nz, shape, shape_b), o...  50.4 us
    pallas_call x1, Pallas kernels, project_back(): pl.pallas_call(functools.partial(project_back_kernel, nd, nz, nb, chunks,...  49.6 us
    pallas_call x1, Pallas kernels, apply(): pl.pallas_call(apply_kernel, grid=(steps,), out_shape=[jax.ShapeDtypeStru...  24.8 us

profile of v6, /device:TPU:0, one launch (start us, length us, event | category | flops | bytes accessed | tf_op | source)
XLA Modules:
  0.0 422.9 jit_solution(15652305457716082735)
XLA Ops:
  0.7 0.8 convert_bitcast_fusion
  1.5 1.0 broadcast_in_dim.13.mask
  2.6 0.6 pad.16.mask_rows
  3.2 0.7 dynamic-slice_convert_fusion
  4.0 0.7 broadcast_in_dim.14.counts
  4.6 1.0 copy.44
  5.7 50.4 %first_gather.1 = (bf16[256,9216]{1,0:T(8,128)(2,1)}, bf16[320,9216]{1,0:T(8,128)(2,1)}, f32[104,1152]{1,0:T(8,128)}, f32[8,1280]{1,0:T(8,128)}, bf16[320,2560]{...) custom-call(f32[537,2304]{1,0:T(8,128)} %block_w.1, f32[320,2560]{1,0:T(8,128)} %head_w.1, ...), custom_call_target="tpu_custom_call" | custom-call | tf_op jit(solution)/shard_map/first_gather/pallas_call | solution.py:405
  56.5 0.7 reshape.96.route
  57.3 88.2 %first_stage.1 = (f32[1024,1152]{1,0:T(8,128)}, f32[4,32,1152]{2,1,0:T(8,128)}, f32[1024,1152]{1,0:T(8,128)}, f32[24,128]{1,0:T(8,128)}, f32[24,128]{1,0:T(8,128...) custom-call(bf16[256,9216]{1,0:T(8,128)(2,1)} %get-tuple-element.89., ...), custom_call_target="tpu_custom_call", output_to_operand_aliasing={{15}: (8, {})} | custom-call | tf_op jit(solution)/shard_map/first_stage/pallas_call | solution.py:1139
  145.6 0.7 broadcast_in_dim.30.labels
  146.3 0.7 reshape.97.gain_out.gain
  146.9 0.8 reshape.98.route
  147.8 0.6 pad.19
  148.4 86.2 %head_stage.1 = (f32[8,320]{1,0:T(8,128)}, f32[24,128]{1,0:T(8,128)}, f32[8,1280]{1,0:T(8,128)}, f32[8,1024]{1,0:T(8,128)}, f32[24,128]{1,0:T(8,128)}, /*index=5...) custom-call(f32[1024,128]{1,0:T(8,128)} %broadcast_in_dim.13.mask, ...), custom_call_target="tpu_custom_call", output_to_operand_aliasing={{10}: (12, {})} | custom-call | tf_op jit(solution)/shard_map/head_stage/pallas_call | solution.py:1529
  234.6 49.6 %project_back.1 = (f32[1024,1152]{1,0:T(8,128)}, f32[24,128]{1,0:T(8,128)}, f32[8,48]{1,0:T(8,128)}, f32[8,8]{1,0:T(8,128)}, f32[8,1152]{1,0:T(8,128)}, /*index=...) custom-call(bf16[4,320,1280]{2,1,0:T(8,128)(2,1)} %get-tuple-element.99.half_h, ...), custom_call_target="tpu_custom_call" | custom-call | tf_op jit(solution)/shard_map/project_back/pallas_call | solution.py:1723
  284.2 104.9 %stage_back.1 = (bf16[256,2304]{1,0:T(8,128)(2,1)}, bf16[320,2304]{1,0:T(8,128)(2,1)}, bf16[320,2560]{1,0:T(8,128)(2,1)}, f32[320,1024]{1,0:T(8,128)}, f32[288,1...) custom-call(bf16[4,320,1152]{2,1,0:T(8,128)(2,1)} %get-tuple-element, ...), custom_call_target="tpu_custom_call" | custom-call | tf_op jit(solution)/shard_map/stage_back/pallas_call | solution.py:2175
  389.0 1.0 reshape.100
  390.1 1.0 reshape.99
  391.1 0.8 concatenate.3
  391.9 0.6 multiply_reduce_fusion
  393.2 0.6 multiply_reduce_fusion.1
  394.5 0.6 add_multiply_fusion
  395.1 24.8 %apply.1 = (f32[288,101]{1,0:T(8,128)}, f32[288,101]{1,0:T(8,128)}, f32[288,101]{1,0:T(8,128)}, f32[537,2304]{1,0:T(8,128)}, f32[537,2304]{1,0:T(8,128)}, /*inde...) custom-call(f32[8,128]{1,0:T(8,128)} %get-tuple-element.132.factors,, ...), custom_call_target="tpu_custom_call" | custom-call | tf_op jit(solution)/shard_map/apply/pallas_call | solution.py:2347
  419.9 1.2 slice.54
  (40 shorter events, 2.6 us)
Async XLA Ops:
  0.7 4.0 copy-start
  5.6 50.4 %copy-start.2 = (f32[5784]{0:T(1024)S(1)}, f32[5784]{0:T(1024)}, u32[]{:S(2)}) copy-start(f32[5784]{0:T(1024)} %param.30) | copy-start | bytes 69412
  5.7 50.9 %slice-start = ((f32[5784]{0:T(1024)}), f32[1536]{0:T(1024)S(1)}, s32[]{:S(2)}) async-start(f32[5784]{0:T(1024)} %param.30), calls=%async_computation | async-start | bytes 16384 | tf_op jit(solution)/shard_map/slice | solution.py:2395
  57.3 88.2 %copy-start.9 = (s32[16]{0:T(128)S(1)}, s32[16]{0:T(128)}, u32[]{:S(2)}) copy-start(s32[16]{0:T(128)} %param.25) | copy-start | bytes 196
  57.3 89.0 %slice-start.1 = ((f32[5784]{0:T(1024)}), f32[640]{0:T(1024)S(1)}, s32[]{:S(2)}) async-start(f32[5784]{0:T(1024)} %param.30), calls=%async_computation.1 | async-start | bytes 8192 | tf_op jit(solution)/shard_map/slice | solution.py:2397
  284.1 106.9 %copy-start.5 = (f32[8,128]{1,0:T(8,128)S(1)}, f32[8,128]{1,0:T(8,128)}, u32[]{:S(2)}) copy-start(f32[8,128]{1,0:T(8,128)} %get-tuple-element.102.proj_sums) | copy-start | bytes 12292
  284.1 110.3 %copy-start.3 = (f32[5784]{0:T(1024)S(1)}, f32[5784]{0:T(1024)}, u32[]{:S(2)}) copy-start(f32[5784]{0:T(1024)} %param.40) | copy-start | bytes 69412
  284.2 110.3 %copy-start.4 = (f32[5784]{0:T(1024)S(1)}, f32[5784]{0:T(1024)}, u32[]{:S(2)}) copy-start(f32[5784]{0:T(1024)} %param.35) | copy-start | bytes 69412
  395.1 26.0 %copy-start.6 = (f32[4,288]{1,0:T(4,128)S(1)}, f32[4,288]{1,0:T(4,128)}, u32[]{:S(2)}) copy-start(f32[4,288]{1,0:T(4,128)} %get-tuple-element.197) | copy-start | bytes 13828
  395.1 26.6 %copy-start.7 = (f32[2,320]{1,0:T(2,128)S(1)}, f32[2,320]{1,0:T(2,128)}, u32[]{:S(2)}) copy-start(f32[2,320]{1,0:T(2,128)} %get-tuple-element.198) | copy-start | bytes 7684
  395.1 27.2 %copy-start.8 = (f32[2,80]{1,0:T(2,128)S(1)}, f32[2,80]{1,0:T(2,128)}, u32[]{:S(2)}) copy-start(f32[2,80]{1,0:T(2,128)} %get-tuple-element.199) | copy-start | bytes 1924
  395.1 27.7 %copy-start.1 = (bf16[16,256,192]{1,2,0:T(8,128)(2,1)S(1)}, bf16[16,256,192]{1,2,0:T(8,128)(2,1)}, u32[]{:S(2)}) copy-start(bf16[16,256,192]{1,2,0:T(8,128)(2,1)} %param.22) | copy-start | bytes 4718596
